TPU v7x, 32 devices: a whole 2x2x4 slice. The times are simulated.
32 devices in a mesh: ctx: 16 (over z, y, x), wsh: 2 (over core).
Axes of the slice: x: 2, y: 2, z: 4, core: 2. Of those that a mesh axis runs over, the one named last changes fastest.
Arguments:
- inputs: bfloat16 [2, 2048, 1024], P('wsh', 'ctx'), may hold values from -6 to 6
- encoder: bfloat16 [2, 256, 1024], P('wsh', 'ctx'), may hold values from -6 to 6
- cotangent: bfloat16 [2, 2048, 1024], P('wsh', 'ctx'), may hold values from -6 to 6
- block_order: int32 [32], replicated, may hold values from 0 to 31, as said below
- bucket_of: int32 [2048], replicated, may hold values from 0 to 31, as said below
- self_gain: bfloat16 [1024], P('wsh'), may hold values from 0.5 to 1.5
- query_weight: bfloat16 [1024, 1024], P('wsh'), may hold values from -0.0234375 to 0.0234375
- key_weight: bfloat16 [1024, 1024], P('wsh'), may hold values from -0.1875 to 0.1875
- value_weight: bfloat16 [1024, 1024], P('wsh'), may hold values from -0.1875 to 0.1875
- out_weight: bfloat16 [1024, 1024], P('wsh'), may hold values from -6 to 6
- bias_table: bfloat16 [32, 16], P('wsh'), may hold values from -6 to 6
- cross_gain: bfloat16 [1024], P('wsh'), may hold values from 0.5 to 1.5
- cross_query: bfloat16 [1024, 1024], P('wsh'), may hold values from -0.0234375 to 0.0234375
- cross_key: bfloat16 [1024, 1024], P('wsh'), may hold values from -0.1875 to 0.1875
- cross_value: bfloat16 [1024, 1024], P('wsh'), may hold values from -0.1875 to 0.1875
- cross_out: bfloat16 [1024, 1024], P('wsh'), may hold values from -6 to 6
- mlp_gain: bfloat16 [1024], P('wsh'), may hold values from 0.5 to 1.5
- gate_weight: bfloat16 [1024, 2816], P('wsh'), may hold values from -0.1875 to 0.1875
- up_weight: bfloat16 [1024, 2816], P('wsh'), may hold values from -0.1875 to 0.1875
- down_weight: bfloat16 [2816, 1024], P('wsh'), may hold values from -0.109375 to 0.109375
Outputs:
- output: bfloat16 [2, 2048, 1024], P('wsh', 'ctx')
- input_grad: bfloat16 [2, 2048, 1024], P('wsh', 'ctx')
- encoder_grad: bfloat16 [2, 256, 1024], P('wsh', 'ctx')
- self_gain_grad: float32 [1024], P('wsh')
- query_weight_grad: float32 [1024, 1024], P('wsh')
- key_weight_grad: float32 [1024, 1024], P('wsh')
- value_weight_grad: float32 [1024, 1024], P('wsh')
- out_weight_grad: float32 [1024, 1024], P('wsh')
- bias_table_grad: float32 [32, 16], P('wsh')
- cross_gain_grad: float32 [1024], P('wsh')
- cross_query_grad: float32 [1024, 1024], P('wsh')
- cross_key_grad: float32 [1024, 1024], P('wsh')
- cross_value_grad: float32 [1024, 1024], P('wsh')
- cross_out_grad: float32 [1024, 1024], P('wsh')
- mlp_gain_grad: float32 [1024], P('wsh')
- gate_weight_grad: float32 [1024, 2816], P('wsh')
- up_weight_grad: float32 [1024, 2816], P('wsh')
- down_weight_grad: float32 [2816, 1024], P('wsh')
Inputs may be any that keep to these rules, and one draw needn't show every extreme that they name: The device at index c of ctx holds stored blocks 2c and 2c + 1; their position blocks are j and 31 - j for one j, each j of 0 to 15 at one device; block_order is a permutation. `bucket_of`: nondecreasing in the offset, 0 at offset 0, every bucket used.
All inputs are finite; a program needn't handle non-finite values.
Results may differ from a plain program's by a relative error of at most 0.024.
Values may be sent and summed in bfloat16 or wider, within the bound.
A program may use at most 448 MiB of HBM per device.

v0:
```python
import jax
import jax.numpy as jnp
from jax import lax
from jax.sharding import PartitionSpec as P

HEADS = 16
HEAD_DIM = 64
BUCKETS = 32


EPSILON = 1e-06
NEG_BIG = -1e30


def rms_norm(values, gain):
    return values * lax.rsqrt(jnp.mean(values * values, axis=-1, keepdims=True) + EPSILON) * gain


def plain_dot(left, right):
    return jnp.dot(left, right, preferred_element_type=jnp.float32)


def left_contract(left, right):
    return lax.dot_general(
        left, right, (((0,), (0,)), ((), ())), preferred_element_type=jnp.float32
    )


def right_contract(left, right):
    return lax.dot_general(
        left, right, (((1,), (1,)), ((), ())), preferred_element_type=jnp.float32
    )


def gelu_product(gate_vals, up_vals):
    return jax.nn.gelu(gate_vals, approximate=True) * up_vals


def norm_back(values, gain, cotan):
    normed, pullback = jax.vjp(rms_norm, values, gain)
    return pullback(cotan)


def lookup_positions(block_order, first_row, row_count, block_len):
    token_ids = first_row + jnp.arange(row_count, dtype=jnp.int32)
    block_ids = token_ids // block_len
    matches = block_ids[:, None] == jnp.arange(block_order.shape[0], dtype=jnp.int32)[None, :]
    starts = jnp.sum(jnp.where(matches, block_order[None, :], 0), axis=1)
    return starts * block_len + token_ids % block_len


def fold_groups(step_fn, carried, pieces, shard_rows):
    piece_rows = pieces[0].shape[0]
    shards = max(1, piece_rows // shard_rows)
    group_limit = max(1, 1152 // shard_rows)
    group_size = max(
        (divisor for divisor in range(1, min(shards, group_limit) + 1) if shards % divisor == 0)
    )
    group_rows = group_size * shard_rows

    def group_step(group_idx, inner_state):
        sub_pieces = tuple(
            (
                lax.dynamic_slice_in_dim(member, group_idx * group_rows, group_rows, 0)
                for member in pieces
            )
        )
        return step_fn(inner_state, sub_pieces, group_idx * group_rows)

    return lax.fori_loop(0, shards // group_size, group_step, carried)


def on_device(
    inputs,
    encoder,
    cotangent,
    block_order,
    bucket_of,
    self_gain,
    query_weight,
    key_weight,
    value_weight,
    out_weight,
    bias_table,
    cross_gain,
    cross_query,
    cross_key,
    cross_value,
    cross_out,
    mlp_gain,
    gate_weight,
    up_weight,
    down_weight,
):
    (
        gain_one,
        query_full,
        key_full,
        value_full,
        out_full,
        bias_rows,
        gain_two,
        cross_query_full,
        cross_key_full,
        cross_value_full,
        cross_out_full,
        gain_three,
        gate_full,
        up_full,
        down_full,
    ) = (
        lax.all_gather(self_gain, "wsh", axis=0, tiled=True),
        lax.all_gather(query_weight, "wsh", axis=0, tiled=True),
        lax.all_gather(key_weight, "wsh", axis=0, tiled=True),
        lax.all_gather(value_weight, "wsh", axis=0, tiled=True),
        lax.all_gather(out_weight, "wsh", axis=0, tiled=True),
        lax.all_gather(bias_table, "wsh", axis=0, tiled=True),
        lax.all_gather(cross_gain, "wsh", axis=0, tiled=True),
        lax.all_gather(cross_query, "wsh", axis=0, tiled=True),
        lax.all_gather(cross_key, "wsh", axis=0, tiled=True),
        lax.all_gather(cross_value, "wsh", axis=0, tiled=True),
        lax.all_gather(cross_out, "wsh", axis=0, tiled=True),
        lax.all_gather(mlp_gain, "wsh", axis=0, tiled=True),
        lax.all_gather(gate_weight, "wsh", axis=0, tiled=True),
        lax.all_gather(up_weight, "wsh", axis=0, tiled=True),
        lax.all_gather(down_weight, "wsh", axis=0, tiled=True),
    )
    gain_one = gain_one.astype(jnp.float32)
    gain_two = gain_two.astype(jnp.float32)
    gain_three = gain_three.astype(jnp.float32)
    resid_in = inputs[0].astype(jnp.float32)
    tokens = resid_in.shape[0]
    block_len = tokens // 2
    head_width = HEADS * HEAD_DIM
    total_rows = tokens * lax.axis_size("ctx")
    own_pos = lookup_positions(block_order, lax.axis_index("ctx") * tokens, tokens, block_len)
    bucket_ids = jnp.arange(BUCKETS, dtype=jnp.int32)
    boundaries = jnp.sum((bucket_of[None, :] < bucket_ids[1:, None]).astype(jnp.int32), axis=1)

    def bucket_indicator_of(clipped):
        bucket = jnp.sum((clipped[None] >= boundaries[:, None, None]).astype(jnp.int32), axis=0)
        return (bucket[None] == bucket_ids[:, None, None]).astype(jnp.bfloat16)

    def query_key_logits(query_heads, key_heads, query_pos, key_pos):
        logits = jnp.einsum(
            "qhe,khe->hqk", query_heads, key_heads, preferred_element_type=jnp.float32
        )
        offset = query_pos[:, None] - key_pos[None, :]
        clipped = jnp.maximum(offset, 0)
        indicator = bucket_indicator_of(clipped)
        rel_bias = jnp.einsum(
            "ouw,om->muw", indicator, bias_rows, preferred_element_type=jnp.float32
        )
        allowed = (offset >= 0)[None]
        return (jnp.where(allowed, logits + rel_bias, NEG_BIG), allowed, indicator)

    normed_one = rms_norm(resid_in, gain_one).astype(jnp.bfloat16)
    query_heads = (
        plain_dot(normed_one, query_full).astype(jnp.bfloat16).reshape(tokens, HEADS, HEAD_DIM)
    )
    key_heads = (
        plain_dot(normed_one, key_full).astype(jnp.bfloat16).reshape(tokens, HEADS, HEAD_DIM)
    )
    value_heads = (
        plain_dot(normed_one, value_full).astype(jnp.bfloat16).reshape(tokens, HEADS, HEAD_DIM)
    )

    def norm_step(carried, pieces, first_row):
        running_max, running_sum = carried
        key_pos = lookup_positions(block_order, first_row, pieces[0].shape[0], block_len)
        logits, allowed, indicator = query_key_logits(query_heads, pieces[0], own_pos, key_pos)
        new_max = jnp.maximum(running_max, jnp.max(logits, axis=-1))
        kept = jnp.where(allowed, jnp.exp(logits - new_max[..., None]), 0.0)
        return (new_max, running_sum * jnp.exp(running_max - new_max) + jnp.sum(kept, axis=-1))

    start_state = (
        jnp.full((HEADS, tokens), NEG_BIG, jnp.float32),
        jnp.zeros((HEADS, tokens), jnp.float32),
    )
    running_max, running_sum = fold_groups(
        norm_step, start_state, (lax.all_gather(key_heads, "ctx", axis=0, tiled=True),), tokens
    )
    log_norm = running_max + jnp.log(running_sum)

    def output_step(carried, pieces, first_row):
        key_pos = lookup_positions(block_order, first_row, pieces[0].shape[0], block_len)
        logits, allowed, indicator = query_key_logits(query_heads, pieces[0], own_pos, key_pos)
        attn_probs = jnp.exp(logits - log_norm[..., None]).astype(jnp.bfloat16)
        return carried + jnp.einsum(
            "hqk,khe->qhe", attn_probs, pieces[1], preferred_element_type=jnp.float32
        )

    zero_heads = jnp.zeros((tokens, HEADS, HEAD_DIM), jnp.float32)
    attn_sum = fold_groups(
        output_step,
        zero_heads,
        (
            lax.all_gather(key_heads, "ctx", axis=0, tiled=True),
            lax.all_gather(value_heads, "ctx", axis=0, tiled=True),
        ),
        tokens,
    )
    attended = attn_sum.reshape(tokens, head_width).astype(jnp.bfloat16)
    after_self = resid_in + plain_dot(attended, out_full)
    normed_two = rms_norm(after_self, gain_two).astype(jnp.bfloat16)
    cross_q_heads = (
        plain_dot(normed_two, cross_query_full)
        .astype(jnp.bfloat16)
        .reshape(tokens, HEADS, HEAD_DIM)
    )
    encoder_rows = encoder[0]
    encoder_key_rows, cross_values = (
        lax.all_gather(
            plain_dot(encoder_rows, cross_key_full).astype(jnp.bfloat16), "ctx", axis=0, tiled=True
        ),
        lax.all_gather(
            plain_dot(encoder_rows, cross_value_full).astype(jnp.bfloat16),
            "ctx",
            axis=0,
            tiled=True,
        ),
    )
    cross_k_heads = encoder_key_rows.reshape(encoder_key_rows.shape[0], HEADS, HEAD_DIM)
    cross_v_heads = cross_values.reshape(cross_values.shape[0], HEADS, HEAD_DIM)
    cross_logits = jnp.einsum(
        "qhe,khe->hqk", cross_q_heads, cross_k_heads, preferred_element_type=jnp.float32
    )
    cross_exact = jnp.exp(cross_logits - jax.nn.logsumexp(cross_logits, axis=-1, keepdims=True))
    cross_probs = cross_exact.astype(jnp.bfloat16)
    cross_mixed = (
        jnp.einsum("hqk,khe->qhe", cross_probs, cross_v_heads, preferred_element_type=jnp.float32)
        .reshape(tokens, head_width)
        .astype(jnp.bfloat16)
    )
    after_cross = after_self + plain_dot(cross_mixed, cross_out_full)
    normed_three = rms_norm(after_cross, gain_three).astype(jnp.bfloat16)
    gate_act = plain_dot(normed_three, gate_full)
    up_act = plain_dot(normed_three, up_full)
    hidden_float, mlp_pull = jax.vjp(gelu_product, gate_act, up_act)
    hidden = hidden_float.astype(jnp.bfloat16)
    result = after_cross + plain_dot(hidden, down_full)
    resid_grad = cotangent[0].astype(jnp.float32)
    branch_three = resid_grad.astype(jnp.bfloat16)
    down_grad = left_contract(hidden, branch_three)
    hidden_state_gradient = right_contract(branch_three, down_full)
    gate_grad, up_grad = mlp_pull(hidden_state_gradient)
    gate_grad = gate_grad.astype(jnp.bfloat16)
    up_grad = up_grad.astype(jnp.bfloat16)
    gate_w_grad = left_contract(normed_three, gate_grad)
    up_w_grad = left_contract(normed_three, up_grad)
    normed_three_grad = right_contract(gate_grad, gate_full) + right_contract(up_grad, up_full)
    part_grad, gain_three_grad = norm_back(after_cross, gain_three, normed_three_grad)
    after_cross_grad = resid_grad + part_grad
    branch_two = after_cross_grad.astype(jnp.bfloat16)
    cross_out_grad = left_contract(cross_mixed, branch_two)
    mix_grad = (
        right_contract(branch_two, cross_out_full)
        .astype(jnp.bfloat16)
        .reshape(tokens, HEADS, HEAD_DIM)
    )
    cross_score_grad = jnp.einsum(
        "qhe,khe->hqk", mix_grad, cross_v_heads, preferred_element_type=jnp.float32
    )
    cross_delta = jnp.sum(cross_exact * cross_score_grad, axis=-1, keepdims=True)
    cross_dlogits = (cross_exact * (cross_score_grad - cross_delta)).astype(jnp.bfloat16)
    cross_q_grad = (
        jnp.einsum("hqk,khe->qhe", cross_dlogits, cross_k_heads, preferred_element_type=jnp.float32)
        .reshape(tokens, head_width)
        .astype(jnp.bfloat16)
    )
    cross_k_part = jnp.einsum(
        "hqk,qhe->khe", cross_dlogits, cross_q_heads, preferred_element_type=jnp.float32
    ).reshape(-1, head_width)
    cross_v_part = jnp.einsum(
        "hqk,qhe->khe", cross_probs, mix_grad, preferred_element_type=jnp.float32
    ).reshape(-1, head_width)
    cross_k_grad, cross_v_grad = (
        lax.psum_scatter(cross_k_part, "ctx", scatter_dimension=0, tiled=True),
        lax.psum_scatter(cross_v_part, "ctx", scatter_dimension=0, tiled=True),
    )
    cross_k_grad = cross_k_grad.astype(jnp.bfloat16)
    cross_v_grad = cross_v_grad.astype(jnp.bfloat16)
    cross_query_grad = left_contract(normed_two, cross_q_grad)
    cross_key_grad = left_contract(encoder_rows, cross_k_grad)
    cross_value_grad = left_contract(encoder_rows, cross_v_grad)
    encoder_grad = (
        right_contract(cross_k_grad, cross_key_full)
        + right_contract(cross_v_grad, cross_value_full)
    ).astype(jnp.bfloat16)
    normed_two_grad = right_contract(cross_q_grad, cross_query_full)
    part_grad, gain_two_grad = norm_back(after_self, gain_two, normed_two_grad)
    after_self_grad = after_cross_grad + part_grad
    branch_one = after_self_grad.astype(jnp.bfloat16)
    out_w_grad = left_contract(attended, branch_one)
    dattn_heads = (
        right_contract(branch_one, out_full).astype(jnp.bfloat16).reshape(tokens, HEADS, HEAD_DIM)
    )
    row_delta = jnp.einsum("qhe,qhe->hq", dattn_heads.astype(jnp.float32), attn_sum)

    def block_grads(
        query_side, grad_side, norm_side, delta_side, query_pos, key_side, value_side, key_pos
    ):
        logits, allowed, indicator = query_key_logits(query_side, key_side, query_pos, key_pos)
        exact = jnp.exp(logits - norm_side[..., None])
        score_grad = jnp.einsum(
            "qhe,khe->hqk", grad_side, value_side, preferred_element_type=jnp.float32
        )
        logits_gradient = (exact * (score_grad - delta_side[..., None])).astype(jnp.bfloat16)
        grad_query = jnp.einsum(
            "hqk,khe->qhe", logits_gradient, key_side, preferred_element_type=jnp.float32
        )
        grad_key = jnp.einsum(
            "hqk,qhe->khe", logits_gradient, query_side, preferred_element_type=jnp.float32
        )
        grad_value = jnp.einsum(
            "hqk,qhe->khe",
            exact.astype(jnp.bfloat16),
            grad_side,
            preferred_element_type=jnp.float32,
        )
        bucket_table_gradient = jnp.einsum(
            "ouw,muw->om", indicator, logits_gradient, preferred_element_type=jnp.float32
        )
        return (grad_query, grad_key, grad_value, bucket_table_gradient)

    zero_table = jnp.zeros((BUCKETS, HEADS), jnp.float32)
    full_zero = jnp.zeros((total_rows, HEADS, HEAD_DIM), jnp.float32)

    def key_grad_step(carried, pieces, first_row):
        query_total, table_total, key_total, value_total = carried
        key_pos = lookup_positions(block_order, first_row, pieces[0].shape[0], block_len)
        grad_query, grad_key, grad_value, bucket_table_gradient = block_grads(
            query_heads, dattn_heads, log_norm, row_delta, own_pos, pieces[0], pieces[1], key_pos
        )
        key_total = lax.dynamic_update_slice_in_dim(key_total, grad_key, first_row, 0)
        value_total = lax.dynamic_update_slice_in_dim(value_total, grad_value, first_row, 0)
        return (
            query_total + grad_query,
            table_total + bucket_table_gradient,
            key_total,
            value_total,
        )

    query_sum, table_grad, key_partial, value_partial = fold_groups(
        key_grad_step,
        (zero_heads, zero_table, full_zero, full_zero),
        (
            lax.all_gather(key_heads, "ctx", axis=0, tiled=True),
            lax.all_gather(value_heads, "ctx", axis=0, tiled=True),
        ),
        tokens,
    )
    key_sum, value_accumulated = (
        lax.psum_scatter(key_partial, "ctx", scatter_dimension=0, tiled=True),
        lax.psum_scatter(value_partial, "ctx", scatter_dimension=0, tiled=True),
    )
    query_grad = query_sum.reshape(tokens, head_width).astype(jnp.bfloat16)
    key_grad = key_sum.reshape(tokens, head_width).astype(jnp.bfloat16)
    value_grad = value_accumulated.reshape(tokens, head_width).astype(jnp.bfloat16)
    query_w_grad = left_contract(normed_one, query_grad)
    key_w_grad = left_contract(normed_one, key_grad)
    value_w_grad = left_contract(normed_one, value_grad)
    normed_one_grad = (
        right_contract(query_grad, query_full)
        + right_contract(key_grad, key_full)
        + right_contract(value_grad, value_full)
    )
    part_grad, gain_one_grad = norm_back(resid_in, gain_one, normed_one_grad)
    input_grad = (after_self_grad + part_grad).astype(jnp.bfloat16)
    (
        sum_gain_one,
        sum_query,
        sum_key,
        sum_value,
        sum_out,
        sum_table,
        sum_gain_two,
        sum_cross_query,
        sum_cross_key,
        sum_cross_value,
        sum_cross_out,
        sum_gain_three,
        sum_gate,
        sum_up,
        sum_down,
    ) = (
        lax.psum_scatter(
            gain_one_grad.astype(jnp.bfloat16), "wsh", scatter_dimension=0, tiled=True
        ).astype(jnp.float32),
        lax.psum_scatter(
            query_w_grad.astype(jnp.bfloat16), "wsh", scatter_dimension=0, tiled=True
        ).astype(jnp.float32),
        lax.psum_scatter(
            key_w_grad.astype(jnp.bfloat16), "wsh", scatter_dimension=0, tiled=True
        ).astype(jnp.float32),
        lax.psum_scatter(
            value_w_grad.astype(jnp.bfloat16), "wsh", scatter_dimension=0, tiled=True
        ).astype(jnp.float32),
        lax.psum_scatter(
            out_w_grad.astype(jnp.bfloat16), "wsh", scatter_dimension=0, tiled=True
        ).astype(jnp.float32),
        lax.psum_scatter(
            table_grad.astype(jnp.bfloat16), "wsh", scatter_dimension=0, tiled=True
        ).astype(jnp.float32),
        lax.psum_scatter(
            gain_two_grad.astype(jnp.bfloat16), "wsh", scatter_dimension=0, tiled=True
        ).astype(jnp.float32),
        lax.psum_scatter(
            cross_query_grad.astype(jnp.bfloat16), "wsh", scatter_dimension=0, tiled=True
        ).astype(jnp.float32),
        lax.psum_scatter(
            cross_key_grad.astype(jnp.bfloat16), "wsh", scatter_dimension=0, tiled=True
        ).astype(jnp.float32),
        lax.psum_scatter(
            cross_value_grad.astype(jnp.bfloat16), "wsh", scatter_dimension=0, tiled=True
        ).astype(jnp.float32),
        lax.psum_scatter(
            cross_out_grad.astype(jnp.bfloat16), "wsh", scatter_dimension=0, tiled=True
        ).astype(jnp.float32),
        lax.psum_scatter(
            gain_three_grad.astype(jnp.bfloat16), "wsh", scatter_dimension=0, tiled=True
        ).astype(jnp.float32),
        lax.psum_scatter(
            gate_w_grad.astype(jnp.bfloat16), "wsh", scatter_dimension=0, tiled=True
        ).astype(jnp.float32),
        lax.psum_scatter(
            up_w_grad.astype(jnp.bfloat16), "wsh", scatter_dimension=0, tiled=True
        ).astype(jnp.float32),
        lax.psum_scatter(
            down_grad.astype(jnp.bfloat16), "wsh", scatter_dimension=0, tiled=True
        ).astype(jnp.float32),
    )
    total_grads = lax.psum(
        (
            sum_gain_one,
            sum_query,
            sum_key,
            sum_value,
            sum_out,
            sum_table,
            sum_gain_two,
            sum_cross_query,
            sum_cross_key,
            sum_cross_value,
            sum_cross_out,
            sum_gain_three,
            sum_gate,
            sum_up,
            sum_down,
        ),
        "ctx",
    )
    return (result.astype(jnp.bfloat16)[None], input_grad[None], encoder_grad[None]) + tuple(
        total_grads
    )


def solution(mesh):
    return jax.shard_map(
        on_device,
        mesh=mesh,
        in_specs=(
            P("wsh", "ctx", None),
            P("wsh", "ctx", None),
            P("wsh", "ctx", None),
            P(),
            P(),
            P("wsh"),
            P("wsh", None),
            P("wsh", None),
            P("wsh", None),
            P("wsh", None),
            P("wsh", None),
            P("wsh"),
            P("wsh", None),
            P("wsh", None),
            P("wsh", None),
            P("wsh", None),
            P("wsh"),
            P("wsh", None),
            P("wsh", None),
            P("wsh", None),
        ),
        out_specs=(
            P("wsh", "ctx", None),
            P("wsh", "ctx", None),
            P("wsh", "ctx", None),
            P("wsh"),
            P("wsh", None),
            P("wsh", None),
            P("wsh", None),
            P("wsh", None),
            P("wsh", None),
            P("wsh"),
            P("wsh", None),
            P("wsh", None),
            P("wsh", None),
            P("wsh", None),
            P("wsh"),
            P("wsh", None),
            P("wsh", None),
            P("wsh", None),
        ),
        check_vma=False,
    )
```

profile of v0, /device:TPU:0, one launch (start us, length us, event | category | flops | bytes accessed | tf_op | source)
XLA Modules:
  0.0 2482.0 jit_solution(8377224542041464236)
XLA Ops:
  12.8 10.1 all-gather.21.cloned.1.call-done
  25.9 10.3 all-gather.17.cloned.1.call-done
  51.9 10.9 all-gather.29.cloned.1.call-done
  64.8 44.3 %all_gather.69 = bf16[256,1024]{1,0:T(8,128)(2,1)S(1)} all-gather(bf16[16,1024]{1,0:T(8,128)(2,1)S(1)} %convolution_convert_fusion.18), channel_id=1, replica_groups=mesh['ctx'=16,'wsh'=2] {'ctx'}, dimensions={0}, use_global_device_ids=true | all-gather | bytes 557056 | tf_op jit(solution)/shard_map/all_gather | solution.py:216
  112.0 43.4 %all_gather.73 = bf16[256,1024]{1,0:T(8,128)(2,1)S(1)} all-gather(bf16[16,1024]{1,0:T(8,128)(2,1)S(1)} %convolution_convert_fusion.17), channel_id=1, replica_groups=mesh['ctx'=16,'wsh'=2] {'ctx'}, dimensions={0}, use_global_device_ids=true | all-gather | bytes 557056 | tf_op jit(solution)/shard_map/all_gather | solution.py:213
  155.6 18.8 all-gather.23.cloned.1.call-done
  174.4 62.1 %while.56 = (s32[]{:T(128)}, f32[16,128]{1,0:T(8,128)S(1)}, f32[16,128]{1,0:T(8,128)S(1)}, s32[128]{0:T(128)S(1)}, s32[32]{0:T(128)S(1)}, /*index=5*/bf16[2048,1...) while((s32[]{:T(128)}, f32[16,128]{1,0:T(8,128)S(1)}, ...), condition=%wide.region_8.9_spmd.clone, body=%wide.region_3.8_spmd.clone.sunk | while | flops 432151552 | bytes 56367552 | solution.py:70
  176.5 5.9 fusion.261
  182.4 8.8 copy.213
  191.4 9.2 fusion.262
  207.6 5.9 fusion.261
  213.5 8.7 copy.213
  222.4 9.2 fusion.262
  236.5 29.5 %all-gather.19.cloned.1.call-done = bf16[2048,16,64]{0,2,1:T(8,128)(2,1)} async-done(((bf16[128,16,64]{0,2,1:T(8,128)(2,1)}), bf16[2048,16,64]{0,2,1:T(8,128)(2,1)}) %all-gather.19.cloned.1.call-update) | async-done | bytes 4194320 | tf_op jit(solution)/shard_map/all_gather | solution.py:199
  266.0 64.3 %while.57 = (s32[]{:T(128)}, f32[128,16,64]{0,2,1:T(8,128)S(1)}, bf16[2048,16,64]{0,2,1:T(8,128)(2,1)}, s32[128]{0:T(128)S(1)}, s32[32]{0:T(128)S(1)}, /*index=5...) while((s32[]{:T(128)}, f32[128,16,64]{0,2,1:T(8,128)S(1)}, ...), condition=%wide.region_12.13_spmd.clone, body=%wide.region_9.12_spmd.clone.sunk | while | flops 696644608 | bytes 42508228 | solution.py:70
  268.5 6.3 fusion.270
  274.8 8.7 copy.215
  283.8 8.8 fusion.271
  294.8 6.3 fusion.270
  301.2 8.7 copy.215
  310.1 9.5 fusion.271
  352.8 6.2 all-gather.41.cloned.1.call-done
  359.0 7.0 multiply_convert_fusion.1
  407.8 109.5 %while.58 = (s32[]{:T(128)}, f32[128,16,64]{0,2,1:T(8,128)S(1)}, f32[32,16]{0,1:T(8,128)S(1)}, f32[2048,16,64]{0,2,1:T(8,128)}, f32[2048,16,64]{0,2,1:T(8,128)},...) while((s32[]{:T(128)}, f32[128,16,64]{0,2,1:T(8,128)S(1)}, ...), condition=%wide.region_23.24_spmd.clone, body=%wide.region_20.23_spmd.clone.sunk | while | flops 1646655488 | bytes 171756144 | solution.py:70
  410.4 5.9 fusion.285
  416.2 8.7 copy.217
  425.1 6.5 fusion.286
  440.0 6.7 copy.218
  455.6 7.1 bitcast_dynamic-update-slice_fusion.5
  470.7 8.7 copy.217
  479.6 6.5 fusion.286
  494.5 6.7 copy.218
  510.1 7.1 bitcast_dynamic-update-slice_fusion.5
  530.7 10.9 reduce-scatter.51.cloned.1.call-done
  559.7 158.3 %reduce-scatter.23.cloned.1.call-done = f32[128,16,64]{0,2,1:T(8,128)} async-done(((f32[2048,16,64]{0,2,1:T(8,128)}), f32[128,16,64]{0,2,1:T(8,128)}) %reduce-scatter.23.cloned.1.call-update) | async-done | bytes 524304 | tf_op jit(solution)/shard_map/reduce_scatter | solution.py:354
  721.5 178.8 %reduce-scatter.25.cloned.1.call-done = f32[128,16,64]{0,2,1:T(8,128)} async-done(((f32[2048,16,64]{0,2,1:T(8,128)}), f32[128,16,64]{0,2,1:T(8,128)}) %reduce-scatter.25.cloned.1.call-update) | async-done | bytes 524304 | tf_op jit(solution)/shard_map/reduce_scatter | solution.py:355
  918.9 7.5 reduce-scatter.27.cloned.1.call-done
  926.4 13.6 reduce-scatter.33.cloned.1.call-done
  940.0 13.6 reduce-scatter.35.cloned.1.call-done
  953.6 13.8 reduce-scatter.41.cloned.1.call-done
  967.4 13.6 reduce-scatter.37.cloned.1.call-done
  981.0 13.6 reduce-scatter.39.cloned.1.call-done
  994.6 17.9 reduce-scatter.43.cloned.1.call-done
  1012.5 17.9 reduce-scatter.45.cloned.1.call-done
  1030.4 17.8 reduce-scatter.47.cloned.1.call-done
  1054.9 7.1 reduce-scatter.29.cloned.1.call-done
  1062.0 13.6 reduce-scatter.31.cloned.1.call-done
  1075.6 1394.3 %all-reduce.6 = (f32[512]{0:T(512)}, f32[512,1024]{1,0:T(8,128)}, f32[512,1024]{1,0:T(8,128)}, f32[512,1024]{1,0:T(8,128)}, f32[512,1024]{1,0:T(8,128)}, /*index...) all-reduce(f32[512]{0:T(512)S(1)} %dynamic-slice_convert_fusion.2, ...), channel_id=1, replica_groups=mesh['ctx'=16,'wsh'=2] {'ctx'}, use_global_device_ids=true, to_apply=%region_31.32 | all-reduce | flops 8521472 | bytes 51131904 | tf_op jit(solution)/shard_map/psum | solution.py:433
  (375 shorter events, 221.0 us)
Async XLA Ops:
  7.2 55.6 %copy-start = (bf16[1,16,1024]{2,1,0:T(8,128)(2,1)S(1)}, bf16[1,16,1024]{2,1,0:T(8,128)(2,1)}, u32[]{:S(2)}) copy-start(bf16[1,16,1024]{2,1,0:T(8,128)(2,1)} %param.27) | copy-start | bytes 98308
  7.2 15.7 all-gather.21.cloned.1.call-start
  8.0 28.3 %all-gather.17.cloned.1.call-start = ((), (), s32[]{:S(2)}) async-start(), calls=%async_computation.16 | async-start | bytes 3145728 | tf_op jit(solution)/shard_map/all_gather | solution.py:115
  8.7 40.9 %all-gather.25.cloned.1.call-start = ((), (), s32[]{:S(2)}) async-start(), calls=%async_computation.20 | async-start | bytes 3145728 | tf_op jit(solution)/shard_map/all_gather | solution.py:113
  9.4 53.3 %all-gather.29.cloned.1.call-start = ((), (), s32[]{:S(2)}) async-start(), calls=%async_computation.22 | async-start | bytes 3145728 | tf_op jit(solution)/shard_map/all_gather | solution.py:121
  10.0 100.0 %all-gather.33.cloned.1.call-start = ((), (), s32[]{:S(2)}) async-start(), calls=%async_computation.24 | async-start | bytes 3145728 | tf_op jit(solution)/shard_map/all_gather | solution.py:120
  10.6 163.8 %all-gather.23.cloned.1.call-start = ((), (), s32[]{:S(2)}) async-start(), calls=%async_computation.19 | async-start | bytes 4456448 | tf_op jit(solution)/shard_map/all_gather | solution.py:198
  12.6 37.0 %copy-start.50 = (f32[2,1,512]{2,1,0:T(1,128)}, f32[2,1,512]{2,1,0:T(1,128)S(1)}, u32[]{:S(2)}) copy-start(f32[2,1,512]{2,1,0:T(1,128)S(1)} %convert_element_type.394) | copy-start | bytes 12292
  12.8 25.6 %copy-start.66 = (f32[128]{0:T(128)}, f32[128]{0:T(128)S(1)}, u32[]{:S(2)}) copy-start(f32[128]{0:T(128)S(1)} %fusion.111) | copy-start | bytes 1540
  12.8 36.8 %copy-start.55 = (f32[128]{0:T(128)}, f32[128]{0:T(128)S(1)}, u32[]{:S(2)}) copy-start(f32[128]{0:T(128)S(1)} %fusion.142) | copy-start | bytes 1540
  25.9 240.2 %all-gather.19.cloned.1.call-start = ((), (), s32[]{:S(2)}) async-start(), calls=%async_computation.17 | async-start | bytes 4456448 | tf_op jit(solution)/shard_map/all_gather | solution.py:199
  39.2 291.3 %all-gather.27.cloned.1.call-start = ((), (), s32[]{:S(2)}) async-start(), calls=%async_computation.21 | async-start | bytes 3145728 | tf_op jit(solution)/shard_map/all_gather | solution.py:116
  40.0 293.2 %all-gather.31.cloned.1.call-start = ((), (), s32[]{:S(2)}) async-start(), calls=%async_computation.23 | async-start | bytes 3145728 | tf_op jit(solution)/shard_map/all_gather | solution.py:119
  40.7 298.8 %all-gather.35.cloned.1.call-start = ((), (), s32[]{:S(2)}) async-start(), calls=%async_computation.25 | async-start | bytes 3145728 | tf_op jit(solution)/shard_map/all_gather | solution.py:122
  41.3 301.4 %all-gather.37.cloned.1.call-start = ((), (), s32[]{:S(2)}) async-start(), calls=%async_computation.26 | async-start | bytes 8650752 | tf_op jit(solution)/shard_map/all_gather | solution.py:124
  42.1 305.3 %all-gather.39.cloned.1.call-start = ((), (), s32[]{:S(2)}) async-start(), calls=%async_computation.27 | async-start | bytes 8650752 | tf_op jit(solution)/shard_map/all_gather | solution.py:125
  42.6 316.3 %all-gather.41.cloned.1.call-start = ((), (), s32[]{:S(2)}) async-start(), calls=%async_computation.28 | async-start | bytes 8650752 | tf_op jit(solution)/shard_map/all_gather | solution.py:126
  43.4 484.2 %reduce-scatter.49.cloned.1.call-start = ((), (), s32[]{:S(2)}) async-start(), calls=%async_computation.42 | async-start | bytes 1114112
  47.4 343.5 %copy-start.53 = (f32[2,1,512]{2,1,0:T(1,128)}, f32[2,1,512]{2,1,0:T(1,128)S(1)}, u32[]{:S(2)}) copy-start(f32[2,1,512]{2,1,0:T(1,128)S(1)} %convert_element_type.395) | copy-start | bytes 12292
  155.6 181.0 %copy-start.28 = (bf16[256,1024]{0,1:T(8,128)(2,1)}, bf16[256,1024]{0,1:T(8,128)(2,1)S(1)}, u32[]{:S(2)}) copy-start(bf16[256,1024]{0,1:T(8,128)(2,1)S(1)} %copy.179) | copy-start | bytes 1572868
  333.1 57.7 %copy-start.7 = (f32[128,1024]{1,0:T(8,128)}, f32[128,1024]{1,0:T(8,128)S(1)}, u32[]{:S(2)}) copy-start(f32[128,1024]{1,0:T(8,128)S(1)} %get-tuple-element.1421) | copy-start | bytes 1572868
  333.2 57.7 %copy-start.60 = (f32[128]{0:T(128)}, f32[128]{0:T(128)S(1)}, u32[]{:S(2)}) copy-start(f32[128]{0:T(128)S(1)} %fusion.143) | copy-start | bytes 1540
  347.4 11.6 copy-start.47
  385.6 156.0 %reduce-scatter.51.cloned.1.call-start = ((), (), s32[]{:S(2)}) async-start(), calls=%async_computation.43 | async-start | bytes 1114112
  399.1 318.9 %reduce-scatter.23.cloned.1.call-start = ((), (), s32[]{:S(2)}) async-start(), calls=%async_computation.29 | async-start | bytes 8912896 | tf_op jit(solution)/shard_map/reduce_scatter | solution.py:354
  517.3 383.1 %reduce-scatter.25.cloned.1.call-start = ((), (), s32[]{:S(2)}) async-start(), calls=%async_computation.30 | async-start | bytes 8912896 | tf_op jit(solution)/shard_map/reduce_scatter | solution.py:355
  517.9 394.9 %reduce-scatter.53.cloned.1.call-start = ((), (), s32[]{:S(2)}) async-start(), calls=%async_computation.44 | async-start | bytes 12288
  518.7 407.7 %reduce-scatter.27.cloned.1.call-start = ((), (), s32[]{:S(2)}) async-start(), calls=%async_computation.31 | async-start | bytes 3145728 | tf_op jit(solution)/shard_map/reduce_scatter | solution.py:390
  521.0 419.0 %reduce-scatter.33.cloned.1.call-start = ((), (), s32[]{:S(2)}) async-start(), calls=%async_computation.34 | async-start | bytes 3145728 | tf_op jit(solution)/shard_map/reduce_scatter | solution.py:399
  523.1 430.5 %reduce-scatter.35.cloned.1.call-start = ((), (), s32[]{:S(2)}) async-start(), calls=%async_computation.35 | async-start | bytes 3145728 | tf_op jit(solution)/shard_map/reduce_scatter | solution.py:408
  525.4 442.0 %reduce-scatter.41.cloned.1.call-start = ((), (), s32[]{:S(2)}) async-start(), calls=%async_computation.38 | async-start | bytes 3145728 | tf_op jit(solution)/shard_map/reduce_scatter | solution.py:417
  527.5 453.5 %reduce-scatter.37.cloned.1.call-start = ((), (), s32[]{:S(2)}) async-start(), calls=%async_computation.36 | async-start | bytes 3145728 | tf_op jit(solution)/shard_map/reduce_scatter | solution.py:411
  530.6 14.0 copy-start.10
  530.6 14.0 copy-start.34
  530.6 464.0 %reduce-scatter.39.cloned.1.call-start = ((), (), s32[]{:S(2)}) async-start(), calls=%async_computation.37 | async-start | bytes 3145728 | tf_op jit(solution)/shard_map/reduce_scatter | solution.py:414
  544.6 467.9 %reduce-scatter.43.cloned.1.call-start = ((), (), s32[]{:S(2)}) async-start(), calls=%async_computation.39 | async-start | bytes 8650752 | tf_op jit(solution)/shard_map/reduce_scatter | solution.py:423
  548.9 481.5 %reduce-scatter.45.cloned.1.call-start = ((), (), s32[]{:S(2)}) async-start(), calls=%async_computation.40 | async-start | bytes 8650752 | tf_op jit(solution)/shard_map/reduce_scatter | solution.py:426
  554.3 493.9 %reduce-scatter.47.cloned.1.call-start = ((), (), s32[]{:S(2)}) async-start(), calls=%async_computation.41 | async-start | bytes 8650752 | tf_op jit(solution)/shard_map/reduce_scatter | solution.py:429
  559.7 502.3 %reduce-scatter.29.cloned.1.call-start = ((), (), s32[]{:S(2)}) async-start(), calls=%async_computation.32 | async-start | bytes 3145728 | tf_op jit(solution)/shard_map/reduce_scatter | solution.py:393
  721.2 183.1 %copy-start.68 = (u32[32]{0:T(128)S(1)}, u32[32]{0:T(128)}, u32[]{:S(2)}) copy-start(u32[32]{0:T(128)} %constant.400) | copy-start | bytes 388
  721.2 184.3 %copy-start.17 = (bf16[1024,1024]{1,0:T(8,128)(2,1)S(1)}, bf16[1024,1024]{1,0:T(8,128)(2,1)}, u32[]{:S(2)}) copy-start(bf16[1024,1024]{1,0:T(8,128)(2,1)} %all-gather.25.cloned.1.call-done) | copy-start | bytes 6291460
  721.3 354.3 %reduce-scatter.31.cloned.1.call-start = ((), (), s32[]{:S(2)}) async-start(), calls=%async_computation.33 | async-start | bytes 3145728 | tf_op jit(solution)/shard_map/reduce_scatter | solution.py:396
  912.5 135.6 %copy-start.15 = (bf16[1024,1024]{1,0:T(8,128)(2,1)S(1)}, bf16[1024,1024]{1,0:T(8,128)(2,1)}, u32[]{:S(2)}) copy-start(bf16[1024,1024]{1,0:T(8,128)(2,1)} %all-gather.21.cloned.1.call-done) | copy-start | bytes 6291460
  915.9 134.4 %copy-start.36 = (bf16[128,16,64]{0,2,1:T(8,128)(2,1)S(1)}, bf16[128,16,64]{0,2,1:T(8,128)(2,1)}, u32[]{:S(2)}) copy-start(bf16[128,16,64]{0,2,1:T(8,128)(2,1)} %copy-done.35) | copy-start | bytes 786436
  918.9 132.4 %copy-start.57 = (bf16[1024]{0:T(1024)(128)(2,1)S(1)}, bf16[1024]{0:T(1024)(128)(2,1)}, u32[]{:S(2)}) copy-start(bf16[1024]{0:T(1024)(128)(2,1)} %get-tuple-element.1323) | copy-start | bytes 6148
  918.9 132.4 %copy-start.59 = (bf16[1024]{0:T(1024)(128)(2,1)S(1)}, bf16[1024]{0:T(1024)(128)(2,1)}, u32[]{:S(2)}) copy-start(bf16[1024]{0:T(1024)(128)(2,1)} %get-tuple-element.1325) | copy-start | bytes 6148
  918.9 135.1 %copy-start.67 = (f32[128]{0:T(128)S(1)}, f32[128]{0:T(128)}, u32[]{:S(2)}) copy-start(f32[128]{0:T(128)} %copy-done.66) | copy-start | bytes 1540
  918.9 135.1 %copy-start.25 = (f32[128,1024]{1,0:T(8,128)S(1)}, f32[128,1024]{1,0:T(8,128)}, u32[]{:S(2)}) copy-start(f32[128,1024]{1,0:T(8,128)} %copy-done.23) | copy-start | bytes 1572868
  (53 other events, 172.4 us)
Sparse Core Ops, SparseCore 0:
  9.6 13.2 all-gather.20
  24.5 11.7 all-gather.16
  37.8 11.7 all-gather.24
  51.0 11.7 all-gather.28
  64.2 11.7 all-gather.32
  79.1 95.2 all-gather.22
  177.6 88.3 all-gather.18
  267.6 8.7 all-gather.26
  277.9 11.7 all-gather.30
  291.1 11.7 all-gather.34
  304.4 17.1 all-gather.36
  323.0 17.1 all-gather.38
  341.8 17.1 all-gather.40
  385.7 78.7 reduce-scatter.48
  467.3 74.2 reduce-scatter.50
  543.7 174.2 reduce-scatter.22
  720.1 180.1 reduce-scatter.24
  903.0 9.7 reduce-scatter.52
  915.6 10.7 reduce-scatter.26
  929.2 10.7 reduce-scatter.32
  942.8 10.7 reduce-scatter.34
  956.5 10.8 reduce-scatter.40
  970.2 10.7 reduce-scatter.36
  983.8 10.8 reduce-scatter.38
  997.5 14.9 reduce-scatter.42
  1015.3 15.0 reduce-scatter.44
  1033.1 15.0 reduce-scatter.46
  1051.1 10.8 reduce-scatter.28
  1064.8 10.7 reduce-scatter.30
where the time goes:
time: 2490 us; the launch traced here: 2480 us
  blocking collectives  1490 us (60%)
  waiting for transfers between devices  592 us (24%)
  matrix products  236 us (9%)
  local copies, waits for them, and re-layouts  103 us (4%)
  other arithmetic  29.3 us (1%)
    psum x1, blocking collectives, on_device(): lax.psum((sum_gain_one, sum_query, sum_key, sum_value, sum_out, sum_table...  1390 us
    reduce_scatter x1, waiting for transfers between devices, on_device(): lax.psum_scatter(value_partial, 'ctx', scatter_dimension=0, tiled=True)  179 us
    reduce_scatter x1, waiting for transfers between devices, on_device(): lax.psum_scatter(key_partial, 'ctx', scatter_dimension=0, tiled=True)  158 us
    dot_general x6, local copies, waits for them, and re-layouts, query_key_logits(): jnp.einsum('ouw,om->muw', indicator, bias_rows, preferred_element_type=jn...  52.3 us
  transfers between devices with their start and end apart: 29, of which 22 were waited for; matrix products, arithmetic and copies ran while one was open for 13% of the time, Pallas kernels for 0%

commit v1 on v0

--- a/solution.py
+++ b/solution.py
@@ -1,6 +1,10 @@
+import functools
+
 import jax
 import jax.numpy as jnp
 from jax import lax
+from jax.experimental import pallas as pl
+from jax.experimental.pallas import tpu as pltpu
 from jax.sharding import PartitionSpec as P
 
 HEADS = 16
@@ -455,9 +459,810 @@
     )
 
 
+F32 = jnp.float32
+BF16 = jnp.bfloat16
+MESH = pl.DeviceIdType.MESH
+TILE = 256
+BLOCK = 64
+MIB = 2**20
+
+
+def dot_nt(left, right):
+    return lax.dot_general(left, right, (((1,), (1,)), ((), ())), preferred_element_type=F32)
+
+
+def vmem_spec():
+    return pl.BlockSpec(memory_space=pltpu.VMEM)
+
+
+def any_spec():
+    return pl.BlockSpec(memory_space=pl.ANY)
+
+
+def greet_all(peers):
+    me, core = lax.axis_index("ctx"), lax.axis_index("wsh")
+    barrier = pltpu.get_barrier_semaphore()
+    for step in range(1, peers):
+        pl.semaphore_signal(
+            barrier, inc=1, device_id=(lax.rem(me + step, peers), core), device_id_type=MESH
+        )
+    pl.semaphore_wait(barrier, peers - 1)
+
+
+def exchange_all(packed, landed, send_sem, recv_sem, own_sem):
+    peers = packed.shape[0]
+    me, core = lax.axis_index("ctx"), lax.axis_index("wsh")
+
+    def copy(step):
+        peer = lax.rem(me + step, peers)
+        return pltpu.make_async_remote_copy(
+            src_ref=packed.at[peer],
+            dst_ref=landed.at[me],
+            send_sem=send_sem.at[step],
+            recv_sem=recv_sem.at[step],
+            device_id=(peer, core),
+            device_id_type=MESH,
+        )
+
+    copies = [copy(step) for step in range(1, peers)]
+    for each in copies:
+        each.start()
+    own = pltpu.make_async_copy(packed.at[me], landed.at[me], own_sem)
+    own.start()
+    own.wait()
+    for each in copies:
+        each.wait()
+
+
+def exchange_scratch(peers):
+    return [
+        pltpu.SemaphoreType.DMA((peers,)),
+        pltpu.SemaphoreType.DMA((peers,)),
+        pltpu.SemaphoreType.DMA,
+    ]
+
+
+def to_heads_kernel(q_ref, k_ref, v_ref, landed, packed, *sems):
+    peers = packed.shape[0]
+    greet_all(peers)
+    for head in range(peers):
+        cols = slice(head * HEAD_DIM, (head + 1) * HEAD_DIM)
+        packed[head, : 2 * BLOCK, :] = jnp.concatenate([q_ref[:, cols], k_ref[:, cols]], axis=1)
+        packed[head, 2 * BLOCK :, :] = jnp.concatenate(
+            [v_ref[:BLOCK, cols], v_ref[BLOCK:, cols]], axis=1
+        )
+    exchange_all(packed, landed, *sems)
+
+
+def to_heads(queries, keys, values):
+    shape = (HEADS, 3 * BLOCK, 2 * HEAD_DIM)
+    return pl.pallas_call(
+        to_heads_kernel,
+        out_shape=jax.ShapeDtypeStruct(shape, BF16),
+        in_specs=[vmem_spec()] * 3,
+        out_specs=vmem_spec(),
+        scratch_shapes=[pltpu.VMEM(shape, BF16)] + exchange_scratch(HEADS),
+        compiler_params=pltpu.CompilerParams(
+            collective_id=1, has_side_effects=True, vmem_limit_bytes=16 * MIB
+        ),
+        name="to_heads",
+    )(queries, keys, values)
+
+
+def rows_to_heads_kernel(g_ref, landed, packed, *sems):
+    peers = packed.shape[0]
+    greet_all(peers)
+    for head in range(peers):
+        cols = slice(head * HEAD_DIM, (head + 1) * HEAD_DIM)
+        packed[head] = jnp.concatenate([g_ref[:BLOCK, cols], g_ref[BLOCK:, cols]], axis=1)
+    exchange_all(packed, landed, *sems)
+
+
+def rows_to_heads(rows):
+    shape = (HEADS, BLOCK, 2 * HEAD_DIM)
+    return pl.pallas_call(
+        rows_to_heads_kernel,
+        out_shape=jax.ShapeDtypeStruct(shape, BF16),
+        in_specs=[vmem_spec()],
+        out_specs=vmem_spec(),
+        scratch_shapes=[pltpu.VMEM(shape, BF16)] + exchange_scratch(HEADS),
+        compiler_params=pltpu.CompilerParams(
+            collective_id=2, has_side_effects=True, vmem_limit_bytes=16 * MIB
+        ),
+        name="rows_to_heads",
+    )(rows)
+
+
+def unpack_pair(landed, pair, rows):
+    left, right = landed[2 * pair, rows, :], landed[2 * pair + 1, rows, :]
+    return (
+        jnp.concatenate([left[:, :HEAD_DIM], right[:, :HEAD_DIM]], axis=1),
+        jnp.concatenate([left[:, HEAD_DIM:], right[:, HEAD_DIM:]], axis=1),
+    )
+
+
+def from_heads_kernel(packed, out_ref, landed, *sems):
+    peers = packed.shape[0]
+    greet_all(peers)
+    exchange_all(packed, landed, *sems)
+    for pair in range(peers // 2):
+        cols = slice(pair * 2 * HEAD_DIM, (pair + 1) * 2 * HEAD_DIM)
+        first, second = unpack_pair(landed, pair, slice(0, BLOCK))
+        out_ref[:BLOCK, cols] = first
+        out_ref[BLOCK:, cols] = second
+
+
+def from_heads(packed):
+    return pl.pallas_call(
+        from_heads_kernel,
+        out_shape=jax.ShapeDtypeStruct((2 * BLOCK, HEADS * HEAD_DIM), BF16),
+        in_specs=[vmem_spec()],
+        out_specs=vmem_spec(),
+        scratch_shapes=[pltpu.VMEM(packed.shape, BF16)] + exchange_scratch(HEADS),
+        compiler_params=pltpu.CompilerParams(
+            collective_id=3, has_side_effects=True, vmem_limit_bytes=16 * MIB
+        ),
+        name="from_heads",
+    )(packed)
+
+
+def grads_from_heads_kernel(packed, q_ref, k_ref, v_ref, landed, *sems):
+    peers = packed.shape[0]
+    greet_all(peers)
+    exchange_all(packed, landed, *sems)
+    for pair in range(peers // 2):
+        cols = slice(pair * 2 * HEAD_DIM, (pair + 1) * 2 * HEAD_DIM)
+        q_ref[:, cols], k_ref[:, cols] = unpack_pair(landed, pair, slice(0, 2 * BLOCK))
+        first, second = unpack_pair(landed, pair, slice(2 * BLOCK, 3 * BLOCK))
+        v_ref[:BLOCK, cols] = first
+        v_ref[BLOCK:, cols] = second
+
+
+def grads_from_heads(packed):
+    return pl.pallas_call(
+        grads_from_heads_kernel,
+        out_shape=[jax.ShapeDtypeStruct((2 * BLOCK, HEADS * HEAD_DIM), BF16)] * 3,
+        in_specs=[vmem_spec()],
+        out_specs=[vmem_spec()] * 3,
+        scratch_shapes=[pltpu.VMEM(packed.shape, BF16)] + exchange_scratch(HEADS),
+        compiler_params=pltpu.CompilerParams(
+            collective_id=4, has_side_effects=True, vmem_limit_bytes=16 * MIB
+        ),
+        name="grads_from_heads",
+    )(packed)
+
+
+def place_tiles(bias_lines, tiles):
+    for apart in range(tiles.shape[0]):
+        line = jnp.broadcast_to(bias_lines[apart : apart + 1, :], (TILE, 2 * TILE))
+        tiles[apart] = pltpu.roll(line, 0, 1, stride=1, stride_axis=0)[:, :TILE]
+
+
+def attend_kernel(order, landed, bias_lines, out_ref, sum_ref, norm_ref, q_s, k_s, vt_s, tiles, ot_s, o_s):
+    blocks = order.shape[0]
+    spans = blocks * BLOCK // TILE
+    for stored in range(blocks):
+        device, half = stored // 2, stored % 2
+        at = pl.ds(pl.multiple_of(order[stored] * BLOCK, BLOCK), BLOCK)
+        pair = landed[device, half * BLOCK : (half + 1) * BLOCK, :]
+        q_s[at, :] = pair[:, :HEAD_DIM]
+        k_s[at, :] = pair[:, HEAD_DIM:]
+        values = landed[device, 2 * BLOCK :, half * HEAD_DIM : (half + 1) * HEAD_DIM]
+        o_s[at, :] = values.astype(F32)
+    vt_s[...] = jnp.transpose(o_s[...], (1, 0)).astype(BF16)
+    place_tiles(bias_lines, tiles)
+    for i in range(spans):
+        at_i = slice(i * TILE, (i + 1) * TILE)
+        queries = q_s[at_i, :]
+        scores = [
+            dot_nt(k_s[j * TILE : (j + 1) * TILE, :], queries) + tiles[i - j] for j in range(i + 1)
+        ]
+        top = functools.reduce(
+            jnp.maximum, [jnp.max(each, axis=0, keepdims=True) for each in scores]
+        )
+        total = jnp.zeros((1, TILE), F32)
+        mixed = jnp.zeros((HEAD_DIM, TILE), F32)
+        for j in range(i + 1):
+            weights = jnp.exp(scores[j] - top)
+            total = total + jnp.sum(weights, axis=0, keepdims=True)
+            mixed = mixed + plain_dot(
+                vt_s[:, j * TILE : (j + 1) * TILE], weights.astype(BF16)
+            )
+        norm_ref[0:1, at_i] = top + jnp.log(total)
+        ot_s[:, at_i] = mixed / total
+    sum_ref[...] = ot_s[...]
+    o_s[...] = jnp.transpose(ot_s[...], (1, 0))
+    for stored in range(blocks):
+        device, half = stored // 2, stored % 2
+        at = pl.ds(pl.multiple_of(order[stored] * BLOCK, BLOCK), BLOCK)
+        out_ref[device, :, half * HEAD_DIM : (half + 1) * HEAD_DIM] = o_s[at, :].astype(BF16)
+
+
+def attend(order, landed, bias_lines):
+    blocks = order.shape[0]
+    length = blocks * BLOCK
+    vmem = pltpu.VMEM
+    return pl.pallas_call(
+        attend_kernel,
+        grid_spec=pltpu.PrefetchScalarGridSpec(
+            num_scalar_prefetch=1,
+            grid=(),
+            in_specs=[vmem_spec()] * 2,
+            out_specs=[vmem_spec()] * 3,
+            scratch_shapes=[
+                vmem((length, HEAD_DIM), BF16),
+                vmem((length, HEAD_DIM), BF16),
+                vmem((HEAD_DIM, length), BF16),
+                vmem((length // TILE, TILE, TILE), F32),
+                vmem((HEAD_DIM, length), F32),
+                vmem((length, HEAD_DIM), F32),
+            ],
+        ),
+        out_shape=[
+            jax.ShapeDtypeStruct((blocks // 2, BLOCK, 2 * HEAD_DIM), BF16),
+            jax.ShapeDtypeStruct((HEAD_DIM, length), F32),
+            jax.ShapeDtypeStruct((1, length), F32),
+        ],
+        compiler_params=pltpu.CompilerParams(vmem_limit_bytes=32 * MIB),
+        cost_estimate=pl.CostEstimate(
+            flops=4 * length * length * HEAD_DIM, bytes_accessed=4 * MIB, transcendentals=length * length // 2
+        ),
+        name="attend",
+    )(order, landed, bias_lines)
+
+
+def attend_back_kernel(
+    order, landed, grad_landed, sums, norm, bias_lines, out_ref, lines_ref,
+    q_s, k_s, v_s, do_s, kt_s, tiles, by_offset, dq_s, dk_s, dv_s, delta_s, dqt_s,
+):
+    blocks = order.shape[0]
+    spans = blocks * BLOCK // TILE
+    for stored in range(blocks):
+        device, half = stored // 2, stored % 2
+        at = pl.ds(pl.multiple_of(order[stored] * BLOCK, BLOCK), BLOCK)
+        cols = slice(half * HEAD_DIM, (half + 1) * HEAD_DIM)
+        pair = landed[device, half * BLOCK : (half + 1) * BLOCK, :]
+        q_s[at, :] = pair[:, :HEAD_DIM]
+        k_s[at, :] = pair[:, HEAD_DIM:]
+        v_s[at, :] = landed[device, 2 * BLOCK :, cols]
+        do_s[at, :] = grad_landed[device, :, cols]
+    place_tiles(bias_lines, tiles)
+    kt_s[...] = jnp.transpose(k_s[...].astype(F32), (1, 0)).astype(BF16)
+    grad_t = jnp.transpose(do_s[...].astype(F32), (1, 0))
+    delta_s[...] = jnp.sum(grad_t * sums[...], axis=0, keepdims=True)
+    by_offset[...] = jnp.zeros_like(by_offset)
+    dk_s[...] = jnp.zeros_like(dk_s)
+    dv_s[...] = jnp.zeros_like(dv_s)
+    for i in range(spans):
+        at_i = slice(i * TILE, (i + 1) * TILE)
+        queries, grads = q_s[at_i, :], do_s[at_i, :]
+        norm_i, delta_i = norm[0:1, at_i], delta_s[0:1, at_i]
+        dqt = jnp.zeros((HEAD_DIM, TILE), F32)
+        for j in range(i + 1):
+            at_j = slice(j * TILE, (j + 1) * TILE)
+            exact = jnp.exp(dot_nt(k_s[at_j, :], queries) + tiles[i - j] - norm_i)
+            dscore = exact * (dot_nt(v_s[at_j, :], grads) - delta_i)
+            by_offset[i - j] += dscore
+            rounded = dscore.astype(BF16)
+            dv_s[at_j, :] += plain_dot(exact.astype(BF16), grads)
+            dk_s[at_j, :] += plain_dot(rounded, queries)
+            dqt = dqt + plain_dot(kt_s[:, at_j], rounded)
+        dqt_s[:, at_i] = dqt
+    dq_s[...] = jnp.transpose(dqt_s[...], (1, 0))
+    for stored in range(blocks):
+        device, half = stored // 2, stored % 2
+        at = pl.ds(pl.multiple_of(order[stored] * BLOCK, BLOCK), BLOCK)
+        rows = slice(half * BLOCK, (half + 1) * BLOCK)
+        out_ref[device, rows, :HEAD_DIM] = dq_s[at, :].astype(BF16)
+        out_ref[device, rows, HEAD_DIM:] = dk_s[at, :].astype(BF16)
+        cols = slice(half * HEAD_DIM, (half + 1) * HEAD_DIM)
+        out_ref[device, 2 * BLOCK :, cols] = dv_s[at, :].astype(BF16)
+    for apart in range(spans):
+        folded = jnp.zeros((8, 2 * TILE), F32)
+        for group in range(TILE // 8):
+            rows = by_offset[apart, 8 * group : 8 * group + 8, :]
+            wide = jnp.concatenate([rows, jnp.zeros((8, TILE), F32)], axis=1)
+            folded = folded + (pltpu.roll(wide, 2 * TILE - 8 * group, 1) if group else wide)
+        line = folded[0:1]
+        for row in range(1, 8):
+            line = line + pltpu.roll(folded[row : row + 1], 2 * TILE - row, 1)
+        lines_ref[apart : apart + 1, :] = line
+
+
+def attend_back(order, landed, grad_landed, sums, norm, bias_lines):
+    blocks = order.shape[0]
+    length = blocks * BLOCK
+    spans = length // TILE
+    vmem = pltpu.VMEM
+    return pl.pallas_call(
+        attend_back_kernel,
+        grid_spec=pltpu.PrefetchScalarGridSpec(
+            num_scalar_prefetch=1,
+            grid=(),
+            in_specs=[vmem_spec()] * 5,
+            out_specs=[vmem_spec()] * 2,
+            scratch_shapes=[vmem((length, HEAD_DIM), BF16)] * 4
+            + [vmem((HEAD_DIM, length), BF16)]
+            + [vmem((spans, TILE, TILE), F32)] * 2
+            + [vmem((length, HEAD_DIM), F32)] * 3
+            + [vmem((1, length), F32), vmem((HEAD_DIM, length), F32)],
+        ),
+        out_shape=[
+            jax.ShapeDtypeStruct((blocks // 2, 3 * BLOCK, 2 * HEAD_DIM), BF16),
+            jax.ShapeDtypeStruct((spans, 2 * TILE), F32),
+        ],
+        compiler_params=pltpu.CompilerParams(vmem_limit_bytes=32 * MIB),
+        cost_estimate=pl.CostEstimate(
+            flops=10 * length * length * HEAD_DIM, bytes_accessed=4 * MIB, transcendentals=length * length // 2
+        ),
+        name="attend_back",
+    )(order, landed, grad_landed, sums, norm, bias_lines)
+
+
+BIT_X, BIT_Y, BIT_Z0, BIT_Z1 = 0, 1, 2, 3
+X_FIRST = (BIT_X, BIT_Y, BIT_Z0, BIT_Z1)
+Y_FIRST = (BIT_Y, BIT_X, BIT_Z0, BIT_Z1)
+Z_FIRST = (BIT_Z0, BIT_Z1, BIT_X, BIT_Y)
+
+
+def flip_pairs(bit, size):
+    return [(at, at ^ (1 << bit)) for at in range(size)]
+
+
+def pick(flag, when_set, when_clear):
+    return jnp.where(flag == 1, when_set, when_clear)
+
+
+def reduce_pieces(left, right, order):
+    peers = lax.axis_size("ctx")
+    me = lax.axis_index("ctx")
+    bits = [(me >> bit) & 1 for bit in order]
+    half = left.shape[1] // 2
+    low, high = left[:, :half], left[:, half:]
+    away = left_contract(pick(bits[0], low, high), right).astype(BF16)
+    came = lax.ppermute(away, "ctx", flip_pairs(order[0], peers))
+    held = (left_contract(pick(bits[0], high, low), right) + came.astype(F32)).astype(BF16)
+    for bit, name in zip(bits[1:3], order[1:3]):
+        half = held.shape[0] // 2
+        low, high = held[:half], held[half:]
+        came = lax.ppermute(pick(bit, low, high), "ctx", flip_pairs(name, peers))
+        held = (pick(bit, high, low).astype(F32) + came.astype(F32)).astype(BF16)
+    half = held.shape[1] // 2
+    low, high = held[:, :half], held[:, half:]
+    came = lax.ppermute(pick(bits[3], low, high), "ctx", flip_pairs(order[3], peers))
+    return (pick(bits[3], high, low).astype(F32) + came.astype(F32)).astype(BF16)
+
+
+def gather_kernel(orders, *refs):
+    count = len(orders)
+    pieces, vec_in = refs[:count], refs[count]
+    wholes, vec_out = refs[count + 1 : 2 * count + 1], refs[2 * count + 1]
+    send_sem, recv_sem, own_sem, vec_send, vec_recv = refs[2 * count + 2 :]
+    me, core = lax.axis_index("ctx"), lax.axis_index("wsh")
+    peers = vec_out.shape[0]
+    x, y, z = lax.rem(me, 2), lax.rem(me // 2, 2), me // 4
+    greet_all(peers)
+
+    def place(zz, yy, xx):
+        return zz * 4 + yy * 2 + xx
+
+    def window(array, at):
+        rows, cols = pieces[array].shape
+        bits = [lax.rem(at // (1 << bit), 2) for bit in orders[array]]
+        block = bits[0] * 4 + bits[1] * 2 + bits[2]
+        return wholes[array].at[
+            pl.ds(pl.multiple_of(block * rows, 16), rows),
+            pl.ds(pl.multiple_of(bits[3] * cols, 128), cols),
+        ]
+
+    UP, DOWN, ACROSS_Y, ACROSS_X = 0, 1, 2, 3
+    targets = {
+        UP: place(lax.rem(z + 1, 4), y, x),
+        DOWN: place(lax.rem(z + 3, 4), y, x),
+        ACROSS_Y: place(z, 1 - y, x),
+        ACROSS_X: place(z, y, 1 - x),
+    }
+    sent = []
+
+    def send(array, at, way, slot, only=None, own=False):
+        def act(what):
+            copy = pltpu.make_async_remote_copy(
+                src_ref=pieces[array] if own else window(array, at),
+                dst_ref=window(array, at),
+                send_sem=send_sem.at[array, way, slot],
+                recv_sem=recv_sem.at[array, at],
+                device_id=(targets[way], core),
+                device_id_type=MESH,
+            )
+            if what == "start":
+                copy.start()
+            else:
+                copy.wait_send()
+
+        def guarded(what):
+            if only is None:
+                act(what)
+            else:
+                pl.when(only)(functools.partial(act, what))
+
+        guarded("start")
+        sent.append(functools.partial(guarded, "end"))
+
+    def arrive(array, at):
+        pltpu.make_async_remote_copy(
+            src_ref=window(array, at),
+            dst_ref=window(array, at),
+            send_sem=own_sem.at[array],
+            recv_sem=recv_sem.at[array, at],
+            device_id=(targets[ACROSS_X], core),
+            device_id_type=MESH,
+        ).wait_recv()
+
+    def along_z(array, zz, at, slot, own=False):
+        send(array, at, UP, slot, only=jnp.logical_and(zz <= z, z < 3), own=own)
+        send(array, at, DOWN, slot, only=jnp.logical_and(zz >= z, z > 0), own=own)
+
+    late_z = [array for array in range(count) if orders[array] == Z_FIRST]
+    early_z = [array for array in range(count) if orders[array] != Z_FIRST]
+
+    def planar(array):
+        if orders[array] == X_FIRST:
+            return ACROSS_Y, ACROSS_X, lambda zz: place(zz, 1 - y, x), lambda zz: place(zz, y, 1 - x)
+        return ACROSS_X, ACROSS_Y, lambda zz: place(zz, y, 1 - x), lambda zz: place(zz, 1 - y, x)
+
+    opposite = lambda zz: place(zz, 1 - y, 1 - x)
+
+    own_copies = [
+        pltpu.make_async_copy(pieces[array], window(array, me), own_sem.at[array])
+        for array in range(count)
+    ]
+    for each in own_copies:
+        each.start()
+    vec_copies = []
+    for step in range(1, peers):
+        peer = lax.rem(me + step, peers)
+        vec_copies.append(
+            pltpu.make_async_remote_copy(
+                src_ref=vec_in,
+                dst_ref=vec_out.at[me],
+                send_sem=vec_send.at[step],
+                recv_sem=vec_recv.at[step],
+                device_id=(peer, core),
+                device_id_type=MESH,
+            )
+        )
+    vec_copies.append(pltpu.make_async_copy(vec_in, vec_out.at[me], vec_recv.at[0]))
+    for each in vec_copies:
+        each.start()
+
+    for array in early_z:
+        along_z(array, z, me, 0, own=True)
+        second, third, _, _ = planar(array)
+        send(array, me, second, 0, own=True)
+        send(array, me, third, 0, own=True)
+    for array in late_z:
+        send(array, me, ACROSS_Y, 0, own=True)
+        send(array, me, ACROSS_X, 0, own=True)
+        along_z(array, z, me, 0, own=True)
+    for array in late_z:
+        at = place(z, 1 - y, x)
+        arrive(array, at)
+        send(array, at, ACROSS_X, 1)
+        along_z(array, z, at, 1)
+    for step in range(1, 4):
+        if step <= 2:
+            for array in late_z:
+                at = place(z, y, 1 - x) if step == 1 else opposite(z)
+                arrive(array, at)
+                along_z(array, z, at, 1 + step)
+        for array in early_z:
+            zz = z ^ step
+            at = place(zz, y, x)
+            second, third, _, _ = planar(array)
+            arrive(array, at)
+            along_z(array, zz, at, step)
+            send(array, at, second, step)
+            send(array, at, third, step)
+    for step in range(4):
+        for array in early_z:
+            second, third, near, _ = planar(array)
+            at = near(z ^ step)
+            arrive(array, at)
+            send(array, at, third, 4 + step)
+        if step:
+            for array in late_z:
+                zz = z ^ step
+                for slot, at in enumerate(
+                    (place(zz, y, x), place(zz, 1 - y, x), place(zz, y, 1 - x), opposite(zz))
+                ):
+                    arrive(array, at)
+                    along_z(array, zz, at, 4 * step + slot)
+    for step in range(4):
+        for array in early_z:
+            _, _, _, far = planar(array)
+            arrive(array, far(z ^ step))
+            arrive(array, opposite(z ^ step))
+    for each in sent:
+        each()
+    for each in own_copies + vec_copies:
+        each.wait()
+
+
+def gather_pieces(pieces, orders, vector):
+    count, peers = len(pieces), lax.axis_size("ctx")
+    dma = pltpu.SemaphoreType.DMA
+    return pl.pallas_call(
+        functools.partial(gather_kernel, orders),
+        out_shape=[
+            jax.ShapeDtypeStruct((8 * piece.shape[0], 2 * piece.shape[1]), BF16) for piece in pieces
+        ]
+        + [jax.ShapeDtypeStruct((peers,) + vector.shape, F32)],
+        in_specs=[any_spec()] * (count + 1),
+        out_specs=[any_spec()] * (count + 1),
+        scratch_shapes=[
+            dma((count, 4, 16)),
+            dma((count, peers)),
+            dma((count,)),
+            dma((peers,)),
+            dma((peers,)),
+        ],
+        compiler_params=pltpu.CompilerParams(collective_id=5, has_side_effects=True),
+        name="gather_pieces",
+    )(*pieces, vector)
+
+
+def on_device_by_heads(
+    inputs,
+    encoder,
+    cotangent,
+    block_order,
+    bucket_of,
+    self_gain,
+    query_weight,
+    key_weight,
+    value_weight,
+    out_weight,
+    bias_table,
+    cross_gain,
+    cross_query,
+    cross_key,
+    cross_value,
+    cross_out,
+    mlp_gain,
+    gate_weight,
+    up_weight,
+    down_weight,
+):
+    core, me = lax.axis_index("wsh"), lax.axis_index("ctx")
+
+    def swap(values):
+        return lax.ppermute(values, "wsh", [(0, 1), (1, 0)])
+
+    def own_half(values):
+        half = values.shape[-1] // 2
+        return pick(core, values[..., half:], values[..., :half])
+
+    def other_half(values):
+        half = values.shape[-1] // 2
+        return pick(core, values[..., :half], values[..., half:])
+
+    def join(own, other, axis):
+        return pick(
+            core,
+            jnp.concatenate([other, own], axis=axis),
+            jnp.concatenate([own, other], axis=axis),
+        )
+
+    def times(values, pair):
+        return plain_dot(own_half(values), pair[0]) + plain_dot(other_half(values), pair[1])
+
+    def times_back(values, pair):
+        return join(right_contract(values, pair[0]), right_contract(values, pair[1]), 1)
+
+    def both_cores(values):
+        return jnp.concatenate([own_half(values), swap(other_half(values))], axis=0)
+
+    def both_whole(values):
+        return jnp.concatenate([values, swap(values)], axis=0)
+
+    small = jnp.concatenate([self_gain, cross_gain, mlp_gain, bias_table.reshape(-1)])
+    small_other = swap(small)
+    width = self_gain.shape[0]
+    gain_one, gain_two, gain_three = (
+        join(small[at * width : (at + 1) * width], small_other[at * width : (at + 1) * width], 0).astype(F32)
+        for at in range(3)
+    )
+    bias_rows = join(bias_table, small_other[3 * width :].reshape(bias_table.shape), 0).astype(F32)
+    query_pair, key_pair, value_pair = (
+        (member, swap(member)) for member in (query_weight, key_weight, value_weight)
+    )
+    out_pair, cross_query_pair, cross_key_pair, cross_value_pair, cross_out_pair = (
+        (member, swap(member))
+        for member in (out_weight, cross_query, cross_key, cross_value, cross_out)
+    )
+    gate_pair, up_pair, down_pair = (
+        (member, swap(member)) for member in (gate_weight, up_weight, down_weight)
+    )
+
+    resid_in = inputs[0].astype(F32)
+    tokens = resid_in.shape[0]
+    head_width = HEADS * HEAD_DIM
+    length = bucket_of.shape[0]
+
+    normed_one = rms_norm(resid_in, gain_one).astype(BF16)
+    queries = times(normed_one, query_pair).astype(BF16)
+    keys = times(normed_one, key_pair).astype(BF16)
+    values = times(normed_one, value_pair).astype(BF16)
+    landed = to_heads(queries, keys, values)
+
+    own_column = jnp.sum(
+        jnp.where(jnp.arange(HEADS)[None, :] == me, bias_rows, 0.0), axis=1, keepdims=True
+    )
+    in_bucket = bucket_of[None, :] == jnp.arange(BUCKETS, dtype=jnp.int32)[:, None]
+    by_offset = jnp.sum(jnp.where(in_bucket, own_column, 0.0), axis=0).reshape(-1, TILE)
+    before = jnp.concatenate([jnp.full((1, TILE), NEG_BIG, F32), by_offset[:-1]], axis=0)
+    bias_lines = jnp.concatenate([by_offset, before], axis=1)
+
+    mixed_packed, attn_sum, log_norm = attend(block_order, landed, bias_lines)
+    attended = from_heads(mixed_packed)
+
+    after_self = resid_in + times(attended, out_pair)
+    normed_two = rms_norm(after_self, gain_two).astype(BF16)
+    cross_q_heads = times(normed_two, cross_query_pair).astype(BF16).reshape(tokens, HEADS, HEAD_DIM)
+    encoder_all = lax.all_gather(encoder[0], "ctx", axis=0, tiled=True)
+    cross_k_heads = times(encoder_all, cross_key_pair).astype(BF16).reshape(-1, HEADS, HEAD_DIM)
+    cross_v_heads = times(encoder_all, cross_value_pair).astype(BF16).reshape(-1, HEADS, HEAD_DIM)
+    cross_logits = jnp.einsum(
+        "qhe,khe->hqk", cross_q_heads, cross_k_heads, preferred_element_type=F32
+    )
+    cross_exact = jnp.exp(cross_logits - jax.nn.logsumexp(cross_logits, axis=-1, keepdims=True))
+    cross_probs = cross_exact.astype(BF16)
+    cross_mixed = (
+        jnp.einsum("hqk,khe->qhe", cross_probs, cross_v_heads, preferred_element_type=F32)
+        .reshape(tokens, head_width)
+        .astype(BF16)
+    )
+    after_cross = after_self + times(cross_mixed, cross_out_pair)
+    normed_three = rms_norm(after_cross, gain_three).astype(BF16)
+    gate_act = times(normed_three, gate_pair)
+    up_act = times(normed_three, up_pair)
+    hidden_float, mlp_pull = jax.vjp(gelu_product, gate_act, up_act)
+    hidden = hidden_float.astype(BF16)
+    result = (after_cross + times(hidden, down_pair)).astype(BF16)
+
+    resid_grad = cotangent[0].astype(F32)
+    branch_three = cotangent[0]
+    down_piece = reduce_pieces(both_cores(hidden), both_whole(branch_three), X_FIRST)
+    gate_grad, up_grad = mlp_pull(times_back(branch_three, down_pair))
+    gate_grad, up_grad = gate_grad.astype(BF16), up_grad.astype(BF16)
+    normed_three_both = both_cores(normed_three)
+    gate_piece = reduce_pieces(normed_three_both, both_whole(gate_grad), Y_FIRST)
+    up_piece = reduce_pieces(normed_three_both, both_whole(up_grad), Z_FIRST)
+    normed_three_grad = times_back(gate_grad, gate_pair) + times_back(up_grad, up_pair)
+    part_grad, gain_three_grad = norm_back(after_cross, gain_three, normed_three_grad)
+    after_cross_grad = resid_grad + part_grad
+    branch_two = after_cross_grad.astype(BF16)
+    cross_out_piece = reduce_pieces(both_cores(cross_mixed), both_whole(branch_two), X_FIRST)
+    mix_grad = times_back(branch_two, cross_out_pair).astype(BF16).reshape(tokens, HEADS, HEAD_DIM)
+    cross_score_grad = jnp.einsum(
+        "qhe,khe->hqk", mix_grad, cross_v_heads, preferred_element_type=F32
+    )
+    cross_delta = jnp.sum(cross_exact * cross_score_grad, axis=-1, keepdims=True)
+    cross_dlogits = (cross_exact * (cross_score_grad - cross_delta)).astype(BF16)
+    cross_q_grad = (
+        jnp.einsum("hqk,khe->qhe", cross_dlogits, cross_k_heads, preferred_element_type=F32)
+        .reshape(tokens, head_width)
+        .astype(BF16)
+    )
+    cross_k_part = jnp.einsum(
+        "hqk,qhe->khe", cross_dlogits, cross_q_heads, preferred_element_type=F32
+    ).reshape(-1, head_width)
+    cross_v_part = jnp.einsum(
+        "hqk,qhe->khe", cross_probs, mix_grad, preferred_element_type=F32
+    ).reshape(-1, head_width)
+    cross_kv_part = jnp.concatenate([cross_k_part, cross_v_part], axis=1).astype(BF16)
+    cross_kv_grad = lax.psum_scatter(cross_kv_part, "ctx", scatter_dimension=0, tiled=True)
+    cross_kv_all = lax.all_gather(cross_kv_grad, "ctx", axis=0, tiled=True)
+    encoder_grad = (
+        times_back(cross_kv_grad[:, :head_width], cross_key_pair)
+        + times_back(cross_kv_grad[:, head_width:], cross_value_pair)
+    ).astype(BF16)
+    cross_kv_w_grad = left_contract(both_cores(encoder_all), both_whole(cross_kv_all))
+    cross_query_piece = reduce_pieces(both_cores(normed_two), both_whole(cross_q_grad), Y_FIRST)
+    normed_two_grad = times_back(cross_q_grad, cross_query_pair)
+    part_grad, gain_two_grad = norm_back(after_self, gain_two, normed_two_grad)
+    after_self_grad = after_cross_grad + part_grad
+    branch_one = after_self_grad.astype(BF16)
+    out_piece = reduce_pieces(both_cores(attended), both_whole(branch_one), Z_FIRST)
+    grad_landed = rows_to_heads(times_back(branch_one, out_pair).astype(BF16))
+    packed_grads, offset_lines = attend_back(
+        block_order, landed, grad_landed, attn_sum, log_norm, bias_lines
+    )
+    query_grad, key_grad, value_grad = grads_from_heads(packed_grads)
+
+    offset_sums = offset_lines[:, :TILE] + jnp.concatenate(
+        [offset_lines[1:, TILE:], jnp.zeros((1, TILE), F32)], axis=0
+    )
+    table_column = jnp.sum(jnp.where(in_bucket, offset_sums.reshape(1, length), 0.0), axis=1)
+    table_grad = jnp.where(jnp.arange(HEADS)[None, :] == me, table_column[:, None], 0.0)
+
+    normed_one_both = both_cores(normed_one)
+    query_piece = reduce_pieces(normed_one_both, both_whole(query_grad), X_FIRST)
+    key_piece = reduce_pieces(normed_one_both, both_whole(key_grad), Y_FIRST)
+    value_piece = reduce_pieces(normed_one_both, both_whole(value_grad), Z_FIRST)
+    normed_one_grad = (
+        times_back(query_grad, query_pair)
+        + times_back(key_grad, key_pair)
+        + times_back(value_grad, value_pair)
+    )
+    part_grad, gain_one_grad = norm_back(resid_in, gain_one, normed_one_grad)
+    input_grad = (after_self_grad + part_grad).astype(BF16)
+
+    vector = jnp.concatenate(
+        [
+            gain_one_grad,
+            gain_two_grad,
+            gain_three_grad,
+            table_grad.reshape(-1),
+            jnp.zeros((512,), F32),
+        ]
+    ).reshape(8, 512)
+    vector = vector + swap(vector)
+    pieces = (
+        down_piece,
+        gate_piece,
+        up_piece,
+        cross_out_piece,
+        cross_query_piece,
+        out_piece,
+        query_piece,
+        key_piece,
+        value_piece,
+    )
+    orders = (X_FIRST, Y_FIRST, Z_FIRST) * 3
+    *wholes, vectors = gather_pieces(pieces, orders, vector)
+    (
+        sum_down,
+        sum_gate,
+        sum_up,
+        sum_cross_out,
+        sum_cross_query,
+        sum_out,
+        sum_query,
+        sum_key,
+        sum_value,
+    ) = (member.astype(F32) for member in wholes)
+    totals = jnp.sum(vectors, axis=0)
+    sum_gain_one, sum_gain_two, sum_gain_three = (
+        own_half(totals[2 * at : 2 * at + 2].reshape(1, -1))[0] for at in range(3)
+    )
+    sum_table = own_half(totals[6:7])[0].reshape(BUCKETS // 2, HEADS)
+    return (
+        result[None],
+        input_grad[None],
+        encoder_grad[None],
+        sum_gain_one,
+        sum_query,
+        sum_key,
+        sum_value,
+        sum_out,
+        sum_table,
+        sum_gain_two,
+        sum_cross_query,
+        cross_kv_w_grad[:, :head_width],
+        cross_kv_w_grad[:, head_width:],
+        sum_cross_out,
+        sum_gain_three,
+        sum_gate,
+        sum_up,
+        sum_down,
+    )
+
+
 def solution(mesh):
+    by_heads = mesh.shape["ctx"] == HEADS and mesh.shape["wsh"] == 2
     return jax.shard_map(
-        on_device,
+        on_device_by_heads if by_heads else on_device,
         mesh=mesh,
         in_specs=(
             P("wsh", "ctx", None),

time: 2490 us -> 702 us (0.28)
  blocking collectives: 1490 us -> 45.4 us
  waiting for transfers between devices: 592 us -> 189 us
  Pallas kernels: 0 us -> 221 us
  matrix products: 236 us -> 103 us
  local copies, waits for them, and re-layouts: 103 us -> 19.2 us
  starting transfers between devices: 1.37 us -> 51.9 us
    psum x1 -> x0, blocking collectives: 1390 us -> none  [on_device(): lax.psum((sum_gain_one, sum_query, sum_key, sum_value, sum_out, sum_table...]
    reduce_scatter x13 -> x1, waiting for transfers between devices: 487 us -> 0.01 us  [on_device_by_heads(): lax.psum_scatter(cross_kv_part, 'ctx', scatter_dimension=0, tiled=True)]
    pallas_call x0 -> x7, Pallas kernels: none -> 221 us  [the longest x1 145 us: gather_pieces(): pl.pallas_call(functools.partial(gather_kernel, orders), out_shape=[jax.S...]
    ppermute x0 -> x66, waiting for transfers between devices: none -> 182 us  [the longest x18 131 us: reduce_pieces(): came = lax.ppermute(pick(bit, low, high), 'ctx', flip_pairs(name, peers))]
    dot_general x28 -> x6, matrix products: 143 us -> 8.42 us  [the longest x1 1.84 us: on_device_by_heads(): jnp.einsum('hqk,qhe->khe', cross_probs, mix_grad, preferred_element_type=...]
    all_gather x13 -> x1, waiting for transfers between devices: 86.2 us -> 6.71 us  [on_device_by_heads(): cross_kv_all = lax.all_gather(cross_kv_grad, 'ctx', axis=0, tiled=True)]
    dot_general x6 -> x0, local copies, waits for them, and re-layouts: 52.3 us -> none  [query_key_logits(): jnp.einsum('ouw,om->muw', indicator, bias_rows, preferred_element_type=jn...]
    ppermute x0 -> x66, starting transfers between devices: none -> 51.8 us  [the longest x18 21.2 us: reduce_pieces(): came = lax.ppermute(pick(bit, low, high), 'ctx', flip_pairs(name, peers))]
  transfers between devices with their start and end apart: 29 -> 68, of which waited for: 22 -> 27; matrix products, arithmetic and copies ran while one was open for 13% -> 23% of each run, Pallas kernels for 0% -> 32%
where the time goes in v1:
time: 702 us; the launch traced here: 693 us
  Pallas kernels  221 us (31%)
  waiting for transfers between devices  189 us (27%)
  matrix products  103 us (15%)
  starting transfers between devices  51.9 us (7%)
  other arithmetic  47.8 us (7%)
  blocking collectives  45.4 us (6%)
  local copies, waits for them, and re-layouts  19.2 us (3%)
  between operations  16.4 us (2%)
    pallas_call x1, Pallas kernels, gather_pieces(): pl.pallas_call(functools.partial(gather_kernel, orders), out_shape=[jax.S...  145 us
    ppermute x18, waiting for transfers between devices, reduce_pieces(): came = lax.ppermute(pick(bit, low, high), 'ctx', flip_pairs(name, peers))  131 us
    all_gather x1, blocking collectives, on_device_by_heads(): encoder_all = lax.all_gather(encoder[0], 'ctx', axis=0, tiled=True)  45.4 us
    dot_general x22, matrix products, plain_dot(): return jnp.dot(left, right, preferred_element_type=jnp.float32)  36.9 us
    dot_general x22, matrix products, right_contract(): lax.dot_general(left, right, (((1,), (1,)), ((), ())), preferred_element_...  36.2 us
    ppermute x9, waiting for transfers between devices, reduce_pieces(): lax.ppermute(pick(bits[3], low, high), 'ctx', flip_pairs(order[3], peers))  31.1 us
    dot_general x19, matrix products, left_contract(): lax.dot_general(left, right, (((0,), (0,)), ((), ())), preferred_element_...  21.5 us
    ppermute x18, starting transfers between devices, reduce_pieces(): came = lax.ppermute(pick(bit, low, high), 'ctx', flip_pairs(name, peers))  21.2 us
  transfers between devices with their start and end apart: 68, of which 27 were waited for; matrix products, arithmetic and copies ran while one was open for 23% of the time, Pallas kernels for 32%

profile of v1, /device:TPU:0, one launch (start us, length us, event | category | flops | bytes accessed | tf_op | source)
XLA Modules:
  0.0 693.1 jit_solution(12336091901085809734)
XLA Ops:
  11.4 45.4 %all-gather = bf16[1,256,1024]{2,1,0:T(8,128)(2,1)S(1)} all-gather(bf16[1,16,1024]{2,1,0:T(8,128)(2,1)} %param.21), channel_id=2, replica_groups=mesh['ctx'=16,'wsh'=2] {'ctx'}, dimensions={1}, use_global_device_ids=true | all-gather | bytes 557056 | tf_op jit(solution)/shard_map/all_gather | solution.py:1112
  59.0 2.7 fusion.148
  61.7 3.8 fusion.120
  76.0 16.5 %to_heads.1.landed = bf16[16,192,128]{2,1,0:T(8,128)(2,1)S(1)} custom-call(bf16[128,1024]{1,0:T(8,128)(2,1)S(1)} %fusion.26.q_ref, bf16[128,1024]{1,0:T(8,128)(2,1)S(1)} %fusion.27.k_ref, bf16[128,1024]{1,0:T(8,128)(2,1)S(1)} %fusion.28.v_ref), custom_call_target="tpu_custom_call" | custom-call | tf_op jit(solution)/shard_map/to_heads/pallas_call | solution.py:539
  92.5 6.0 attend.1
  98.5 12.5 %from_heads.1 = bf16[128,1024]{1,0:T(8,128)(2,1)S(1)} custom-call(bf16[16,64,128]{2,1,0:T(8,128)(2,1)S(1)} %get-tuple-element.36.packed), custom_call_target="tpu_custom_call" | custom-call | tf_op jit(solution)/shard_map/from_heads/pallas_call | solution.py:596
  142.8 2.8 fusion.122
  148.2 3.5 fusion.13
  151.7 3.4 fusion.156
  156.2 2.9 fusion.157
  159.0 2.9 fusion.155
  178.7 11.8 %rows_to_heads.1.grad_landed = bf16[16,64,128]{2,1,0:T(8,128)(2,1)S(1)} custom-call(bf16[128,1024]{1,0:T(8,128)(2,1)S(1)} %fusion.43.g_ref), custom_call_target="tpu_custom_call" | custom-call | tf_op jit(solution)/shard_map/rows_to_heads/pallas_call | solution.py:563
  190.5 10.2 %attend_back.1 = (bf16[16,192,128]{2,1,0:T(8,128)(2,1)S(1)}, f32[8,512]{1,0:T(8,128)S(1)}) custom-call(s32[32]{0:T(128)S(1)} %copy-done, bf16[16,192,128]{2,1,0:T(8,128)(2,1)S(1)} %to_heads.1.landed, bf16[16,64,128]{2,1,0:T(8,128)(2,1)S(1)} %rows_to_heads.1.grad_landed, f32[64,2048]{1,0:T(8,128)S(1)} %get-tuple-element.37.sums, ...), custom_call_target="tpu_custom_call" | custom-call | flops 2684354560 | bytes 4194304 | tf_op jit(solution)/shard_map/attend_back/pallas_call | solution.py:777
  200.7 18.8 %grads_from_heads.1 = (bf16[128,1024]{1,0:T(8,128)(2,1)S(1)}, bf16[128,1024]{1,0:T(8,128)(2,1)S(1)}, bf16[128,1024]{1,0:T(8,128)(2,1)S(1)}) custom-call(bf16[16,192,128]{2,1,0:T(8,128)(2,1)S(1)} %get-tuple-element.39.packed), custom_call_target="tpu_custom_call" | custom-call | tf_op jit(solution)/shard_map/grads_from_heads/pallas_call | solution.py:622
  221.5 3.4 fusion.154
  233.5 3.2 fusion.30
  252.7 4.7 collective-permute-start.59
  258.2 2.6 collective-permute-start.54
  264.8 7.3 %collective-permute-done.59 = bf16[256,1024]{1,0:T(8,128)(2,1)S(1)} collective-permute-done((bf16[256,1024]{1,0:T(8,128)(2,1)S(1)}, bf16[256,1024]{1,0:T(8,128)(2,1)S(1)}, u32[]{:S(2)}, u32[]{:S(2)}) %collective-permute-start.59) | collective-permute-done | bytes 524320 | tf_op jit(solution)/shard_map/ppermute | solution.py:823
  278.8 9.2 %collective-permute-done.49 = bf16[256,1024]{1,0:T(8,128)(2,1)S(1)} collective-permute-done((bf16[256,1024]{1,0:T(8,128)(2,1)S(1)}, bf16[256,1024]{1,0:T(8,128)(2,1)S(1)}, u32[]{:S(2)}, u32[]{:S(2)}) %collective-permute-start.49) | collective-permute-done | bytes 524320 | tf_op jit(solution)/shard_map/ppermute | solution.py:823
  288.0 3.9 collective-permute-start.20
  293.7 5.3 collective-permute-start.60
  300.6 33.2 %collective-permute-done.32 = bf16[128,1024]{1,0:T(8,128)(2,1)S(1)} collective-permute-done((bf16[128,1024]{1,0:T(8,128)(2,1)S(1)}, bf16[128,1024]{1,0:T(8,128)(2,1)S(1)}, u32[]{:S(2)}, u32[]{:S(2)}) %collective-permute-start.32) | collective-permute-done | bytes 262176 | tf_op jit(solution)/shard_map/ppermute | solution.py:828
  335.5 6.2 collective-permute-done.55
  344.2 11.0 %collective-permute-done.44 = bf16[128,1024]{1,0:T(8,128)(2,1)S(1)} collective-permute-done((bf16[128,1024]{1,0:T(8,128)(2,1)S(1)}, bf16[128,1024]{1,0:T(8,128)(2,1)S(1)}, u32[]{:S(2)}, u32[]{:S(2)}) %collective-permute-start.44) | collective-permute-done | bytes 262176 | tf_op jit(solution)/shard_map/ppermute | solution.py:828
  355.8 7.2 %collective-permute-done.38 = bf16[128,1024]{1,0:T(8,128)(2,1)S(1)} collective-permute-done((bf16[128,1024]{1,0:T(8,128)(2,1)S(1)}, bf16[128,1024]{1,0:T(8,128)(2,1)S(1)}, u32[]{:S(2)}, u32[]{:S(2)}) %collective-permute-start.38) | collective-permute-done | bytes 262176 | tf_op jit(solution)/shard_map/ppermute | solution.py:828
  363.2 20.4 %collective-permute-done.33 = bf16[64,1024]{1,0:T(8,128)(2,1)S(1)} collective-permute-done((bf16[64,1024]{1,0:T(8,128)(2,1)S(1)}, bf16[64,1024]{1,0:T(8,128)(2,1)S(1)}, u32[]{:S(2)}, u32[]{:S(2)}) %collective-permute-start.33) | collective-permute-done | bytes 131104 | tf_op jit(solution)/shard_map/ppermute | solution.py:828
  384.3 4.2 collective-permute-done.61
  389.0 5.2 collective-permute-done.56
  394.5 4.6 collective-permute-done.51
  400.2 3.9 collective-permute-done.45
  404.5 4.6 collective-permute-done.39
  409.5 5.7 collective-permute-done.34
  420.1 4.5 collective-permute-done.57
  425.3 4.5 collective-permute-done.52
  432.0 2.9 collective-permute-done.46
  435.5 4.5 collective-permute-done.40
  452.4 2.6 collective-permute-start.21
  460.9 12.7 %collective-permute-done.16 = bf16[176,1024]{1,0:T(8,128)(2,1)S(1)} collective-permute-done((bf16[176,1024]{1,0:T(8,128)(2,1)S(1)}, bf16[176,1024]{1,0:T(8,128)(2,1)S(1)}, u32[]{:S(2)}, u32[]{:S(2)}) %collective-permute-start.16) | collective-permute-done | bytes 360480 | tf_op jit(solution)/shard_map/ppermute | solution.py:828
  476.3 14.6 %collective-permute-done.26 = bf16[128,2816]{1,0:T(8,128)(2,1)S(1)} collective-permute-done((bf16[128,2816]{1,0:T(8,128)(2,1)S(1)}, bf16[128,2816]{1,0:T(8,128)(2,1)S(1)}, u32[]{:S(2)}, u32[]{:S(2)}) %collective-permute-start.26) | collective-permute-done | bytes 720928 | tf_op jit(solution)/shard_map/ppermute | solution.py:828
  495.2 3.6 collective-permute-done.27
  499.4 5.0 collective-permute-done.23
  505.1 6.7 all-gather.3.cloned.1.call-done
  512.5 145.0 %gather_pieces.1 = (bf16[1408,1024]{1,0:T(8,128)(2,1)}, bf16[512,2816]{1,0:T(8,128)(2,1)}, bf16[512,2816]{1,0:T(8,128)(2,1)}, bf16[512,1024]{1,0:T(8,128)(2,1)},...) custom-call(bf16[176,512]{1,0:T(8,128)(2,1)} %add_convert_fusion.15., ...), custom_call_target="tpu_custom_call" | custom-call | tf_op jit(solution)/shard_map/gather_pieces/pallas_call | solution.py:994
  659.9 2.8 convert_element_type.616
  671.6 2.9 convert_element_type.622
  674.5 2.9 convert_element_type.623
  677.5 3.2 convert_element_type.624
  (488 shorter events, 169.4 us)
Async XLA Ops:
  7.2 437.0 %reduce-scatter.4.cloned.1.call-start = ((), (), s32[]{:S(2)}) async-start(), calls=%async_computation.2 | async-start | bytes 1114112 | tf_op jit(solution)/shard_map/reduce_scatter | solution.py:1164
  8.8 56.7 %collective-permute-start = (bf16[1792]{0:T(1024)(128)(2,1)S(1)}, bf16[1792]{0:T(1024)(128)(2,1)S(1)}, u32[]{:S(2)}, u32[]{:S(2)}) collective-permute-start(bf16[1792]{0:T(1024)(128)(2,1)S(1)} %pad_maximum_fusion.33), channel_id=1, source_target_pairs={{0,1},{1,0},{2,3},{3,2},{4,5},{5,4},{6,7},{7,6},{8,9},{9,8},{10,11... | collective-permute-start | bytes 10760 | tf_op jit(solution)/shard_map/ppermute | solution.py:1039
  9.3 60.8 %collective-permute-start.1 = (bf16[512,1024]{1,0:T(8,128)(2,1)}, bf16[512,1024]{1,0:T(8,128)(2,1)}, u32[]{:S(2)}, u32[]{:S(2)}) collective-permute-start(bf16[512,1024]{1,0:T(8,128)(2,1)} %param.26), channel_id=1, source_target_pairs={{0,1},{1,0},{2,3},{3,2},{4,5},{5,4},{6,7},{7,6},{8,9},{9,8},{10,11... | collective-permute-start | bytes 3145736 | tf_op jit(solution)/shard_map/ppermute | solution.py:1039
  9.3 62.9 %collective-permute-start.2 = (bf16[512,1024]{1,0:T(8,128)(2,1)}, bf16[512,1024]{1,0:T(8,128)(2,1)}, u32[]{:S(2)}, u32[]{:S(2)}) collective-permute-start(bf16[512,1024]{1,0:T(8,128)(2,1)} %param.27), channel_id=1, source_target_pairs={{0,1},{1,0},{2,3},{3,2},{4,5},{5,4},{6,7},{7,6},{8,9},{9,8},{10,11... | collective-permute-start | bytes 3145736 | tf_op jit(solution)/shard_map/ppermute | solution.py:1039
  9.8 64.2 %collective-permute-start.3 = (bf16[512,1024]{1,0:T(8,128)(2,1)}, bf16[512,1024]{1,0:T(8,128)(2,1)}, u32[]{:S(2)}, u32[]{:S(2)}) collective-permute-start(bf16[512,1024]{1,0:T(8,128)(2,1)} %param.28), channel_id=1, source_target_pairs={{0,1},{1,0},{2,3},{3,2},{4,5},{5,4},{6,7},{7,6},{8,9},{9,8},{10,11... | collective-permute-start | bytes 3145736 | tf_op jit(solution)/shard_map/ppermute | solution.py:1039
  9.9 107.1 %collective-permute-start.7 = (bf16[512,1024]{1,0:T(8,128)(2,1)}, bf16[512,1024]{1,0:T(8,128)(2,1)}, u32[]{:S(2)}, u32[]{:S(2)}) collective-permute-start(bf16[512,1024]{1,0:T(8,128)(2,1)} %param.33), channel_id=1, source_target_pairs={{0,1},{1,0},{2,3},{3,2},{4,5},{5,4},{6,7},{7,6},{8,9},{9,8},{10,11... | collective-permute-start | bytes 3145736 | tf_op jit(solution)/shard_map/ppermute | solution.py:1039
  69.2 53.4 %collective-permute-start.5 = (bf16[512,1024]{1,0:T(8,128)(2,1)}, bf16[512,1024]{1,0:T(8,128)(2,1)}, u32[]{:S(2)}, u32[]{:S(2)}) collective-permute-start(bf16[512,1024]{1,0:T(8,128)(2,1)} %param.34), channel_id=1, source_target_pairs={{0,1},{1,0},{2,3},{3,2},{4,5},{5,4},{6,7},{7,6},{8,9},{9,8},{10,11... | collective-permute-start | bytes 3145736 | tf_op jit(solution)/shard_map/ppermute | solution.py:1039
  70.1 72.7 %collective-permute-start.11 = (bf16[1408,1024]{1,0:T(8,128)(2,1)}, bf16[1408,1024]{1,0:T(8,128)(2,1)}, u32[]{:S(2)}, u32[]{:S(2)}) collective-permute-start(bf16[1408,1024]{1,0:T(8,128)(2,1)} %param.39), channel_id=1, source_target_pairs={{0,1},{1,0},{2,3},{3,2},{4,5},{5,4},{6,7},{7,6},{8,9},{9,8},{10,11... | collective-permute-start | bytes 8650760 | tf_op jit(solution)/shard_map/ppermute | solution.py:1039
  72.2 39.2 %collective-permute-start.4 = (bf16[512,1024]{1,0:T(8,128)(2,1)S(1)}, bf16[512,1024]{1,0:T(8,128)(2,1)S(1)}, u32[]{:S(2)}, u32[]{:S(2)}) collective-permute-start(bf16[512,1024]{1,0:T(8,128)(2,1)S(1)} %copy-done.32), channel_id=1, source_target_pairs={{0,1},{1,0},{2,3},{3,2},{4,5},{5,4},{6,7},{7,6},{8,9},{9,8},{10,11... | collective-permute-start | bytes 3145736 | tf_op jit(solution)/shard_map/ppermute | solution.py:1039
  74.0 39.9 %collective-permute-start.6 = (bf16[512,1024]{1,0:T(8,128)(2,1)S(1)}, bf16[512,1024]{1,0:T(8,128)(2,1)S(1)}, u32[]{:S(2)}, u32[]{:S(2)}) collective-permute-start(bf16[512,1024]{1,0:T(8,128)(2,1)S(1)} %copy-done.18), channel_id=1, source_target_pairs={{0,1},{1,0},{2,3},{3,2},{4,5},{5,4},{6,7},{7,6},{8,9},{9,8},{10,11... | collective-permute-start | bytes 3145736 | tf_op jit(solution)/shard_map/ppermute | solution.py:1039
  111.5 24.9 %collective-permute-start.8 = (bf16[512,1024]{1,0:T(8,128)(2,1)}, bf16[512,1024]{1,0:T(8,128)(2,1)}, u32[]{:S(2)}, u32[]{:S(2)}) collective-permute-start(bf16[512,1024]{1,0:T(8,128)(2,1)} %param.35), channel_id=1, source_target_pairs={{0,1},{1,0},{2,3},{3,2},{4,5},{5,4},{6,7},{7,6},{8,9},{9,8},{10,11... | collective-permute-start | bytes 3145736 | tf_op jit(solution)/shard_map/ppermute | solution.py:1039
  113.9 34.2 %collective-permute-start.9 = (bf16[512,2816]{1,0:T(8,128)(2,1)}, bf16[512,2816]{1,0:T(8,128)(2,1)}, u32[]{:S(2)}, u32[]{:S(2)}) collective-permute-start(bf16[512,2816]{1,0:T(8,128)(2,1)} %param.37), channel_id=1, source_target_pairs={{0,1},{1,0},{2,3},{3,2},{4,5},{5,4},{6,7},{7,6},{8,9},{9,8},{10,11... | collective-permute-start | bytes 8650760 | tf_op jit(solution)/shard_map/ppermute | solution.py:1039
  117.0 28.7 %collective-permute-start.10 = (bf16[512,2816]{1,0:T(8,128)(2,1)}, bf16[512,2816]{1,0:T(8,128)(2,1)}, u32[]{:S(2)}, u32[]{:S(2)}) collective-permute-start(bf16[512,2816]{1,0:T(8,128)(2,1)} %param.38), channel_id=1, source_target_pairs={{0,1},{1,0},{2,3},{3,2},{4,5},{5,4},{6,7},{7,6},{8,9},{9,8},{10,11... | collective-permute-start | bytes 8650760 | tf_op jit(solution)/shard_map/ppermute | solution.py:1039
  122.7 120.5 %collective-permute-start.35 = (bf16[128,512]{1,0:T(8,128)(2,1)}, bf16[128,512]{1,0:T(8,128)(2,1)}, u32[]{:S(2)}, u32[]{:S(2)}) collective-permute-start(bf16[128,512]{1,0:T(8,128)(2,1)} %get-tuple-element.83), channel_id=1, source_target_pairs={{0,1},{1,0},{2,3},{3,2},{4,5},{5,4},{6,7},{7,6},{8,9},{9,8},{10,11... | collective-permute-start | bytes 393224 | tf_op jit(solution)/shard_map/ppermute | solution.py:1039
  141.9 99.1 %collective-permute-start.29 = (bf16[128,512]{1,0:T(8,128)(2,1)}, bf16[128,512]{1,0:T(8,128)(2,1)}, u32[]{:S(2)}, u32[]{:S(2)}) collective-permute-start(bf16[128,512]{1,0:T(8,128)(2,1)} %get-tuple-element.79), channel_id=1, source_target_pairs={{0,1},{1,0},{2,3},{3,2},{4,5},{5,4},{6,7},{7,6},{8,9},{9,8},{10,11... | collective-permute-start | bytes 393224 | tf_op jit(solution)/shard_map/ppermute | solution.py:1039
  164.8 76.6 %collective-permute-start.30 = (bf16[128,1024]{1,0:T(8,128)(2,1)}, bf16[128,1024]{1,0:T(8,128)(2,1)}, u32[]{:S(2)}, u32[]{:S(2)}) collective-permute-start(bf16[128,1024]{1,0:T(8,128)(2,1)} %fusion.135), channel_id=1, source_target_pairs={{0,1},{1,0},{2,3},{3,2},{4,5},{5,4},{6,7},{7,6},{8,9},{9,8},{10,11... | collective-permute-start | bytes 786440 | tf_op jit(solution)/shard_map/ppermute | solution.py:1039
  174.6 68.9 %collective-permute-start.36 = (bf16[128,1024]{0,1:T(8,128)(2,1)}, bf16[128,1024]{0,1:T(8,128)(2,1)}, u32[]{:S(2)}, u32[]{:S(2)}) collective-permute-start(bf16[128,1024]{0,1:T(8,128)(2,1)} %bitcast.14), channel_id=1, source_target_pairs={{0,1},{1,0},{2,3},{3,2},{4,5},{5,4},{6,7},{7,6},{8,9},{9,8},{10,11... | collective-permute-start | bytes 786440 | tf_op jit(solution)/shard_map/ppermute | solution.py:1039
  238.0 7.6 %collective-permute-start.42 = (bf16[128,1024]{1,0:T(8,128)(2,1)S(1)}, bf16[128,1024]{1,0:T(8,128)(2,1)}, u32[]{:S(2)}, u32[]{:S(2)}) collective-permute-start(bf16[128,1024]{1,0:T(8,128)(2,1)S(1)} %copy-done.46), channel_id=1, source_target_pairs={{0,1},{1,0},{2,3},{3,2},{4,5},{5,4},{6,7},{7,6},{8,9},{9,8},{10,11... | collective-permute-start | bytes 786440 | tf_op jit(solution)/shard_map/ppermute | solution.py:1039
  239.6 272.2 %all-gather.3.cloned.1.call-start = ((), (), s32[]{:S(2)}) async-start(), calls=%async_computation.1 | async-start | bytes 1114112 | tf_op jit(solution)/shard_map/all_gather | solution.py:1165
  243.1 438.2 %collective-permute-start.64 = (bf16[256,512]{1,0:T(8,128)(2,1)}, bf16[256,512]{1,0:T(8,128)(2,1)}, u32[]{:S(2)}, u32[]{:S(2)}) collective-permute-start(bf16[256,512]{1,0:T(8,128)(2,1)} %get-tuple-element.71), channel_id=1, source_target_pairs={{0,1},{1,0},{2,3},{3,2},{4,5},{5,4},{6,7},{7,6},{8,9},{9,8},{10,11... | collective-permute-start | bytes 786440 | tf_op jit(solution)/shard_map/ppermute | solution.py:1039
  245.2 7.5 %collective-permute-start.12 = (bf16[128,1408]{1,0:T(8,128)(2,1)}, bf16[128,1408]{1,0:T(8,128)(2,1)S(1)}, u32[]{:S(2)}, u32[]{:S(2)}) collective-permute-start(bf16[128,1408]{1,0:T(8,128)(2,1)} %get-tuple-element.69), channel_id=1, source_target_pairs={{0,1},{1,0},{2,3},{3,2},{4,5},{5,4},{6,7},{7,6},{8,9},{9,8},{10,11... | collective-permute-start | bytes 1081352 | tf_op jit(solution)/shard_map/ppermute | solution.py:1039
  245.6 12.6 %collective-permute-start.24 = (bf16[128,2816]{1,0:T(8,128)(2,1)S(1)}, bf16[128,2816]{1,0:T(8,128)(2,1)S(1)}, u32[]{:S(2)}, u32[]{:S(2)}) collective-permute-start(bf16[128,2816]{1,0:T(8,128)(2,1)S(1)} %copy-done.9), channel_id=1, source_target_pairs={{0,1},{1,0},{2,3},{3,2},{4,5},{5,4},{6,7},{7,6},{8,9},{9,8},{10,11... | collective-permute-start | bytes 2162696 | tf_op jit(solution)/shard_map/ppermute | solution.py:1039
  250.2 12.3 %collective-permute-start.19 = (bf16[128,2816]{1,0:T(8,128)(2,1)S(1)}, bf16[128,2816]{1,0:T(8,128)(2,1)S(1)}, u32[]{:S(2)}, u32[]{:S(2)}) collective-permute-start(bf16[128,2816]{1,0:T(8,128)(2,1)S(1)} %copy-done.11), channel_id=1, source_target_pairs={{0,1},{1,0},{2,3},{3,2},{4,5},{5,4},{6,7},{7,6},{8,9},{9,8},{10,11... | collective-permute-start | bytes 2162696 | tf_op jit(solution)/shard_map/ppermute | solution.py:1039
  250.9 23.1 %collective-permute-start.31 = (bf16[256,1024]{1,0:T(8,128)(2,1)S(1)}, bf16[256,1024]{1,0:T(8,128)(2,1)S(1)}, u32[]{:S(2)}, u32[]{:S(2)}) collective-permute-start(bf16[256,1024]{1,0:T(8,128)(2,1)S(1)} %convolution_convert_fusion.8), channel_id=1, source_target_pairs={{0,2},{2,0},{4,6},{6,4},{8,10},{10,8},{12,14},{14,12},{16,18},{18,... | collective-permute-start | bytes 1572872 | tf_op jit(solution)/shard_map/ppermute | solution.py:823
  252.7 19.3 %collective-permute-start.59 = (bf16[256,1024]{1,0:T(8,128)(2,1)S(1)}, bf16[256,1024]{1,0:T(8,128)(2,1)S(1)}, u32[]{:S(2)}, u32[]{:S(2)}) collective-permute-start(bf16[256,1024]{1,0:T(8,128)(2,1)S(1)} %convolution_convert_fusion.3), channel_id=1, source_target_pairs={{0,8},{2,10},{4,12},{6,14},{8,0},{10,2},{12,4},{14,6},{16,24},{18,... | collective-permute-start | bytes 1572872 | tf_op jit(solution)/shard_map/ppermute | solution.py:823
  258.2 18.0 %collective-permute-start.54 = (bf16[256,1024]{1,0:T(8,128)(2,1)S(1)}, bf16[256,1024]{1,0:T(8,128)(2,1)S(1)}, u32[]{:S(2)}, u32[]{:S(2)}) collective-permute-start(bf16[256,1024]{1,0:T(8,128)(2,1)S(1)} %convolution_convert_fusion.4), channel_id=1, source_target_pairs={{0,4},{2,6},{4,0},{6,2},{8,12},{10,14},{12,8},{14,10},{16,20},{18,... | collective-permute-start | bytes 1572872 | tf_op jit(solution)/shard_map/ppermute | solution.py:823
  262.5 25.5 %collective-permute-start.49 = (bf16[256,1024]{1,0:T(8,128)(2,1)S(1)}, bf16[256,1024]{1,0:T(8,128)(2,1)S(1)}, u32[]{:S(2)}, u32[]{:S(2)}) collective-permute-start(bf16[256,1024]{1,0:T(8,128)(2,1)S(1)} %convolution_convert_fusion.5), channel_id=1, source_target_pairs={{0,2},{2,0},{4,6},{6,4},{8,10},{10,8},{12,14},{14,12},{16,18},{18,... | collective-permute-start | bytes 1572872 | tf_op jit(solution)/shard_map/ppermute | solution.py:823
  272.0 20.3 %collective-permute-start.43 = (bf16[256,1024]{1,0:T(8,128)(2,1)S(1)}, bf16[256,1024]{1,0:T(8,128)(2,1)S(1)}, u32[]{:S(2)}, u32[]{:S(2)}) collective-permute-start(bf16[256,1024]{1,0:T(8,128)(2,1)S(1)} %convolution_convert_fusion.6), channel_id=1, source_target_pairs={{0,8},{2,10},{4,12},{6,14},{8,0},{10,2},{12,4},{14,6},{16,24},{18,... | collective-permute-start | bytes 1572872 | tf_op jit(solution)/shard_map/ppermute | solution.py:823
  274.0 19.7 %collective-permute-start.37 = (bf16[256,1024]{1,0:T(8,128)(2,1)S(1)}, bf16[256,1024]{1,0:T(8,128)(2,1)S(1)}, u32[]{:S(2)}, u32[]{:S(2)}) collective-permute-start(bf16[256,1024]{1,0:T(8,128)(2,1)S(1)} %convolution_convert_fusion.7), channel_id=1, source_target_pairs={{0,4},{2,6},{4,0},{6,2},{8,12},{10,14},{12,8},{14,10},{16,20},{18,... | collective-permute-start | bytes 1572872 | tf_op jit(solution)/shard_map/ppermute | solution.py:823
  276.2 164.5 %collective-permute-start.14 = (bf16[704,1024]{1,0:T(8,128)(2,1)S(1)}, bf16[704,1024]{1,0:T(8,128)(2,1)S(1)}, u32[]{:S(2)}, u32[]{:S(2)}) collective-permute-start(bf16[704,1024]{1,0:T(8,128)(2,1)S(1)} %convolution_convert_fusion.2), channel_id=1, source_target_pairs={{0,2},{2,0},{4,6},{6,4},{8,10},{10,8},{12,14},{14,12},{16,18},{18,... | collective-permute-start | bytes 4325384 | tf_op jit(solution)/shard_map/ppermute | solution.py:823
  288.0 162.3 %collective-permute-start.20 = (bf16[256,2816]{1,0:T(8,128)(2,1)}, bf16[256,2816]{1,0:T(8,128)(2,1)}, u32[]{:S(2)}, u32[]{:S(2)}) collective-permute-start(bf16[256,2816]{1,0:T(8,128)(2,1)} %convolution_convert_fusion.1), channel_id=1, source_target_pairs={{0,4},{2,6},{4,0},{6,2},{8,12},{10,14},{12,8},{14,10},{16,20},{18,... | collective-permute-start | bytes 4325384 | tf_op jit(solution)/shard_map/ppermute | solution.py:823
  292.3 41.5 %collective-permute-start.32 = (bf16[128,1024]{1,0:T(8,128)(2,1)S(1)}, bf16[128,1024]{1,0:T(8,128)(2,1)S(1)}, u32[]{:S(2)}, u32[]{:S(2)}) collective-permute-start(bf16[128,1024]{1,0:T(8,128)(2,1)S(1)} %broadcast_select_fusion.13), channel_id=1, source_target_pairs={{0,4},{2,6},{4,0},{6,2},{8,12},{10,14},{12,8},{14,10},{16,20},{18,... | collective-permute-start | bytes 786440 | tf_op jit(solution)/shard_map/ppermute | solution.py:828
  293.7 40.3 %collective-permute-start.60 = (bf16[128,1024]{1,0:T(8,128)(2,1)S(1)}, bf16[128,1024]{1,0:T(8,128)(2,1)S(1)}, u32[]{:S(2)}, u32[]{:S(2)}) collective-permute-start(bf16[128,1024]{1,0:T(8,128)(2,1)S(1)} %broadcast_select_fusion.8), channel_id=1, source_target_pairs={{0,16},{2,18},{4,20},{6,22},{8,24},{10,26},{12,28},{14,30},{16,0},... | collective-permute-start | bytes 786440 | tf_op jit(solution)/shard_map/ppermute | solution.py:828
  333.8 7.9 %collective-permute-start.55 = (bf16[128,1024]{1,0:T(8,128)(2,1)S(1)}, bf16[128,1024]{1,0:T(8,128)(2,1)S(1)}, u32[]{:S(2)}, u32[]{:S(2)}) collective-permute-start(bf16[128,1024]{1,0:T(8,128)(2,1)S(1)} %broadcast_select_fusion.10), channel_id=1, source_target_pairs={{0,2},{2,0},{4,6},{6,4},{8,10},{10,8},{12,14},{14,12},{16,18},{18,... | collective-permute-start | bytes 786440 | tf_op jit(solution)/shard_map/ppermute | solution.py:828
  334.0 9.9 %collective-permute-start.50 = (bf16[128,1024]{1,0:T(8,128)(2,1)S(1)}, bf16[128,1024]{1,0:T(8,128)(2,1)S(1)}, u32[]{:S(2)}, u32[]{:S(2)}) collective-permute-start(bf16[128,1024]{1,0:T(8,128)(2,1)S(1)} %broadcast_select_fusion.12), channel_id=1, source_target_pairs={{0,4},{2,6},{4,0},{6,2},{8,12},{10,14},{12,8},{14,10},{16,20},{18,... | collective-permute-start | bytes 786440 | tf_op jit(solution)/shard_map/ppermute | solution.py:828
  341.7 13.6 %collective-permute-start.44 = (bf16[128,1024]{1,0:T(8,128)(2,1)S(1)}, bf16[128,1024]{1,0:T(8,128)(2,1)S(1)}, u32[]{:S(2)}, u32[]{:S(2)}) collective-permute-start(bf16[128,1024]{1,0:T(8,128)(2,1)S(1)} %broadcast_select_fusion.9), channel_id=1, source_target_pairs={{0,16},{2,18},{4,20},{6,22},{8,24},{10,26},{12,28},{14,30},{16,0},... | collective-permute-start | bytes 786440 | tf_op jit(solution)/shard_map/ppermute | solution.py:828
  343.9 111.1 %collective-permute-start.25 = (bf16[256,2816]{1,0:T(8,128)(2,1)}, bf16[256,2816]{1,0:T(8,128)(2,1)}, u32[]{:S(2)}, u32[]{:S(2)}) collective-permute-start(bf16[256,2816]{1,0:T(8,128)(2,1)} %convolution_convert_fusion), channel_id=1, source_target_pairs={{0,8},{2,10},{4,12},{6,14},{8,0},{10,2},{12,4},{14,6},{16,24},{18,... | collective-permute-start | bytes 4325384 | tf_op jit(solution)/shard_map/ppermute | solution.py:823
  355.3 7.7 %collective-permute-start.38 = (bf16[128,1024]{1,0:T(8,128)(2,1)S(1)}, bf16[128,1024]{1,0:T(8,128)(2,1)S(1)}, u32[]{:S(2)}, u32[]{:S(2)}) collective-permute-start(bf16[128,1024]{1,0:T(8,128)(2,1)S(1)} %broadcast_select_fusion.11), channel_id=1, source_target_pairs={{0,2},{2,0},{4,6},{6,4},{8,10},{10,8},{12,14},{14,12},{16,18},{18,... | collective-permute-start | bytes 786440 | tf_op jit(solution)/shard_map/ppermute | solution.py:828
  363.0 20.6 %collective-permute-start.33 = (bf16[64,1024]{1,0:T(8,128)(2,1)S(1)}, bf16[64,1024]{1,0:T(8,128)(2,1)S(1)}, u32[]{:S(2)}, u32[]{:S(2)}) collective-permute-start(bf16[64,1024]{1,0:T(8,128)(2,1)S(1)} %broadcast_select_fusion.24), channel_id=1, source_target_pairs={{0,8},{2,10},{4,12},{6,14},{8,0},{10,2},{12,4},{14,6},{16,24},{18,... | collective-permute-start | bytes 393224 | tf_op jit(solution)/shard_map/ppermute | solution.py:828
  442.6 14.3 %collective-permute-start.15 = (bf16[352,1024]{1,0:T(8,128)(2,1)S(1)}, bf16[352,1024]{1,0:T(8,128)(2,1)}, u32[]{:S(2)}, u32[]{:S(2)}) collective-permute-start(bf16[352,1024]{1,0:T(8,128)(2,1)S(1)} %broadcast_select_fusion.2), channel_id=1, source_target_pairs={{0,4},{2,6},{4,0},{6,2},{8,12},{10,14},{12,8},{14,10},{16,20},{18,... | collective-permute-start | bytes 2162696 | tf_op jit(solution)/shard_map/ppermute | solution.py:828
  452.4 21.5 %collective-permute-start.21 = (bf16[128,2816]{1,0:T(8,128)(2,1)S(1)}, bf16[128,2816]{1,0:T(8,128)(2,1)S(1)}, u32[]{:S(2)}, u32[]{:S(2)}) collective-permute-start(bf16[128,2816]{1,0:T(8,128)(2,1)S(1)} %broadcast_select_fusion.1), channel_id=1, source_target_pairs={{0,2},{2,0},{4,6},{6,4},{8,10},{10,8},{12,14},{14,12},{16,18},{18,... | collective-permute-start | bytes 2162696 | tf_op jit(solution)/shard_map/ppermute | solution.py:828
  458.5 15.1 %collective-permute-start.16 = (bf16[176,1024]{1,0:T(8,128)(2,1)S(1)}, bf16[176,1024]{1,0:T(8,128)(2,1)S(1)}, u32[]{:S(2)}, u32[]{:S(2)}) collective-permute-start(bf16[176,1024]{1,0:T(8,128)(2,1)S(1)} %broadcast_select_fusion.5), channel_id=1, source_target_pairs={{0,8},{2,10},{4,12},{6,14},{8,0},{10,2},{12,4},{14,6},{16,24},{18,... | collective-permute-start | bytes 1081352 | tf_op jit(solution)/shard_map/ppermute | solution.py:828
  458.7 32.2 %collective-permute-start.26 = (bf16[128,2816]{1,0:T(8,128)(2,1)S(1)}, bf16[128,2816]{1,0:T(8,128)(2,1)S(1)}, u32[]{:S(2)}, u32[]{:S(2)}) collective-permute-start(bf16[128,2816]{1,0:T(8,128)(2,1)S(1)} %broadcast_select_fusion), channel_id=1, source_target_pairs={{0,16},{2,18},{4,20},{6,22},{8,24},{10,26},{12,28},{14,30},{16,0},... | collective-permute-start | bytes 2162696 | tf_op jit(solution)/shard_map/ppermute | solution.py:828
  473.8 20.4 %collective-permute-start.17 = (bf16[176,512]{1,0:T(8,128)(2,1)S(1)}, bf16[176,512]{1,0:T(8,128)(2,1)S(1)}, u32[]{:S(2)}, u32[]{:S(2)}) collective-permute-start(bf16[176,512]{1,0:T(8,128)(2,1)S(1)} %broadcast_select_fusion.18), channel_id=1, source_target_pairs={{0,16},{2,18},{4,20},{6,22},{8,24},{10,26},{12,28},{14,30},{16,0},... | collective-permute-start | bytes 540680 | tf_op jit(solution)/shard_map/ppermute | solution.py:832
  474.2 20.7 %collective-permute-start.22 = (bf16[64,2816]{1,0:T(8,128)(2,1)S(1)}, bf16[64,2816]{1,0:T(8,128)(2,1)S(1)}, u32[]{:S(2)}, u32[]{:S(2)}) collective-permute-start(bf16[64,2816]{1,0:T(8,128)(2,1)S(1)} %broadcast_select_fusion.4), channel_id=1, source_target_pairs={{0,8},{2,10},{4,12},{6,14},{8,0},{10,2},{12,4},{14,6},{16,24},{18,... | collective-permute-start | bytes 1081352 | tf_op jit(solution)/shard_map/ppermute | solution.py:828
  495.1 9.2 %collective-permute-start.23 = (bf16[64,1408]{1,0:T(8,128)(2,1)S(1)}, bf16[64,1408]{1,0:T(8,128)(2,1)S(1)}, u32[]{:S(2)}, u32[]{:S(2)}) collective-permute-start(bf16[64,1408]{1,0:T(8,128)(2,1)S(1)} %broadcast_select_fusion.17), channel_id=1, source_target_pairs={{0,16},{2,18},{4,20},{6,22},{8,24},{10,26},{12,28},{14,30},{16,0},... | collective-permute-start | bytes 540680 | tf_op jit(solution)/shard_map/ppermute | solution.py:832
  498.9 12.9 %collective-permute-start.28 = (bf16[64,1408]{1,0:T(8,128)(2,1)S(1)}, bf16[64,1408]{1,0:T(8,128)(2,1)S(1)}, u32[]{:S(2)}, u32[]{:S(2)}) collective-permute-start(bf16[64,1408]{1,0:T(8,128)(2,1)S(1)} %broadcast_select_fusion.16), channel_id=1, source_target_pairs={{0,4},{2,6},{4,0},{6,2},{8,12},{10,14},{12,8},{14,10},{16,20},{18,... | collective-permute-start | bytes 540680 | tf_op jit(solution)/shard_map/ppermute | solution.py:832
  511.8 169.5 %collective-permute-start.65 = (bf16[256,2048]{1,0:T(8,128)(2,1)}, bf16[256,2048]{1,0:T(8,128)(2,1)S(1)}, u32[]{:S(2)}, u32[]{:S(2)}) collective-permute-start(bf16[256,2048]{1,0:T(8,128)(2,1)} %all-gather.3.cloned.1.call-done), channel_id=1, source_target_pairs={{0,1},{1,0},{2,3},{3,2},{4,5},{5,4},{6,7},{7,6},{8,9},{9,8},{10,11... | collective-permute-start | bytes 3145736 | tf_op jit(solution)/shard_map/ppermute | solution.py:1039
  (108 other events, 569.5 us)
Sparse Core Ops, SparseCore 0:
  239.7 84.9 reduce-scatter.3
  444.3 67.3 all-gather.2

commit v2 on v1

--- a/solution.py
+++ b/solution.py
@@ -522,31 +522,52 @@
     ]
 
 
-def to_heads_kernel(q_ref, k_ref, v_ref, landed, packed, *sems):
+def to_heads_kernel(q_ref, k_ref, v_ref, rows_ref, landed, rows_out, packed, rows_send, rows_recv, rows_own, *sems):
     peers = packed.shape[0]
+    me, core = lax.axis_index("ctx"), lax.axis_index("wsh")
     greet_all(peers)
+    copies = []
+    for step in range(1, peers):
+        copies.append(
+            pltpu.make_async_remote_copy(
+                src_ref=rows_ref,
+                dst_ref=rows_out.at[me],
+                send_sem=rows_send.at[step],
+                recv_sem=rows_recv.at[step],
+                device_id=(lax.rem(me + step, peers), core),
+                device_id_type=MESH,
+            )
+        )
+    copies.append(pltpu.make_async_copy(rows_ref, rows_out.at[me], rows_own))
     for head in range(peers):
         cols = slice(head * HEAD_DIM, (head + 1) * HEAD_DIM)
         packed[head, : 2 * BLOCK, :] = jnp.concatenate([q_ref[:, cols], k_ref[:, cols]], axis=1)
         packed[head, 2 * BLOCK :, :] = jnp.concatenate(
             [v_ref[:BLOCK, cols], v_ref[BLOCK:, cols]], axis=1
         )
+    for each in copies:
+        each.start()
     exchange_all(packed, landed, *sems)
-
-
-def to_heads(queries, keys, values):
+    for each in copies:
+        each.wait()
+
+
+def to_heads(queries, keys, values, rows):
     shape = (HEADS, 3 * BLOCK, 2 * HEAD_DIM)
     return pl.pallas_call(
         to_heads_kernel,
-        out_shape=jax.ShapeDtypeStruct(shape, BF16),
-        in_specs=[vmem_spec()] * 3,
-        out_specs=vmem_spec(),
-        scratch_shapes=[pltpu.VMEM(shape, BF16)] + exchange_scratch(HEADS),
+        out_shape=[
+            jax.ShapeDtypeStruct(shape, BF16),
+            jax.ShapeDtypeStruct((HEADS,) + rows.shape, BF16),
+        ],
+        in_specs=[vmem_spec()] * 4,
+        out_specs=[vmem_spec()] * 2,
+        scratch_shapes=[pltpu.VMEM(shape, BF16)] + exchange_scratch(HEADS) * 2,
         compiler_params=pltpu.CompilerParams(
             collective_id=1, has_side_effects=True, vmem_limit_bytes=16 * MIB
         ),
         name="to_heads",
-    )(queries, keys, values)
+    )(queries, keys, values, rows)
 
 
 def rows_to_heads_kernel(g_ref, landed, packed, *sems):
@@ -799,216 +820,412 @@
     )(order, landed, grad_landed, sums, norm, bias_lines)
 
 
-BIT_X, BIT_Y, BIT_Z0, BIT_Z1 = 0, 1, 2, 3
-X_FIRST = (BIT_X, BIT_Y, BIT_Z0, BIT_Z1)
-Y_FIRST = (BIT_Y, BIT_X, BIT_Z0, BIT_Z1)
-Z_FIRST = (BIT_Z0, BIT_Z1, BIT_X, BIT_Y)
-
-
-def flip_pairs(bit, size):
-    return [(at, at ^ (1 << bit)) for at in range(size)]
+BIT_X, BIT_Y = 0, 1
 
 
 def pick(flag, when_set, when_clear):
     return jnp.where(flag == 1, when_set, when_clear)
 
 
-def reduce_pieces(left, right, order):
+UP, DOWN, ACROSS_Y, ACROSS_X = 0, 1, 2, 3
+
+
+class Product:
+    def __init__(self, left, right, first, tall, route):
+        self.left, self.right, self.first, self.tall, self.route = left, right, first, tall, route
+
+
+def weight_grad_kernel(products, left_count, *refs):
+    count = len(products)
+    refs = list(refs)
+
+    def take(number):
+        taken = refs[:number]
+        del refs[:number]
+        return taken
+
+    lefts, rights, (vec_in,) = take(left_count), take(count), take(1)
+    wholes, (vec_out,) = take(count), take(1)
+    left_all, left_pass, left_t = take(left_count), take(left_count), take(left_count)
+    right_all, away, came, held, up_in, down_in = (take(count) for _ in range(6))
+    (
+        left_send,
+        left_recv,
+        right_send,
+        right_recv,
+        pair_send,
+        pair_recv,
+        line_send,
+        line_recv,
+        out_send,
+        out_recv,
+        own_sem,
+        vec_send,
+        vec_recv,
+    ) = refs
+    me, core = lax.axis_index("ctx"), lax.axis_index("wsh")
     peers = lax.axis_size("ctx")
-    me = lax.axis_index("ctx")
-    bits = [(me >> bit) & 1 for bit in order]
-    half = left.shape[1] // 2
-    low, high = left[:, :half], left[:, half:]
-    away = left_contract(pick(bits[0], low, high), right).astype(BF16)
-    came = lax.ppermute(away, "ctx", flip_pairs(order[0], peers))
-    held = (left_contract(pick(bits[0], high, low), right) + came.astype(F32)).astype(BF16)
-    for bit, name in zip(bits[1:3], order[1:3]):
-        half = held.shape[0] // 2
-        low, high = held[:half], held[half:]
-        came = lax.ppermute(pick(bit, low, high), "ctx", flip_pairs(name, peers))
-        held = (pick(bit, high, low).astype(F32) + came.astype(F32)).astype(BF16)
-    half = held.shape[1] // 2
-    low, high = held[:, :half], held[:, half:]
-    came = lax.ppermute(pick(bits[3], low, high), "ctx", flip_pairs(order[3], peers))
-    return (pick(bits[3], high, low).astype(F32) + came.astype(F32)).astype(BF16)
-
-
-def gather_kernel(orders, *refs):
-    count = len(orders)
-    pieces, vec_in = refs[:count], refs[count]
-    wholes, vec_out = refs[count + 1 : 2 * count + 1], refs[2 * count + 1]
-    send_sem, recv_sem, own_sem, vec_send, vec_recv = refs[2 * count + 2 :]
-    me, core = lax.axis_index("ctx"), lax.axis_index("wsh")
-    peers = vec_out.shape[0]
+    tokens = lefts[0].shape[0]
     x, y, z = lax.rem(me, 2), lax.rem(me // 2, 2), me // 4
-    greet_all(peers)
+
+    barrier = pltpu.get_barrier_semaphore()
+    for step in range(1, peers):
+        for side in (core, 1 - core):
+            pl.semaphore_signal(
+                barrier, inc=1, device_id=(lax.rem(me + step, peers), side), device_id_type=MESH
+            )
+    pl.semaphore_signal(barrier, inc=1, device_id=(me, 1 - core), device_id_type=MESH)
+    pl.semaphore_wait(barrier, 2 * peers - 1)
 
     def place(zz, yy, xx):
         return zz * 4 + yy * 2 + xx
 
-    def window(array, at):
-        rows, cols = pieces[array].shape
-        bits = [lax.rem(at // (1 << bit), 2) for bit in orders[array]]
-        block = bits[0] * 4 + bits[1] * 2 + bits[2]
-        return wholes[array].at[
-            pl.ds(pl.multiple_of(block * rows, 16), rows),
-            pl.ds(pl.multiple_of(bits[3] * cols, 128), cols),
-        ]
-
-    UP, DOWN, ACROSS_Y, ACROSS_X = 0, 1, 2, 3
     targets = {
         UP: place(lax.rem(z + 1, 4), y, x),
         DOWN: place(lax.rem(z + 3, 4), y, x),
         ACROSS_Y: place(z, 1 - y, x),
         ACROSS_X: place(z, y, 1 - x),
     }
-    sent = []
-
-    def send(array, at, way, slot, only=None, own=False):
-        def act(what):
-            copy = pltpu.make_async_remote_copy(
-                src_ref=pieces[array] if own else window(array, at),
-                dst_ref=window(array, at),
-                send_sem=send_sem.at[array, way, slot],
-                recv_sem=recv_sem.at[array, at],
-                device_id=(targets[way], core),
-                device_id_type=MESH,
-            )
-            if what == "start":
-                copy.start()
-            else:
-                copy.wait_send()
-
-        def guarded(what):
-            if only is None:
-                act(what)
-            else:
-                pl.when(only)(functools.partial(act, what))
-
-        guarded("start")
-        sent.append(functools.partial(guarded, "end"))
-
-    def arrive(array, at):
-        pltpu.make_async_remote_copy(
-            src_ref=window(array, at),
-            dst_ref=window(array, at),
-            send_sem=own_sem.at[array],
-            recv_sem=recv_sem.at[array, at],
-            device_id=(targets[ACROSS_X], core),
+    finish = []
+
+    def remote(src, dst, send_sem, recv_sem, ctx, side):
+        return pltpu.make_async_remote_copy(
+            src_ref=src,
+            dst_ref=dst,
+            send_sem=send_sem,
+            recv_sem=recv_sem,
+            device_id=(ctx, side),
             device_id_type=MESH,
-        ).wait_recv()
-
-    def along_z(array, zz, at, slot, own=False):
-        send(array, at, UP, slot, only=jnp.logical_and(zz <= z, z < 3), own=own)
-        send(array, at, DOWN, slot, only=jnp.logical_and(zz >= z, z > 0), own=own)
-
-    late_z = [array for array in range(count) if orders[array] == Z_FIRST]
-    early_z = [array for array in range(count) if orders[array] != Z_FIRST]
-
-    def planar(array):
-        if orders[array] == X_FIRST:
-            return ACROSS_Y, ACROSS_X, lambda zz: place(zz, 1 - y, x), lambda zz: place(zz, y, 1 - x)
-        return ACROSS_X, ACROSS_Y, lambda zz: place(zz, y, 1 - x), lambda zz: place(zz, 1 - y, x)
-
-    opposite = lambda zz: place(zz, 1 - y, 1 - x)
-
-    own_copies = [
-        pltpu.make_async_copy(pieces[array], window(array, me), own_sem.at[array])
-        for array in range(count)
-    ]
-    for each in own_copies:
-        each.start()
-    vec_copies = []
+        )
+
+    def launch(copy, only=None):
+        if only is None:
+            copy.start()
+            finish.append(copy.wait_send)
+        else:
+            pl.when(only)(copy.start)
+            finish.append(lambda: pl.when(only)(copy.wait_send))
+
+    def arrived(dst, recv_sem):
+        remote(dst, dst, own_sem.at[0], recv_sem, me, 1 - core).wait_recv()
+
+    def lanes(ref, at, width):
+        return ref.at[:, pl.ds(pl.multiple_of(at * width, 128), width)]
+
+    def rows(ref, at, height):
+        return ref.at[pl.ds(pl.multiple_of(at * height, 16), height)]
+
+    def slot(ref, index):
+        return ref.at[pl.ds(index * tokens, tokens)]
+
+    def axes(product):
+        along_x, along_y = (x, ACROSS_X), (y, ACROSS_Y)
+        return (along_x, along_y) if product.first == BIT_X else (along_y, along_x)
+
+    left_axis = {product.left: product for product in products}
+
+    def send_left(at):
+        (_, way), _ = axes(left_axis[at])
+        half = left_all[at].shape[1]
+        launch(remote(lanes(lefts[at], core, half), slot(left_all[at], 1), left_send.at[at, 0], left_recv.at[at, 0], targets[way], core))
+        launch(remote(lanes(lefts[at], 1 - core, half), left_pass[at], left_send.at[at, 1], left_recv.at[at, 1], targets[way], core))
+        launch(remote(lanes(lefts[at], 1 - core, half), slot(left_all[at], 2), left_send.at[at, 2], left_recv.at[at, 2], me, 1 - core))
+        own = pltpu.make_async_copy(lanes(lefts[at], core, half), slot(left_all[at], 0), left_send.at[at, 4])
+        own.start()
+        return own
+
+    def send_right(at):
+        (mine, way), _ = axes(products[at])
+        half = right_all[at].shape[1]
+        launch(remote(lanes(rights[at], 1 - mine, half), slot(right_all[at], 1), right_send.at[at, 0], right_recv.at[at, 0], targets[way], core))
+        launch(remote(lanes(rights[at], mine, half), slot(right_all[at], 2), right_send.at[at, 1], right_recv.at[at, 1], me, 1 - core))
+        own = pltpu.make_async_copy(lanes(rights[at], mine, half), slot(right_all[at], 0), right_send.at[at, 3])
+        own.start()
+        return own
+
+    seen = set()
+    owns = {}
+    for at, product in enumerate(products):
+        if product.left not in seen:
+            seen.add(product.left)
+            owns["left", product.left] = send_left(product.left)
+        owns["right", at] = send_right(at)
+
     for step in range(1, peers):
         peer = lax.rem(me + step, peers)
-        vec_copies.append(
-            pltpu.make_async_remote_copy(
-                src_ref=vec_in,
-                dst_ref=vec_out.at[me],
-                send_sem=vec_send.at[step],
-                recv_sem=vec_recv.at[step],
-                device_id=(peer, core),
-                device_id_type=MESH,
-            )
-        )
-    vec_copies.append(pltpu.make_async_copy(vec_in, vec_out.at[me], vec_recv.at[0]))
-    for each in vec_copies:
-        each.start()
-
-    for array in early_z:
-        along_z(array, z, me, 0, own=True)
-        second, third, _, _ = planar(array)
-        send(array, me, second, 0, own=True)
-        send(array, me, third, 0, own=True)
-    for array in late_z:
-        send(array, me, ACROSS_Y, 0, own=True)
-        send(array, me, ACROSS_X, 0, own=True)
-        along_z(array, z, me, 0, own=True)
-    for array in late_z:
-        at = place(z, 1 - y, x)
-        arrive(array, at)
-        send(array, at, ACROSS_X, 1)
-        along_z(array, z, at, 1)
-    for step in range(1, 4):
-        if step <= 2:
-            for array in late_z:
-                at = place(z, y, 1 - x) if step == 1 else opposite(z)
-                arrive(array, at)
-                along_z(array, z, at, 1 + step)
-        for array in early_z:
-            zz = z ^ step
-            at = place(zz, y, x)
-            second, third, _, _ = planar(array)
-            arrive(array, at)
-            along_z(array, zz, at, step)
-            send(array, at, second, step)
-            send(array, at, third, step)
-    for step in range(4):
-        for array in early_z:
-            second, third, near, _ = planar(array)
-            at = near(z ^ step)
-            arrive(array, at)
-            send(array, at, third, 4 + step)
-        if step:
-            for array in late_z:
-                zz = z ^ step
-                for slot, at in enumerate(
-                    (place(zz, y, x), place(zz, 1 - y, x), place(zz, y, 1 - x), opposite(zz))
-                ):
-                    arrive(array, at)
-                    along_z(array, zz, at, 4 * step + slot)
-    for step in range(4):
-        for array in early_z:
-            _, _, _, far = planar(array)
-            arrive(array, far(z ^ step))
-            arrive(array, opposite(z ^ step))
-    for each in sent:
+        for offset, side in ((0, core), (peers, 1 - core)):
+            launch(remote(vec_in, vec_out.at[core * peers + me], vec_send.at[offset + step], vec_recv.at[core * peers + me], peer, side))
+    launch(remote(vec_in, vec_out.at[core * peers + me], vec_send.at[peers], vec_recv.at[core * peers + me], me, 1 - core))
+    own_vec = pltpu.make_async_copy(vec_in, vec_out.at[core * peers + me], vec_send.at[0])
+    own_vec.start()
+
+    passed = set()
+
+    def pass_on(at):
+        left = products[at].left
+        if left not in passed:
+            passed.add(left)
+            arrived(slot(left_all[left], 1), left_recv.at[left, 0])
+            arrived(left_pass[left], left_recv.at[left, 1])
+            launch(remote(left_pass[left], slot(left_all[left], 3), left_send.at[left, 3], left_recv.at[left, 3], me, 1 - core))
+        arrived(slot(right_all[at], 1), right_recv.at[at, 0])
+        launch(remote(slot(right_all[at], 1), slot(right_all[at], 3), right_send.at[at, 2], right_recv.at[at, 2], me, 1 - core))
+
+    def multiply(at, out, half):
+        product = products[at]
+        left, right = left_t[product.left], right_all[at]
+        height, width = out.shape
+        step = 256 if height <= 256 else 128 if height % 256 else 256
+        if product.tall:
+            columns = pl.ds(pl.multiple_of(half * width, 128), width)
+
+            def strip(index, carry):
+                band = pl.ds(pl.multiple_of(index * 176, 16), 176)
+                out[band, :] = plain_dot(left[band, :], right[:, columns]).astype(BF16)
+                return carry
+
+            lax.fori_loop(0, height // 176, strip, 0)
+        else:
+            band = pl.ds(pl.multiple_of(half * height, 16), height)
+
+            def strip(index, carry):
+                columns = pl.ds(pl.multiple_of(index * 256, 128), 256)
+                out[:, columns] = plain_dot(left[band, :], right[:, columns]).astype(BF16)
+                return carry
+
+            lax.fori_loop(0, width // 256, strip, 0)
+            if width % 256:
+                out[:, width - 128 :] = plain_dot(left[band, :], right[:, width - 128 :]).astype(BF16)
+
+    turned = set()
+
+    def product_away(at):
+        left = products[at].left
+        if left not in turned:
+            turned.add(left)
+            arrived(slot(left_all[left], 2), left_recv.at[left, 2])
+            arrived(slot(left_all[left], 3), left_recv.at[left, 3])
+            owns["left", left].wait()
+            height = left_t[left].shape[0]
+
+            def turn(index, carry):
+                band = pl.ds(pl.multiple_of(index * 128, 128), 128)
+                left_t[left][band, :] = jnp.transpose(left_all[left][:, band], (1, 0))
+                return carry
+
+            lax.fori_loop(0, height // 128, turn, 0)
+        arrived(slot(right_all[at], 2), right_recv.at[at, 1])
+        arrived(slot(right_all[at], 3), right_recv.at[at, 2])
+        owns["right", at].wait()
+        _, (mine, way) = axes(products[at])
+        multiply(at, away[at], 1 - mine)
+        launch(remote(away[at], came[at], pair_send.at[at], pair_recv.at[at], targets[way], core))
+        multiply(at, held[at], mine)
+
+    def add(into, more):
+        into[...] = (into[...].astype(F32) + more[...].astype(F32)).astype(BF16)
+
+    def add_pair(at):
+        arrived(came[at], pair_recv.at[at])
+        add(held[at], came[at])
+
+    def line_step(at, step):
+        height = held[at].shape[0] // 4
+        for side, buffer, behind, chunk, way in (
+            (0, up_in[at], z, lax.rem(z + 3 - step, 4), UP),
+            (1, down_in[at], 3 - z, lax.rem(z + step + 1, 4), DOWN),
+        ):
+            recv_sem = line_recv.at[at, side, chunk]
+
+            def land(buffer=buffer, chunk=chunk, recv_sem=recv_sem):
+                arrived(rows(buffer, chunk, height), recv_sem)
+                add(rows(held[at], chunk, height), rows(buffer, chunk, height))
+
+            pl.when(jnp.logical_and(behind > 0, behind <= step))(land)
+            if step < 3:
+                launch(
+                    remote(
+                        rows(held[at], chunk, height),
+                        rows(buffer, chunk, height),
+                        line_send.at[at, side, chunk],
+                        recv_sem,
+                        targets[way],
+                        core,
+                    ),
+                    only=behind <= step,
+                )
+
+    def own_piece(at):
+        return rows(held[at], z, held[at].shape[0] // 4)
+
+    def window(at, where):
+        product = products[at]
+        height, width = held[at].shape
+        height //= 4
+        xx, yy, zz = lax.rem(where, 2), lax.rem(where // 2, 2), where // 4
+        one, two = (xx, yy) if product.first == BIT_X else (yy, xx)
+        row, column = (zz, one * 2 + two) if product.tall else (two * 4 + zz, one)
+        return wholes[at].at[
+            pl.ds(pl.multiple_of(row * height, 16), height),
+            pl.ds(pl.multiple_of(column * width, 128), width),
+        ]
+
+    def send(at, where, way, index, only=None, own=False):
+        launch(
+            remote(
+                own_piece(at) if own else window(at, where),
+                window(at, where),
+                out_send.at[at, way, index],
+                out_recv.at[at, where],
+                targets[way],
+                core,
+            ),
+            only,
+        )
+
+    def arrive(at, where, only=None):
+        def act():
+            arrived(window(at, where), out_recv.at[at, where])
+
+        if only is None:
+            act()
+        else:
+            pl.when(only)(act)
+
+    def near(way, zz):
+        return place(zz, 1 - y, x) if way == ACROSS_Y else place(zz, y, 1 - x)
+
+    def opposite(zz):
+        return place(zz, 1 - y, 1 - x)
+
+    def from_line(apart):
+        return (
+            (z >= apart, lax.rem(z + 4 - apart, 4), UP, jnp.logical_and(z >= apart, z < 3)),
+            (z + apart <= 3, lax.rem(z + apart, 4), DOWN, jnp.logical_and(z + apart <= 3, z > 0)),
+        )
+
+    def gather_step(at, step):
+        z_first, second, third = products[at].route
+        if step == 0:
+            own = pltpu.make_async_copy(own_piece(at), window(at, me), own_sem.at[at])
+            own.start()
+            finish.append(own.wait)
+            if not z_first:
+                send(at, me, second, 0, own=True)
+                send(at, me, third, 0, own=True)
+            send(at, me, UP, 0, only=z < 3, own=True)
+            send(at, me, DOWN, 0, only=z > 0, own=True)
+            if z_first:
+                send(at, me, second, 0, own=True)
+                send(at, me, third, 0, own=True)
+        elif z_first:
+            if step <= 3:
+                for side, (there, zz, way, on) in enumerate(from_line(step)):
+                    where = place(zz, y, x)
+                    arrive(at, where, there)
+                    send(at, where, way, step, on)
+                    send(at, where, second, 2 * step + side, there)
+                    send(at, where, third, 2 * step + side, there)
+            elif step <= 7:
+                where = near(second, z ^ (step - 4))
+                arrive(at, where)
+                send(at, where, third, 4 + step)
+            elif step == 8:
+                for turn in range(4):
+                    arrive(at, near(third, z ^ turn))
+                    arrive(at, opposite(z ^ turn))
+        else:
+            if step == 1:
+                where = near(second, z)
+                arrive(at, where)
+                send(at, where, third, 1)
+                send(at, where, UP, 1, z < 3)
+                send(at, where, DOWN, 1, z > 0)
+            elif step == 2:
+                for index, where in ((2, near(third, z)), (3, opposite(z))):
+                    arrive(at, where)
+                    send(at, where, UP, index, z < 3)
+                    send(at, where, DOWN, index, z > 0)
+            elif step <= 5:
+                for there, zz, way, on in from_line(step - 2):
+                    for index, where in enumerate(
+                        (place(zz, y, x), near(second, zz), near(third, zz), opposite(zz))
+                    ):
+                        arrive(at, where, there)
+                        send(at, where, way, 4 * (step - 2) + index, on)
+
+    for at in range(count):
+        pass_on(at)
+        if at:
+            product_away(at - 1)
+    product_away(count - 1)
+    for time in range(count + 4):
+        if time < count:
+            add_pair(time)
+        for step in range(4):
+            if 0 <= time - step < count:
+                line_step(time - step, step)
+        if time >= 4:
+            gather_step(time - 4, 0)
+    for step in range(1, 9):
+        for at in range(count):
+            gather_step(at, step)
+
+    for step in range(1, peers):
+        peer = lax.rem(me + step, peers)
+        for side in (core, 1 - core):
+            arrived(vec_out.at[side * peers + peer], vec_recv.at[side * peers + peer])
+    arrived(vec_out.at[(1 - core) * peers + me], vec_recv.at[(1 - core) * peers + me])
+    own_vec.wait()
+    for each in finish:
         each()
-    for each in own_copies + vec_copies:
-        each.wait()
-
-
-def gather_pieces(pieces, orders, vector):
-    count, peers = len(pieces), lax.axis_size("ctx")
+
+
+def weight_grads(products, lefts, rights, vector):
+    count, peers = len(products), lax.axis_size("ctx")
+    tokens = lefts[0].shape[0]
     dma = pltpu.SemaphoreType.DMA
+    vmem = pltpu.VMEM
+    halves = [left.shape[1] // 2 for left in lefts]
+    helds = []
+    for product, right in zip(products, rights):
+        height, width = halves[product.left], right.shape[1] // 2
+        helds.append((height, width // 2) if product.tall else (height // 2, width))
+    lands = [vmem(shape, BF16) for shape in helds]
     return pl.pallas_call(
-        functools.partial(gather_kernel, orders),
+        functools.partial(weight_grad_kernel, products, len(lefts)),
         out_shape=[
-            jax.ShapeDtypeStruct((8 * piece.shape[0], 2 * piece.shape[1]), BF16) for piece in pieces
+            jax.ShapeDtypeStruct((halves[product.left], right.shape[1]), BF16)
+            for product, right in zip(products, rights)
         ]
-        + [jax.ShapeDtypeStruct((peers,) + vector.shape, F32)],
-        in_specs=[any_spec()] * (count + 1),
-        out_specs=[any_spec()] * (count + 1),
-        scratch_shapes=[
+        + [jax.ShapeDtypeStruct((2 * peers,) + vector.shape, F32)],
+        in_specs=[vmem_spec()] * (len(lefts) + count + 1),
+        out_specs=[any_spec()] * count + [vmem_spec()],
+        scratch_shapes=[vmem((4 * tokens, half), BF16) for half in halves]
+        + [vmem((tokens, half), BF16) for half in halves]
+        + [vmem((half, 4 * tokens), BF16) for half in halves]
+        + [vmem((4 * tokens, right.shape[1] // 2), BF16) for right in rights]
+        + lands * 5
+        + [
+            dma((len(lefts), 5)),
+            dma((len(lefts), 4)),
+            dma((count, 4)),
+            dma((count, 3)),
+            dma((count,)),
+            dma((count,)),
+            dma((count, 2, 4)),
+            dma((count, 2, 4)),
             dma((count, 4, 16)),
             dma((count, peers)),
             dma((count,)),
-            dma((peers,)),
-            dma((peers,)),
+            dma((2 * peers,)),
+            dma((2 * peers,)),
         ],
-        compiler_params=pltpu.CompilerParams(collective_id=5, has_side_effects=True),
-        name="gather_pieces",
-    )(*pieces, vector)
+        compiler_params=pltpu.CompilerParams(
+            collective_id=5, has_side_effects=True, vmem_limit_bytes=52 * MIB
+        ),
+        name="weight_grads",
+    )(*lefts, *rights, vector)
 
 
 def on_device_by_heads(
@@ -1093,7 +1310,8 @@
     queries = times(normed_one, query_pair).astype(BF16)
     keys = times(normed_one, key_pair).astype(BF16)
     values = times(normed_one, value_pair).astype(BF16)
-    landed = to_heads(queries, keys, values)
+    landed, encoder_all = to_heads(queries, keys, values, encoder[0])
+    encoder_all = encoder_all.reshape(-1, encoder.shape[2])
 
     own_column = jnp.sum(
         jnp.where(jnp.arange(HEADS)[None, :] == me, bias_rows, 0.0), axis=1, keepdims=True
@@ -1109,7 +1327,6 @@
     after_self = resid_in + times(attended, out_pair)
     normed_two = rms_norm(after_self, gain_two).astype(BF16)
     cross_q_heads = times(normed_two, cross_query_pair).astype(BF16).reshape(tokens, HEADS, HEAD_DIM)
-    encoder_all = lax.all_gather(encoder[0], "ctx", axis=0, tiled=True)
     cross_k_heads = times(encoder_all, cross_key_pair).astype(BF16).reshape(-1, HEADS, HEAD_DIM)
     cross_v_heads = times(encoder_all, cross_value_pair).astype(BF16).reshape(-1, HEADS, HEAD_DIM)
     cross_logits = jnp.einsum(
@@ -1132,17 +1349,12 @@
 
     resid_grad = cotangent[0].astype(F32)
     branch_three = cotangent[0]
-    down_piece = reduce_pieces(both_cores(hidden), both_whole(branch_three), X_FIRST)
     gate_grad, up_grad = mlp_pull(times_back(branch_three, down_pair))
     gate_grad, up_grad = gate_grad.astype(BF16), up_grad.astype(BF16)
-    normed_three_both = both_cores(normed_three)
-    gate_piece = reduce_pieces(normed_three_both, both_whole(gate_grad), Y_FIRST)
-    up_piece = reduce_pieces(normed_three_both, both_whole(up_grad), Z_FIRST)
     normed_three_grad = times_back(gate_grad, gate_pair) + times_back(up_grad, up_pair)
     part_grad, gain_three_grad = norm_back(after_cross, gain_three, normed_three_grad)
     after_cross_grad = resid_grad + part_grad
     branch_two = after_cross_grad.astype(BF16)
-    cross_out_piece = reduce_pieces(both_cores(cross_mixed), both_whole(branch_two), X_FIRST)
     mix_grad = times_back(branch_two, cross_out_pair).astype(BF16).reshape(tokens, HEADS, HEAD_DIM)
     cross_score_grad = jnp.einsum(
         "qhe,khe->hqk", mix_grad, cross_v_heads, preferred_element_type=F32
@@ -1168,12 +1380,10 @@
         + times_back(cross_kv_grad[:, head_width:], cross_value_pair)
     ).astype(BF16)
     cross_kv_w_grad = left_contract(both_cores(encoder_all), both_whole(cross_kv_all))
-    cross_query_piece = reduce_pieces(both_cores(normed_two), both_whole(cross_q_grad), Y_FIRST)
     normed_two_grad = times_back(cross_q_grad, cross_query_pair)
     part_grad, gain_two_grad = norm_back(after_self, gain_two, normed_two_grad)
     after_self_grad = after_cross_grad + part_grad
     branch_one = after_self_grad.astype(BF16)
-    out_piece = reduce_pieces(both_cores(attended), both_whole(branch_one), Z_FIRST)
     grad_landed = rows_to_heads(times_back(branch_one, out_pair).astype(BF16))
     packed_grads, offset_lines = attend_back(
         block_order, landed, grad_landed, attn_sum, log_norm, bias_lines
@@ -1186,10 +1396,6 @@
     table_column = jnp.sum(jnp.where(in_bucket, offset_sums.reshape(1, length), 0.0), axis=1)
     table_grad = jnp.where(jnp.arange(HEADS)[None, :] == me, table_column[:, None], 0.0)
 
-    normed_one_both = both_cores(normed_one)
-    query_piece = reduce_pieces(normed_one_both, both_whole(query_grad), X_FIRST)
-    key_piece = reduce_pieces(normed_one_both, both_whole(key_grad), Y_FIRST)
-    value_piece = reduce_pieces(normed_one_both, both_whole(value_grad), Z_FIRST)
     normed_one_grad = (
         times_back(query_grad, query_pair)
         + times_back(key_grad, key_pair)
@@ -1207,30 +1413,36 @@
             jnp.zeros((512,), F32),
         ]
     ).reshape(8, 512)
-    vector = vector + swap(vector)
-    pieces = (
-        down_piece,
-        gate_piece,
-        up_piece,
-        cross_out_piece,
-        cross_query_piece,
-        out_piece,
-        query_piece,
-        key_piece,
-        value_piece,
-    )
-    orders = (X_FIRST, Y_FIRST, Z_FIRST) * 3
-    *wholes, vectors = gather_pieces(pieces, orders, vector)
+    z_then_yx, z_then_xy, z_last = (
+        (True, ACROSS_Y, ACROSS_X),
+        (True, ACROSS_X, ACROSS_Y),
+        (False, ACROSS_Y, ACROSS_X),
+    )
+    lefts = (normed_three, hidden, cross_mixed, normed_two, attended, normed_one)
+    products = (
+        Product(0, gate_grad, BIT_Y, False, z_then_yx),
+        Product(1, branch_three, BIT_X, True, z_then_yx),
+        Product(0, up_grad, BIT_Y, False, z_then_xy),
+        Product(5, query_grad, BIT_X, False, z_then_xy),
+        Product(2, branch_two, BIT_Y, False, z_last),
+        Product(5, key_grad, BIT_X, False, z_then_xy),
+        Product(3, cross_q_grad, BIT_Y, False, z_last),
+        Product(5, value_grad, BIT_X, False, z_then_xy),
+        Product(4, branch_one, BIT_Y, False, z_last),
+    )
+    *wholes, vectors = weight_grads(
+        products, lefts, [product.right for product in products], vector
+    )
     (
+        sum_gate,
         sum_down,
-        sum_gate,
         sum_up,
+        sum_query,
         sum_cross_out,
+        sum_key,
         sum_cross_query,
+        sum_value,
         sum_out,
-        sum_query,
-        sum_key,
-        sum_value,
     ) = (member.astype(F32) for member in wholes)
     totals = jnp.sum(vectors, axis=0)
     sum_gain_one, sum_gain_two, sum_gain_three = (

time: 702 us -> 549 us (0.78)
  waiting for transfers between devices: 189 us -> 17.8 us
  Pallas kernels: 221 us -> 359 us
  starting transfers between devices: 51.9 us -> 3.9 us
  blocking collectives: 45.4 us -> 0 us
  other arithmetic: 47.8 us -> 36.5 us
  matrix products: 103 us -> 93.1 us
    ppermute x36 -> x0, waiting for transfers between devices: 179 us -> none  [the longest x18 131 us: reduce_pieces(): came = lax.ppermute(pick(bit, low, high), 'ctx', flip_pairs(name, peers))]
    pallas_call x2, Pallas kernels: 161 us -> 292 us  [the longest x1 262 us: weight_grads(): pl.pallas_call(functools.partial(weight_grad_kernel, products, len(lefts)...]
    all_gather x1 -> x0, blocking collectives: 45.4 us -> none  [on_device_by_heads(): encoder_all = lax.all_gather(encoder[0], 'ctx', axis=0, tiled=True)]
    ppermute x36 -> x0, starting transfers between devices: 43.5 us -> none  [the longest x18 21.2 us: reduce_pieces(): came = lax.ppermute(pick(bit, low, high), 'ctx', flip_pairs(name, peers))]
    dot_general x19 -> x1, matrix products: 21.5 us -> 2.59 us  [left_contract(): lax.dot_general(left, right, (((0,), (0,)), ((), ())), preferred_element_...]
    reduce_scatter x1, waiting for transfers between devices: 0.01 us -> 17.7 us  [on_device_by_heads(): lax.psum_scatter(cross_kv_part, 'ctx', scatter_dimension=0, tiled=True)]
    convert_element_type x27 -> x0, other arithmetic: 9.69 us -> none  [the longest x9 6.16 us: reduce_pieces(): (pick(bits[3], high, low).astype(F32) + came.astype(F32)).astype(BF16)]
    dot_general x22, matrix products: 36.2 us -> 45.2 us  [right_contract(): lax.dot_general(left, right, (((1,), (1,)), ((), ())), preferred_element_...]
  transfers between devices with their start and end apart: 68 -> 16, of which waited for: 27 -> 1; matrix products, arithmetic and copies ran while one was open for 23% -> 25% of each run, Pallas kernels for 32% -> 66%
where the time goes in v2:
time: 549 us; the launch traced here: 540 us
  Pallas kernels  359 us (65%)
  matrix products  93.1 us (17%)
  other arithmetic  36.5 us (7%)
  waiting for transfers between devices  17.8 us (3%)
  between operations  15.4 us (3%)
  local copies, waits for them, and re-layouts  15.2 us (3%)
    pallas_call x1, Pallas kernels, weight_grads(): pl.pallas_call(functools.partial(weight_grad_kernel, products, len(lefts)...  262 us
    dot_general x22, matrix products, right_contract(): lax.dot_general(left, right, (((1,), (1,)), ((), ())), preferred_element_...  45.2 us
    dot_general x22, matrix products, plain_dot(): return jnp.dot(left, right, preferred_element_type=jnp.float32)  38.4 us
    pallas_call x1, Pallas kernels, to_heads(): pl.pallas_call(to_heads_kernel, out_shape=[jax.ShapeDtypeStruct(shape, BF...  30.9 us
    pallas_call x1, Pallas kernels, grads_from_heads(): pl.pallas_call(grads_from_heads_kernel, out_shape=[jax.ShapeDtypeStruct((...  22 us
    convert_element_type x9, other arithmetic, on_device_by_heads(): member.astype(F32)  19.8 us
    reduce_scatter x1, waiting for transfers between devices, on_device_by_heads(): lax.psum_scatter(cross_kv_part, 'ctx', scatter_dimension=0, tiled=True)  17.7 us
    pallas_call x1, Pallas kernels, from_heads(): pl.pallas_call(from_heads_kernel, out_shape=jax.ShapeDtypeStruct((2 * BLO...  14.9 us
  transfers between devices with their start and end apart: 16, of which 1 were waited for; matrix products, arithmetic and copies ran while one was open for 25% of the time, Pallas kernels for 66%

profile of v2, /device:TPU:0, one launch (start us, length us, event | category | flops | bytes accessed | tf_op | source)
XLA Modules:
  0.0 540.5 jit_solution(14010730120245578669)
XLA Ops:
  11.4 3.9 fusion.96
  23.6 30.9 %to_heads.1 = (bf16[16,192,128]{2,1,0:T(8,128)(2,1)S(1)}, bf16[16,16,1024]{2,1,0:T(8,128)(2,1)S(1)}) custom-call(bf16[128,1024]{1,0:T(8,128)(2,1)S(1)} %fusion.18.q_ref, bf16[128,1024]{1,0:T(8,128)(2,1)S(1)} %fusion.19.k_ref, bf16[128,1024]{1,0:T(8,128)(2,1)S(1)} %fusion.20.v_ref, bf16[16,1024]{1,0:T(8,128)(2,1)S(1)} %bitcast.150), custom_call_target="tpu_custom_call" | custom-call | tf_op jit(solution)/shard_map/to_heads/pallas_call | solution.py:557
  54.5 6.0 %attend.1 = (bf16[16,64,128]{2,1,0:T(8,128)(2,1)S(1)}, f32[64,2048]{1,0:T(8,128)S(1)}, f32[1,2048]{1,0:T(1,128)S(1)}) custom-call(s32[32]{0:T(128)S(1)} %copy-done.4, bf16[16,192,128]{2,1,0:T(8,128)(2,1)S(1)} %get-tuple-element.38.landed, f32[8,512]{1,0:T(8,128)S(1)} %select_maximum_fusion.bias_lines), custom_call_target="tpu_custom_call" | custom-call | flops 1073741824 | bytes 4194304 | tf_op jit(solution)/shard_map/attend/pallas_call | solution.py:706
  60.5 14.9 %from_heads.1.refs_4_ = bf16[128,1024]{1,0:T(8,128)(2,1)S(1)} custom-call(bf16[16,64,128]{2,1,0:T(8,128)(2,1)S(1)} %get-tuple-element.39.packed), custom_call_target="tpu_custom_call" | custom-call | tf_op jit(solution)/shard_map/from_heads/pallas_call | solution.py:617
  77.0 1.6 multiply_reduce_fusion.6
  82.0 1.8 fusion.115
  84.3 2.5 fusion.13
  88.2 1.9 fusion.114
  90.1 1.8 fusion.110
  91.9 2.5 fusion.12
  95.7 2.5 exponential_reduce_fusion
  102.2 1.6 multiply_reduce_fusion.5
  103.9 2.4 fusion.86
  106.3 2.4 fusion.87
  108.8 2.8 fusion.98
  111.6 2.5 convolution_add_fusion
  114.1 4.4 fusion.11
  118.5 3.4 fusion.117
  121.9 2.9 fusion.119
  124.8 2.9 fusion.118
  127.7 2.9 fusion.116
  131.0 2.1 fusion.121
  133.1 2.1 fusion.120
  141.4 1.8 copy.77.refs_12_
  143.2 2.2 pad_maximum_fusion
  145.4 2.3 copy.81
  147.8 1.9 fusion.122
  152.2 1.8 fusion.125
  154.0 1.7 fusion.124
  155.8 12.9 %rows_to_heads.1.grad_landed = bf16[16,64,128]{2,1,0:T(8,128)(2,1)S(1)} custom-call(bf16[128,1024]{1,0:T(8,128)(2,1)S(1)} %fusion.35.g_ref), custom_call_target="tpu_custom_call" | custom-call | tf_op jit(solution)/shard_map/rows_to_heads/pallas_call | solution.py:584
  168.8 10.2 %attend_back.1 = (bf16[16,192,128]{2,1,0:T(8,128)(2,1)S(1)}, f32[8,512]{1,0:T(8,128)S(1)}) custom-call(s32[32]{0:T(128)S(1)} %copy-done.4, bf16[16,192,128]{2,1,0:T(8,128)(2,1)S(1)} %get-tuple-element.38.landed, bf16[16,64,128]{2,1,0:T(8,128)(2,1)S(1)} %rows_to_heads.1.grad_landed, f32[64,2048]{1,0:T(8,128)S(1)} %get-tuple-element.41.sums, ...), custom_call_target="tpu_custom_call" | custom-call | flops 2684354560 | bytes 4194304 | tf_op jit(solution)/shard_map/attend_back/pallas_call | solution.py:798
  179.0 22.0 %grads_from_heads.1 = (bf16[128,1024]{1,0:T(8,128)(2,1)S(1)}, bf16[128,1024]{1,0:T(8,128)(2,1)S(1)}, bf16[128,1024]{1,0:T(8,128)(2,1)S(1)}) custom-call(bf16[16,192,128]{2,1,0:T(8,128)(2,1)S(1)} %get-tuple-element.43.packed), custom_call_target="tpu_custom_call" | custom-call | tf_op jit(solution)/shard_map/grads_from_heads/pallas_call | solution.py:643
  201.4 1.8 fusion.127
  203.2 1.7 fusion.129
  205.5 1.8 fusion.130
  207.2 1.7 fusion.128
  209.0 1.7 fusion.126
  211.7 17.7 %reduce-scatter.4.cloned.1.call-done = bf16[16,2048]{1,0:T(8,128)(2,1)} async-done(((bf16[256,2048]{1,0:T(8,128)(2,1)}), bf16[16,2048]{1,0:T(8,128)(2,1)}) %reduce-scatter.4.cloned.1.call-update) | async-done | bytes 65552 | tf_op jit(solution)/shard_map/reduce_scatter | solution.py:1376
  229.5 261.6 %weight_grads.1 = (bf16[512,2816]{1,0:T(8,128)(2,1)}, bf16[1408,1024]{1,0:T(8,128)(2,1)}, bf16[512,2816]{1,0:T(8,128)(2,1)}, bf16[512,1024]{1,0:T(8,128)(2,1)}, ...) custom-call(bf16[128,1024]{1,0:T(8,128)(2,1)S(1)} %multiply_convert_, ...), custom_call_target="tpu_custom_call" | custom-call | tf_op jit(solution)/shard_map/weight_grads/pallas_call | solution.py:1195
  493.4 2.4 fusion.42
  495.8 3.1 fusion.22
  499.6 2.8 convert_element_type.180
  511.3 2.9 convert_element_type.186
  514.2 2.9 convert_element_type.187
  517.2 3.3 convert_element_type.188
  521.3 1.7 convolution_bitcast_fusion.3
  528.5 2.6 fusion
  531.1 2.3 fusion.108
  (226 shorter events, 53.6 us)
Async XLA Ops:
  7.2 8.4 %copy-start.49 = (bf16[16,16]{1,0:T(8,128)(2,1)S(1)}, bf16[16,16]{1,0:T(8,128)(2,1)}, u32[]{:S(2)}) copy-start(bf16[16,16]{1,0:T(8,128)(2,1)} %param.30) | copy-start | bytes 1540
  7.2 8.4 %copy-start.50 = (bf16[512]{0:T(512)(128)(2,1)S(1)}, bf16[512]{0:T(512)(128)(2,1)}, u32[]{:S(2)}) copy-start(bf16[512]{0:T(512)(128)(2,1)} %param.36) | copy-start | bytes 3076
  7.2 8.4 %copy-start.51 = (bf16[512]{0:T(512)(128)(2,1)S(1)}, bf16[512]{0:T(512)(128)(2,1)}, u32[]{:S(2)}) copy-start(bf16[512]{0:T(512)(128)(2,1)} %param.25) | copy-start | bytes 3076
  7.2 222.2 %reduce-scatter.4.cloned.1.call-start = ((), (), s32[]{:S(2)}) async-start(), calls=%async_computation.2 | async-start | bytes 1114112 | tf_op jit(solution)/shard_map/reduce_scatter | solution.py:1376
  8.0 7.7 %copy-start.48 = (s32[2048]{0:T(1024)S(1)}, s32[2048]{0:T(1024)}, u32[]{:S(2)}) copy-start(s32[2048]{0:T(1024)} %param.24) | copy-start | bytes 24580
  8.8 6.6 %collective-permute-start = (bf16[1792]{0:T(1024)(128)(2,1)S(1)}, bf16[1792]{0:T(1024)(128)(2,1)S(1)}, u32[]{:S(2)}, u32[]{:S(2)}) collective-permute-start(bf16[1792]{0:T(1024)(128)(2,1)S(1)} %pad_maximum_fusion.1), channel_id=1, source_target_pairs={{0,1},{1,0},{2,3},{3,2},{4,5},{5,4},{6,7},{7,6},{8,9},{9,8},{10,11... | collective-permute-start | bytes 10760 | tf_op jit(solution)/shard_map/ppermute | solution.py:1256
  9.2 8.5 %collective-permute-start.1 = (bf16[512,1024]{1,0:T(8,128)(2,1)}, bf16[512,1024]{1,0:T(8,128)(2,1)}, u32[]{:S(2)}, u32[]{:S(2)}) collective-permute-start(bf16[512,1024]{1,0:T(8,128)(2,1)} %param.26), channel_id=1, source_target_pairs={{0,1},{1,0},{2,3},{3,2},{4,5},{5,4},{6,7},{7,6},{8,9},{9,8},{10,11... | collective-permute-start | bytes 3145736 | tf_op jit(solution)/shard_map/ppermute | solution.py:1256
  9.3 10.5 %collective-permute-start.2 = (bf16[512,1024]{1,0:T(8,128)(2,1)}, bf16[512,1024]{1,0:T(8,128)(2,1)}, u32[]{:S(2)}, u32[]{:S(2)}) collective-permute-start(bf16[512,1024]{1,0:T(8,128)(2,1)} %param.27), channel_id=1, source_target_pairs={{0,1},{1,0},{2,3},{3,2},{4,5},{5,4},{6,7},{7,6},{8,9},{9,8},{10,11... | collective-permute-start | bytes 3145736 | tf_op jit(solution)/shard_map/ppermute | solution.py:1256
  9.7 11.8 %collective-permute-start.3 = (bf16[512,1024]{1,0:T(8,128)(2,1)}, bf16[512,1024]{1,0:T(8,128)(2,1)}, u32[]{:S(2)}, u32[]{:S(2)}) collective-permute-start(bf16[512,1024]{1,0:T(8,128)(2,1)} %param.28), channel_id=1, source_target_pairs={{0,1},{1,0},{2,3},{3,2},{4,5},{5,4},{6,7},{7,6},{8,9},{9,8},{10,11... | collective-permute-start | bytes 3145736 | tf_op jit(solution)/shard_map/ppermute | solution.py:1256
  9.8 98.9 %collective-permute-start.11 = (bf16[1408,1024]{1,0:T(8,128)(2,1)}, bf16[1408,1024]{1,0:T(8,128)(2,1)}, u32[]{:S(2)}, u32[]{:S(2)}) collective-permute-start(bf16[1408,1024]{1,0:T(8,128)(2,1)} %param.39), channel_id=1, source_target_pairs={{0,1},{1,0},{2,3},{3,2},{4,5},{5,4},{6,7},{7,6},{8,9},{9,8},{10,11... | collective-permute-start | bytes 8650760 | tf_op jit(solution)/shard_map/ppermute | solution.py:1256
  10.3 5.7 %copy-start.9 = (bf16[1,128,1024]{2,1,0:T(8,128)(2,1)S(1)}, bf16[1,128,1024]{2,1,0:T(8,128)(2,1)}, u32[]{:S(2)}) copy-start(bf16[1,128,1024]{2,1,0:T(8,128)(2,1)} %param.20) | copy-start | bytes 786436
  11.4 4.7 copy-start.52
  11.4 4.7 copy-start.23
  15.3 61.6 %collective-permute-start.4 = (bf16[512,1024]{1,0:T(8,128)(2,1)}, bf16[512,1024]{1,0:T(8,128)(2,1)}, u32[]{:S(2)}, u32[]{:S(2)}) collective-permute-start(bf16[512,1024]{1,0:T(8,128)(2,1)} %param.29), channel_id=1, source_target_pairs={{0,1},{1,0},{2,3},{3,2},{4,5},{5,4},{6,7},{7,6},{8,9},{9,8},{10,11... | collective-permute-start | bytes 3145736 | tf_op jit(solution)/shard_map/ppermute | solution.py:1256
  17.9 61.3 %collective-permute-start.6 = (bf16[512,1024]{1,0:T(8,128)(2,1)S(1)}, bf16[512,1024]{1,0:T(8,128)(2,1)S(1)}, u32[]{:S(2)}, u32[]{:S(2)}) collective-permute-start(bf16[512,1024]{1,0:T(8,128)(2,1)S(1)} %copy-done.19), channel_id=1, source_target_pairs={{0,1},{1,0},{2,3},{3,2},{4,5},{5,4},{6,7},{7,6},{8,9},{9,8},{10,11... | collective-permute-start | bytes 3145736 | tf_op jit(solution)/shard_map/ppermute | solution.py:1256
  19.8 3.8 copy-start.3
  19.8 34.7 %copy-start.4 = (s32[32]{0:T(128)S(1)}, s32[32]{0:T(128)}, u32[]{:S(2)}) copy-start(s32[32]{0:T(128)} %order.3) | copy-start | bytes 388
  19.8 64.0 %collective-permute-start.7 = (bf16[512,1024]{1,0:T(8,128)(2,1)}, bf16[512,1024]{1,0:T(8,128)(2,1)}, u32[]{:S(2)}, u32[]{:S(2)}) collective-permute-start(bf16[512,1024]{1,0:T(8,128)(2,1)} %param.33), channel_id=1, source_target_pairs={{0,1},{1,0},{2,3},{3,2},{4,5},{5,4},{6,7},{7,6},{8,9},{9,8},{10,11... | collective-permute-start | bytes 3145736 | tf_op jit(solution)/shard_map/ppermute | solution.py:1256
  21.6 70.3 %collective-permute-start.5 = (bf16[512,1024]{1,0:T(8,128)(2,1)}, bf16[512,1024]{1,0:T(8,128)(2,1)}, u32[]{:S(2)}, u32[]{:S(2)}) collective-permute-start(bf16[512,1024]{1,0:T(8,128)(2,1)} %param.34), channel_id=1, source_target_pairs={{0,1},{1,0},{2,3},{3,2},{4,5},{5,4},{6,7},{7,6},{8,9},{9,8},{10,11... | collective-permute-start | bytes 3145736 | tf_op jit(solution)/shard_map/ppermute | solution.py:1256
  77.0 25.2 %collective-permute-start.8 = (bf16[512,1024]{1,0:T(8,128)(2,1)}, bf16[512,1024]{1,0:T(8,128)(2,1)}, u32[]{:S(2)}, u32[]{:S(2)}) collective-permute-start(bf16[512,1024]{1,0:T(8,128)(2,1)} %param.35), channel_id=1, source_target_pairs={{0,1},{1,0},{2,3},{3,2},{4,5},{5,4},{6,7},{7,6},{8,9},{9,8},{10,11... | collective-permute-start | bytes 3145736 | tf_op jit(solution)/shard_map/ppermute | solution.py:1256
  78.7 23.5 %copy-start.7 = (f32[128,1024]{1,0:T(8,128)}, f32[128,1024]{1,0:T(8,128)S(1)}, u32[]{:S(2)}) copy-start(f32[128,1024]{1,0:T(8,128)S(1)} %get-tuple-element.84) | copy-start | bytes 1572868
  79.1 35.0 %collective-permute-start.9 = (bf16[512,2816]{1,0:T(8,128)(2,1)}, bf16[512,2816]{1,0:T(8,128)(2,1)}, u32[]{:S(2)}, u32[]{:S(2)}) collective-permute-start(bf16[512,2816]{1,0:T(8,128)(2,1)} %param.37), channel_id=1, source_target_pairs={{0,1},{1,0},{2,3},{3,2},{4,5},{5,4},{6,7},{7,6},{8,9},{9,8},{10,11... | collective-permute-start | bytes 8650760 | tf_op jit(solution)/shard_map/ppermute | solution.py:1256
  82.0 6.1 %copy-start.27 = (bf16[256,512]{1,0:T(8,128)(2,1)}, bf16[256,512]{1,0:T(8,128)(2,1)S(1)}, u32[]{:S(2)}) copy-start(bf16[256,512]{1,0:T(8,128)(2,1)S(1)} %get-tuple-element.74) | copy-start | bytes 786436
  83.8 27.8 %collective-permute-start.10 = (bf16[512,2816]{1,0:T(8,128)(2,1)}, bf16[512,2816]{1,0:T(8,128)(2,1)}, u32[]{:S(2)}, u32[]{:S(2)}) collective-permute-start(bf16[512,2816]{1,0:T(8,128)(2,1)} %param.38), channel_id=1, source_target_pairs={{0,1},{1,0},{2,3},{3,2},{4,5},{5,4},{6,7},{7,6},{8,9},{9,8},{10,11... | collective-permute-start | bytes 8650760 | tf_op jit(solution)/shard_map/ppermute | solution.py:1256
  88.1 3.7 copy-start.13
  91.9 436.6 %collective-permute-start.12 = (bf16[256,512]{1,0:T(8,128)(2,1)}, bf16[256,512]{1,0:T(8,128)(2,1)}, u32[]{:S(2)}, u32[]{:S(2)}) collective-permute-start(bf16[256,512]{1,0:T(8,128)(2,1)} %get-tuple-element.73), channel_id=1, source_target_pairs={{0,1},{1,0},{2,3},{3,2},{4,5},{5,4},{6,7},{7,6},{8,9},{9,8},{10,11... | collective-permute-start | bytes 786440 | tf_op jit(solution)/shard_map/ppermute | solution.py:1256
  95.7 3.8 copy-start.15
  118.5 6.3 %copy-start.12 = (bf16[128,2816]{1,0:T(8,128)(2,1)}, bf16[128,2816]{1,0:T(8,128)(2,1)S(1)}, u32[]{:S(2)}) copy-start(bf16[128,2816]{1,0:T(8,128)(2,1)S(1)} %get-tuple-element.71.refs_8_) | copy-start | bytes 2162692
  118.5 9.1 %copy-start.11 = (bf16[128,2816]{1,0:T(8,128)(2,1)}, bf16[128,2816]{1,0:T(8,128)(2,1)S(1)}, u32[]{:S(2)}) copy-start(bf16[128,2816]{1,0:T(8,128)(2,1)S(1)} %get-tuple-element.70.refs_6_) | copy-start | bytes 2162692
  130.8 4.5 copy-start.17
  130.8 4.5 copy-start.6
  131.0 4.2 copy-start.30
  133.1 3.6 copy-start.16
  147.7 351.2 %all-gather.2.cloned.1.call-start = ((), (), s32[]{:S(2)}) async-start(), calls=%async_computation.1 | async-start | bytes 1114112 | tf_op jit(solution)/shard_map/all_gather | solution.py:1377
  147.8 3.3 copy-start.8
  147.8 3.3 copy-start.18
  147.8 3.3 copy-start.35
  152.2 16.6 %copy-start.29 = (bf16[128,1024]{1,0:T(8,128)(2,1)}, bf16[128,1024]{1,0:T(8,128)(2,1)S(1)}, u32[]{:S(2)}) copy-start(bf16[128,1024]{1,0:T(8,128)(2,1)S(1)} %get-tuple-element.65.refs_14_) | copy-start | bytes 786436
  201.0 4.4 copy-start.2
  201.1 6.2 %copy-start.1 = (bf16[128,1024]{1,0:T(8,128)(2,1)}, bf16[128,1024]{1,0:T(8,128)(2,1)S(1)}, u32[]{:S(2)}) copy-start(bf16[128,1024]{1,0:T(8,128)(2,1)S(1)} %get-tuple-element.45.refs_11_) | copy-start | bytes 786436
  201.4 3.5 copy-start.24
  205.5 5.2 copy-start.10
  229.5 263.9 %copy-start.34 = (bf16[128,2816]{1,0:T(8,128)(2,1)S(1)}, bf16[128,2816]{1,0:T(8,128)(2,1)}, u32[]{:S(2)}) copy-start(bf16[128,2816]{1,0:T(8,128)(2,1)} %get-tuple-element.72.refs_1_) | copy-start | bytes 2162692
  498.9 3.5 copy-start.44
  498.9 29.6 %collective-permute-start.13 = (bf16[256,2048]{1,0:T(8,128)(2,1)}, bf16[256,2048]{1,0:T(8,128)(2,1)}, u32[]{:S(2)}, u32[]{:S(2)}) collective-permute-start(bf16[256,2048]{1,0:T(8,128)(2,1)} %all-gather.2.cloned.1.call-done), channel_id=1, source_target_pairs={{0,1},{1,0},{2,3},{3,2},{4,5},{5,4},{6,7},{7,6},{8,9},{9,8},{10,11... | collective-permute-start | bytes 3145736 | tf_op jit(solution)/shard_map/ppermute | solution.py:1256
  517.2 4.2 copy-start.47
  521.3 7.2 %copy-start.28 = (bf16[256,512]{1,0:T(8,128)(2,1)S(1)}, bf16[256,512]{1,0:T(8,128)(2,1)}, u32[]{:S(2)}) copy-start(bf16[256,512]{1,0:T(8,128)(2,1)} %copy-done.27) | copy-start | bytes 786436
  521.3 7.2 %copy-start.45 = (bf16[256,2048]{1,0:T(8,128)(2,1)S(1)}, bf16[256,2048]{1,0:T(8,128)(2,1)}, u32[]{:S(2)}) copy-start(bf16[256,2048]{1,0:T(8,128)(2,1)} %all-gather.2.cloned.1.call-done) | copy-start | bytes 3145732
  (21 other events, 40.7 us)
Sparse Core Ops, SparseCore 0:
  147.8 81.4 reduce-scatter.3
  232.5 58.9 all-gather.1

commit v3 on v2

--- a/solution.py
+++ b/solution.py
@@ -570,30 +570,6 @@
     )(queries, keys, values, rows)
 
 
-def rows_to_heads_kernel(g_ref, landed, packed, *sems):
-    peers = packed.shape[0]
-    greet_all(peers)
-    for head in range(peers):
-        cols = slice(head * HEAD_DIM, (head + 1) * HEAD_DIM)
-        packed[head] = jnp.concatenate([g_ref[:BLOCK, cols], g_ref[BLOCK:, cols]], axis=1)
-    exchange_all(packed, landed, *sems)
-
-
-def rows_to_heads(rows):
-    shape = (HEADS, BLOCK, 2 * HEAD_DIM)
-    return pl.pallas_call(
-        rows_to_heads_kernel,
-        out_shape=jax.ShapeDtypeStruct(shape, BF16),
-        in_specs=[vmem_spec()],
-        out_specs=vmem_spec(),
-        scratch_shapes=[pltpu.VMEM(shape, BF16)] + exchange_scratch(HEADS),
-        compiler_params=pltpu.CompilerParams(
-            collective_id=2, has_side_effects=True, vmem_limit_bytes=16 * MIB
-        ),
-        name="rows_to_heads",
-    )(rows)
-
-
 def unpack_pair(landed, pair, rows):
     left, right = landed[2 * pair, rows, :], landed[2 * pair + 1, rows, :]
     return (
@@ -624,32 +600,6 @@
             collective_id=3, has_side_effects=True, vmem_limit_bytes=16 * MIB
         ),
         name="from_heads",
-    )(packed)
-
-
-def grads_from_heads_kernel(packed, q_ref, k_ref, v_ref, landed, *sems):
-    peers = packed.shape[0]
-    greet_all(peers)
-    exchange_all(packed, landed, *sems)
-    for pair in range(peers // 2):
-        cols = slice(pair * 2 * HEAD_DIM, (pair + 1) * 2 * HEAD_DIM)
-        q_ref[:, cols], k_ref[:, cols] = unpack_pair(landed, pair, slice(0, 2 * BLOCK))
-        first, second = unpack_pair(landed, pair, slice(2 * BLOCK, 3 * BLOCK))
-        v_ref[:BLOCK, cols] = first
-        v_ref[BLOCK:, cols] = second
-
-
-def grads_from_heads(packed):
-    return pl.pallas_call(
-        grads_from_heads_kernel,
-        out_shape=[jax.ShapeDtypeStruct((2 * BLOCK, HEADS * HEAD_DIM), BF16)] * 3,
-        in_specs=[vmem_spec()],
-        out_specs=[vmem_spec()] * 3,
-        scratch_shapes=[pltpu.VMEM(packed.shape, BF16)] + exchange_scratch(HEADS),
-        compiler_params=pltpu.CompilerParams(
-            collective_id=4, has_side_effects=True, vmem_limit_bytes=16 * MIB
-        ),
-        name="grads_from_heads",
     )(packed)
 
 
@@ -732,21 +682,35 @@
     )(order, landed, bias_lines)
 
 
-def attend_back_kernel(
-    order, landed, grad_landed, sums, norm, bias_lines, out_ref, lines_ref,
+def attend_back(
+    order, held_at, landed, grad_landed, sums, norm, bias_lines, out_ref, lines_ref,
     q_s, k_s, v_s, do_s, kt_s, tiles, by_offset, dq_s, dk_s, dv_s, delta_s, dqt_s,
 ):
     blocks = order.shape[0]
     spans = blocks * BLOCK // TILE
+    def stored_rows(stored):
+        return slice(stored * BLOCK, (stored + 1) * BLOCK), stored // 2, slice(
+            stored % 2 * HEAD_DIM, (stored % 2 + 1) * HEAD_DIM
+        )
+
+    def in_order(into, staged):
+        for block in range(blocks):
+            at = slice(block * BLOCK, (block + 1) * BLOCK)
+            into[at, :] = staged[pl.ds(held_at[block] * BLOCK, BLOCK), :].astype(BF16)
+
     for stored in range(blocks):
-        device, half = stored // 2, stored % 2
-        at = pl.ds(pl.multiple_of(order[stored] * BLOCK, BLOCK), BLOCK)
-        cols = slice(half * HEAD_DIM, (half + 1) * HEAD_DIM)
-        pair = landed[device, half * BLOCK : (half + 1) * BLOCK, :]
-        q_s[at, :] = pair[:, :HEAD_DIM]
-        k_s[at, :] = pair[:, HEAD_DIM:]
-        v_s[at, :] = landed[device, 2 * BLOCK :, cols]
-        do_s[at, :] = grad_landed[device, :, cols]
+        at, device, cols = stored_rows(stored)
+        pair = landed[device, stored % 2 * BLOCK : (stored % 2 + 1) * BLOCK, :].astype(F32)
+        dq_s[at, :] = pair[:, :HEAD_DIM]
+        dk_s[at, :] = pair[:, HEAD_DIM:]
+        dv_s[at, :] = landed[device, 2 * BLOCK :, cols].astype(F32)
+    in_order(q_s, dq_s)
+    in_order(k_s, dk_s)
+    in_order(v_s, dv_s)
+    for stored in range(blocks):
+        at, device, cols = stored_rows(stored)
+        dq_s[at, :] = grad_landed[device, :, cols].astype(F32)
+    in_order(do_s, dq_s)
     place_tiles(bias_lines, tiles)
     kt_s[...] = jnp.transpose(k_s[...].astype(F32), (1, 0)).astype(BF16)
     grad_t = jnp.transpose(do_s[...].astype(F32), (1, 0))
@@ -772,11 +736,11 @@
     dq_s[...] = jnp.transpose(dqt_s[...], (1, 0))
     for stored in range(blocks):
         device, half = stored // 2, stored % 2
-        at = pl.ds(pl.multiple_of(order[stored] * BLOCK, BLOCK), BLOCK)
+        at = pl.ds(order[stored] * BLOCK, BLOCK)
         rows = slice(half * BLOCK, (half + 1) * BLOCK)
+        cols = slice(half * HEAD_DIM, (half + 1) * HEAD_DIM)
         out_ref[device, rows, :HEAD_DIM] = dq_s[at, :].astype(BF16)
         out_ref[device, rows, HEAD_DIM:] = dk_s[at, :].astype(BF16)
-        cols = slice(half * HEAD_DIM, (half + 1) * HEAD_DIM)
         out_ref[device, 2 * BLOCK :, cols] = dv_s[at, :].astype(BF16)
     for apart in range(spans):
         folded = jnp.zeros((8, 2 * TILE), F32)
@@ -790,37 +754,8 @@
         lines_ref[apart : apart + 1, :] = line
 
 
-def attend_back(order, landed, grad_landed, sums, norm, bias_lines):
-    blocks = order.shape[0]
-    length = blocks * BLOCK
-    spans = length // TILE
-    vmem = pltpu.VMEM
-    return pl.pallas_call(
-        attend_back_kernel,
-        grid_spec=pltpu.PrefetchScalarGridSpec(
-            num_scalar_prefetch=1,
-            grid=(),
-            in_specs=[vmem_spec()] * 5,
-            out_specs=[vmem_spec()] * 2,
-            scratch_shapes=[vmem((length, HEAD_DIM), BF16)] * 4
-            + [vmem((HEAD_DIM, length), BF16)]
-            + [vmem((spans, TILE, TILE), F32)] * 2
-            + [vmem((length, HEAD_DIM), F32)] * 3
-            + [vmem((1, length), F32), vmem((HEAD_DIM, length), F32)],
-        ),
-        out_shape=[
-            jax.ShapeDtypeStruct((blocks // 2, 3 * BLOCK, 2 * HEAD_DIM), BF16),
-            jax.ShapeDtypeStruct((spans, 2 * TILE), F32),
-        ],
-        compiler_params=pltpu.CompilerParams(vmem_limit_bytes=32 * MIB),
-        cost_estimate=pl.CostEstimate(
-            flops=10 * length * length * HEAD_DIM, bytes_accessed=4 * MIB, transcendentals=length * length // 2
-        ),
-        name="attend_back",
-    )(order, landed, grad_landed, sums, norm, bias_lines)
-
-
 BIT_X, BIT_Y = 0, 1
+FAR_LEFTS, FAR_RIGHTS = 2, 3
 
 
 def pick(flag, when_set, when_clear):
@@ -833,6 +768,9 @@
 class Product:
     def __init__(self, left, right, first, tall, route):
         self.left, self.right, self.first, self.tall, self.route = left, right, first, tall, route
+
+
+SUMMED = -1
 
 
 def weight_grad_kernel(products, left_count, *refs):
@@ -844,10 +782,32 @@
         del refs[:number]
         return taken
 
-    lefts, rights, (vec_in,) = take(left_count), take(count), take(1)
-    wholes, (vec_out,) = take(count), take(1)
+    lefts, rights = take(left_count), take(count - 3)
+    left_far, right_far = take(FAR_LEFTS), take(FAR_RIGHTS)
+    (
+        order,
+        held_at,
+        grad_rows,
+        landed,
+        attn_sum,
+        log_norm,
+        bias_lines,
+        in_bucket,
+        resid_in,
+        gain_one,
+        resid_grad,
+        gains,
+    ) = take(12)
+    weights = take(10)
+    wholes, (vec_out, input_grad, encoder_grad, kv_both) = take(count - 1), take(4)
+    kv_at = [product.left for product in products].index(SUMMED)
+    wholes.insert(kv_at, kv_both.at[0])
     left_all, left_pass, left_t = take(left_count), take(left_count), take(left_count)
-    right_all, away, came, held, up_in, down_in = (take(count) for _ in range(6))
+    right_all, away, came, held, line_in = (take(count) for _ in range(5))
+    rights += take(3)
+    grad_packed, grad_landed, back_packed, back_landed, lines = take(5)
+    attention_scratch = take(12)
+    vec_in, vec_sums, vec_landed, weight_buffer, normed_grad = take(5)
     (
         left_send,
         left_recv,
@@ -862,6 +822,10 @@
         own_sem,
         vec_send,
         vec_recv,
+        all_send,
+        all_recv,
+        all_own,
+        weight_sem,
     ) = refs
     me, core = lax.axis_index("ctx"), lax.axis_index("wsh")
     peers = lax.axis_size("ctx")
@@ -875,6 +839,11 @@
                 barrier, inc=1, device_id=(lax.rem(me + step, peers), side), device_id_type=MESH
             )
     pl.semaphore_signal(barrier, inc=1, device_id=(me, 1 - core), device_id_type=MESH)
+    for head in range(peers):
+        cols = slice(head * HEAD_DIM, (head + 1) * HEAD_DIM)
+        grad_packed[head] = jnp.concatenate(
+            [grad_rows[:BLOCK, cols], grad_rows[BLOCK:, cols]], axis=1
+        )
     pl.semaphore_wait(barrier, 2 * peers - 1)
 
     def place(zz, yy, xx):
@@ -923,46 +892,93 @@
         return (along_x, along_y) if product.first == BIT_X else (along_y, along_x)
 
     left_axis = {product.left: product for product in products}
+    far_rights = [at for at in range(count) if 0 <= products[at].left < FAR_LEFTS]
+
+    def local(src, dst, sem):
+        copy = pltpu.make_async_copy(src, dst, sem)
+        copy.start()
+        return copy
 
     def send_left(at):
         (_, way), _ = axes(left_axis[at])
         half = left_all[at].shape[1]
-        launch(remote(lanes(lefts[at], core, half), slot(left_all[at], 1), left_send.at[at, 0], left_recv.at[at, 0], targets[way], core))
-        launch(remote(lanes(lefts[at], 1 - core, half), left_pass[at], left_send.at[at, 1], left_recv.at[at, 1], targets[way], core))
+        copies = [local(lanes(lefts[at], core, half), slot(left_all[at], 0), left_send.at[at, 4])]
         launch(remote(lanes(lefts[at], 1 - core, half), slot(left_all[at], 2), left_send.at[at, 2], left_recv.at[at, 2], me, 1 - core))
-        own = pltpu.make_async_copy(lanes(lefts[at], core, half), slot(left_all[at], 0), left_send.at[at, 4])
-        own.start()
-        return own
+        if at < FAR_LEFTS:
+            copies.append(local(lanes(left_far[at], core, half), slot(left_all[at], 1), left_send.at[at, 5]))
+            launch(remote(lanes(left_far[at], 1 - core, half), slot(left_all[at], 3), left_send.at[at, 3], left_recv.at[at, 3], me, 1 - core))
+        else:
+            launch(remote(lanes(lefts[at], core, half), slot(left_all[at], 1), left_send.at[at, 0], left_recv.at[at, 0], targets[way], core))
+            launch(remote(lanes(lefts[at], 1 - core, half), left_pass[at], left_send.at[at, 1], left_recv.at[at, 1], targets[way], core))
+        return copies
 
     def send_right(at):
         (mine, way), _ = axes(products[at])
         half = right_all[at].shape[1]
-        launch(remote(lanes(rights[at], 1 - mine, half), slot(right_all[at], 1), right_send.at[at, 0], right_recv.at[at, 0], targets[way], core))
+        if products[at].left == SUMMED:
+            launch(remote(lanes(rights[at], 1 - mine, half), right_all[at], right_send.at[at, 0], right_recv.at[at, 0], targets[way], core))
+            return []
+        copies = [local(lanes(rights[at], mine, half), slot(right_all[at], 0), right_send.at[at, 3])]
         launch(remote(lanes(rights[at], mine, half), slot(right_all[at], 2), right_send.at[at, 1], right_recv.at[at, 1], me, 1 - core))
-        own = pltpu.make_async_copy(lanes(rights[at], mine, half), slot(right_all[at], 0), right_send.at[at, 3])
+        if at in far_rights:
+            far = right_far[far_rights.index(at)]
+            copies.append(local(far, slot(right_all[at], 1), right_send.at[at, 4]))
+            launch(remote(far, slot(right_all[at], 3), right_send.at[at, 2], right_recv.at[at, 2], me, 1 - core))
+        else:
+            launch(remote(lanes(rights[at], 1 - mine, half), slot(right_all[at], 1), right_send.at[at, 0], right_recv.at[at, 0], targets[way], core))
+        return copies
+
+    def to_all(which, source, target):
+        copies = []
+        for step in range(1, peers):
+            peer = lax.rem(me + step, peers)
+            copies.append(
+                remote(source(peer), target(me), all_send.at[which, step], all_recv.at[which, step], peer, core)
+            )
+            launch(copies[-1])
+        own = pltpu.make_async_copy(source(me), target(me), all_own.at[which])
         own.start()
-        return own
+
+        def wait():
+            own.wait()
+            for each in copies:
+                each.wait_recv()
+
+        return wait
 
     seen = set()
     owns = {}
-    for at, product in enumerate(products):
-        if product.left not in seen:
-            seen.add(product.left)
-            owns["left", product.left] = send_left(product.left)
-        owns["right", at] = send_right(at)
-
-    for step in range(1, peers):
-        peer = lax.rem(me + step, peers)
-        for offset, side in ((0, core), (peers, 1 - core)):
-            launch(remote(vec_in, vec_out.at[core * peers + me], vec_send.at[offset + step], vec_recv.at[core * peers + me], peer, side))
-    launch(remote(vec_in, vec_out.at[core * peers + me], vec_send.at[peers], vec_recv.at[core * peers + me], me, 1 - core))
-    own_vec = pltpu.make_async_copy(vec_in, vec_out.at[core * peers + me], vec_send.at[0])
-    own_vec.start()
+
+    def send_operands(some):
+        for at in some:
+            left = products[at].left
+            if left not in seen and left != SUMMED:
+                seen.add(left)
+                owns["left", left] = send_left(left)
+            owns["right", at] = send_right(at)
+
+    def vector_step(step):
+        if step == 0:
+            source, ctx, side = vec_in.at[1 - core], me, 1 - core
+        else:
+            source, ctx, side = vec_sums.at[step - 1], me ^ (1 << (step - 1)), core
+        launch(remote(source, vec_landed.at[step], vec_send.at[step], vec_recv.at[step], ctx, side))
+
+    def vector_add(step):
+        arrived(vec_landed.at[step], vec_recv.at[step])
+        total = (vec_sums[step - 1] if step else vec_in[core]) + vec_landed[step]
+        if step < 4:
+            vec_sums[step] = total
+            vector_step(step + 1)
+        else:
+            vec_out[...] = total
 
     passed = set()
 
     def pass_on(at):
         left = products[at].left
+        if left == SUMMED or at in far_rights:
+            return
         if left not in passed:
             passed.add(left)
             arrived(slot(left_all[left], 1), left_recv.at[left, 0])
@@ -1001,11 +1017,22 @@
 
     def product_away(at):
         left = products[at].left
+        _, (mine, way) = axes(products[at])
+        if left == SUMMED:
+            (first_mine, _), _ = axes(products[at])
+            arrived(right_all[at], right_recv.at[at, 0])
+            height = held[at].shape[0]
+            for out, half in ((away[at], 1 - mine), (held[at], mine)):
+                own = lanes(rows(rights[at], half, height), first_mine, held[at].shape[1])
+                out[...] = (own[...].astype(F32) + rows(right_all[at], half, height)[...].astype(F32)).astype(BF16)
+            launch(remote(away[at], came[at], pair_send.at[at], pair_recv.at[at], targets[way], core))
+            return
         if left not in turned:
             turned.add(left)
             arrived(slot(left_all[left], 2), left_recv.at[left, 2])
             arrived(slot(left_all[left], 3), left_recv.at[left, 3])
-            owns["left", left].wait()
+            for each in owns["left", left]:
+                each.wait()
             height = left_t[left].shape[0]
 
             def turn(index, carry):
@@ -1016,8 +1043,8 @@
             lax.fori_loop(0, height // 128, turn, 0)
         arrived(slot(right_all[at], 2), right_recv.at[at, 1])
         arrived(slot(right_all[at], 3), right_recv.at[at, 2])
-        owns["right", at].wait()
-        _, (mine, way) = axes(products[at])
+        for each in owns["right", at]:
+            each.wait()
         multiply(at, away[at], 1 - mine)
         launch(remote(away[at], came[at], pair_send.at[at], pair_recv.at[at], targets[way], core))
         multiply(at, held[at], mine)
@@ -1031,22 +1058,23 @@
 
     def line_step(at, step):
         height = held[at].shape[0] // 4
-        for side, buffer, behind, chunk, way in (
-            (0, up_in[at], z, lax.rem(z + 3 - step, 4), UP),
-            (1, down_in[at], 3 - z, lax.rem(z + step + 1, 4), DOWN),
+        for side, behind, chunk, way in (
+            (0, z, lax.rem(z + 3 - step, 4), UP),
+            (1, 3 - z, lax.rem(z + step + 1, 4), DOWN),
         ):
             recv_sem = line_recv.at[at, side, chunk]
-
-            def land(buffer=buffer, chunk=chunk, recv_sem=recv_sem):
-                arrived(rows(buffer, chunk, height), recv_sem)
-                add(rows(held[at], chunk, height), rows(buffer, chunk, height))
+            landing = rows(line_in[at], chunk + 1 - side, height)
+
+            def land(landing=landing, chunk=chunk, recv_sem=recv_sem):
+                arrived(landing, recv_sem)
+                add(rows(held[at], chunk, height), landing)
 
             pl.when(jnp.logical_and(behind > 0, behind <= step))(land)
             if step < 3:
                 launch(
                     remote(
                         rows(held[at], chunk, height),
-                        rows(buffer, chunk, height),
+                        landing,
                         line_send.at[at, side, chunk],
                         recv_sem,
                         targets[way],
@@ -1107,9 +1135,9 @@
     def gather_step(at, step):
         z_first, second, third = products[at].route
         if step == 0:
-            own = pltpu.make_async_copy(own_piece(at), window(at, me), own_sem.at[at])
-            own.start()
-            finish.append(own.wait)
+            owns["piece", at] = local(own_piece(at), window(at, me), own_sem.at[at])
+            if at != kv_at:
+                finish.append(owns["piece", at].wait)
             if not z_first:
                 send(at, me, second, 0, own=True)
                 send(at, me, third, 0, own=True)
@@ -1154,62 +1182,206 @@
                         arrive(at, where, there)
                         send(at, where, way, 4 * (step - 2) + index, on)
 
-    for at in range(count):
+    def reduce_step(at, step):
+        if step == 0:
+            add_pair(at)
+        if step < 4:
+            line_step(at, step)
+        else:
+            gather_step(at, 0)
+
+    def load_weight(index):
+        return pltpu.make_async_copy(
+            weights[index], weight_buffer.at[index % 2], weight_sem.at[index % 2]
+        )
+
+    def input_gradient():
+        load_weight(0).start()
+        for index in range(6):
+            load_weight(index + 1).start()
+            load_weight(index).wait()
+            columns = lanes(normed_grad, core if index < 3 else 1 - core, normed_grad.shape[1] // 2)
+            term = dot_nt(rights[count - 3 + index % 3][...], weight_buffer[index % 2])
+            if index % 3:
+                columns[...] += term
+            else:
+                columns[...] = term
+        width = resid_in.shape[1]
+        cotan, values = normed_grad[...], resid_in[...]
+        rate = lax.rsqrt(jnp.mean(values * values, axis=1, keepdims=True) + EPSILON)
+        scaled = cotan * gain_one[...]
+        slope = jnp.mean(scaled * values, axis=1, keepdims=True)
+        back = rate * scaled - values * (rate * rate * rate) * slope
+        input_grad[...] = (resid_grad[...] + back).astype(BF16)
+        gain_grad = jnp.sum(cotan * values * rate, axis=0, keepdims=True)
+        column = jnp.zeros((BUCKETS, 1), F32)
+        for apart in range(lines.shape[0]):
+            sums = lines[apart : apart + 1, :TILE]
+            if apart + 1 < lines.shape[0]:
+                sums = sums + lines[apart + 1 : apart + 2, TILE:]
+            column = column + jnp.sum(in_bucket[apart] * sums, axis=1, keepdims=True)
+        place_at = lax.broadcasted_iota(jnp.int32, (BUCKETS, 128), 1)
+        table = jnp.where(place_at == me, column, 0.0)
+        for half in range(2):
+            for index in range(4):
+                start = (4 * half + index) * 128
+                vec_in[half, index : index + 1, :] = gain_grad[:, start : start + 128]
+            vec_in[half, 4:16, :] = gains[half]
+            vec_in[half, 16:, :] = table[half * (BUCKETS // 2) : (half + 1) * (BUCKETS // 2)]
+        vector_step(0)
+
+    def encoder_gradient():
+        own = kv_both[0, pl.ds(pl.multiple_of(me * encoder_grad.shape[0], 16), encoder_grad.shape[0]), :]
+        width = own.shape[1] // 2
+        for side in (0, 1):
+            terms = []
+            for index in (6 + 2 * side, 7 + 2 * side):
+                if index < 9:
+                    load_weight(index + 1).start()
+                load_weight(index).wait()
+                part = slice((index % 2) * width, (index % 2 + 1) * width)
+                terms.append(dot_nt(own[:, part], weight_buffer[index % 2]))
+            columns = lanes(encoder_grad, core if side == 0 else 1 - core, width // 2)
+            columns[...] = (terms[0] + terms[1]).astype(BF16)
+
+    early, late = range(count - 3), range(count - 3, count)
+    near_by = [at for at in early if at in far_rights]
+    others = [at for at in early if at not in far_rights]
+
+    def wave(some):
+        for time in range(len(some) + 4):
+            for step in range(5):
+                if 0 <= time - step < len(some):
+                    reduce_step(some[time - step], step)
+            yield
+
+    grad_arrival = to_all(0, lambda peer: grad_packed.at[peer], lambda mine: grad_landed.at[mine])
+    send_operands(near_by)
+    send_operands(others)
+    for at in near_by:
+        product_away(at)
+    grad_arrival()
+    attend_back(
+        order, held_at, landed, grad_landed, attn_sum, log_norm, bias_lines, back_packed, lines,
+        *attention_scratch,
+    )
+    back_arrival = to_all(1, lambda peer: back_packed.at[peer], lambda mine: back_landed.at[mine])
+    early_wave = wave(near_by + others)
+    for index, at in enumerate(others):
         pass_on(at)
-        if at:
-            product_away(at - 1)
-    product_away(count - 1)
-    for time in range(count + 4):
-        if time < count:
-            add_pair(time)
-        for step in range(4):
-            if 0 <= time - step < count:
-                line_step(time - step, step)
-        if time >= 4:
-            gather_step(time - 4, 0)
+        if index:
+            product_away(others[index - 1])
+    product_away(others[-1])
+    next(early_wave)
+    next(early_wave)
+    back_arrival()
+    dq_ref, dk_ref, dv_ref = rights[count - 3 :]
+    for pair in range(peers // 2):
+        cols = slice(pair * 2 * HEAD_DIM, (pair + 1) * 2 * HEAD_DIM)
+        dq_ref[:, cols], dk_ref[:, cols] = unpack_pair(back_landed, pair, slice(0, 2 * BLOCK))
+        first, second = unpack_pair(back_landed, pair, slice(2 * BLOCK, 3 * BLOCK))
+        dv_ref[:BLOCK, cols] = first
+        dv_ref[BLOCK:, cols] = second
+    send_operands(late)
+    input_gradient()
+    for _ in early_wave:
+        pass
+    for at in late:
+        pass_on(at)
+    vector_add(0)
+    for at in late:
+        product_away(at)
+    for at in early:
+        gather_step(at, 1)
+    for time, _ in enumerate(wave(list(late))):
+        if time in (1, 3, 5):
+            for at in early:
+                gather_step(at, 2 + time // 2)
+            vector_add(1 + time // 2)
+    vector_add(4)
     for step in range(1, 9):
-        for at in range(count):
+        for at in late:
             gather_step(at, step)
-
-    for step in range(1, peers):
-        peer = lax.rem(me + step, peers)
-        for side in (core, 1 - core):
-            arrived(vec_out.at[side * peers + peer], vec_recv.at[side * peers + peer])
-    arrived(vec_out.at[(1 - core) * peers + me], vec_recv.at[(1 - core) * peers + me])
-    own_vec.wait()
+        if step >= 5:
+            for at in early:
+                gather_step(at, step)
+        if step == 5:
+            owns["piece", kv_at].wait()
+            launch(
+                remote(kv_both.at[0], kv_both.at[1], all_send.at[0, 0], all_recv.at[0, 0], me, 1 - core)
+            )
+            encoder_gradient()
+    arrived(kv_both.at[1], all_recv.at[0, 0])
     for each in finish:
         each()
 
 
-def weight_grads(products, lefts, rights, vector):
+def weight_grads(products, lefts, rights, left_far, right_far, others, weights):
     count, peers = len(products), lax.axis_size("ctx")
     tokens = lefts[0].shape[0]
+    length = others[4].shape[1]
+    kv_at = [product.left for product in products].index(SUMMED)
+    kv_rows, kv_width = rights[kv_at].shape
+    spans = length // TILE
     dma = pltpu.SemaphoreType.DMA
     vmem = pltpu.VMEM
+    width = HEADS * HEAD_DIM
     halves = [left.shape[1] // 2 for left in lefts]
+    widths = [right.shape[1] for right in rights] + [width] * 3
     helds = []
-    for product, right in zip(products, rights):
-        height, width = halves[product.left], right.shape[1] // 2
-        helds.append((height, width // 2) if product.tall else (height // 2, width))
+    for product, right in zip(products, widths):
+        height = kv_rows if product.left == SUMMED else halves[product.left]
+        helds.append((height, right // 4) if product.tall else (height // 2, right // 2))
     lands = [vmem(shape, BF16) for shape in helds]
+    chunk = (peers, BLOCK, 2 * HEAD_DIM)
+    chunks = (peers, 3 * BLOCK, 2 * HEAD_DIM)
+    smem_spec = pl.BlockSpec(memory_space=pltpu.SMEM)
     return pl.pallas_call(
         functools.partial(weight_grad_kernel, products, len(lefts)),
         out_shape=[
-            jax.ShapeDtypeStruct((halves[product.left], right.shape[1]), BF16)
-            for product, right in zip(products, rights)
+            jax.ShapeDtypeStruct((halves[product.left], right), BF16)
+            for product, right in zip(products, widths)
+            if product.left != SUMMED
         ]
-        + [jax.ShapeDtypeStruct((2 * peers,) + vector.shape, F32)],
-        in_specs=[vmem_spec()] * (len(lefts) + count + 1),
-        out_specs=[any_spec()] * count + [vmem_spec()],
+        + [
+            jax.ShapeDtypeStruct((32, 128), F32),
+            jax.ShapeDtypeStruct((tokens, width), BF16),
+            jax.ShapeDtypeStruct((kv_rows // peers, width), BF16),
+            jax.ShapeDtypeStruct((2, kv_rows, kv_width), BF16),
+        ],
+        in_specs=[vmem_spec()] * (len(lefts) + len(rights) + len(left_far) + len(right_far))
+        + [smem_spec] * 2
+        + [vmem_spec()] * (len(others) - 2)
+        + [any_spec()] * len(weights),
+        out_specs=[any_spec()] * (count - 1) + [vmem_spec()] * 4,
         scratch_shapes=[vmem((4 * tokens, half), BF16) for half in halves]
         + [vmem((tokens, half), BF16) for half in halves]
         + [vmem((half, 4 * tokens), BF16) for half in halves]
-        + [vmem((4 * tokens, right.shape[1] // 2), BF16) for right in rights]
-        + lands * 5
         + [
-            dma((len(lefts), 5)),
+            vmem((kv_rows if product.left == SUMMED else 4 * tokens, right // 2), BF16)
+            for product, right in zip(products, widths)
+        ]
+        + lands * 3
+        + [vmem((5 * height // 4, width_held), BF16) for height, width_held in helds]
+        + [vmem((tokens, width), BF16)] * 3
+        + [vmem(chunk, BF16), vmem(chunk, BF16), vmem(chunks, BF16), vmem(chunks, BF16)]
+        + [vmem((spans, 2 * TILE), F32)]
+        + [vmem((length, HEAD_DIM), BF16)] * 4
+        + [vmem((HEAD_DIM, length), BF16)]
+        + [vmem((spans, TILE, TILE), F32)] * 2
+        + [vmem((length, HEAD_DIM), F32)] * 3
+        + [vmem((1, length), F32), vmem((HEAD_DIM, length), F32)]
+        + [
+            vmem((2, 32, 128), F32),
+            vmem((4, 32, 128), F32),
+            vmem((5, 32, 128), F32),
+            vmem((2,) + weights[0].shape, BF16),
+            vmem((tokens, width), F32),
+        ]
+        + [
+            dma((len(lefts), 6)),
             dma((len(lefts), 4)),
-            dma((count, 4)),
+            dma((count, 5)),
             dma((count, 3)),
             dma((count,)),
             dma((count,)),
@@ -1218,14 +1390,18 @@
             dma((count, 4, 16)),
             dma((count, peers)),
             dma((count,)),
-            dma((2 * peers,)),
-            dma((2 * peers,)),
+            dma((5,)),
+            dma((5,)),
+            dma((2, peers)),
+            dma((2, peers)),
+            dma((2,)),
+            dma((2,)),
         ],
         compiler_params=pltpu.CompilerParams(
-            collective_id=5, has_side_effects=True, vmem_limit_bytes=52 * MIB
+            collective_id=5, has_side_effects=True, vmem_limit_bytes=60 * MIB
         ),
         name="weight_grads",
-    )(*lefts, *rights, vector)
+    )(*lefts, *rights, *left_far, *right_far, *others, *weights)
 
 
 def on_device_by_heads(
@@ -1255,6 +1431,16 @@
     def swap(values):
         return lax.ppermute(values, "wsh", [(0, 1), (1, 0)])
 
+    def along_x(values):
+        return lax.ppermute(values, "ctx", [(at, at ^ 1) for at in range(HEADS)])
+
+    def along_y(values):
+        return lax.ppermute(values, "ctx", [(at, at ^ 2) for at in range(HEADS)])
+
+    def other_column(values, bit):
+        half = values.shape[1] // 2
+        return pick(bit & 1, values[:, :half], values[:, half:])
+
     def own_half(values):
         half = values.shape[-1] // 2
         return pick(core, values[..., half:], values[..., :half])
@@ -1278,9 +1464,6 @@
 
     def both_cores(values):
         return jnp.concatenate([own_half(values), swap(other_half(values))], axis=0)
-
-    def both_whole(values):
-        return jnp.concatenate([values, swap(values)], axis=0)
 
     small = jnp.concatenate([self_gain, cross_gain, mlp_gain, bias_table.reshape(-1)])
     small_other = swap(small)
@@ -1373,46 +1556,21 @@
         "hqk,qhe->khe", cross_probs, mix_grad, preferred_element_type=F32
     ).reshape(-1, head_width)
     cross_kv_part = jnp.concatenate([cross_k_part, cross_v_part], axis=1).astype(BF16)
-    cross_kv_grad = lax.psum_scatter(cross_kv_part, "ctx", scatter_dimension=0, tiled=True)
-    cross_kv_all = lax.all_gather(cross_kv_grad, "ctx", axis=0, tiled=True)
-    encoder_grad = (
-        times_back(cross_kv_grad[:, :head_width], cross_key_pair)
-        + times_back(cross_kv_grad[:, head_width:], cross_value_pair)
-    ).astype(BF16)
-    cross_kv_w_grad = left_contract(both_cores(encoder_all), both_whole(cross_kv_all))
     normed_two_grad = times_back(cross_q_grad, cross_query_pair)
     part_grad, gain_two_grad = norm_back(after_self, gain_two, normed_two_grad)
     after_self_grad = after_cross_grad + part_grad
     branch_one = after_self_grad.astype(BF16)
-    grad_landed = rows_to_heads(times_back(branch_one, out_pair).astype(BF16))
-    packed_grads, offset_lines = attend_back(
-        block_order, landed, grad_landed, attn_sum, log_norm, bias_lines
-    )
-    query_grad, key_grad, value_grad = grads_from_heads(packed_grads)
-
-    offset_sums = offset_lines[:, :TILE] + jnp.concatenate(
-        [offset_lines[1:, TILE:], jnp.zeros((1, TILE), F32)], axis=0
-    )
-    table_column = jnp.sum(jnp.where(in_bucket, offset_sums.reshape(1, length), 0.0), axis=1)
-    table_grad = jnp.where(jnp.arange(HEADS)[None, :] == me, table_column[:, None], 0.0)
-
-    normed_one_grad = (
-        times_back(query_grad, query_pair)
-        + times_back(key_grad, key_pair)
-        + times_back(value_grad, value_pair)
-    )
-    part_grad, gain_one_grad = norm_back(resid_in, gain_one, normed_one_grad)
-    input_grad = (after_self_grad + part_grad).astype(BF16)
-
-    vector = jnp.concatenate(
-        [
-            gain_one_grad,
-            gain_two_grad,
-            gain_three_grad,
-            table_grad.reshape(-1),
-            jnp.zeros((512,), F32),
-        ]
-    ).reshape(8, 512)
+    dattn = times_back(branch_one, out_pair).astype(BF16)
+    block_ids = jnp.arange(block_order.shape[0], dtype=jnp.int32)
+    held_at = jnp.sum(
+        jnp.where(block_order[None, :] == block_ids[:, None], block_ids[None, :], 0), axis=1
+    )
+    gains = jnp.concatenate(
+        [gain_two_grad.reshape(2, 4, 128), gain_three_grad.reshape(2, 4, 128), jnp.zeros((2, 4, 128), F32)],
+        axis=1,
+    )
+    bucket_tiles = in_bucket.astype(F32).reshape(BUCKETS, -1, TILE).transpose(1, 0, 2)
+
     z_then_yx, z_then_xy, z_last = (
         (True, ACROSS_Y, ACROSS_X),
         (True, ACROSS_X, ACROSS_Y),
@@ -1423,32 +1581,56 @@
         Product(0, gate_grad, BIT_Y, False, z_then_yx),
         Product(1, branch_three, BIT_X, True, z_then_yx),
         Product(0, up_grad, BIT_Y, False, z_then_xy),
-        Product(5, query_grad, BIT_X, False, z_then_xy),
-        Product(2, branch_two, BIT_Y, False, z_last),
-        Product(5, key_grad, BIT_X, False, z_then_xy),
+        Product(SUMMED, cross_kv_part, BIT_X, False, z_last),
+        Product(2, branch_two, BIT_X, False, z_last),
         Product(3, cross_q_grad, BIT_Y, False, z_last),
-        Product(5, value_grad, BIT_X, False, z_then_xy),
         Product(4, branch_one, BIT_Y, False, z_last),
-    )
-    *wholes, vectors = weight_grads(
-        products, lefts, [product.right for product in products], vector
+        Product(5, None, BIT_X, False, z_then_xy),
+        Product(5, None, BIT_X, False, z_then_xy),
+        Product(5, None, BIT_X, False, z_then_xy),
+    )
+    *wholes, totals, input_grad, encoder_grad, cross_kv_both = weight_grads(
+        products,
+        lefts,
+        [product.right for product in products[:7]],
+        (along_y(normed_three), along_x(hidden)),
+        (along_y(other_column(gate_grad, me >> 1)), along_x(other_column(branch_three, me)), along_y(other_column(up_grad, me >> 1))),
+        (
+            block_order,
+            held_at,
+            dattn,
+            landed,
+            attn_sum,
+            log_norm,
+            bias_lines,
+            bucket_tiles,
+            resid_in,
+            gain_one[None, :],
+            after_self_grad,
+            gains,
+        ),
+        [pair[0] for pair in (query_pair, key_pair, value_pair)]
+        + [pair[1] for pair in (query_pair, key_pair, value_pair)]
+        + [cross_key_pair[0], cross_value_pair[0], cross_key_pair[1], cross_value_pair[1]],
+    )
+    cross_kv_w_grad = left_contract(
+        both_cores(encoder_all), cross_kv_both.reshape(-1, 2 * head_width)
     )
     (
         sum_gate,
         sum_down,
         sum_up,
+        sum_cross_out,
+        sum_cross_query,
+        sum_out,
         sum_query,
-        sum_cross_out,
         sum_key,
-        sum_cross_query,
         sum_value,
-        sum_out,
     ) = (member.astype(F32) for member in wholes)
-    totals = jnp.sum(vectors, axis=0)
     sum_gain_one, sum_gain_two, sum_gain_three = (
-        own_half(totals[2 * at : 2 * at + 2].reshape(1, -1))[0] for at in range(3)
-    )
-    sum_table = own_half(totals[6:7])[0].reshape(BUCKETS // 2, HEADS)
+        totals[4 * at : 4 * at + 4].reshape(-1) for at in range(3)
+    )
+    sum_table = totals[16:, :HEADS]
     return (
         result[None],
         input_grad[None],

time: 549 us -> 479 us (0.87)
  matrix products: 93.1 us -> 65.1 us
  Pallas kernels: 359 us -> 337 us
  between operations: 15.4 us -> 2.2 us
  waiting for transfers between devices: 17.8 us -> 5.37 us
  starting transfers between devices: 3.9 us -> 12.7 us
    pallas_call x3 -> x0, Pallas kernels: 45.2 us -> none  [the longest x1 22 us: grads_from_heads(): pl.pallas_call(grads_from_heads_kernel, out_shape=[jax.ShapeDtypeStruct((...]
    pallas_call x1, Pallas kernels: 262 us -> 287 us  [weight_grads(): pl.pallas_call(functools.partial(weight_grad_kernel, products, len(lefts)...]
    dot_general x22 -> x12, matrix products: 45.2 us -> 24.3 us  [right_contract(): lax.dot_general(left, right, (((1,), (1,)), ((), ())), preferred_element_...]
    reduce_scatter x1 -> x0, waiting for transfers between devices: 17.7 us -> none  [on_device_by_heads(): lax.psum_scatter(cross_kv_part, 'ctx', scatter_dimension=0, tiled=True)]
    ppermute x0 -> x5, starting transfers between devices: none -> 9.09 us  [the longest x3 5.06 us: along_y(): return lax.ppermute(values, 'ctx', [(at, at ^ 2) for at in range(HEADS)])]
  transfers between devices with their start and end apart: 16 -> 18, of which waited for: 1 -> 1; matrix products, arithmetic and copies ran while one was open for 25% -> 20% of each run, Pallas kernels for 66% -> 72%
where the time goes in v3:
time: 479 us; the launch traced here: 471 us
  Pallas kernels  337 us (70%)
  matrix products  65.1 us (14%)
  other arithmetic  35.3 us (7%)
  local copies, waits for them, and re-layouts  13.1 us (3%)
  starting transfers between devices  12.7 us (3%)
  waiting for transfers between devices  5.37 us (1%)
    pallas_call x1, Pallas kernels, weight_grads(): pl.pallas_call(functools.partial(weight_grad_kernel, products, len(lefts)...  287 us
    dot_general x22, matrix products, plain_dot(): return jnp.dot(left, right, preferred_element_type=jnp.float32)  35.3 us
    pallas_call x1, Pallas kernels, to_heads(): pl.pallas_call(to_heads_kernel, out_shape=[jax.ShapeDtypeStruct(shape, BF...  28.9 us
    dot_general x12, matrix products, right_contract(): lax.dot_general(left, right, (((1,), (1,)), ((), ())), preferred_element_...  24.3 us
    convert_element_type x9, other arithmetic, on_device_by_heads(): member.astype(F32)  19.7 us
    pallas_call x1, Pallas kernels, from_heads(): pl.pallas_call(from_heads_kernel, out_shape=jax.ShapeDtypeStruct((2 * BLO...  15 us
  transfers between devices with their start and end apart: 18, of which 1 were waited for; matrix products, arithmetic and copies ran while one was open for 20% of the time, Pallas kernels for 72%

profile of v3, /device:TPU:0, one launch (start us, length us, event | category | flops | bytes accessed | tf_op | source)
XLA Modules:
  0.0 470.9 jit_solution(15796812826034890576)
XLA Ops:
  2.6 1.6 slice_select_fusion.2
  4.2 2.5 collective-permute-start.15
  8.5 1.8 bitcast_convert_fusion.refs_26_
  10.4 3.9 fusion.76
  19.2 1.5 fusion.14.q_ref
  21.2 1.5 fusion.15.k_ref
  23.0 1.5 fusion.16.v_ref
  24.6 28.9 %to_heads.1 = (bf16[16,192,128]{2,1,0:T(8,128)(2,1)S(1)}, bf16[16,16,1024]{2,1,0:T(8,128)(2,1)S(1)}) custom-call(bf16[128,1024]{1,0:T(8,128)(2,1)S(1)} %fusion.14.q_ref, bf16[128,1024]{1,0:T(8,128)(2,1)S(1)} %fusion.15.k_ref, bf16[128,1024]{1,0:T(8,128)(2,1)S(1)} %fusion.16.v_ref, bf16[16,1024]{1,0:T(8,128)(2,1)S(1)} %bitcast.114), custom_call_target="tpu_custom_call" | custom-call | tf_op jit(solution)/shard_map/to_heads/pallas_call | solution.py:557
  53.5 6.0 %attend.1 = (bf16[16,64,128]{2,1,0:T(8,128)(2,1)S(1)}, f32[64,2048]{1,0:T(8,128)S(1)}, f32[1,2048]{1,0:T(1,128)S(1)}) custom-call(s32[32]{0:T(128)S(1)} %copy-done.6, bf16[16,192,128]{2,1,0:T(8,128)(2,1)S(1)} %get-tuple-element.36.landed.refs_21_, f32[8,512]{1,0:T(8,128)S(1)} %select_maximum_fusion.bias_lines.refs_24_), custom_call_target="tpu_custom_call" | custom-call | flops 1073741824 | bytes 4194304 | tf_op jit(solution)/shard_map/attend/pallas_call | solution.py:656
  59.6 15.0 %from_heads.1.refs_4_ = bf16[128,1024]{1,0:T(8,128)(2,1)S(1)} custom-call(bf16[16,64,128]{2,1,0:T(8,128)(2,1)S(1)} %get-tuple-element.37.packed), custom_call_target="tpu_custom_call" | custom-call | tf_op jit(solution)/shard_map/from_heads/pallas_call | solution.py:593
  77.5 1.9 fusion.94
  79.9 1.7 fusion.9
  81.9 1.9 fusion.93
  84.4 2.5 fusion.8
  86.9 1.2 copy.63
  89.5 1.6 fusion.41
  91.2 1.6 multiply_reduce_fusion.5
  93.7 3.0 collective-permute-start.12
  96.7 2.5 fusion.67
  99.2 2.5 fusion.68
  101.8 2.8 fusion.78
  104.7 2.6 convolution_add_fusion
  107.3 4.5 multiply_convert_fusion.1
  111.8 3.4 fusion.98
  115.2 3.0 fusion.96
  119.1 1.7 fusion.29
  120.8 1.5 collective-permute-start.13
  122.3 2.9 fusion.95
  125.2 2.9 fusion.97
  128.9 1.8 fusion.100
  130.7 1.7 fusion.99
  136.8 1.8 collective-permute-start.16
  141.5 3.5 fusion.18
  149.6 5.3 %collective-permute-done.16.refs_17_ = bf16[128,1408]{1,0:T(8,128)(2,1)} collective-permute-done((bf16[128,1408]{1,0:T(8,128)(2,1)S(1)}, bf16[128,1408]{1,0:T(8,128)(2,1)}, u32[]{:S(2)}, u32[]{:S(2)}) %collective-permute-start.16) | collective-permute-done | bytes 360480 | tf_op jit(solution)/shard_map/ppermute | solution.py:1438
  154.9 287.2 %weight_grads.1 = (bf16[512,2816]{1,0:T(8,128)(2,1)}, bf16[1408,1024]{1,0:T(8,128)(2,1)}, bf16[512,2816]{1,0:T(8,128)(2,1)}, bf16[512,1024]{1,0:T(8,128)(2,1)}, ...) custom-call(bf16[128,1024]{1,0:T(8,128)(2,1)} %multiply_convert_fusi, ...), custom_call_target="tpu_custom_call" | custom-call | tf_op jit(solution)/shard_map/weight_grads/pallas_call | solution.py:1339
  442.2 1.4 slice.173
  443.5 2.8 convert_element_type.177
  446.3 1.6 convert_element_type.178
  447.9 1.6 convert_element_type.179
  449.5 1.6 convert_element_type.180
  451.0 1.6 convert_element_type.181
  452.6 1.6 convert_element_type.182
  454.2 1.3 slice_bitcast_fusion
  455.5 1.3 fusion.24
  456.8 2.4 fusion.87
  460.0 2.9 convert_element_type.183
  462.9 2.9 convert_element_type.184
  465.9 3.2 convert_element_type.185
  (215 shorter events, 31.2 us)
Async XLA Ops:
  2.2 13.7 %collective-permute-start = (bf16[1792]{0:T(1024)(128)(2,1)S(1)}, bf16[1792]{0:T(1024)(128)(2,1)S(1)}, u32[]{:S(2)}, u32[]{:S(2)}) collective-permute-start(bf16[1792]{0:T(1024)(128)(2,1)S(1)} %pad_maximum_fusion.1), channel_id=1, source_target_pairs={{0,1},{1,0},{2,3},{3,2},{4,5},{5,4},{6,7},{7,6},{8,9},{9,8},{10,11... | collective-permute-start | bytes 10760 | tf_op jit(solution)/shard_map/ppermute | solution.py:1432
  4.2 143.7 %collective-permute-start.15 = (bf16[128,512]{1,0:T(8,128)(2,1)}, bf16[128,512]{1,0:T(8,128)(2,1)}, u32[]{:S(2)}, u32[]{:S(2)}) collective-permute-start(bf16[128,512]{1,0:T(8,128)(2,1)} %slice_select_fusion.2), channel_id=1, source_target_pairs={{0,2},{2,0},{4,6},{6,4},{8,10},{10,8},{12,14},{14,12},{16,18},{18,... | collective-permute-start | bytes 393224 | tf_op jit(solution)/shard_map/ppermute | solution.py:1435
  6.7 11.7 %collective-permute-start.1 = (bf16[512,1024]{1,0:T(8,128)(2,1)}, bf16[512,1024]{1,0:T(8,128)(2,1)}, u32[]{:S(2)}, u32[]{:S(2)}) collective-permute-start(bf16[512,1024]{1,0:T(8,128)(2,1)} %refs_30_.1), channel_id=1, source_target_pairs={{0,1},{1,0},{2,3},{3,2},{4,5},{5,4},{6,7},{7,6},{8,9},{9,8},{10,11... | collective-permute-start | bytes 3145736 | tf_op jit(solution)/shard_map/ppermute | solution.py:1432
  7.0 13.8 %collective-permute-start.2 = (bf16[512,1024]{1,0:T(8,128)(2,1)}, bf16[512,1024]{1,0:T(8,128)(2,1)}, u32[]{:S(2)}, u32[]{:S(2)}) collective-permute-start(bf16[512,1024]{1,0:T(8,128)(2,1)} %refs_31_.1), channel_id=1, source_target_pairs={{0,1},{1,0},{2,3},{3,2},{4,5},{5,4},{6,7},{7,6},{8,9},{9,8},{10,11... | collective-permute-start | bytes 3145736 | tf_op jit(solution)/shard_map/ppermute | solution.py:1432
  7.3 94.5 %collective-permute-start.11 = (bf16[1408,1024]{1,0:T(8,128)(2,1)}, bf16[1408,1024]{1,0:T(8,128)(2,1)}, u32[]{:S(2)}, u32[]{:S(2)}) collective-permute-start(bf16[1408,1024]{1,0:T(8,128)(2,1)} %param.39), channel_id=1, source_target_pairs={{0,1},{1,0},{2,3},{3,2},{4,5},{5,4},{6,7},{7,6},{8,9},{9,8},{10,11... | collective-permute-start | bytes 8650760 | tf_op jit(solution)/shard_map/ppermute | solution.py:1432
  10.3 4.0 copy-start.6
  10.3 4.6 copy-start.52
  10.3 5.4 %copy-start.54 = (bf16[512]{0:T(512)(128)(2,1)S(1)}, bf16[512]{0:T(512)(128)(2,1)}, u32[]{:S(2)}) copy-start(bf16[512]{0:T(512)(128)(2,1)} %param.25) | copy-start | bytes 3076
  10.3 5.5 %copy-start.30 = (bf16[512,1024]{1,0:T(8,128)(2,1)S(1)}, bf16[512,1024]{1,0:T(8,128)(2,1)}, u32[]{:S(2)}) copy-start(bf16[512,1024]{1,0:T(8,128)(2,1)} %refs_32_.1) | copy-start | bytes 3145732
  10.4 5.9 %copy-start.53 = (bf16[16,16]{1,0:T(8,128)(2,1)S(1)}, bf16[16,16]{1,0:T(8,128)(2,1)}, u32[]{:S(2)}) copy-start(bf16[16,16]{1,0:T(8,128)(2,1)} %param.30) | copy-start | bytes 1540
  10.4 6.2 %copy-start.55 = (bf16[512]{0:T(512)(128)(2,1)S(1)}, bf16[512]{0:T(512)(128)(2,1)}, u32[]{:S(2)}) copy-start(bf16[512]{0:T(512)(128)(2,1)} %param.36) | copy-start | bytes 3076
  10.4 6.2 %copy-start.56 = (bf16[512]{0:T(512)(128)(2,1)S(1)}, bf16[512]{0:T(512)(128)(2,1)}, u32[]{:S(2)}) copy-start(bf16[512]{0:T(512)(128)(2,1)} %param.31) | copy-start | bytes 3076
  10.4 6.2 %copy-start.19 = (bf16[1,128,1024]{2,1,0:T(8,128)(2,1)S(1)}, bf16[1,128,1024]{2,1,0:T(8,128)(2,1)}, u32[]{:S(2)}) copy-start(bf16[1,128,1024]{2,1,0:T(8,128)(2,1)} %param.20) | copy-start | bytes 786436
  14.3 3.4 copy-start.29
  15.8 6.9 %collective-permute-start.3 = (bf16[512,1024]{1,0:T(8,128)(2,1)S(1)}, bf16[512,1024]{1,0:T(8,128)(2,1)}, u32[]{:S(2)}, u32[]{:S(2)}) collective-permute-start(bf16[512,1024]{1,0:T(8,128)(2,1)S(1)} %copy-done.30), channel_id=1, source_target_pairs={{0,1},{1,0},{2,3},{3,2},{4,5},{5,4},{6,7},{7,6},{8,9},{9,8},{10,11... | collective-permute-start | bytes 3145736 | tf_op jit(solution)/shard_map/ppermute | solution.py:1432
  16.6 36.9 %copy-start.3 = (f32[8,512]{1,0:T(8,128)}, f32[8,512]{1,0:T(8,128)S(1)}, u32[]{:S(2)}) copy-start(f32[8,512]{1,0:T(8,128)S(1)} %select_maximum_fusion.bias_lines.refs_24_) | copy-start | bytes 49156
  19.0 55.9 %collective-permute-start.4 = (bf16[512,1024]{1,0:T(8,128)(2,1)S(1)}, bf16[512,1024]{1,0:T(8,128)(2,1)S(1)}, u32[]{:S(2)}, u32[]{:S(2)}) collective-permute-start(bf16[512,1024]{1,0:T(8,128)(2,1)S(1)} %copy-done.20), channel_id=1, source_target_pairs={{0,1},{1,0},{2,3},{3,2},{4,5},{5,4},{6,7},{7,6},{8,9},{9,8},{10,11... | collective-permute-start | bytes 3145736 | tf_op jit(solution)/shard_map/ppermute | solution.py:1432
  20.8 3.8 copy-start.4
  20.8 55.1 %collective-permute-start.6 = (bf16[512,1024]{1,0:T(8,128)(2,1)S(1)}, bf16[512,1024]{1,0:T(8,128)(2,1)S(1)}, u32[]{:S(2)}, u32[]{:S(2)}) collective-permute-start(bf16[512,1024]{1,0:T(8,128)(2,1)S(1)} %copy-done.17), channel_id=1, source_target_pairs={{0,1},{1,0},{2,3},{3,2},{4,5},{5,4},{6,7},{7,6},{8,9},{9,8},{10,11... | collective-permute-start | bytes 3145736 | tf_op jit(solution)/shard_map/ppermute | solution.py:1432
  22.7 56.6 %collective-permute-start.7 = (bf16[512,1024]{1,0:T(8,128)(2,1)}, bf16[512,1024]{1,0:T(8,128)(2,1)}, u32[]{:S(2)}, u32[]{:S(2)}) collective-permute-start(bf16[512,1024]{1,0:T(8,128)(2,1)} %refs_36_.1), channel_id=1, source_target_pairs={{0,1},{1,0},{2,3},{3,2},{4,5},{5,4},{6,7},{7,6},{8,9},{9,8},{10,11... | collective-permute-start | bytes 3145736 | tf_op jit(solution)/shard_map/ppermute | solution.py:1432
  53.5 21.1 %copy-start.1 = (bf16[16,192,128]{2,1,0:T(8,128)(2,1)}, bf16[16,192,128]{2,1,0:T(8,128)(2,1)S(1)}, u32[]{:S(2)}) copy-start(bf16[16,192,128]{2,1,0:T(8,128)(2,1)S(1)} %get-tuple-element.36.landed.refs_21_) | copy-start | bytes 2359300
  59.5 15.9 %copy-start.2 = (f32[64,2048]{1,0:T(8,128)}, f32[64,2048]{1,0:T(8,128)S(1)}, u32[]{:S(2)}) copy-start(f32[64,2048]{1,0:T(8,128)S(1)} %get-tuple-element.39.refs_22_) | copy-start | bytes 1572868
  59.5 15.9 %copy-start.5 = (f32[1,2048]{1,0:T(1,128)}, f32[1,2048]{1,0:T(1,128)S(1)}, u32[]{:S(2)}) copy-start(f32[1,2048]{1,0:T(1,128)S(1)} %get-tuple-element.40.refs_23_) | copy-start | bytes 24580
  74.9 9.4 %collective-permute-start.5 = (bf16[512,1024]{1,0:T(8,128)(2,1)}, bf16[512,1024]{1,0:T(8,128)(2,1)}, u32[]{:S(2)}, u32[]{:S(2)}) collective-permute-start(bf16[512,1024]{1,0:T(8,128)(2,1)} %refs_37_.1), channel_id=1, source_target_pairs={{0,1},{1,0},{2,3},{3,2},{4,5},{5,4},{6,7},{7,6},{8,9},{9,8},{10,11... | collective-permute-start | bytes 3145736 | tf_op jit(solution)/shard_map/ppermute | solution.py:1432
  75.9 15.2 %collective-permute-start.8 = (bf16[512,1024]{1,0:T(8,128)(2,1)}, bf16[512,1024]{1,0:T(8,128)(2,1)}, u32[]{:S(2)}, u32[]{:S(2)}) collective-permute-start(bf16[512,1024]{1,0:T(8,128)(2,1)} %param.35), channel_id=1, source_target_pairs={{0,1},{1,0},{2,3},{3,2},{4,5},{5,4},{6,7},{7,6},{8,9},{9,8},{10,11... | collective-permute-start | bytes 3145736 | tf_op jit(solution)/shard_map/ppermute | solution.py:1432
  77.4 6.3 %copy-start.37 = (bf16[128,1024]{0,1:T(8,128)(2,1)}, bf16[128,1024]{0,1:T(8,128)(2,1)S(1)}, u32[]{:S(2)}) copy-start(bf16[128,1024]{0,1:T(8,128)(2,1)S(1)} %copy.64) | copy-start | bytes 786436
  77.5 4.1 copy-start.39
  77.5 4.3 copy-start.26
  79.4 27.9 %collective-permute-start.9 = (bf16[512,2816]{1,0:T(8,128)(2,1)}, bf16[512,2816]{1,0:T(8,128)(2,1)}, u32[]{:S(2)}, u32[]{:S(2)}) collective-permute-start(bf16[512,2816]{1,0:T(8,128)(2,1)} %param.37), channel_id=1, source_target_pairs={{0,1},{1,0},{2,3},{3,2},{4,5},{5,4},{6,7},{7,6},{8,9},{9,8},{10,11... | collective-permute-start | bytes 8650760 | tf_op jit(solution)/shard_map/ppermute | solution.py:1432
  84.3 20.4 %collective-permute-start.10 = (bf16[512,2816]{1,0:T(8,128)(2,1)}, bf16[512,2816]{1,0:T(8,128)(2,1)}, u32[]{:S(2)}, u32[]{:S(2)}) collective-permute-start(bf16[512,2816]{1,0:T(8,128)(2,1)} %param.38), channel_id=1, source_target_pairs={{0,1},{1,0},{2,3},{3,2},{4,5},{5,4},{6,7},{7,6},{8,9},{9,8},{10,11... | collective-permute-start | bytes 8650760 | tf_op jit(solution)/shard_map/ppermute | solution.py:1432
  89.5 3.3 copy-start.35
  93.7 55.9 %collective-permute-start.12 = (bf16[128,1024]{1,0:T(8,128)(2,1)}, bf16[128,1024]{1,0:T(8,128)(2,1)}, u32[]{:S(2)}, u32[]{:S(2)}) collective-permute-start(bf16[128,1024]{1,0:T(8,128)(2,1)} %multiply_convert_fusion.3.refs_0_), channel_id=1, source_target_pairs={{0,4},{2,6},{4,0},{6,2},{8,12},{10,14},{12,8},{14,10},{16,20},{18,... | collective-permute-start | bytes 786440 | tf_op jit(solution)/shard_map/ppermute | solution.py:1438
  111.8 10.5 %copy-start.8 = (bf16[128,2816]{1,0:T(8,128)(2,1)}, bf16[128,2816]{1,0:T(8,128)(2,1)S(1)}, u32[]{:S(2)}) copy-start(bf16[128,2816]{1,0:T(8,128)(2,1)S(1)} %get-tuple-element.64.refs_6_) | copy-start | bytes 2162692
  111.8 13.4 %copy-start.7 = (bf16[128,2816]{1,0:T(8,128)(2,1)}, bf16[128,2816]{1,0:T(8,128)(2,1)S(1)}, u32[]{:S(2)}) copy-start(bf16[128,2816]{1,0:T(8,128)(2,1)S(1)} %get-tuple-element.63.refs_8_) | copy-start | bytes 2162692
  115.2 3.9 copy-start.9
  120.8 34.1 %collective-permute-start.13 = (bf16[128,2816]{1,0:T(8,128)(2,1)}, bf16[128,2816]{1,0:T(8,128)(2,1)}, u32[]{:S(2)}, u32[]{:S(2)}) collective-permute-start(bf16[128,2816]{1,0:T(8,128)(2,1)} %get-tuple-element.65.refs_1_), channel_id=1, source_target_pairs={{0,2},{2,0},{4,6},{6,4},{8,10},{10,8},{12,14},{14,12},{16,18},{18,... | collective-permute-start | bytes 2162696 | tf_op jit(solution)/shard_map/ppermute | solution.py:1435
  128.9 4.1 copy-start.16
  135.0 3.6 copy-start.18
  135.5 3.6 copy-start.25
  136.6 13.0 %collective-permute-start.14 = (bf16[128,1408]{1,0:T(8,128)(2,1)}, bf16[128,1408]{1,0:T(8,128)(2,1)}, u32[]{:S(2)}, u32[]{:S(2)}) collective-permute-start(bf16[128,1408]{1,0:T(8,128)(2,1)} %slice_select_fusion.1), channel_id=1, source_target_pairs={{0,4},{2,6},{4,0},{6,2},{8,12},{10,14},{12,8},{14,10},{16,20},{18,... | collective-permute-start | bytes 1081352 | tf_op jit(solution)/shard_map/ppermute | solution.py:1438
  136.8 18.1 %collective-permute-start.16 = (bf16[128,1408]{1,0:T(8,128)(2,1)S(1)}, bf16[128,1408]{1,0:T(8,128)(2,1)}, u32[]{:S(2)}, u32[]{:S(2)}) collective-permute-start(bf16[128,1408]{1,0:T(8,128)(2,1)S(1)} %slice_select_fusion), channel_id=1, source_target_pairs={{0,4},{2,6},{4,0},{6,2},{8,12},{10,14},{12,8},{14,10},{16,20},{18,... | collective-permute-start | bytes 1081352 | tf_op jit(solution)/shard_map/ppermute | solution.py:1438
  140.9 4.0 copy-start.15
  141.4 3.5 copy-start.23
  147.9 307.6 %collective-permute-start.17 = (bf16[256,512]{1,0:T(8,128)(2,1)S(1)}, bf16[256,512]{1,0:T(8,128)(2,1)S(1)}, u32[]{:S(2)}, u32[]{:S(2)}) collective-permute-start(bf16[256,512]{1,0:T(8,128)(2,1)S(1)} %copy-done.41), channel_id=1, source_target_pairs={{0,1},{1,0},{2,3},{3,2},{4,5},{5,4},{6,7},{7,6},{8,9},{9,8},{10,11... | collective-permute-start | bytes 786440 | tf_op jit(solution)/shard_map/ppermute | solution.py:1432
  442.1 4.2 copy-start.48
  456.8 3.1 copy-start.33
  465.9 3.3 copy-start.50
  465.9 4.0 copy-start.51
  (27 other events, 51.0 us)

commit v4 on v3

--- a/solution.py
+++ b/solution.py
@@ -810,8 +810,10 @@
     vec_in, vec_sums, vec_landed, weight_buffer, normed_grad = take(5)
     (
         left_send,
+        left_own,
         left_recv,
         right_send,
+        right_own,
         right_recv,
         pair_send,
         pair_recv,
@@ -825,6 +827,7 @@
         all_send,
         all_recv,
         all_own,
+        kv_sem,
         weight_sem,
     ) = refs
     me, core = lax.axis_index("ctx"), lax.axis_index("wsh")
@@ -834,17 +837,16 @@
 
     barrier = pltpu.get_barrier_semaphore()
     for step in range(1, peers):
-        for side in (core, 1 - core):
-            pl.semaphore_signal(
-                barrier, inc=1, device_id=(lax.rem(me + step, peers), side), device_id_type=MESH
-            )
+        pl.semaphore_signal(
+            barrier, inc=1, device_id=(lax.rem(me + step, peers), core), device_id_type=MESH
+        )
     pl.semaphore_signal(barrier, inc=1, device_id=(me, 1 - core), device_id_type=MESH)
     for head in range(peers):
         cols = slice(head * HEAD_DIM, (head + 1) * HEAD_DIM)
         grad_packed[head] = jnp.concatenate(
             [grad_rows[:BLOCK, cols], grad_rows[BLOCK:, cols]], axis=1
         )
-    pl.semaphore_wait(barrier, 2 * peers - 1)
+    pl.semaphore_wait(barrier, peers)
 
     def place(zz, yy, xx):
         return zz * 4 + yy * 2 + xx
@@ -870,13 +872,14 @@
     def launch(copy, only=None):
         if only is None:
             copy.start()
-            finish.append(copy.wait_send)
         else:
             pl.when(only)(copy.start)
-            finish.append(lambda: pl.when(only)(copy.wait_send))
-
-    def arrived(dst, recv_sem):
-        remote(dst, dst, own_sem.at[0], recv_sem, me, 1 - core).wait_recv()
+
+    def arrived(ref, sem):
+        remote(ref, ref, own_sem.at[0], sem, me, 1 - core).wait_recv()
+
+    def left_here(ref, sem):
+        finish.append(lambda: remote(ref, ref, sem, own_sem.at[0], me, 1 - core).wait_send())
 
     def lanes(ref, at, width):
         return ref.at[:, pl.ds(pl.multiple_of(at * width, 128), width)]
@@ -902,47 +905,52 @@
     def send_left(at):
         (_, way), _ = axes(left_axis[at])
         half = left_all[at].shape[1]
-        copies = [local(lanes(lefts[at], core, half), slot(left_all[at], 0), left_send.at[at, 4])]
-        launch(remote(lanes(lefts[at], 1 - core, half), slot(left_all[at], 2), left_send.at[at, 2], left_recv.at[at, 2], me, 1 - core))
+        send_sem, recv_sem = left_send.at[at], left_recv.at[at]
+        mine, others = lanes(lefts[at], core, half), lanes(lefts[at], 1 - core, half)
+        copies = [local(mine, slot(left_all[at], 0), left_own.at[at])]
+        launch(remote(others, slot(left_all[at], 2), send_sem, recv_sem.at[2], me, 1 - core))
         if at < FAR_LEFTS:
-            copies.append(local(lanes(left_far[at], core, half), slot(left_all[at], 1), left_send.at[at, 5]))
-            launch(remote(lanes(left_far[at], 1 - core, half), slot(left_all[at], 3), left_send.at[at, 3], left_recv.at[at, 3], me, 1 - core))
+            far_mine, far_others = lanes(left_far[at], core, half), lanes(left_far[at], 1 - core, half)
+            copies.append(local(far_mine, slot(left_all[at], 1), left_own.at[at]))
+            launch(remote(far_others, slot(left_all[at], 3), send_sem, recv_sem.at[3], me, 1 - core))
+            left_here(left_all[at].at[: 2 * tokens], send_sem)
         else:
-            launch(remote(lanes(lefts[at], core, half), slot(left_all[at], 1), left_send.at[at, 0], left_recv.at[at, 0], targets[way], core))
-            launch(remote(lanes(lefts[at], 1 - core, half), left_pass[at], left_send.at[at, 1], left_recv.at[at, 1], targets[way], core))
-        return copies
+            launch(remote(mine, slot(left_all[at], 1), send_sem, recv_sem.at[0], targets[way], core))
+            launch(remote(others, left_pass[at], send_sem, recv_sem.at[1], targets[way], core))
+            left_here(left_all[at], send_sem)
+        return left_all[at].at[: len(copies) * tokens], left_own.at[at]
 
     def send_right(at):
         (mine, way), _ = axes(products[at])
         half = right_all[at].shape[1]
+        send_sem, recv_sem = right_send.at[at], right_recv.at[at]
+        own, others = lanes(rights[at], mine, half), lanes(rights[at], 1 - mine, half)
         if products[at].left == SUMMED:
-            launch(remote(lanes(rights[at], 1 - mine, half), right_all[at], right_send.at[at, 0], right_recv.at[at, 0], targets[way], core))
-            return []
-        copies = [local(lanes(rights[at], mine, half), slot(right_all[at], 0), right_send.at[at, 3])]
-        launch(remote(lanes(rights[at], mine, half), slot(right_all[at], 2), right_send.at[at, 1], right_recv.at[at, 1], me, 1 - core))
+            launch(remote(others, right_all[at], send_sem, recv_sem.at[0], targets[way], core))
+            left_here(right_all[at], send_sem)
+            return None
+        copies = [local(own, slot(right_all[at], 0), right_own.at[at])]
+        launch(remote(own, slot(right_all[at], 2), send_sem, recv_sem.at[1], me, 1 - core))
         if at in far_rights:
             far = right_far[far_rights.index(at)]
-            copies.append(local(far, slot(right_all[at], 1), right_send.at[at, 4]))
-            launch(remote(far, slot(right_all[at], 3), right_send.at[at, 2], right_recv.at[at, 2], me, 1 - core))
+            copies.append(local(far, slot(right_all[at], 1), right_own.at[at]))
+            launch(remote(far, slot(right_all[at], 3), send_sem, recv_sem.at[2], me, 1 - core))
+            left_here(right_all[at].at[: 2 * tokens], send_sem)
         else:
-            launch(remote(lanes(rights[at], 1 - mine, half), slot(right_all[at], 1), right_send.at[at, 0], right_recv.at[at, 0], targets[way], core))
-        return copies
+            launch(remote(others, slot(right_all[at], 1), send_sem, recv_sem.at[0], targets[way], core))
+            left_here(right_all[at].at[: 3 * tokens], send_sem)
+        return right_all[at].at[: len(copies) * tokens], right_own.at[at]
 
     def to_all(which, source, target):
-        copies = []
         for step in range(1, peers):
             peer = lax.rem(me + step, peers)
-            copies.append(
-                remote(source(peer), target(me), all_send.at[which, step], all_recv.at[which, step], peer, core)
-            )
-            launch(copies[-1])
-        own = pltpu.make_async_copy(source(me), target(me), all_own.at[which])
-        own.start()
+            launch(remote(source.at[peer], target.at[me], all_send.at[which], all_recv.at[which], peer, core))
+        own = local(source.at[me], target.at[me], all_own.at[which])
+        left_here(source.at[1:], all_send.at[which])
 
         def wait():
             own.wait()
-            for each in copies:
-                each.wait_recv()
+            arrived(target.at[1:], all_recv.at[which])
 
         return wait
 
@@ -957,12 +965,17 @@
                 owns["left", left] = send_left(left)
             owns["right", at] = send_right(at)
 
+    def own_slots(key):
+        ref, sem = owns[key]
+        pltpu.make_async_copy(ref, ref, sem).wait()
+
     def vector_step(step):
         if step == 0:
             source, ctx, side = vec_in.at[1 - core], me, 1 - core
         else:
             source, ctx, side = vec_sums.at[step - 1], me ^ (1 << (step - 1)), core
         launch(remote(source, vec_landed.at[step], vec_send.at[step], vec_recv.at[step], ctx, side))
+        left_here(source, vec_send.at[step])
 
     def vector_add(step):
         arrived(vec_landed.at[step], vec_recv.at[step])
@@ -983,9 +996,9 @@
             passed.add(left)
             arrived(slot(left_all[left], 1), left_recv.at[left, 0])
             arrived(left_pass[left], left_recv.at[left, 1])
-            launch(remote(left_pass[left], slot(left_all[left], 3), left_send.at[left, 3], left_recv.at[left, 3], me, 1 - core))
+            launch(remote(left_pass[left], slot(left_all[left], 3), left_send.at[left], left_recv.at[left, 3], me, 1 - core))
         arrived(slot(right_all[at], 1), right_recv.at[at, 0])
-        launch(remote(slot(right_all[at], 1), slot(right_all[at], 3), right_send.at[at, 2], right_recv.at[at, 2], me, 1 - core))
+        launch(remote(slot(right_all[at], 1), slot(right_all[at], 3), right_send.at[at], right_recv.at[at, 2], me, 1 - core))
 
     def multiply(at, out, half):
         product = products[at]
@@ -1026,13 +1039,13 @@
                 own = lanes(rows(rights[at], half, height), first_mine, held[at].shape[1])
                 out[...] = (own[...].astype(F32) + rows(right_all[at], half, height)[...].astype(F32)).astype(BF16)
             launch(remote(away[at], came[at], pair_send.at[at], pair_recv.at[at], targets[way], core))
+            left_here(away[at], pair_send.at[at])
             return
         if left not in turned:
             turned.add(left)
             arrived(slot(left_all[left], 2), left_recv.at[left, 2])
             arrived(slot(left_all[left], 3), left_recv.at[left, 3])
-            for each in owns["left", left]:
-                each.wait()
+            own_slots(("left", left))
             height = left_t[left].shape[0]
 
             def turn(index, carry):
@@ -1043,10 +1056,10 @@
             lax.fori_loop(0, height // 128, turn, 0)
         arrived(slot(right_all[at], 2), right_recv.at[at, 1])
         arrived(slot(right_all[at], 3), right_recv.at[at, 2])
-        for each in owns["right", at]:
-            each.wait()
+        own_slots(("right", at))
         multiply(at, away[at], 1 - mine)
         launch(remote(away[at], came[at], pair_send.at[at], pair_recv.at[at], targets[way], core))
+        left_here(away[at], pair_send.at[at])
         multiply(at, held[at], mine)
 
     def add(into, more):
@@ -1062,7 +1075,7 @@
             (0, z, lax.rem(z + 3 - step, 4), UP),
             (1, 3 - z, lax.rem(z + step + 1, 4), DOWN),
         ):
-            recv_sem = line_recv.at[at, side, chunk]
+            recv_sem = line_recv.at[at, side, lax.rem(chunk + 2, 3) if side == 0 else lax.rem(chunk, 3)]
             landing = rows(line_in[at], chunk + 1 - side, height)
 
             def land(landing=landing, chunk=chunk, recv_sem=recv_sem):
@@ -1075,13 +1088,15 @@
                     remote(
                         rows(held[at], chunk, height),
                         landing,
-                        line_send.at[at, side, chunk],
+                        line_send.at[at],
                         recv_sem,
                         targets[way],
                         core,
                     ),
                     only=behind <= step,
                 )
+        if step == 3:
+            left_here(held[at].at[: 3 * height], line_send.at[at])
 
     def own_piece(at):
         return rows(held[at], z, held[at].shape[0] // 4)
@@ -1098,28 +1113,31 @@
             pl.ds(pl.multiple_of(column * width, 128), width),
         ]
 
-    def send(at, where, way, index, only=None, own=False):
+    def send(at, where, way, arrival, only=None, own=False):
         launch(
             remote(
                 own_piece(at) if own else window(at, where),
                 window(at, where),
-                out_send.at[at, way, index],
-                out_recv.at[at, where],
+                out_send.at[at, min(way, ACROSS_Y)],
+                out_recv.at[at, arrival],
                 targets[way],
                 core,
             ),
             only,
         )
 
-    def arrive(at, where, only=None):
+    def arrive(at, where, arrival, only=None):
         def act():
-            arrived(window(at, where), out_recv.at[at, where])
+            arrived(window(at, where), out_recv.at[at, arrival])
 
         if only is None:
             act()
         else:
             pl.when(only)(act)
 
+    def quarters(at, number):
+        return wholes[at].at[: wholes[at].shape[0] // 4 * number]
+
     def near(way, zz):
         return place(zz, 1 - y, x) if way == ACROSS_Y else place(zz, y, 1 - x)
 
@@ -1131,6 +1149,17 @@
             (z >= apart, lax.rem(z + 4 - apart, 4), UP, jnp.logical_and(z >= apart, z < 3)),
             (z + apart <= 3, lax.rem(z + apart, 4), DOWN, jnp.logical_and(z + apart <= 3, z > 0)),
         )
+
+    def line_sent(at, piece_groups):
+        for number in (1, 2, 3):
+            for way, here in ((UP, z == number - 1), (DOWN, z == 4 - number)):
+                ref, sem = piece_groups(number), out_send.at[at, way]
+                finish.append(
+                    functools.partial(
+                        pl.when(here),
+                        lambda ref=ref, sem=sem: remote(ref, ref, sem, own_sem.at[0], me, 1 - core).wait_send(),
+                    )
+                )
 
     def gather_step(at, step):
         z_first, second, third = products[at].route
@@ -1138,49 +1167,54 @@
             owns["piece", at] = local(own_piece(at), window(at, me), own_sem.at[at])
             if at != kv_at:
                 finish.append(owns["piece", at].wait)
-            if not z_first:
+            if z_first:
+                send(at, me, UP, z, z < 3, own=True)
+                send(at, me, DOWN, z, z > 0, own=True)
+                send(at, me, second, 4 + z, own=True)
+                send(at, me, third, 8, own=True)
+                left_here(quarters(at, 3), out_send.at[at, ACROSS_Y])
+                line_sent(at, lambda number: held[at].at[: held[at].shape[0] // 4 * number])
+            else:
                 send(at, me, second, 0, own=True)
-                send(at, me, third, 0, own=True)
-            send(at, me, UP, 0, only=z < 3, own=True)
-            send(at, me, DOWN, 0, only=z > 0, own=True)
-            if z_first:
-                send(at, me, second, 0, own=True)
-                send(at, me, third, 0, own=True)
+                send(at, me, third, 1, own=True)
+                send(at, me, UP, 4 + z, z < 3, own=True)
+                send(at, me, DOWN, 4 + z, z > 0, own=True)
+                left_here(held[at].at[: held[at].shape[0] // 4 * 3], out_send.at[at, ACROSS_Y])
+                line_sent(at, lambda number: quarters(at, number))
         elif z_first:
             if step <= 3:
-                for side, (there, zz, way, on) in enumerate(from_line(step)):
+                for there, zz, way, on in from_line(step):
                     where = place(zz, y, x)
-                    arrive(at, where, there)
-                    send(at, where, way, step, on)
-                    send(at, where, second, 2 * step + side, there)
-                    send(at, where, third, 2 * step + side, there)
+                    arrive(at, where, zz, there)
+                    send(at, where, way, zz, on)
+                    send(at, where, second, 4 + zz, there)
+                    send(at, where, third, 8, there)
             elif step <= 7:
-                where = near(second, z ^ (step - 4))
-                arrive(at, where)
-                send(at, where, third, 4 + step)
+                zz = z ^ (step - 4)
+                where = near(second, zz)
+                arrive(at, where, 4 + zz)
+                send(at, where, third, 8)
             elif step == 8:
-                for turn in range(4):
-                    arrive(at, near(third, z ^ turn))
-                    arrive(at, opposite(z ^ turn))
+                arrived(quarters(at, 2), out_recv.at[at, 8])
         else:
             if step == 1:
                 where = near(second, z)
-                arrive(at, where)
-                send(at, where, third, 1)
-                send(at, where, UP, 1, z < 3)
-                send(at, where, DOWN, 1, z > 0)
+                arrive(at, where, 0)
+                send(at, where, third, 2)
+                send(at, where, UP, 4 + z, z < 3)
+                send(at, where, DOWN, 4 + z, z > 0)
             elif step == 2:
-                for index, where in ((2, near(third, z)), (3, opposite(z))):
-                    arrive(at, where)
-                    send(at, where, UP, index, z < 3)
-                    send(at, where, DOWN, index, z > 0)
+                for arrival, where in ((1, near(third, z)), (2, opposite(z))):
+                    arrive(at, where, arrival)
+                    send(at, where, UP, 4 + z, z < 3)
+                    send(at, where, DOWN, 4 + z, z > 0)
             elif step <= 5:
                 for there, zz, way, on in from_line(step - 2):
-                    for index, where in enumerate(
-                        (place(zz, y, x), near(second, zz), near(third, zz), opposite(zz))
-                    ):
-                        arrive(at, where, there)
-                        send(at, where, way, 4 * (step - 2) + index, on)
+                    pl.when(there)(
+                        functools.partial(arrived, quarters(at, 1), out_recv.at[at, 4 + zz])
+                    )
+                    for where in (place(zz, y, x), near(second, zz), near(third, zz), opposite(zz)):
+                        send(at, where, way, 4 + zz, on)
 
     def reduce_step(at, step):
         if step == 0:
@@ -1255,9 +1289,16 @@
                     reduce_step(some[time - step], step)
             yield
 
-    grad_arrival = to_all(0, lambda peer: grad_packed.at[peer], lambda mine: grad_landed.at[mine])
+    def gather_all(some, step):
+        for at in some:
+            gather_step(at, step)
+
+    def slots(of, number):
+        for _ in range(number):
+            next(of, None)
+
+    grad_arrival = to_all(0, grad_packed, grad_landed)
     send_operands(near_by)
-    send_operands(others)
     for at in near_by:
         product_away(at)
     grad_arrival()
@@ -1265,15 +1306,10 @@
         order, held_at, landed, grad_landed, attn_sum, log_norm, bias_lines, back_packed, lines,
         *attention_scratch,
     )
-    back_arrival = to_all(1, lambda peer: back_packed.at[peer], lambda mine: back_landed.at[mine])
-    early_wave = wave(near_by + others)
-    for index, at in enumerate(others):
-        pass_on(at)
-        if index:
-            product_away(others[index - 1])
-    product_away(others[-1])
-    next(early_wave)
-    next(early_wave)
+    back_arrival = to_all(1, back_packed, back_landed)
+    send_operands(others)
+    near_wave, other_wave, late_wave = wave(near_by), wave(others), wave(list(late))
+    slots(near_wave, 4)
     back_arrival()
     dq_ref, dk_ref, dv_ref = rights[count - 3 :]
     for pair in range(peers // 2):
@@ -1283,35 +1319,55 @@
         dv_ref[:BLOCK, cols] = first
         dv_ref[BLOCK:, cols] = second
     send_operands(late)
+    slots(near_wave, 4)
+    for index, at in enumerate(others):
+        pass_on(at)
+        if index:
+            product_away(others[index - 1])
+    product_away(others[-1])
+    gather_all(near_by, 1)
     input_gradient()
-    for _ in early_wave:
-        pass
+    gather_all(near_by, 2)
+    slots(other_wave, 2)
     for at in late:
         pass_on(at)
-    vector_add(0)
     for at in late:
         product_away(at)
-    for at in early:
-        gather_step(at, 1)
-    for time, _ in enumerate(wave(list(late))):
-        if time in (1, 3, 5):
-            for at in early:
-                gather_step(at, 2 + time // 2)
-            vector_add(1 + time // 2)
+    vector_add(0)
+    gather_all(near_by, 3)
+    slots(other_wave, 3)
+    gather_all(near_by, 4)
+    vector_add(1)
+    slots(late_wave, 1)
+    slots(other_wave, 3)
+    slots(late_wave, 1)
+    gather_all(near_by, 5)
+    gather_all(others, 1)
+    slots(late_wave, 1)
+    vector_add(2)
+    gather_all(near_by, 6)
+    gather_all(others, 2)
+    slots(late_wave, 1)
+    vector_add(3)
+    slots(late_wave, 1)
+    gather_all(near_by, 7)
+    gather_all(others, 3)
+    slots(late_wave, 1)
+    slots(late_wave, 1)
     vector_add(4)
-    for step in range(1, 9):
-        for at in late:
-            gather_step(at, step)
-        if step >= 5:
-            for at in early:
-                gather_step(at, step)
-        if step == 5:
-            owns["piece", kv_at].wait()
-            launch(
-                remote(kv_both.at[0], kv_both.at[1], all_send.at[0, 0], all_recv.at[0, 0], me, 1 - core)
-            )
-            encoder_gradient()
-    arrived(kv_both.at[1], all_recv.at[0, 0])
+    gather_all(late, 1)
+    gather_all(others, 4)
+    gather_all(late, 2)
+    gather_all(others, 5)
+    gather_all(late, 3)
+    owns["piece", kv_at].wait()
+    launch(remote(kv_both.at[0], kv_both.at[1], kv_sem.at[0], kv_sem.at[1], me, 1 - core))
+    left_here(kv_both.at[0], kv_sem.at[0])
+    encoder_gradient()
+    for step in range(4, 9):
+        gather_all(late, step)
+    gather_all(near_by, 8)
+    arrived(kv_both.at[1], kv_sem.at[1])
     for each in finish:
         each()
 
@@ -1349,7 +1405,9 @@
             jax.ShapeDtypeStruct((kv_rows // peers, width), BF16),
             jax.ShapeDtypeStruct((2, kv_rows, kv_width), BF16),
         ],
-        in_specs=[vmem_spec()] * (len(lefts) + len(rights) + len(left_far) + len(right_far))
+        in_specs=[any_spec()] * len(lefts)
+        + [vmem_spec() if product.left == SUMMED else any_spec() for product in products[: len(rights)]]
+        + [any_spec()] * (len(left_far) + len(right_far))
         + [smem_spec] * 2
         + [vmem_spec()] * (len(others) - 2)
         + [any_spec()] * len(weights),
@@ -1379,21 +1437,24 @@
             vmem((tokens, width), F32),
         ]
         + [
-            dma((len(lefts), 6)),
+            dma((len(lefts),)),
+            dma((len(lefts),)),
             dma((len(lefts), 4)),
-            dma((count, 5)),
+            dma((count,)),
+            dma((count,)),
             dma((count, 3)),
             dma((count,)),
             dma((count,)),
-            dma((count, 2, 4)),
-            dma((count, 2, 4)),
-            dma((count, 4, 16)),
-            dma((count, peers)),
+            dma((count,)),
+            dma((count, 2, 3)),
+            dma((count, 3)),
+            dma((count, 9)),
             dma((count,)),
             dma((5,)),
             dma((5,)),
-            dma((2, peers)),
-            dma((2, peers)),
+            dma((2,)),
+            dma((2,)),
+            dma((2,)),
             dma((2,)),
             dma((2,)),
         ],

time: 479 us -> 458 us (0.956)
  Pallas kernels: 337 us -> 316 us
    pallas_call x1, Pallas kernels: 287 us -> 266 us  [weight_grads(): pl.pallas_call(functools.partial(weight_grad_kernel, products, len(lefts)...]
  transfers between devices with their start and end apart: 18 -> 18, of which waited for: 1 -> 1; matrix products, arithmetic and copies ran while one was open for 20% -> 21% of each run, Pallas kernels for 72% -> 70%
where the time goes in v4:
time: 458 us; the launch traced here: 450 us
  Pallas kernels  316 us (69%)
  matrix products  65.1 us (14%)
  other arithmetic  35.1 us (8%)
  local copies, waits for them, and re-layouts  13.1 us (3%)
  starting transfers between devices  12.7 us (3%)
  waiting for transfers between devices  5.37 us (1%)
    pallas_call x1, Pallas kernels, weight_grads(): pl.pallas_call(functools.partial(weight_grad_kernel, products, len(lefts)...  266 us
    dot_general x22, matrix products, plain_dot(): return jnp.dot(left, right, preferred_element_type=jnp.float32)  35.3 us
    pallas_call x1, Pallas kernels, to_heads(): pl.pallas_call(to_heads_kernel, out_shape=[jax.ShapeDtypeStruct(shape, BF...  28.9 us
    dot_general x12, matrix products, right_contract(): lax.dot_general(left, right, (((1,), (1,)), ((), ())), preferred_element_...  24.3 us
    convert_element_type x9, other arithmetic, on_device_by_heads(): member.astype(F32)  19.7 us
    pallas_call x1, Pallas kernels, from_heads(): pl.pallas_call(from_heads_kernel, out_shape=jax.ShapeDtypeStruct((2 * BLO...  15 us
  transfers between devices with their start and end apart: 18, of which 1 were waited for; matrix products, arithmetic and copies ran while one was open for 21% of the time, Pallas kernels for 70%

profile of v4, /device:TPU:0, one launch (start us, length us, event | category | flops | bytes accessed | tf_op | source)
XLA Modules:
  0.0 449.9 jit_solution(9828010502650537224)
XLA Ops:
  2.6 1.6 slice_select_fusion.2
  4.2 2.5 collective-permute-start.15
  8.5 1.8 bitcast_convert_fusion.refs_26_
  10.4 3.9 fusion.76
  19.2 1.5 fusion.14.q_ref
  21.2 1.5 fusion.15.k_ref
  23.0 1.5 fusion.16.v_ref
  24.6 28.9 %to_heads.1 = (bf16[16,192,128]{2,1,0:T(8,128)(2,1)S(1)}, bf16[16,16,1024]{2,1,0:T(8,128)(2,1)S(1)}) custom-call(bf16[128,1024]{1,0:T(8,128)(2,1)S(1)} %fusion.14.q_ref, bf16[128,1024]{1,0:T(8,128)(2,1)S(1)} %fusion.15.k_ref, bf16[128,1024]{1,0:T(8,128)(2,1)S(1)} %fusion.16.v_ref, bf16[16,1024]{1,0:T(8,128)(2,1)S(1)} %bitcast.114), custom_call_target="tpu_custom_call" | custom-call | tf_op jit(solution)/shard_map/to_heads/pallas_call | solution.py:557
  53.5 6.0 %attend.1 = (bf16[16,64,128]{2,1,0:T(8,128)(2,1)S(1)}, f32[64,2048]{1,0:T(8,128)S(1)}, f32[1,2048]{1,0:T(1,128)S(1)}) custom-call(s32[32]{0:T(128)S(1)} %copy-done.6, bf16[16,192,128]{2,1,0:T(8,128)(2,1)S(1)} %get-tuple-element.36.landed.refs_21_, f32[8,512]{1,0:T(8,128)S(1)} %select_maximum_fusion.bias_lines.refs_24_), custom_call_target="tpu_custom_call" | custom-call | flops 1073741824 | bytes 4194304 | tf_op jit(solution)/shard_map/attend/pallas_call | solution.py:656
  59.6 15.0 %from_heads.1.refs_4_ = bf16[128,1024]{1,0:T(8,128)(2,1)S(1)} custom-call(bf16[16,64,128]{2,1,0:T(8,128)(2,1)S(1)} %get-tuple-element.37.packed), custom_call_target="tpu_custom_call" | custom-call | tf_op jit(solution)/shard_map/from_heads/pallas_call | solution.py:593
  77.5 1.9 fusion.94
  79.9 1.7 fusion.9
  81.9 1.9 fusion.93
  84.4 2.5 fusion.8
  86.9 1.2 copy.63
  89.5 1.6 fusion.41
  91.2 1.6 multiply_reduce_fusion.5
  93.7 3.0 collective-permute-start.12
  96.7 2.5 fusion.67
  99.2 2.5 fusion.68
  101.8 2.8 fusion.78
  104.7 2.6 convolution_add_fusion
  107.3 4.5 %multiply_convert_fusion.1 = (bf16[128,2816]{1,0:T(8,128)(2,1)S(1)}, bf16[128,2816]{1,0:T(8,128)(2,1)S(1)}, bf16[128,2816]{1,0:T(8,128)(2,1)}) fusion(f32[128,1408]{1,0:T(8,128)S(1)} %fusion.78, f32[128,1408]{1,0:T(8,128)S(1)} %copy-done.49, pred[]{:T(512)S(6)} %eq.37, f32[128,2816]{1,0:T(8,128)S(1)} %convolution_add_fusion, f32[128,2816]{1,0:T(8,128)S(1)} %fusion.68, ...), kind=kOutput, calls=%fused_computation.17 | convolution fusion | flops 379977728 | bytes 9634816 | tf_op jit(solution)/shard_map/dot_general | solution.py:24
  111.8 3.4 fusion.98
  115.2 3.0 fusion.96
  119.1 1.7 fusion.29
  120.8 1.5 collective-permute-start.13
  122.3 2.9 fusion.95
  125.2 2.9 fusion.97
  128.7 1.8 fusion.100
  130.5 1.7 fusion.99
  136.6 1.8 collective-permute-start.16
  141.2 3.5 fusion.18
  149.3 5.3 %collective-permute-done.16.refs_17_ = bf16[128,1408]{1,0:T(8,128)(2,1)} collective-permute-done((bf16[128,1408]{1,0:T(8,128)(2,1)S(1)}, bf16[128,1408]{1,0:T(8,128)(2,1)}, u32[]{:S(2)}, u32[]{:S(2)}) %collective-permute-start.16) | collective-permute-done | bytes 360480 | tf_op jit(solution)/shard_map/ppermute | solution.py:1499
  154.7 266.4 %weight_grads.1 = (bf16[512,2816]{1,0:T(8,128)(2,1)}, bf16[1408,1024]{1,0:T(8,128)(2,1)}, bf16[512,2816]{1,0:T(8,128)(2,1)}, bf16[512,1024]{1,0:T(8,128)(2,1)}, ...) custom-call(bf16[128,1024]{1,0:T(8,128)(2,1)} %multiply_convert_fusi, ...), custom_call_target="tpu_custom_call" | custom-call | tf_op jit(solution)/shard_map/weight_grads/pallas_call | solution.py:1395
  421.1 1.4 slice.173
  422.5 2.8 convert_element_type.177
  425.3 1.6 convert_element_type.178
  426.8 1.6 convert_element_type.179
  428.4 1.6 convert_element_type.180
  430.0 1.6 convert_element_type.181
  431.6 1.6 convert_element_type.182
  433.1 1.3 slice_bitcast_fusion
  434.5 1.3 fusion.24
  435.8 2.4 fusion.87
  438.9 2.9 convert_element_type.183
  441.9 2.9 convert_element_type.184
  444.8 3.2 convert_element_type.185
  (215 shorter events, 30.9 us)
Async XLA Ops:
  2.2 13.7 %collective-permute-start = (bf16[1792]{0:T(1024)(128)(2,1)S(1)}, bf16[1792]{0:T(1024)(128)(2,1)S(1)}, u32[]{:S(2)}, u32[]{:S(2)}) collective-permute-start(bf16[1792]{0:T(1024)(128)(2,1)S(1)} %pad_maximum_fusion.1), channel_id=1, source_target_pairs={{0,1},{1,0},{2,3},{3,2},{4,5},{5,4},{6,7},{7,6},{8,9},{9,8},{10,11... | collective-permute-start | bytes 10760 | tf_op jit(solution)/shard_map/ppermute | solution.py:1493
  4.2 143.4 %collective-permute-start.15 = (bf16[128,512]{1,0:T(8,128)(2,1)}, bf16[128,512]{1,0:T(8,128)(2,1)}, u32[]{:S(2)}, u32[]{:S(2)}) collective-permute-start(bf16[128,512]{1,0:T(8,128)(2,1)} %slice_select_fusion.2), channel_id=1, source_target_pairs={{0,2},{2,0},{4,6},{6,4},{8,10},{10,8},{12,14},{14,12},{16,18},{18,... | collective-permute-start | bytes 393224 | tf_op jit(solution)/shard_map/ppermute | solution.py:1496
  6.7 11.7 %collective-permute-start.1 = (bf16[512,1024]{1,0:T(8,128)(2,1)}, bf16[512,1024]{1,0:T(8,128)(2,1)}, u32[]{:S(2)}, u32[]{:S(2)}) collective-permute-start(bf16[512,1024]{1,0:T(8,128)(2,1)} %refs_30_.1), channel_id=1, source_target_pairs={{0,1},{1,0},{2,3},{3,2},{4,5},{5,4},{6,7},{7,6},{8,9},{9,8},{10,11... | collective-permute-start | bytes 3145736 | tf_op jit(solution)/shard_map/ppermute | solution.py:1493
  7.0 13.8 %collective-permute-start.2 = (bf16[512,1024]{1,0:T(8,128)(2,1)}, bf16[512,1024]{1,0:T(8,128)(2,1)}, u32[]{:S(2)}, u32[]{:S(2)}) collective-permute-start(bf16[512,1024]{1,0:T(8,128)(2,1)} %refs_31_.1), channel_id=1, source_target_pairs={{0,1},{1,0},{2,3},{3,2},{4,5},{5,4},{6,7},{7,6},{8,9},{9,8},{10,11... | collective-permute-start | bytes 3145736 | tf_op jit(solution)/shard_map/ppermute | solution.py:1493
  7.3 94.5 %collective-permute-start.11 = (bf16[1408,1024]{1,0:T(8,128)(2,1)}, bf16[1408,1024]{1,0:T(8,128)(2,1)}, u32[]{:S(2)}, u32[]{:S(2)}) collective-permute-start(bf16[1408,1024]{1,0:T(8,128)(2,1)} %param.39), channel_id=1, source_target_pairs={{0,1},{1,0},{2,3},{3,2},{4,5},{5,4},{6,7},{7,6},{8,9},{9,8},{10,11... | collective-permute-start | bytes 8650760 | tf_op jit(solution)/shard_map/ppermute | solution.py:1493
  10.3 4.0 copy-start.6
  10.3 4.6 %copy-start.52 = (s32[2048]{0:T(1024)S(1)}, s32[2048]{0:T(1024)}, u32[]{:S(2)}) copy-start(s32[2048]{0:T(1024)} %param.24) | copy-start | bytes 24580
  10.3 5.4 %copy-start.54 = (bf16[512]{0:T(512)(128)(2,1)S(1)}, bf16[512]{0:T(512)(128)(2,1)}, u32[]{:S(2)}) copy-start(bf16[512]{0:T(512)(128)(2,1)} %param.25) | copy-start | bytes 3076
  10.3 5.5 %copy-start.30 = (bf16[512,1024]{1,0:T(8,128)(2,1)S(1)}, bf16[512,1024]{1,0:T(8,128)(2,1)}, u32[]{:S(2)}) copy-start(bf16[512,1024]{1,0:T(8,128)(2,1)} %refs_32_.1) | copy-start | bytes 3145732
  10.4 5.9 %copy-start.53 = (bf16[16,16]{1,0:T(8,128)(2,1)S(1)}, bf16[16,16]{1,0:T(8,128)(2,1)}, u32[]{:S(2)}) copy-start(bf16[16,16]{1,0:T(8,128)(2,1)} %param.30) | copy-start | bytes 1540
  10.4 6.2 %copy-start.55 = (bf16[512]{0:T(512)(128)(2,1)S(1)}, bf16[512]{0:T(512)(128)(2,1)}, u32[]{:S(2)}) copy-start(bf16[512]{0:T(512)(128)(2,1)} %param.36) | copy-start | bytes 3076
  10.4 6.2 %copy-start.56 = (bf16[512]{0:T(512)(128)(2,1)S(1)}, bf16[512]{0:T(512)(128)(2,1)}, u32[]{:S(2)}) copy-start(bf16[512]{0:T(512)(128)(2,1)} %param.31) | copy-start | bytes 3076
  10.4 6.2 %copy-start.19 = (bf16[1,128,1024]{2,1,0:T(8,128)(2,1)S(1)}, bf16[1,128,1024]{2,1,0:T(8,128)(2,1)}, u32[]{:S(2)}) copy-start(bf16[1,128,1024]{2,1,0:T(8,128)(2,1)} %param.20) | copy-start | bytes 786436
  14.3 3.4 copy-start.29
  15.8 6.9 %collective-permute-start.3 = (bf16[512,1024]{1,0:T(8,128)(2,1)S(1)}, bf16[512,1024]{1,0:T(8,128)(2,1)}, u32[]{:S(2)}, u32[]{:S(2)}) collective-permute-start(bf16[512,1024]{1,0:T(8,128)(2,1)S(1)} %copy-done.30), channel_id=1, source_target_pairs={{0,1},{1,0},{2,3},{3,2},{4,5},{5,4},{6,7},{7,6},{8,9},{9,8},{10,11... | collective-permute-start | bytes 3145736 | tf_op jit(solution)/shard_map/ppermute | solution.py:1493
  16.6 36.9 %copy-start.3 = (f32[8,512]{1,0:T(8,128)}, f32[8,512]{1,0:T(8,128)S(1)}, u32[]{:S(2)}) copy-start(f32[8,512]{1,0:T(8,128)S(1)} %select_maximum_fusion.bias_lines.refs_24_) | copy-start | bytes 49156
  19.0 55.9 %collective-permute-start.4 = (bf16[512,1024]{1,0:T(8,128)(2,1)S(1)}, bf16[512,1024]{1,0:T(8,128)(2,1)S(1)}, u32[]{:S(2)}, u32[]{:S(2)}) collective-permute-start(bf16[512,1024]{1,0:T(8,128)(2,1)S(1)} %copy-done.20), channel_id=1, source_target_pairs={{0,1},{1,0},{2,3},{3,2},{4,5},{5,4},{6,7},{7,6},{8,9},{9,8},{10,11... | collective-permute-start | bytes 3145736 | tf_op jit(solution)/shard_map/ppermute | solution.py:1493
  20.8 3.8 copy-start.4
  20.8 55.1 %collective-permute-start.6 = (bf16[512,1024]{1,0:T(8,128)(2,1)S(1)}, bf16[512,1024]{1,0:T(8,128)(2,1)S(1)}, u32[]{:S(2)}, u32[]{:S(2)}) collective-permute-start(bf16[512,1024]{1,0:T(8,128)(2,1)S(1)} %copy-done.17), channel_id=1, source_target_pairs={{0,1},{1,0},{2,3},{3,2},{4,5},{5,4},{6,7},{7,6},{8,9},{9,8},{10,11... | collective-permute-start | bytes 3145736 | tf_op jit(solution)/shard_map/ppermute | solution.py:1493
  22.7 56.6 %collective-permute-start.7 = (bf16[512,1024]{1,0:T(8,128)(2,1)}, bf16[512,1024]{1,0:T(8,128)(2,1)}, u32[]{:S(2)}, u32[]{:S(2)}) collective-permute-start(bf16[512,1024]{1,0:T(8,128)(2,1)} %refs_36_.1), channel_id=1, source_target_pairs={{0,1},{1,0},{2,3},{3,2},{4,5},{5,4},{6,7},{7,6},{8,9},{9,8},{10,11... | collective-permute-start | bytes 3145736 | tf_op jit(solution)/shard_map/ppermute | solution.py:1493
  53.5 21.1 %copy-start.1 = (bf16[16,192,128]{2,1,0:T(8,128)(2,1)}, bf16[16,192,128]{2,1,0:T(8,128)(2,1)S(1)}, u32[]{:S(2)}) copy-start(bf16[16,192,128]{2,1,0:T(8,128)(2,1)S(1)} %get-tuple-element.36.landed.refs_21_) | copy-start | bytes 2359300
  59.5 15.9 %copy-start.2 = (f32[64,2048]{1,0:T(8,128)}, f32[64,2048]{1,0:T(8,128)S(1)}, u32[]{:S(2)}) copy-start(f32[64,2048]{1,0:T(8,128)S(1)} %get-tuple-element.39.refs_22_) | copy-start | bytes 1572868
  59.6 15.9 %copy-start.5 = (f32[1,2048]{1,0:T(1,128)}, f32[1,2048]{1,0:T(1,128)S(1)}, u32[]{:S(2)}) copy-start(f32[1,2048]{1,0:T(1,128)S(1)} %get-tuple-element.40.refs_23_) | copy-start | bytes 24580
  74.9 9.4 %collective-permute-start.5 = (bf16[512,1024]{1,0:T(8,128)(2,1)}, bf16[512,1024]{1,0:T(8,128)(2,1)}, u32[]{:S(2)}, u32[]{:S(2)}) collective-permute-start(bf16[512,1024]{1,0:T(8,128)(2,1)} %refs_37_.1), channel_id=1, source_target_pairs={{0,1},{1,0},{2,3},{3,2},{4,5},{5,4},{6,7},{7,6},{8,9},{9,8},{10,11... | collective-permute-start | bytes 3145736 | tf_op jit(solution)/shard_map/ppermute | solution.py:1493
  75.9 15.2 %collective-permute-start.8 = (bf16[512,1024]{1,0:T(8,128)(2,1)}, bf16[512,1024]{1,0:T(8,128)(2,1)}, u32[]{:S(2)}, u32[]{:S(2)}) collective-permute-start(bf16[512,1024]{1,0:T(8,128)(2,1)} %param.35), channel_id=1, source_target_pairs={{0,1},{1,0},{2,3},{3,2},{4,5},{5,4},{6,7},{7,6},{8,9},{9,8},{10,11... | collective-permute-start | bytes 3145736 | tf_op jit(solution)/shard_map/ppermute | solution.py:1493
  77.4 6.3 %copy-start.37 = (bf16[128,1024]{0,1:T(8,128)(2,1)}, bf16[128,1024]{0,1:T(8,128)(2,1)S(1)}, u32[]{:S(2)}) copy-start(bf16[128,1024]{0,1:T(8,128)(2,1)S(1)} %copy.64) | copy-start | bytes 786436
  77.5 4.1 copy-start.39
  77.5 4.3 copy-start.26
  79.4 27.9 %collective-permute-start.9 = (bf16[512,2816]{1,0:T(8,128)(2,1)}, bf16[512,2816]{1,0:T(8,128)(2,1)}, u32[]{:S(2)}, u32[]{:S(2)}) collective-permute-start(bf16[512,2816]{1,0:T(8,128)(2,1)} %param.37), channel_id=1, source_target_pairs={{0,1},{1,0},{2,3},{3,2},{4,5},{5,4},{6,7},{7,6},{8,9},{9,8},{10,11... | collective-permute-start | bytes 8650760 | tf_op jit(solution)/shard_map/ppermute | solution.py:1493
  84.3 20.4 %collective-permute-start.10 = (bf16[512,2816]{1,0:T(8,128)(2,1)}, bf16[512,2816]{1,0:T(8,128)(2,1)}, u32[]{:S(2)}, u32[]{:S(2)}) collective-permute-start(bf16[512,2816]{1,0:T(8,128)(2,1)} %param.38), channel_id=1, source_target_pairs={{0,1},{1,0},{2,3},{3,2},{4,5},{5,4},{6,7},{7,6},{8,9},{9,8},{10,11... | collective-permute-start | bytes 8650760 | tf_op jit(solution)/shard_map/ppermute | solution.py:1493
  89.5 3.3 copy-start.35
  93.7 55.7 %collective-permute-start.12 = (bf16[128,1024]{1,0:T(8,128)(2,1)}, bf16[128,1024]{1,0:T(8,128)(2,1)}, u32[]{:S(2)}, u32[]{:S(2)}) collective-permute-start(bf16[128,1024]{1,0:T(8,128)(2,1)} %multiply_convert_fusion.3.refs_0_), channel_id=1, source_target_pairs={{0,4},{2,6},{4,0},{6,2},{8,12},{10,14},{12,8},{14,10},{16,20},{18,... | collective-permute-start | bytes 786440 | tf_op jit(solution)/shard_map/ppermute | solution.py:1499
  111.8 10.5 %copy-start.8 = (bf16[128,2816]{1,0:T(8,128)(2,1)}, bf16[128,2816]{1,0:T(8,128)(2,1)S(1)}, u32[]{:S(2)}) copy-start(bf16[128,2816]{1,0:T(8,128)(2,1)S(1)} %get-tuple-element.64.refs_6_) | copy-start | bytes 2162692
  111.8 13.4 %copy-start.7 = (bf16[128,2816]{1,0:T(8,128)(2,1)}, bf16[128,2816]{1,0:T(8,128)(2,1)S(1)}, u32[]{:S(2)}) copy-start(bf16[128,2816]{1,0:T(8,128)(2,1)S(1)} %get-tuple-element.63.refs_8_) | copy-start | bytes 2162692
  115.2 3.9 copy-start.9
  120.8 33.9 %collective-permute-start.13 = (bf16[128,2816]{1,0:T(8,128)(2,1)}, bf16[128,2816]{1,0:T(8,128)(2,1)}, u32[]{:S(2)}, u32[]{:S(2)}) collective-permute-start(bf16[128,2816]{1,0:T(8,128)(2,1)} %get-tuple-element.65.refs_1_), channel_id=1, source_target_pairs={{0,2},{2,0},{4,6},{6,4},{8,10},{10,8},{12,14},{14,12},{16,18},{18,... | collective-permute-start | bytes 2162696 | tf_op jit(solution)/shard_map/ppermute | solution.py:1496
  128.7 4.1 copy-start.16
  134.7 3.6 copy-start.18
  135.2 3.6 copy-start.25
  136.4 13.0 %collective-permute-start.14 = (bf16[128,1408]{1,0:T(8,128)(2,1)}, bf16[128,1408]{1,0:T(8,128)(2,1)}, u32[]{:S(2)}, u32[]{:S(2)}) collective-permute-start(bf16[128,1408]{1,0:T(8,128)(2,1)} %slice_select_fusion.1), channel_id=1, source_target_pairs={{0,4},{2,6},{4,0},{6,2},{8,12},{10,14},{12,8},{14,10},{16,20},{18,... | collective-permute-start | bytes 1081352 | tf_op jit(solution)/shard_map/ppermute | solution.py:1499
  136.6 18.1 %collective-permute-start.16 = (bf16[128,1408]{1,0:T(8,128)(2,1)S(1)}, bf16[128,1408]{1,0:T(8,128)(2,1)}, u32[]{:S(2)}, u32[]{:S(2)}) collective-permute-start(bf16[128,1408]{1,0:T(8,128)(2,1)S(1)} %slice_select_fusion), channel_id=1, source_target_pairs={{0,4},{2,6},{4,0},{6,2},{8,12},{10,14},{12,8},{14,10},{16,20},{18,... | collective-permute-start | bytes 1081352 | tf_op jit(solution)/shard_map/ppermute | solution.py:1499
  140.7 4.0 copy-start.15
  141.2 3.5 copy-start.23
  147.7 286.8 %collective-permute-start.17 = (bf16[256,512]{1,0:T(8,128)(2,1)S(1)}, bf16[256,512]{1,0:T(8,128)(2,1)S(1)}, u32[]{:S(2)}, u32[]{:S(2)}) collective-permute-start(bf16[256,512]{1,0:T(8,128)(2,1)S(1)} %copy-done.41), channel_id=1, source_target_pairs={{0,1},{1,0},{2,3},{3,2},{4,5},{5,4},{6,7},{7,6},{8,9},{9,8},{10,11... | collective-permute-start | bytes 786440 | tf_op jit(solution)/shard_map/ppermute | solution.py:1493
  421.1 4.2 copy-start.48
  435.8 3.1 copy-start.33
  444.8 3.3 copy-start.50
  444.8 4.0 copy-start.51
  (27 other events, 51.0 us)

commit v5 on v4

--- a/solution.py
+++ b/solution.py
@@ -1,4 +1,5 @@
 import functools
+from typing import Any, NamedTuple
 
 import jax
 import jax.numpy as jnp
@@ -465,6 +466,7 @@
 TILE = 256
 BLOCK = 64
 MIB = 2**20
+GELU_RATE, GELU_CUBE = 0.7978845608, 0.044715
 
 
 def dot_nt(left, right):
@@ -477,97 +479,6 @@
 
 def any_spec():
     return pl.BlockSpec(memory_space=pl.ANY)
-
-
-def greet_all(peers):
-    me, core = lax.axis_index("ctx"), lax.axis_index("wsh")
-    barrier = pltpu.get_barrier_semaphore()
-    for step in range(1, peers):
-        pl.semaphore_signal(
-            barrier, inc=1, device_id=(lax.rem(me + step, peers), core), device_id_type=MESH
-        )
-    pl.semaphore_wait(barrier, peers - 1)
-
-
-def exchange_all(packed, landed, send_sem, recv_sem, own_sem):
-    peers = packed.shape[0]
-    me, core = lax.axis_index("ctx"), lax.axis_index("wsh")
-
-    def copy(step):
-        peer = lax.rem(me + step, peers)
-        return pltpu.make_async_remote_copy(
-            src_ref=packed.at[peer],
-            dst_ref=landed.at[me],
-            send_sem=send_sem.at[step],
-            recv_sem=recv_sem.at[step],
-            device_id=(peer, core),
-            device_id_type=MESH,
-        )
-
-    copies = [copy(step) for step in range(1, peers)]
-    for each in copies:
-        each.start()
-    own = pltpu.make_async_copy(packed.at[me], landed.at[me], own_sem)
-    own.start()
-    own.wait()
-    for each in copies:
-        each.wait()
-
-
-def exchange_scratch(peers):
-    return [
-        pltpu.SemaphoreType.DMA((peers,)),
-        pltpu.SemaphoreType.DMA((peers,)),
-        pltpu.SemaphoreType.DMA,
-    ]
-
-
-def to_heads_kernel(q_ref, k_ref, v_ref, rows_ref, landed, rows_out, packed, rows_send, rows_recv, rows_own, *sems):
-    peers = packed.shape[0]
-    me, core = lax.axis_index("ctx"), lax.axis_index("wsh")
-    greet_all(peers)
-    copies = []
-    for step in range(1, peers):
-        copies.append(
-            pltpu.make_async_remote_copy(
-                src_ref=rows_ref,
-                dst_ref=rows_out.at[me],
-                send_sem=rows_send.at[step],
-                recv_sem=rows_recv.at[step],
-                device_id=(lax.rem(me + step, peers), core),
-                device_id_type=MESH,
-            )
-        )
-    copies.append(pltpu.make_async_copy(rows_ref, rows_out.at[me], rows_own))
-    for head in range(peers):
-        cols = slice(head * HEAD_DIM, (head + 1) * HEAD_DIM)
-        packed[head, : 2 * BLOCK, :] = jnp.concatenate([q_ref[:, cols], k_ref[:, cols]], axis=1)
-        packed[head, 2 * BLOCK :, :] = jnp.concatenate(
-            [v_ref[:BLOCK, cols], v_ref[BLOCK:, cols]], axis=1
-        )
-    for each in copies:
-        each.start()
-    exchange_all(packed, landed, *sems)
-    for each in copies:
-        each.wait()
-
-
-def to_heads(queries, keys, values, rows):
-    shape = (HEADS, 3 * BLOCK, 2 * HEAD_DIM)
-    return pl.pallas_call(
-        to_heads_kernel,
-        out_shape=[
-            jax.ShapeDtypeStruct(shape, BF16),
-            jax.ShapeDtypeStruct((HEADS,) + rows.shape, BF16),
-        ],
-        in_specs=[vmem_spec()] * 4,
-        out_specs=[vmem_spec()] * 2,
-        scratch_shapes=[pltpu.VMEM(shape, BF16)] + exchange_scratch(HEADS) * 2,
-        compiler_params=pltpu.CompilerParams(
-            collective_id=1, has_side_effects=True, vmem_limit_bytes=16 * MIB
-        ),
-        name="to_heads",
-    )(queries, keys, values, rows)
 
 
 def unpack_pair(landed, pair, rows):
@@ -578,48 +489,44 @@
     )
 
 
-def from_heads_kernel(packed, out_ref, landed, *sems):
-    peers = packed.shape[0]
-    greet_all(peers)
-    exchange_all(packed, landed, *sems)
-    for pair in range(peers // 2):
-        cols = slice(pair * 2 * HEAD_DIM, (pair + 1) * 2 * HEAD_DIM)
-        first, second = unpack_pair(landed, pair, slice(0, BLOCK))
-        out_ref[:BLOCK, cols] = first
-        out_ref[BLOCK:, cols] = second
-
-
-def from_heads(packed):
-    return pl.pallas_call(
-        from_heads_kernel,
-        out_shape=jax.ShapeDtypeStruct((2 * BLOCK, HEADS * HEAD_DIM), BF16),
-        in_specs=[vmem_spec()],
-        out_specs=vmem_spec(),
-        scratch_shapes=[pltpu.VMEM(packed.shape, BF16)] + exchange_scratch(HEADS),
-        compiler_params=pltpu.CompilerParams(
-            collective_id=3, has_side_effects=True, vmem_limit_bytes=16 * MIB
-        ),
-        name="from_heads",
-    )(packed)
-
-
 def place_tiles(bias_lines, tiles):
     for apart in range(tiles.shape[0]):
         line = jnp.broadcast_to(bias_lines[apart : apart + 1, :], (TILE, 2 * TILE))
         tiles[apart] = pltpu.roll(line, 0, 1, stride=1, stride_axis=0)[:, :TILE]
 
 
-def attend_kernel(order, landed, bias_lines, out_ref, sum_ref, norm_ref, q_s, k_s, vt_s, tiles, ot_s, o_s):
-    blocks = order.shape[0]
+def attend_scratch(blocks):
+    length = blocks * BLOCK
+    vmem = pltpu.VMEM
+    return [
+        vmem((length, HEAD_DIM), BF16),
+        vmem((length, HEAD_DIM), BF16),
+        vmem((HEAD_DIM, length), BF16),
+        vmem((length // TILE, TILE, TILE), F32),
+        vmem((length, HEAD_DIM), F32),
+        vmem((length, HEAD_DIM), F32),
+    ]
+
+
+def attend(order, held_at, pairs, lone, bias_lines, out_ref, sum_ref, norm_ref, q_s, k_s, vt_s, tiles, staged, o_s):
+    blocks = held_at.shape[0]
     spans = blocks * BLOCK // TILE
+
+    def in_order(into):
+        for block in range(blocks):
+            at = slice(block * BLOCK, (block + 1) * BLOCK)
+            into[at, :] = staged[pl.ds(held_at[block] * BLOCK, BLOCK), :].astype(into.dtype)
+
+    for side, into in ((0, q_s), (1, k_s)):
+        for device in range(blocks // 2):
+            at = slice(2 * device * BLOCK, 2 * (device + 1) * BLOCK)
+            staged[at, :] = pairs[device, :, side * HEAD_DIM : (side + 1) * HEAD_DIM].astype(F32)
+        in_order(into)
     for stored in range(blocks):
-        device, half = stored // 2, stored % 2
-        at = pl.ds(pl.multiple_of(order[stored] * BLOCK, BLOCK), BLOCK)
-        pair = landed[device, half * BLOCK : (half + 1) * BLOCK, :]
-        q_s[at, :] = pair[:, :HEAD_DIM]
-        k_s[at, :] = pair[:, HEAD_DIM:]
-        values = landed[device, 2 * BLOCK :, half * HEAD_DIM : (half + 1) * HEAD_DIM]
-        o_s[at, :] = values.astype(F32)
+        at = slice(stored * BLOCK, (stored + 1) * BLOCK)
+        cols = slice(stored % 2 * HEAD_DIM, (stored % 2 + 1) * HEAD_DIM)
+        staged[at, :] = lone[stored // 2, :, cols].astype(F32)
+    in_order(o_s)
     vt_s[...] = jnp.transpose(o_s[...], (1, 0)).astype(BF16)
     place_tiles(bias_lines, tiles)
     for i in range(spans):
@@ -640,50 +547,15 @@
                 vt_s[:, j * TILE : (j + 1) * TILE], weights.astype(BF16)
             )
         norm_ref[0:1, at_i] = top + jnp.log(total)
-        ot_s[:, at_i] = mixed / total
-    sum_ref[...] = ot_s[...]
-    o_s[...] = jnp.transpose(ot_s[...], (1, 0))
+        sum_ref[:, at_i] = mixed / total
+    o_s[...] = jnp.transpose(sum_ref[...], (1, 0))
     for stored in range(blocks):
-        device, half = stored // 2, stored % 2
-        at = pl.ds(pl.multiple_of(order[stored] * BLOCK, BLOCK), BLOCK)
-        out_ref[device, :, half * HEAD_DIM : (half + 1) * HEAD_DIM] = o_s[at, :].astype(BF16)
-
-
-def attend(order, landed, bias_lines):
-    blocks = order.shape[0]
-    length = blocks * BLOCK
-    vmem = pltpu.VMEM
-    return pl.pallas_call(
-        attend_kernel,
-        grid_spec=pltpu.PrefetchScalarGridSpec(
-            num_scalar_prefetch=1,
-            grid=(),
-            in_specs=[vmem_spec()] * 2,
-            out_specs=[vmem_spec()] * 3,
-            scratch_shapes=[
-                vmem((length, HEAD_DIM), BF16),
-                vmem((length, HEAD_DIM), BF16),
-                vmem((HEAD_DIM, length), BF16),
-                vmem((length // TILE, TILE, TILE), F32),
-                vmem((HEAD_DIM, length), F32),
-                vmem((length, HEAD_DIM), F32),
-            ],
-        ),
-        out_shape=[
-            jax.ShapeDtypeStruct((blocks // 2, BLOCK, 2 * HEAD_DIM), BF16),
-            jax.ShapeDtypeStruct((HEAD_DIM, length), F32),
-            jax.ShapeDtypeStruct((1, length), F32),
-        ],
-        compiler_params=pltpu.CompilerParams(vmem_limit_bytes=32 * MIB),
-        cost_estimate=pl.CostEstimate(
-            flops=4 * length * length * HEAD_DIM, bytes_accessed=4 * MIB, transcendentals=length * length // 2
-        ),
-        name="attend",
-    )(order, landed, bias_lines)
+        cols = slice(stored % 2 * HEAD_DIM, (stored % 2 + 1) * HEAD_DIM)
+        out_ref[stored // 2, :, cols] = o_s[pl.ds(order[stored] * BLOCK, BLOCK), :].astype(BF16)
 
 
 def attend_back(
-    order, held_at, landed, grad_landed, sums, norm, bias_lines, out_ref, lines_ref,
+    order, held_at, pairs, lone, grad_landed, sums, norm, bias_lines, out_ref, lines_ref,
     q_s, k_s, v_s, do_s, kt_s, tiles, by_offset, dq_s, dk_s, dv_s, delta_s, dqt_s,
 ):
     blocks = order.shape[0]
@@ -700,10 +572,10 @@
 
     for stored in range(blocks):
         at, device, cols = stored_rows(stored)
-        pair = landed[device, stored % 2 * BLOCK : (stored % 2 + 1) * BLOCK, :].astype(F32)
+        pair = pairs[device, stored % 2 * BLOCK : (stored % 2 + 1) * BLOCK, :].astype(F32)
         dq_s[at, :] = pair[:, :HEAD_DIM]
         dk_s[at, :] = pair[:, HEAD_DIM:]
-        dv_s[at, :] = landed[device, 2 * BLOCK :, cols].astype(F32)
+        dv_s[at, :] = lone[device, :, cols].astype(F32)
     in_order(q_s, dq_s)
     in_order(k_s, dk_s)
     in_order(v_s, dv_s)
@@ -754,15 +626,476 @@
         lines_ref[apart : apart + 1, :] = line
 
 
+class Weights(NamedTuple):
+    query: Any
+    key: Any
+    value: Any
+    out: Any
+    cross_key: Any
+    cross_value: Any
+    cross_query: Any
+    cross_out: Any
+    gate: Any
+    up: Any
+    down: Any
+
+
+W = Weights(*range(11))
+LENT = (W.query, W.key, W.value, W.cross_key, W.cross_value)
+
+
+class Made(NamedTuple):
+    normed_one: Any
+    pairs: Any
+    lone: Any
+    attn_sum: Any
+    log_norm: Any
+    attended: Any
+    normed_two: Any
+    cross_mixed: Any
+    normed_three: Any
+    hidden: Any
+    gate_grad: Any
+    up_grad: Any
+    branch_two: Any
+    cross_q_grad: Any
+    branch_one: Any
+    dattn: Any
+    kv_part: Any
+    resid_grad: Any
+    result: Any
+    gain_grads: Any
+    gain_one: Any
+    bias_lines: Any
+    encoder_both: Any
+
+
+class Far(NamedTuple):
+    normed_three: Any
+    hidden: Any
+    gate: Any
+    up: Any
+    branch_three: Any
+
+
+class Scratch(NamedTuple):
+    small_far: Any
+    table_far: Any
+    pairs_out: Any
+    lone_out: Any
+    encoder_all: Any
+    mixed_out: Any
+    mixed_in: Any
+    cross_keys: Any
+    cross_values: Any
+    cross_queries: Any
+    cross_exact: Any
+    after_self: Any
+    after_cross: Any
+    gate_act: Any
+    up_act: Any
+    mix_grad: Any
+
+
+def norm_parts(values):
+    return lax.rsqrt(jnp.mean(values * values, axis=1, keepdims=True) + EPSILON)
+
+
+def norm_backward(values, gain, cotan):
+    rate = norm_parts(values)
+    scaled = cotan * gain
+    slope = jnp.mean(scaled * values, axis=1, keepdims=True)
+    return (
+        rate * scaled - values * (rate * rate * rate) * slope,
+        jnp.sum(cotan * values * rate, axis=0, keepdims=True),
+    )
+
+
+def layer_kernel(tokens_in, cotangent, encoder, small, table, in_bucket, held_at, order, *refs):
+    refs = list(refs)
+
+    def take(number):
+        taken = refs[:number]
+        del refs[:number]
+        return taken
+
+    sources = take(len(W))
+    out = Made(*take(len(Made._fields)))
+    far = Far(*take(len(Far._fields)))
+    lent = take(len(LENT))
+    weights = take(len(W))
+    own = Scratch(*take(len(Scratch._fields)))
+    (own_sem, weight_own, weight_send, weight_recv, lent_send, lent_recv, far_send, far_recv, all_own, all_send, all_recv) = refs
+    me, core = lax.axis_index("ctx"), lax.axis_index("wsh")
+    peers = lax.axis_size("ctx")
+    x, y = lax.rem(me, 2), lax.rem(me // 2, 2)
+    tokens, width = tokens_in.shape
+    finish = []
+
+    barrier = pltpu.get_barrier_semaphore()
+    for step in range(1, peers):
+        pl.semaphore_signal(
+            barrier, inc=1, device_id=(lax.rem(me + step, peers), core), device_id_type=MESH
+        )
+    pl.semaphore_signal(barrier, inc=1, device_id=(me, 1 - core), device_id_type=MESH)
+
+    def half_rows(ref, side):
+        half = ref.shape[0] // 2
+        return ref.at[pl.ds(pl.multiple_of(side * half, 16), half)]
+
+    def remote(src, dst, send_sem, recv_sem, ctx, side):
+        return pltpu.make_async_remote_copy(
+            src_ref=src,
+            dst_ref=dst,
+            send_sem=send_sem,
+            recv_sem=recv_sem,
+            device_id=(ctx, side),
+            device_id_type=MESH,
+        )
+
+    def arrived(ref, sem):
+        remote(ref, ref, own_sem, sem, me, 1 - core).wait_recv()
+
+    def launch(src, dst, send_sem, recv_sem, ctx, side):
+        remote(src, dst, send_sem, recv_sem, ctx, side).start()
+        finish.append(lambda: remote(src, src, send_sem, own_sem, me, 1 - core).wait_send())
+
+    local = {}
+    for at in W:
+        local[at] = pltpu.make_async_copy(sources[at], half_rows(weights[at], core), weight_own.at[at])
+        local[at].start()
+    pl.semaphore_wait(barrier, peers)
+
+    launch(small, own.small_far, far_send.at[5], far_recv.at[5], me, 1 - core)
+    launch(table, own.table_far, far_send.at[6], far_recv.at[6], me, 1 - core)
+    for at in W:
+        launch(sources[at], half_rows(weights[at], core), weight_send.at[at], weight_recv.at[at], me, 1 - core)
+    for at, source in enumerate(LENT):
+        launch(sources[source], lent[at], lent_send.at[at], lent_recv.at[at], me, 1 - core)
+
+    def weight(at):
+        if at in local:
+            local.pop(at).wait()
+            arrived(half_rows(weights[at], 1 - core), weight_recv.at[at])
+        return weights[at]
+
+    def to_all(which, source, target, spread=True):
+        for step in range(1, peers):
+            peer = lax.rem(me + step, peers)
+            remote(
+                source.at[peer] if spread else source, target.at[me], all_send.at[which], all_recv.at[which], peer, core
+            ).start()
+        kept = pltpu.make_async_copy(source.at[me] if spread else source, target.at[me], all_own.at[which])
+        kept.start()
+        finish.append(lambda: remote(target.at[1:], target.at[1:], all_send.at[which], own_sem, me, 1 - core).wait_send())
+
+        def wait():
+            kept.wait()
+            arrived(target.at[1:], all_recv.at[which])
+
+        return wait
+
+    def tiles_of(total):
+        return [slice(at, at + 256) for at in range(0, total, 256)]
+
+    def times(values, name):
+        ref = weight(name)
+        return jnp.concatenate([plain_dot(values, ref[:, cols]) for cols in tiles_of(ref.shape[1])], axis=1)
+
+    def times_back(values, name):
+        ref = weight(name)
+        return jnp.concatenate([dot_nt(values, ref[cols, :]) for cols in tiles_of(ref.shape[0])], axis=1)
+
+    def head(at):
+        return slice(at * HEAD_DIM, (at + 1) * HEAD_DIM)
+
+    def head_pair(at):
+        return slice(2 * at * HEAD_DIM, 2 * (at + 1) * HEAD_DIM)
+
+    arrived(own.small_far, far_recv.at[5])
+    arrived(own.table_far, far_recv.at[6])
+
+    def both(mine, others, axis):
+        first = jnp.where(core == 0, mine, others)
+        second = jnp.where(core == 0, others, mine)
+        return jnp.concatenate([first, second], axis=axis)
+
+    gain_one, gain_two, gain_three = (
+        both(small[at : at + 1, :], own.small_far[at : at + 1, :], 1) for at in range(3)
+    )
+    out.gain_one[...] = gain_one
+    whole_table = both(table[...], own.table_far[...], 0)
+    lane = lax.broadcasted_iota(jnp.int32, whole_table.shape, 1)
+    column = jnp.sum(jnp.where(lane == me, whole_table, 0.0), axis=1, keepdims=True)
+    spans = in_bucket.shape[0]
+    for apart in range(spans):
+        line = jnp.sum(in_bucket[apart] * column, axis=0, keepdims=True)
+        out.bias_lines[apart : apart + 1, :TILE] = line
+        if apart + 1 < spans:
+            out.bias_lines[apart + 1 : apart + 2, TILE:] = line
+    out.bias_lines[0:1, TILE:] = jnp.full((1, TILE), NEG_BIG, F32)
+
+    resid = tokens_in[...].astype(F32)
+    out.normed_one[...] = (resid * norm_parts(resid) * gain_one).astype(BF16)
+    normed_one = out.normed_one[...]
+    queries = times(normed_one, W.query).astype(BF16)
+    keys = times(normed_one, W.key).astype(BF16)
+    for at in range(peers):
+        own.pairs_out[at] = jnp.concatenate([queries[:, head(at)], keys[:, head(at)]], axis=1)
+    pairs_arrival = to_all(0, own.pairs_out, out.pairs)
+    values = times(normed_one, W.value).astype(BF16)
+    for at in range(peers):
+        own.lone_out[at] = jnp.concatenate(
+            [values[:BLOCK, head(at)], values[BLOCK:, head(at)]], axis=1
+        )
+    lone_arrival = to_all(1, own.lone_out, out.lone)
+    encoder_arrival = to_all(2, encoder, own.encoder_all, spread=False)
+    launch(
+        cotangent.at[:, pl.ds(pl.multiple_of((1 - x) * (width // 2), 128), width // 2)],
+        far.branch_three, far_send.at[4], far_recv.at[4], me ^ 1, core,
+    )
+    place_bias = out.bias_lines
+    pairs_arrival()
+    lone_arrival()
+    pl.run_scoped(
+        functools.partial(
+            attend, order, held_at, out.pairs, out.lone, place_bias, own.mixed_out, out.attn_sum, out.log_norm
+        ),
+        *attend_scratch(held_at.shape[0]),
+    )
+    mixed_arrival = to_all(3, own.mixed_out, own.mixed_in)
+
+    encoder_arrival()
+    encoder_rows = jnp.concatenate([own.encoder_all[at] for at in range(peers)], axis=0)
+    half = width // 2
+    count = encoder_rows.shape[0]
+    out.encoder_both[:count, :] = jnp.where(core == 0, encoder_rows[:, :half], encoder_rows[:, half:])
+    own.cross_keys[...] = times(encoder_rows, W.cross_key).astype(BF16)
+    own.cross_values[...] = times(encoder_rows, W.cross_value).astype(BF16)
+
+    mixed_arrival()
+    for pair in range(peers // 2):
+        first, second = unpack_pair(own.mixed_in, pair, slice(0, BLOCK))
+        out.attended[:BLOCK, head_pair(pair)] = first
+        out.attended[BLOCK:, head_pair(pair)] = second
+    own.after_self[...] = tokens_in[...].astype(F32) + times(out.attended[...], W.out)
+    after_self = own.after_self[...]
+    out.normed_two[...] = (after_self * norm_parts(after_self) * gain_two).astype(BF16)
+    own.cross_queries[...] = times(out.normed_two[...], W.cross_query).astype(BF16)
+
+    for pair in range(peers // 2):
+        mixed = []
+        for at in (2 * pair, 2 * pair + 1):
+            scores = dot_nt(own.cross_keys[:, head(at)], own.cross_queries[:, head(at)])
+            weight_t = jnp.exp(scores - jnp.max(scores, axis=0, keepdims=True))
+            exact = weight_t / jnp.sum(weight_t, axis=0, keepdims=True)
+            own.cross_exact[at] = exact
+            mixed.append(left_contract(exact.astype(BF16), own.cross_values[:, head(at)]))
+        out.cross_mixed[:, head_pair(pair)] = jnp.concatenate(mixed, axis=1).astype(BF16)
+    own.after_cross[...] = own.after_self[...] + times(out.cross_mixed[...], W.cross_out)
+    after_cross = own.after_cross[...]
+    out.normed_three[...] = (after_cross * norm_parts(after_cross) * gain_three).astype(BF16)
+    launch(out.normed_three, far.normed_three, far_send.at[0], far_recv.at[0], me ^ 2, core)
+
+    normed_three = out.normed_three[...]
+    gate, up, down = weight(W.gate), weight(W.up), weight(W.down)
+    for cols in tiles_of(gate.shape[1]):
+        gate_act = plain_dot(normed_three, gate[:, cols])
+        up_act = plain_dot(normed_three, up[:, cols])
+        own.gate_act[:, cols] = gate_act
+        own.up_act[:, cols] = up_act
+        curve = jnp.tanh(GELU_RATE * (gate_act + GELU_CUBE * gate_act * gate_act * gate_act))
+        out.hidden[:, cols] = (0.5 * gate_act * (1.0 + curve) * up_act).astype(BF16)
+    launch(out.hidden, far.hidden, far_send.at[1], far_recv.at[1], me ^ 1, core)
+    out.result[...] = (own.after_cross[...] + times(out.hidden[...], W.down)).astype(BF16)
+
+    branch_three = cotangent[...]
+    for cols in tiles_of(down.shape[0]):
+        hidden_grad = dot_nt(branch_three, down[cols, :])
+        gate_act, up_act = own.gate_act[:, cols], own.up_act[:, cols]
+        square = gate_act * gate_act
+        curve = jnp.tanh(GELU_RATE * (gate_act + GELU_CUBE * gate_act * square))
+        rise = 0.5 * (1.0 + curve) + 0.5 * gate_act * (1.0 - curve * curve) * (
+            GELU_RATE * (1.0 + 3.0 * GELU_CUBE * square)
+        )
+        out.gate_grad[:, cols] = (hidden_grad * up_act * rise).astype(BF16)
+        out.up_grad[:, cols] = (hidden_grad * (0.5 * gate_act * (1.0 + curve))).astype(BF16)
+    for at, mine in ((2, out.gate_grad), (3, out.up_grad)):
+        half = mine.shape[1] // 2
+        launch(
+            mine.at[:, pl.ds(pl.multiple_of((1 - y) * half, 128), half)],
+            far[at], far_send.at[at], far_recv.at[at], me ^ 2, core,
+        )
+    normed_grad = times_back(out.gate_grad[...], W.gate) + times_back(out.up_grad[...], W.up)
+    back, gain_three_grad = norm_backward(own.after_cross[...], gain_three, normed_grad)
+    out.resid_grad[...] = cotangent[...].astype(F32) + back
+    out.branch_two[...] = out.resid_grad[...].astype(BF16)
+
+    own.mix_grad[...] = times_back(out.branch_two[...], W.cross_out).astype(BF16)
+    for pair in range(peers // 2):
+        terms = []
+        for at in (2 * pair, 2 * pair + 1):
+            exact = own.cross_exact[at]
+            grads = own.mix_grad[:, head(at)]
+            score_grad = dot_nt(own.cross_values[:, head(at)], grads)
+            slope = jnp.sum(exact * score_grad, axis=0, keepdims=True)
+            rounded = (exact * (score_grad - slope)).astype(BF16)
+            terms.append(
+                (
+                    left_contract(rounded, own.cross_keys[:, head(at)]),
+                    plain_dot(rounded, own.cross_queries[:, head(at)]),
+                    plain_dot(exact.astype(BF16), grads),
+                )
+            )
+        cols = head_pair(pair)
+        values_cols = slice(width + cols.start, width + cols.stop)
+        for ref, into, at in ((out.cross_q_grad, cols, 0), (out.kv_part, cols, 1), (out.kv_part, values_cols, 2)):
+            ref[:, into] = jnp.concatenate([terms[0][at], terms[1][at]], axis=1).astype(BF16)
+    normed_grad = times_back(out.cross_q_grad[...], W.cross_query)
+    back, gain_two_grad = norm_backward(own.after_self[...], gain_two, normed_grad)
+    out.resid_grad[...] += back
+    out.branch_one[...] = out.resid_grad[...].astype(BF16)
+    out.dattn[...] = times_back(out.branch_one[...], W.out).astype(BF16)
+
+    for half in range(2):
+        for index in range(4):
+            cols = slice((4 * half + index) * 128, (4 * half + index + 1) * 128)
+            out.gain_grads[half, index : index + 1, :] = gain_two_grad[:, cols]
+            out.gain_grads[half, 4 + index : 5 + index, :] = gain_three_grad[:, cols]
+        out.gain_grads[half, 8:, :] = jnp.zeros((4, 128), F32)
+
+    other_half = pl.ds(pl.multiple_of((1 - core) * (width // 2), 128), width // 2)
+    for at in range(peers):
+        rows_at = own.encoder_all.shape[1]
+        remote(
+            own.encoder_all.at[at, :, other_half],
+            out.encoder_both.at[count + at * rows_at : count + (at + 1) * rows_at],
+            far_send.at[7], far_recv.at[7], me, 1 - core,
+        ).start()
+    arrived(out.encoder_both.at[count:], far_recv.at[7])
+    finish.append(
+        lambda: remote(
+            out.encoder_both.at[count:], out.encoder_both.at[count:], far_send.at[7], own_sem, me, 1 - core
+        ).wait_send()
+    )
+    for at, ref in enumerate(far):
+        arrived(ref, far_recv.at[at])
+    for at, ref in enumerate(lent):
+        arrived(ref, lent_recv.at[at])
+    for each in finish:
+        each()
+
+
+def layer(tokens_in, cotangent, encoder, small, table, in_bucket, held_at, order, sources):
+    peers = lax.axis_size("ctx")
+    tokens, width = tokens_in.shape
+    hidden = sources.gate.shape[1]
+    blocks = held_at.shape[0]
+    length = blocks * BLOCK
+    rows = encoder.shape[0] * peers
+    dma, vmem = pltpu.SemaphoreType.DMA, pltpu.VMEM
+
+    def shaped(*shape):
+        return jax.ShapeDtypeStruct(shape, BF16)
+
+    def exact(*shape):
+        return jax.ShapeDtypeStruct(shape, F32)
+
+    square, wide, half_wide = shaped(tokens, width), shaped(tokens, hidden), shaped(tokens, hidden // 2)
+    pairs, lone = (peers, 2 * BLOCK, 2 * HEAD_DIM), (peers, BLOCK, 2 * HEAD_DIM)
+    outputs = Made(
+        normed_one=square,
+        pairs=shaped(*pairs),
+        lone=shaped(*lone),
+        attn_sum=exact(HEAD_DIM, length),
+        log_norm=exact(1, length),
+        attended=square,
+        normed_two=square,
+        cross_mixed=square,
+        normed_three=square,
+        hidden=wide,
+        gate_grad=wide,
+        up_grad=wide,
+        branch_two=square,
+        cross_q_grad=square,
+        branch_one=square,
+        dattn=square,
+        kv_part=shaped(rows, 2 * width),
+        resid_grad=exact(tokens, width),
+        result=square,
+        gain_grads=exact(2, 12, 128),
+        gain_one=exact(1, width),
+        bias_lines=exact(length // TILE, 2 * TILE),
+        encoder_both=shaped(2 * rows, width // 2),
+    )
+    fars = Far(
+        normed_three=square, hidden=wide, gate=half_wide, up=half_wide, branch_three=shaped(tokens, width // 2)
+    )
+    buffers = Scratch(
+        small_far=vmem(small.shape, F32),
+        table_far=vmem(table.shape, F32),
+        pairs_out=vmem(pairs, BF16),
+        lone_out=vmem(lone, BF16),
+        encoder_all=vmem((peers,) + encoder.shape, BF16),
+        mixed_out=vmem(lone, BF16),
+        mixed_in=vmem(lone, BF16),
+        cross_keys=vmem((rows, width), BF16),
+        cross_values=vmem((rows, width), BF16),
+        cross_queries=vmem((tokens, width), BF16),
+        cross_exact=vmem((HEADS, rows, tokens), F32),
+        after_self=vmem((tokens, width), F32),
+        after_cross=vmem((tokens, width), F32),
+        gate_act=vmem((tokens, hidden), F32),
+        up_act=vmem((tokens, hidden), F32),
+        mix_grad=vmem((tokens, width), BF16),
+    )
+    smem_spec = pl.BlockSpec(memory_space=pltpu.SMEM)
+    results = pl.pallas_call(
+        layer_kernel,
+        out_shape=[*outputs, *fars, *(shaped(*sources[at].shape) for at in LENT)],
+        in_specs=[vmem_spec()] * 6 + [smem_spec] * 2 + [any_spec()] * len(W),
+        out_specs=[vmem_spec()] * len(outputs) + [any_spec()] * (len(fars) + len(LENT)),
+        scratch_shapes=[vmem((2 * each.shape[0], each.shape[1]), BF16) for each in sources]
+        + list(buffers)
+        + [
+            dma,
+            dma((len(W),)),
+            dma((len(W),)),
+            dma((len(W),)),
+            dma((len(LENT),)),
+            dma((len(LENT),)),
+            dma((8,)),
+            dma((8,)),
+            dma((4,)),
+            dma((4,)),
+            dma((4,)),
+        ],
+        compiler_params=pltpu.CompilerParams(
+            collective_id=1, has_side_effects=True, vmem_limit_bytes=62 * MIB
+        ),
+        name="layer",
+    )(tokens_in, cotangent, encoder, small, table, in_bucket, held_at, order, *sources)
+    made, results = results[: len(outputs)], results[len(outputs) :]
+    return Made(*made), Far(*results[: len(fars)]), results[len(fars) :]
+
+
 BIT_X, BIT_Y = 0, 1
 FAR_LEFTS, FAR_RIGHTS = 2, 3
-
-
-def pick(flag, when_set, when_clear):
-    return jnp.where(flag == 1, when_set, when_clear)
+SCHEDULE = (
+    1, 256, 17, 0, 4, 5, 16, 32, 33, 2, 257, 18, 21, 49, 34, 48, 65, 64, 3, 20,
+    50, 6, 36, 81, 258, 7, 37, 8, 22, 19, 35, 9, 80, 38, 23, 96, 39, 112, 51, 66,
+    24, 53, 25, 97, 67, 128, 40, 52, 82, 259, 54, 144, 98, 69, 68, 114, 55, 83, 56, 113,
+    130, 85, 41, 84, 146, 72, 71, 70, 101, 99, 160, 100, 115, 117, 86, 162, 102, 133, 116, 88,
+    178, 87, 194, 104, 129, 260, 118, 176, 57, 103, 120, 132, 119, 131, 73, 136, 147, 89, 135, 148,
+    134, 105, 150, 192, 166, 121, 182, 149, 145, 210, 137, 163, 198, 152, 151, 168, 179, 153, 167, 184,
+    161, 183, 164, 199, 208, 215, 195, 214, 180, 261, 200, 211, 231, 226, 165, 196, 181, 262, 212, 216,
+    224, 169, 232, 177, 185, 227, 228, 197, 201, 217, 240, 213, 229, 230, 233, 242, 243, 265, 263, 247,
+    193, 264, 209, 246, 225, 248, 244, 245, 241, 249,
+)
 
 
 UP, DOWN, ACROSS_Y, ACROSS_X = 0, 1, 2, 3
+LEFT, RIGHT, PIECE = 0, 1, 2
 
 
 class Product:
@@ -788,7 +1121,8 @@
         order,
         held_at,
         grad_rows,
-        landed,
+        pairs,
+        lone,
         attn_sum,
         log_norm,
         bias_lines,
@@ -797,7 +1131,7 @@
         gain_one,
         resid_grad,
         gains,
-    ) = take(12)
+    ) = take(13)
     weights = take(10)
     wholes, (vec_out, input_grad, encoder_grad, kv_both) = take(count - 1), take(4)
     kv_at = [product.left for product in products].index(SUMMED)
@@ -962,8 +1296,8 @@
             left = products[at].left
             if left not in seen and left != SUMMED:
                 seen.add(left)
-                owns["left", left] = send_left(left)
-            owns["right", at] = send_right(at)
+                owns[LEFT, left] = send_left(left)
+            owns[RIGHT, at] = send_right(at)
 
     def own_slots(key):
         ref, sem = owns[key]
@@ -1045,7 +1379,7 @@
             turned.add(left)
             arrived(slot(left_all[left], 2), left_recv.at[left, 2])
             arrived(slot(left_all[left], 3), left_recv.at[left, 3])
-            own_slots(("left", left))
+            own_slots((LEFT, left))
             height = left_t[left].shape[0]
 
             def turn(index, carry):
@@ -1056,7 +1390,7 @@
             lax.fori_loop(0, height // 128, turn, 0)
         arrived(slot(right_all[at], 2), right_recv.at[at, 1])
         arrived(slot(right_all[at], 3), right_recv.at[at, 2])
-        own_slots(("right", at))
+        own_slots((RIGHT, at))
         multiply(at, away[at], 1 - mine)
         launch(remote(away[at], came[at], pair_send.at[at], pair_recv.at[at], targets[way], core))
         left_here(away[at], pair_send.at[at])
@@ -1164,9 +1498,9 @@
     def gather_step(at, step):
         z_first, second, third = products[at].route
         if step == 0:
-            owns["piece", at] = local(own_piece(at), window(at, me), own_sem.at[at])
+            owns[PIECE, at] = local(own_piece(at), window(at, me), own_sem.at[at])
             if at != kv_at:
-                finish.append(owns["piece", at].wait)
+                finish.append(owns[PIECE, at].wait)
             if z_first:
                 send(at, me, UP, z, z < 3, own=True)
                 send(at, me, DOWN, z, z > 0, own=True)
@@ -1216,14 +1550,6 @@
                     for where in (place(zz, y, x), near(second, zz), near(third, zz), opposite(zz)):
                         send(at, where, way, 4 + zz, on)
 
-    def reduce_step(at, step):
-        if step == 0:
-            add_pair(at)
-        if step < 4:
-            line_step(at, step)
-        else:
-            gather_step(at, 0)
-
     def load_weight(index):
         return pltpu.make_async_copy(
             weights[index], weight_buffer.at[index % 2], weight_sem.at[index % 2]
@@ -1241,7 +1567,7 @@
             else:
                 columns[...] = term
         width = resid_in.shape[1]
-        cotan, values = normed_grad[...], resid_in[...]
+        cotan, values = normed_grad[...], resid_in[...].astype(F32)
         rate = lax.rsqrt(jnp.mean(values * values, axis=1, keepdims=True) + EPSILON)
         scaled = cotan * gain_one[...]
         slope = jnp.mean(scaled * values, axis=1, keepdims=True)
@@ -1278,95 +1604,55 @@
             columns = lanes(encoder_grad, core if side == 0 else 1 - core, width // 2)
             columns[...] = (terms[0] + terms[1]).astype(BF16)
 
-    early, late = range(count - 3), range(count - 3, count)
-    near_by = [at for at in early if at in far_rights]
-    others = [at for at in early if at not in far_rights]
-
-    def wave(some):
-        for time in range(len(some) + 4):
-            for step in range(5):
-                if 0 <= time - step < len(some):
-                    reduce_step(some[time - step], step)
-            yield
-
-    def gather_all(some, step):
-        for at in some:
-            gather_step(at, step)
-
-    def slots(of, number):
-        for _ in range(number):
-            next(of, None)
-
-    grad_arrival = to_all(0, grad_packed, grad_landed)
-    send_operands(near_by)
-    for at in near_by:
-        product_away(at)
-    grad_arrival()
-    attend_back(
-        order, held_at, landed, grad_landed, attn_sum, log_norm, bias_lines, back_packed, lines,
-        *attention_scratch,
-    )
-    back_arrival = to_all(1, back_packed, back_landed)
-    send_operands(others)
-    near_wave, other_wave, late_wave = wave(near_by), wave(others), wave(list(late))
-    slots(near_wave, 4)
-    back_arrival()
-    dq_ref, dk_ref, dv_ref = rights[count - 3 :]
-    for pair in range(peers // 2):
-        cols = slice(pair * 2 * HEAD_DIM, (pair + 1) * 2 * HEAD_DIM)
-        dq_ref[:, cols], dk_ref[:, cols] = unpack_pair(back_landed, pair, slice(0, 2 * BLOCK))
-        first, second = unpack_pair(back_landed, pair, slice(2 * BLOCK, 3 * BLOCK))
-        dv_ref[:BLOCK, cols] = first
-        dv_ref[BLOCK:, cols] = second
-    send_operands(late)
-    slots(near_wave, 4)
-    for index, at in enumerate(others):
-        pass_on(at)
-        if index:
-            product_away(others[index - 1])
-    product_away(others[-1])
-    gather_all(near_by, 1)
-    input_gradient()
-    gather_all(near_by, 2)
-    slots(other_wave, 2)
-    for at in late:
-        pass_on(at)
-    for at in late:
-        product_away(at)
-    vector_add(0)
-    gather_all(near_by, 3)
-    slots(other_wave, 3)
-    gather_all(near_by, 4)
-    vector_add(1)
-    slots(late_wave, 1)
-    slots(other_wave, 3)
-    slots(late_wave, 1)
-    gather_all(near_by, 5)
-    gather_all(others, 1)
-    slots(late_wave, 1)
-    vector_add(2)
-    gather_all(near_by, 6)
-    gather_all(others, 2)
-    slots(late_wave, 1)
-    vector_add(3)
-    slots(late_wave, 1)
-    gather_all(near_by, 7)
-    gather_all(others, 3)
-    slots(late_wave, 1)
-    slots(late_wave, 1)
-    vector_add(4)
-    gather_all(late, 1)
-    gather_all(others, 4)
-    gather_all(late, 2)
-    gather_all(others, 5)
-    gather_all(late, 3)
-    owns["piece", kv_at].wait()
-    launch(remote(kv_both.at[0], kv_both.at[1], kv_sem.at[0], kv_sem.at[1], me, 1 - core))
-    left_here(kv_both.at[0], kv_sem.at[0])
-    encoder_gradient()
-    for step in range(4, 9):
-        gather_all(late, step)
-    gather_all(near_by, 8)
+    later = {}
+
+    def grads_leave():
+        later[0] = to_all(0, grad_packed, grad_landed)
+
+    def attention():
+        later[0]()
+        attend_back(
+            order, held_at, pairs, lone, grad_landed, attn_sum, log_norm, bias_lines, back_packed, lines,
+            *attention_scratch,
+        )
+        later[1] = to_all(1, back_packed, back_landed)
+
+    def grads_return():
+        later[1]()
+        dq_ref, dk_ref, dv_ref = rights[count - 3 :]
+        for pair in range(peers // 2):
+            cols = slice(pair * 2 * HEAD_DIM, (pair + 1) * 2 * HEAD_DIM)
+            dq_ref[:, cols], dk_ref[:, cols] = unpack_pair(back_landed, pair, slice(0, 2 * BLOCK))
+            first, second = unpack_pair(back_landed, pair, slice(2 * BLOCK, 3 * BLOCK))
+            dv_ref[:BLOCK, cols] = first
+            dv_ref[BLOCK:, cols] = second
+
+    def kv_gathered():
+        owns[PIECE, kv_at].wait()
+        launch(remote(kv_both.at[0], kv_both.at[1], kv_sem.at[0], kv_sem.at[1], me, 1 - core))
+        left_here(kv_both.at[0], kv_sem.at[0])
+        encoder_gradient()
+
+    single = [grads_leave, attention, grads_return, input_gradient]
+    single += [functools.partial(vector_add, step) for step in range(5)] + [kv_gathered]
+    for code in SCHEDULE:
+        stage, at = divmod(code, 16)
+        if stage == 0:
+            send_operands([at])
+        elif stage == 1:
+            pass_on(at)
+        elif stage == 2:
+            product_away(at)
+        elif stage == 3:
+            add_pair(at)
+            line_step(at, 0)
+        elif stage < 7:
+            line_step(at, stage - 3)
+        elif stage < 16:
+            gather_step(at, stage - 7)
+        else:
+            single[at]()
+
     arrived(kv_both.at[1], kv_sem.at[1])
     for each in finish:
         each()
@@ -1375,7 +1661,7 @@
 def weight_grads(products, lefts, rights, left_far, right_far, others, weights):
     count, peers = len(products), lax.axis_size("ctx")
     tokens = lefts[0].shape[0]
-    length = others[4].shape[1]
+    length = others[5].shape[1]
     kv_at = [product.left for product in products].index(SUMMED)
     kv_rows, kv_width = rights[kv_at].shape
     spans = length // TILE
@@ -1487,195 +1773,81 @@
     up_weight,
     down_weight,
 ):
-    core, me = lax.axis_index("wsh"), lax.axis_index("ctx")
-
-    def swap(values):
-        return lax.ppermute(values, "wsh", [(0, 1), (1, 0)])
-
-    def along_x(values):
-        return lax.ppermute(values, "ctx", [(at, at ^ 1) for at in range(HEADS)])
-
-    def along_y(values):
-        return lax.ppermute(values, "ctx", [(at, at ^ 2) for at in range(HEADS)])
-
-    def other_column(values, bit):
-        half = values.shape[1] // 2
-        return pick(bit & 1, values[:, :half], values[:, half:])
-
-    def own_half(values):
-        half = values.shape[-1] // 2
-        return pick(core, values[..., half:], values[..., :half])
-
-    def other_half(values):
-        half = values.shape[-1] // 2
-        return pick(core, values[..., :half], values[..., half:])
-
-    def join(own, other, axis):
-        return pick(
-            core,
-            jnp.concatenate([other, own], axis=axis),
-            jnp.concatenate([own, other], axis=axis),
-        )
-
-    def times(values, pair):
-        return plain_dot(own_half(values), pair[0]) + plain_dot(other_half(values), pair[1])
-
-    def times_back(values, pair):
-        return join(right_contract(values, pair[0]), right_contract(values, pair[1]), 1)
-
-    def both_cores(values):
-        return jnp.concatenate([own_half(values), swap(other_half(values))], axis=0)
-
-    small = jnp.concatenate([self_gain, cross_gain, mlp_gain, bias_table.reshape(-1)])
-    small_other = swap(small)
-    width = self_gain.shape[0]
-    gain_one, gain_two, gain_three = (
-        join(small[at * width : (at + 1) * width], small_other[at * width : (at + 1) * width], 0).astype(F32)
-        for at in range(3)
-    )
-    bias_rows = join(bias_table, small_other[3 * width :].reshape(bias_table.shape), 0).astype(F32)
-    query_pair, key_pair, value_pair = (
-        (member, swap(member)) for member in (query_weight, key_weight, value_weight)
-    )
-    out_pair, cross_query_pair, cross_key_pair, cross_value_pair, cross_out_pair = (
-        (member, swap(member))
-        for member in (out_weight, cross_query, cross_key, cross_value, cross_out)
-    )
-    gate_pair, up_pair, down_pair = (
-        (member, swap(member)) for member in (gate_weight, up_weight, down_weight)
-    )
-
-    resid_in = inputs[0].astype(F32)
-    tokens = resid_in.shape[0]
-    head_width = HEADS * HEAD_DIM
-    length = bucket_of.shape[0]
-
-    normed_one = rms_norm(resid_in, gain_one).astype(BF16)
-    queries = times(normed_one, query_pair).astype(BF16)
-    keys = times(normed_one, key_pair).astype(BF16)
-    values = times(normed_one, value_pair).astype(BF16)
-    landed, encoder_all = to_heads(queries, keys, values, encoder[0])
-    encoder_all = encoder_all.reshape(-1, encoder.shape[2])
-
-    own_column = jnp.sum(
-        jnp.where(jnp.arange(HEADS)[None, :] == me, bias_rows, 0.0), axis=1, keepdims=True
-    )
-    in_bucket = bucket_of[None, :] == jnp.arange(BUCKETS, dtype=jnp.int32)[:, None]
-    by_offset = jnp.sum(jnp.where(in_bucket, own_column, 0.0), axis=0).reshape(-1, TILE)
-    before = jnp.concatenate([jnp.full((1, TILE), NEG_BIG, F32), by_offset[:-1]], axis=0)
-    bias_lines = jnp.concatenate([by_offset, before], axis=1)
-
-    mixed_packed, attn_sum, log_norm = attend(block_order, landed, bias_lines)
-    attended = from_heads(mixed_packed)
-
-    after_self = resid_in + times(attended, out_pair)
-    normed_two = rms_norm(after_self, gain_two).astype(BF16)
-    cross_q_heads = times(normed_two, cross_query_pair).astype(BF16).reshape(tokens, HEADS, HEAD_DIM)
-    cross_k_heads = times(encoder_all, cross_key_pair).astype(BF16).reshape(-1, HEADS, HEAD_DIM)
-    cross_v_heads = times(encoder_all, cross_value_pair).astype(BF16).reshape(-1, HEADS, HEAD_DIM)
-    cross_logits = jnp.einsum(
-        "qhe,khe->hqk", cross_q_heads, cross_k_heads, preferred_element_type=F32
-    )
-    cross_exact = jnp.exp(cross_logits - jax.nn.logsumexp(cross_logits, axis=-1, keepdims=True))
-    cross_probs = cross_exact.astype(BF16)
-    cross_mixed = (
-        jnp.einsum("hqk,khe->qhe", cross_probs, cross_v_heads, preferred_element_type=F32)
-        .reshape(tokens, head_width)
-        .astype(BF16)
-    )
-    after_cross = after_self + times(cross_mixed, cross_out_pair)
-    normed_three = rms_norm(after_cross, gain_three).astype(BF16)
-    gate_act = times(normed_three, gate_pair)
-    up_act = times(normed_three, up_pair)
-    hidden_float, mlp_pull = jax.vjp(gelu_product, gate_act, up_act)
-    hidden = hidden_float.astype(BF16)
-    result = (after_cross + times(hidden, down_pair)).astype(BF16)
-
-    resid_grad = cotangent[0].astype(F32)
-    branch_three = cotangent[0]
-    gate_grad, up_grad = mlp_pull(times_back(branch_three, down_pair))
-    gate_grad, up_grad = gate_grad.astype(BF16), up_grad.astype(BF16)
-    normed_three_grad = times_back(gate_grad, gate_pair) + times_back(up_grad, up_pair)
-    part_grad, gain_three_grad = norm_back(after_cross, gain_three, normed_three_grad)
-    after_cross_grad = resid_grad + part_grad
-    branch_two = after_cross_grad.astype(BF16)
-    mix_grad = times_back(branch_two, cross_out_pair).astype(BF16).reshape(tokens, HEADS, HEAD_DIM)
-    cross_score_grad = jnp.einsum(
-        "qhe,khe->hqk", mix_grad, cross_v_heads, preferred_element_type=F32
-    )
-    cross_delta = jnp.sum(cross_exact * cross_score_grad, axis=-1, keepdims=True)
-    cross_dlogits = (cross_exact * (cross_score_grad - cross_delta)).astype(BF16)
-    cross_q_grad = (
-        jnp.einsum("hqk,khe->qhe", cross_dlogits, cross_k_heads, preferred_element_type=F32)
-        .reshape(tokens, head_width)
-        .astype(BF16)
-    )
-    cross_k_part = jnp.einsum(
-        "hqk,qhe->khe", cross_dlogits, cross_q_heads, preferred_element_type=F32
-    ).reshape(-1, head_width)
-    cross_v_part = jnp.einsum(
-        "hqk,qhe->khe", cross_probs, mix_grad, preferred_element_type=F32
-    ).reshape(-1, head_width)
-    cross_kv_part = jnp.concatenate([cross_k_part, cross_v_part], axis=1).astype(BF16)
-    normed_two_grad = times_back(cross_q_grad, cross_query_pair)
-    part_grad, gain_two_grad = norm_back(after_self, gain_two, normed_two_grad)
-    after_self_grad = after_cross_grad + part_grad
-    branch_one = after_self_grad.astype(BF16)
-    dattn = times_back(branch_one, out_pair).astype(BF16)
-    block_ids = jnp.arange(block_order.shape[0], dtype=jnp.int32)
+    blocks = block_order.shape[0]
+    block_ids = jnp.arange(blocks, dtype=jnp.int32)
     held_at = jnp.sum(
         jnp.where(block_order[None, :] == block_ids[:, None], block_ids[None, :], 0), axis=1
     )
-    gains = jnp.concatenate(
-        [gain_two_grad.reshape(2, 4, 128), gain_three_grad.reshape(2, 4, 128), jnp.zeros((2, 4, 128), F32)],
-        axis=1,
-    )
-    bucket_tiles = in_bucket.astype(F32).reshape(BUCKETS, -1, TILE).transpose(1, 0, 2)
-
-    z_then_yx, z_then_xy, z_last = (
+    bucket_ids = jnp.arange(BUCKETS, dtype=jnp.int32)[None, :, None]
+    bucket_tiles = (bucket_of.reshape(-1, 1, TILE) == bucket_ids).astype(F32)
+    small = jnp.concatenate(
+        [jnp.stack([self_gain, cross_gain, mlp_gain]).astype(F32), jnp.zeros((5,) + self_gain.shape, F32)]
+    )
+    table = jnp.pad(bias_table.astype(F32), ((0, 0), (0, 128 - HEADS)))
+    sources = Weights(
+        query=query_weight,
+        key=key_weight,
+        value=value_weight,
+        out=out_weight,
+        cross_key=cross_key,
+        cross_value=cross_value,
+        cross_query=cross_query,
+        cross_out=cross_out,
+        gate=gate_weight,
+        up=up_weight,
+        down=down_weight,
+    )
+    made, far, lent = layer(
+        inputs[0], cotangent[0], encoder[0], small, table, bucket_tiles, held_at, block_order, sources
+    )
+
+    z_then_yx, z_then_xy, yx_then_z, xy_then_z = (
         (True, ACROSS_Y, ACROSS_X),
         (True, ACROSS_X, ACROSS_Y),
         (False, ACROSS_Y, ACROSS_X),
-    )
-    lefts = (normed_three, hidden, cross_mixed, normed_two, attended, normed_one)
+        (False, ACROSS_X, ACROSS_Y),
+    )
+    lefts = (
+        made.normed_three, made.hidden, made.cross_mixed, made.normed_two, made.attended, made.normed_one
+    )
     products = (
-        Product(0, gate_grad, BIT_Y, False, z_then_yx),
-        Product(1, branch_three, BIT_X, True, z_then_yx),
-        Product(0, up_grad, BIT_Y, False, z_then_xy),
-        Product(SUMMED, cross_kv_part, BIT_X, False, z_last),
-        Product(2, branch_two, BIT_X, False, z_last),
-        Product(3, cross_q_grad, BIT_Y, False, z_last),
-        Product(4, branch_one, BIT_Y, False, z_last),
+        Product(0, made.gate_grad, BIT_Y, False, z_then_xy),
+        Product(1, cotangent[0], BIT_X, True, xy_then_z),
+        Product(0, made.up_grad, BIT_Y, False, z_then_yx),
+        Product(SUMMED, made.kv_part, BIT_X, False, z_then_yx),
+        Product(2, made.branch_two, BIT_X, False, z_then_xy),
+        Product(3, made.cross_q_grad, BIT_Y, False, z_then_xy),
+        Product(4, made.branch_one, BIT_Y, False, z_then_yx),
+        Product(5, None, BIT_X, False, z_then_yx),
         Product(5, None, BIT_X, False, z_then_xy),
-        Product(5, None, BIT_X, False, z_then_xy),
-        Product(5, None, BIT_X, False, z_then_xy),
+        Product(5, None, BIT_X, False, z_then_yx),
     )
     *wholes, totals, input_grad, encoder_grad, cross_kv_both = weight_grads(
         products,
         lefts,
         [product.right for product in products[:7]],
-        (along_y(normed_three), along_x(hidden)),
-        (along_y(other_column(gate_grad, me >> 1)), along_x(other_column(branch_three, me)), along_y(other_column(up_grad, me >> 1))),
-        (
+        [far.normed_three, far.hidden],
+        [far.gate, far.branch_three, far.up],
+        [
             block_order,
             held_at,
-            dattn,
-            landed,
-            attn_sum,
-            log_norm,
-            bias_lines,
+            made.dattn,
+            made.pairs,
+            made.lone,
+            made.attn_sum,
+            made.log_norm,
+            made.bias_lines,
             bucket_tiles,
-            resid_in,
-            gain_one[None, :],
-            after_self_grad,
-            gains,
-        ),
-        [pair[0] for pair in (query_pair, key_pair, value_pair)]
-        + [pair[1] for pair in (query_pair, key_pair, value_pair)]
-        + [cross_key_pair[0], cross_value_pair[0], cross_key_pair[1], cross_value_pair[1]],
-    )
+            inputs[0],
+            made.gain_one,
+            made.resid_grad,
+            made.gain_grads,
+        ],
+        [query_weight, key_weight, value_weight, *lent[:3], cross_key, cross_value, *lent[3:]],
+    )
+    head_width = HEADS * HEAD_DIM
     cross_kv_w_grad = left_contract(
-        both_cores(encoder_all), cross_kv_both.reshape(-1, 2 * head_width)
+        made.encoder_both, cross_kv_both.reshape(-1, 2 * head_width)
     )
     (
         sum_gate,
@@ -1693,7 +1865,7 @@
     )
     sum_table = totals[16:, :HEADS]
     return (
-        result[None],
+        made.result[None],
         input_grad[None],
         encoder_grad[None],
         sum_gain_one,

time: 458 us -> 341 us (0.74)
  matrix products: 65.1 us -> 2.87 us
  Pallas kernels: 316 us -> 299 us
  other arithmetic: 35.1 us -> 22.4 us
  starting transfers between devices: 12.7 us -> 0 us
  waiting for transfers between devices: 5.37 us -> 0 us
    dot_general x40 -> x0, matrix products: 63.8 us -> none  [the longest x22 35.3 us: plain_dot(): return jnp.dot(left, right, preferred_element_type=jnp.float32)]
    pallas_call x1, Pallas kernels: 266 us -> 218 us  [weight_grads(): pl.pallas_call(functools.partial(weight_grad_kernel, products, len(lefts)...]
    pallas_call x3 -> x1, Pallas kernels: 49.9 us -> 80.7 us  [layer(): pl.pallas_call(layer_kernel, out_shape=[*outputs, *fars, *(shaped(*source...]
    ppermute x18 -> x0, starting transfers between devices: 12.7 us -> none  [the longest x3 5.06 us: along_y(): return lax.ppermute(values, 'ctx', [(at, at ^ 2) for at in range(HEADS)])]
    convert_element_type x12 -> x1, other arithmetic: 7.12 us -> 0.73 us  [on_device_by_heads(): bucket_tiles = (bucket_of.reshape(-1, 1, TILE) == bucket_ids).astype(F32)]
    ppermute x18 -> x0, waiting for transfers between devices: 5.37 us -> none  [the longest x3 5.33 us: along_y(): return lax.ppermute(values, 'ctx', [(at, at ^ 2) for at in range(HEADS)])]
  transfers between devices with their start and end apart: 18 -> 0, of which waited for: 1 -> 0; matrix products, arithmetic and copies ran while one was open for 21% -> 0% of each run, Pallas kernels for 70% -> 0%
where the time goes in v5:
time: 341 us; the launch traced here: 334 us
  Pallas kernels  299 us (88%)
  other arithmetic  22.4 us (7%)
  local copies, waits for them, and re-layouts  9.14 us (3%)
    pallas_call x1, Pallas kernels, weight_grads(): pl.pallas_call(functools.partial(weight_grad_kernel, products, len(lefts)...  218 us
    pallas_call x1, Pallas kernels, layer(): pl.pallas_call(layer_kernel, out_shape=[*outputs, *fars, *(shaped(*source...  80.7 us
    convert_element_type x9, other arithmetic, on_device_by_heads(): member.astype(F32)  18.5 us

profile of v5, /device:TPU:0, one launch (start us, length us, event | category | flops | bytes accessed | tf_op | source)
XLA Modules:
  0.0 334.5 jit_solution(5104448932206730977)
XLA Ops:
  0.7 0.7 eq.28
  1.4 0.7 fusion.in_bucket.refs_26_
  2.1 1.3 select_reduce_fusion.held_at.refs_19_
  3.4 0.7 stack.12
  4.0 0.7 stack.13
  4.7 0.7 stack.14
  5.4 0.6 fusion.6.small
  6.0 1.3 pad_convert_fusion.table
  7.3 80.7 %layer.1 = (bf16[128,1024]{1,0:T(8,128)(2,1)}, bf16[16,128,128]{2,1,0:T(8,128)(2,1)}, bf16[16,64,128]{2,1,0:T(8,128)(2,1)}, f32[64,2048]{1,0:T(8,128)}, f32[1,20...) custom-call(bf16[128,1024]{1,0:T(8,128)(2,1)} %bitcast.16, ...), custom_call_target="tpu_custom_call" | custom-call | tf_op jit(solution)/shard_map/layer/pallas_call | solution.py:1053
  88.0 0.0 copy-start.9
  88.0 218.5 %weight_grads.1 = (bf16[512,2816]{1,0:T(8,128)(2,1)}, bf16[1408,1024]{1,0:T(8,128)(2,1)}, bf16[512,2816]{1,0:T(8,128)(2,1)}, bf16[512,1024]{1,0:T(8,128)(2,1)}, ...) custom-call(bf16[128,1024]{1,0:T(8,128)(2,1)} %get-tuple-element.65., ...), custom_call_target="tpu_custom_call" | custom-call | tf_op jit(solution)/shard_map/weight_grads/pallas_call | solution.py:1681
  306.5 0.0 copy-done.9
  306.5 2.9 fusion.8
  309.3 0.0 copy-start.2
  309.4 2.4 fusion.7
  311.7 0.8 copy-done.2
  312.5 0.0 copy-start.1
  312.5 2.9 convert_element_type.41
  315.4 0.0 copy-done.1
  315.4 0.0 copy-start
  315.4 2.9 convert_element_type.42
  318.4 0.0 copy-done
  318.4 0.0 copy-start.8
  318.4 3.2 convert_element_type.43
  321.6 0.0 copy-start.7
  321.6 0.0 copy-done.8
  321.6 1.6 convert_element_type.35
  323.2 0.0 copy-start.6
  323.2 0.0 copy-done.7
  323.2 1.6 convert_element_type.36
  324.8 0.0 copy-done.6
  324.8 1.6 convert_element_type.37
  326.4 0.0 copy-done.5
  326.4 1.6 convert_element_type.38
  327.9 0.0 copy-done.4
  327.9 1.6 convert_element_type.39
  329.5 0.0 copy-done.3
  329.5 0.0 copy-start.12
  329.5 1.6 convert_element_type.40
  331.1 0.0 copy-done.13
  331.1 0.6 slice.19
  331.7 0.6 slice_bitcast_fusion
  332.3 0.0 copy-done.10
  332.3 0.7 copy.41
  333.0 0.0 copy-done.11
  333.0 0.7 copy.42
  333.7 0.0 copy-done.12
  333.7 0.6 copy.43
  (6 shorter events, 0.0 us)
Async XLA Ops:
  88.0 218.5 %copy-start.9 = (bf16[512,512]{1,0:T(8,128)(2,1)S(1)}, bf16[512,512]{1,0:T(8,128)(2,1)}, u32[]{:S(2)}) copy-start(bf16[512,512]{1,0:T(8,128)(2,1)} %get-tuple-element.104) | copy-start | bytes 1572868
  309.3 3.1 copy-start.2
  312.5 2.9 copy-start.1
  315.4 2.9 copy-start
  318.4 3.3 copy-start.8
  321.6 1.6 copy-start.7
  323.2 1.6 copy-start.6
  324.8 1.6 copy-start.5
  326.4 1.6 copy-start.4
  327.9 1.6 copy-start.3
  329.5 1.6 copy-start.13
  329.5 2.8 copy-start.10
  329.5 3.5 %copy-start.11 = (bf16[128,1024]{1,0:T(8,128)(2,1)S(1)}, bf16[128,1024]{1,0:T(8,128)(2,1)}, u32[]{:S(2)}) copy-start(bf16[128,1024]{1,0:T(8,128)(2,1)} %get-tuple-element.96) | copy-start | bytes 786436
  329.5 4.2 %copy-start.12 = (bf16[16,1024]{1,0:T(8,128)(2,1)S(1)}, bf16[16,1024]{1,0:T(8,128)(2,1)}, u32[]{:S(2)}) copy-start(bf16[16,1024]{1,0:T(8,128)(2,1)} %get-tuple-element.97) | copy-start | bytes 98308

commit v6 on v5

--- a/solution.py
+++ b/solution.py
@@ -673,9 +673,30 @@
 class Far(NamedTuple):
     normed_three: Any
     hidden: Any
+    cross_mixed: Any
+    normed_two: Any
+    attended: Any
+    normed_one: Any
     gate: Any
+    branch_three: Any
     up: Any
-    branch_three: Any
+    branch_two: Any
+
+
+BIT_X, BIT_Y = 0, 1
+FAR = Far(*range(10))
+FAR_AXIS = Far(
+    normed_three=BIT_Y,
+    hidden=BIT_X,
+    cross_mixed=BIT_X,
+    normed_two=BIT_X,
+    attended=BIT_Y,
+    normed_one=BIT_X,
+    gate=BIT_Y,
+    branch_three=BIT_X,
+    up=BIT_Y,
+    branch_two=BIT_X,
+)
 
 
 class Scratch(NamedTuple):
@@ -760,14 +781,22 @@
         remote(src, dst, send_sem, recv_sem, ctx, side).start()
         finish.append(lambda: remote(src, src, send_sem, own_sem, me, 1 - core).wait_send())
 
+    def to_pair(at, source, halves=False):
+        bit = FAR_AXIS[at]
+        if halves:
+            half = source.shape[1] // 2
+            source = source.at[:, pl.ds(pl.multiple_of((1 - (x, y)[bit]) * half, 128), half)]
+        launch(source, far[at], far_send.at[at], far_recv.at[at], me ^ (1 << bit), core)
+
+    small_sem, table_sem, encoder_sem = (len(Far._fields) + at for at in range(3))
     local = {}
     for at in W:
         local[at] = pltpu.make_async_copy(sources[at], half_rows(weights[at], core), weight_own.at[at])
         local[at].start()
     pl.semaphore_wait(barrier, peers)
 
-    launch(small, own.small_far, far_send.at[5], far_recv.at[5], me, 1 - core)
-    launch(table, own.table_far, far_send.at[6], far_recv.at[6], me, 1 - core)
+    launch(small, own.small_far, far_send.at[small_sem], far_recv.at[small_sem], me, 1 - core)
+    launch(table, own.table_far, far_send.at[table_sem], far_recv.at[table_sem], me, 1 - core)
     for at in W:
         launch(sources[at], half_rows(weights[at], core), weight_send.at[at], weight_recv.at[at], me, 1 - core)
     for at, source in enumerate(LENT):
@@ -812,8 +841,8 @@
     def head_pair(at):
         return slice(2 * at * HEAD_DIM, 2 * (at + 1) * HEAD_DIM)
 
-    arrived(own.small_far, far_recv.at[5])
-    arrived(own.table_far, far_recv.at[6])
+    arrived(own.small_far, far_recv.at[small_sem])
+    arrived(own.table_far, far_recv.at[table_sem])
 
     def both(mine, others, axis):
         first = jnp.where(core == 0, mine, others)
@@ -850,10 +879,8 @@
         )
     lone_arrival = to_all(1, own.lone_out, out.lone)
     encoder_arrival = to_all(2, encoder, own.encoder_all, spread=False)
-    launch(
-        cotangent.at[:, pl.ds(pl.multiple_of((1 - x) * (width // 2), 128), width // 2)],
-        far.branch_three, far_send.at[4], far_recv.at[4], me ^ 1, core,
-    )
+    to_pair(FAR.branch_three, cotangent, halves=True)
+    to_pair(FAR.normed_one, out.normed_one)
     place_bias = out.bias_lines
     pairs_arrival()
     lone_arrival()
@@ -878,9 +905,11 @@
         first, second = unpack_pair(own.mixed_in, pair, slice(0, BLOCK))
         out.attended[:BLOCK, head_pair(pair)] = first
         out.attended[BLOCK:, head_pair(pair)] = second
+    to_pair(FAR.attended, out.attended)
     own.after_self[...] = tokens_in[...].astype(F32) + times(out.attended[...], W.out)
     after_self = own.after_self[...]
     out.normed_two[...] = (after_self * norm_parts(after_self) * gain_two).astype(BF16)
+    to_pair(FAR.normed_two, out.normed_two)
     own.cross_queries[...] = times(out.normed_two[...], W.cross_query).astype(BF16)
 
     for pair in range(peers // 2):
@@ -892,10 +921,11 @@
             own.cross_exact[at] = exact
             mixed.append(left_contract(exact.astype(BF16), own.cross_values[:, head(at)]))
         out.cross_mixed[:, head_pair(pair)] = jnp.concatenate(mixed, axis=1).astype(BF16)
+    to_pair(FAR.cross_mixed, out.cross_mixed)
     own.after_cross[...] = own.after_self[...] + times(out.cross_mixed[...], W.cross_out)
     after_cross = own.after_cross[...]
     out.normed_three[...] = (after_cross * norm_parts(after_cross) * gain_three).astype(BF16)
-    launch(out.normed_three, far.normed_three, far_send.at[0], far_recv.at[0], me ^ 2, core)
+    to_pair(FAR.normed_three, out.normed_three)
 
     normed_three = out.normed_three[...]
     gate, up, down = weight(W.gate), weight(W.up), weight(W.down)
@@ -906,31 +936,33 @@
         own.up_act[:, cols] = up_act
         curve = jnp.tanh(GELU_RATE * (gate_act + GELU_CUBE * gate_act * gate_act * gate_act))
         out.hidden[:, cols] = (0.5 * gate_act * (1.0 + curve) * up_act).astype(BF16)
-    launch(out.hidden, far.hidden, far_send.at[1], far_recv.at[1], me ^ 1, core)
+    to_pair(FAR.hidden, out.hidden)
     out.result[...] = (own.after_cross[...] + times(out.hidden[...], W.down)).astype(BF16)
 
     branch_three = cotangent[...]
-    for cols in tiles_of(down.shape[0]):
-        hidden_grad = dot_nt(branch_three, down[cols, :])
-        gate_act, up_act = own.gate_act[:, cols], own.up_act[:, cols]
-        square = gate_act * gate_act
-        curve = jnp.tanh(GELU_RATE * (gate_act + GELU_CUBE * gate_act * square))
-        rise = 0.5 * (1.0 + curve) + 0.5 * gate_act * (1.0 - curve * curve) * (
-            GELU_RATE * (1.0 + 3.0 * GELU_CUBE * square)
-        )
-        out.gate_grad[:, cols] = (hidden_grad * up_act * rise).astype(BF16)
-        out.up_grad[:, cols] = (hidden_grad * (0.5 * gate_act * (1.0 + curve))).astype(BF16)
-    for at, mine in ((2, out.gate_grad), (3, out.up_grad)):
-        half = mine.shape[1] // 2
-        launch(
-            mine.at[:, pl.ds(pl.multiple_of((1 - y) * half, 128), half)],
-            far[at], far_send.at[at], far_recv.at[at], me ^ 2, core,
-        )
+    half = down.shape[0] // 2
+    for side in (1 - y, y):
+        for start in range(0, half, 256):
+            size = min(256, half - start)
+            cols = pl.ds(pl.multiple_of(side * half + start, 128), size)
+            hidden_grad = dot_nt(branch_three, down[pl.ds(pl.multiple_of(side * half + start, 128), size), :])
+            gate_act, up_act = own.gate_act[:, cols], own.up_act[:, cols]
+            square = gate_act * gate_act
+            curve = jnp.tanh(GELU_RATE * (gate_act + GELU_CUBE * gate_act * square))
+            rise = 0.5 * (1.0 + curve) + 0.5 * gate_act * (1.0 - curve * curve) * (
+                GELU_RATE * (1.0 + 3.0 * GELU_CUBE * square)
+            )
+            out.gate_grad[:, cols] = (hidden_grad * up_act * rise).astype(BF16)
+            out.up_grad[:, cols] = (hidden_grad * (0.5 * gate_act * (1.0 + curve))).astype(BF16)
+        if side is not y:
+            to_pair(FAR.gate, out.gate_grad, halves=True)
+            to_pair(FAR.up, out.up_grad, halves=True)
     normed_grad = times_back(out.gate_grad[...], W.gate) + times_back(out.up_grad[...], W.up)
     back, gain_three_grad = norm_backward(own.after_cross[...], gain_three, normed_grad)
     out.resid_grad[...] = cotangent[...].astype(F32) + back
     out.branch_two[...] = out.resid_grad[...].astype(BF16)
 
+    to_pair(FAR.branch_two, out.branch_two, halves=True)
     own.mix_grad[...] = times_back(out.branch_two[...], W.cross_out).astype(BF16)
     for pair in range(peers // 2):
         terms = []
@@ -970,12 +1002,12 @@
         remote(
             own.encoder_all.at[at, :, other_half],
             out.encoder_both.at[count + at * rows_at : count + (at + 1) * rows_at],
-            far_send.at[7], far_recv.at[7], me, 1 - core,
+            far_send.at[encoder_sem], far_recv.at[encoder_sem], me, 1 - core,
         ).start()
-    arrived(out.encoder_both.at[count:], far_recv.at[7])
+    arrived(out.encoder_both.at[count:], far_recv.at[encoder_sem])
     finish.append(
         lambda: remote(
-            out.encoder_both.at[count:], out.encoder_both.at[count:], far_send.at[7], own_sem, me, 1 - core
+            out.encoder_both.at[count:], out.encoder_both.at[count:], far_send.at[encoder_sem], own_sem, me, 1 - core
         ).wait_send()
     )
     for at, ref in enumerate(far):
@@ -1028,8 +1060,18 @@
         bias_lines=exact(length // TILE, 2 * TILE),
         encoder_both=shaped(2 * rows, width // 2),
     )
+    half_square = shaped(tokens, width // 2)
     fars = Far(
-        normed_three=square, hidden=wide, gate=half_wide, up=half_wide, branch_three=shaped(tokens, width // 2)
+        normed_three=square,
+        hidden=wide,
+        cross_mixed=square,
+        normed_two=square,
+        attended=square,
+        normed_one=square,
+        gate=half_wide,
+        branch_three=half_square,
+        up=half_wide,
+        branch_two=half_square,
     )
     buffers = Scratch(
         small_far=vmem(small.shape, F32),
@@ -1064,8 +1106,8 @@
             dma((len(W),)),
             dma((len(LENT),)),
             dma((len(LENT),)),
-            dma((8,)),
-            dma((8,)),
+            dma((len(fars) + 3,)),
+            dma((len(fars) + 3,)),
             dma((4,)),
             dma((4,)),
             dma((4,)),
@@ -1079,18 +1121,17 @@
     return Made(*made), Far(*results[: len(fars)]), results[len(fars) :]
 
 
-BIT_X, BIT_Y = 0, 1
-FAR_LEFTS, FAR_RIGHTS = 2, 3
+FAR_LEFTS, FAR_RIGHTS = 6, (0, 1, 2, 4)
 SCHEDULE = (
-    1, 256, 17, 0, 4, 5, 16, 32, 33, 2, 257, 18, 21, 49, 34, 48, 65, 64, 3, 20,
-    50, 6, 36, 81, 258, 7, 37, 8, 22, 19, 35, 9, 80, 38, 23, 96, 39, 112, 51, 66,
-    24, 53, 25, 97, 67, 128, 40, 52, 82, 259, 54, 144, 98, 69, 68, 114, 55, 83, 56, 113,
-    130, 85, 41, 84, 146, 72, 71, 70, 101, 99, 160, 100, 115, 117, 86, 162, 102, 133, 116, 88,
-    178, 87, 194, 104, 129, 260, 118, 176, 57, 103, 120, 132, 119, 131, 73, 136, 147, 89, 135, 148,
-    134, 105, 150, 192, 166, 121, 182, 149, 145, 210, 137, 163, 198, 152, 151, 168, 179, 153, 167, 184,
-    161, 183, 164, 199, 208, 215, 195, 214, 180, 261, 200, 211, 231, 226, 165, 196, 181, 262, 212, 216,
-    224, 169, 232, 177, 185, 227, 228, 197, 201, 217, 240, 213, 229, 230, 233, 242, 243, 265, 263, 247,
-    193, 264, 209, 246, 225, 248, 244, 245, 241, 249,
+    0, 256, 5, 16, 32, 3, 2, 257, 1, 6, 18, 4, 48, 34, 21, 17, 19, 37, 22, 33,
+    20, 64, 38, 53, 35, 80, 69, 50, 96, 112, 258, 66, 7, 36, 49, 8, 128, 51, 65, 144,
+    23, 67, 82, 52, 160, 39, 81, 24, 259, 98, 68, 97, 113, 54, 40, 84, 9, 83, 55, 85,
+    114, 70, 129, 71, 99, 101, 117, 115, 176, 25, 145, 87, 133, 56, 260, 86, 100, 161, 192, 72,
+    103, 116, 131, 102, 118, 41, 119, 130, 134, 146, 147, 57, 88, 73, 149, 104, 163, 150, 165, 162,
+    89, 179, 132, 135, 178, 194, 105, 177, 195, 166, 193, 121, 120, 148, 151, 137, 210, 136, 211, 153,
+    261, 169, 185, 167, 209, 226, 164, 208, 182, 224, 152, 181, 180, 201, 227, 262, 197, 183, 198, 217,
+    196, 225, 212, 168, 199, 233, 263, 243, 214, 228, 265, 213, 229, 230, 184, 240, 200, 264, 249, 215,
+    241, 245, 216, 231, 247, 242, 244, 232, 248, 246,
 )
 
 
@@ -1116,7 +1157,7 @@
         return taken
 
     lefts, rights = take(left_count), take(count - 3)
-    left_far, right_far = take(FAR_LEFTS), take(FAR_RIGHTS)
+    left_far, right_far = take(FAR_LEFTS), take(len(FAR_RIGHTS))
     (
         order,
         held_at,
@@ -1136,7 +1177,7 @@
     wholes, (vec_out, input_grad, encoder_grad, kv_both) = take(count - 1), take(4)
     kv_at = [product.left for product in products].index(SUMMED)
     wholes.insert(kv_at, kv_both.at[0])
-    left_all, left_pass, left_t = take(left_count), take(left_count), take(left_count)
+    left_all, left_t = take(left_count), take(left_count)
     right_all, away, came, held, line_in = (take(count) for _ in range(5))
     rights += take(3)
     grad_packed, grad_landed, back_packed, back_landed, lines = take(5)
@@ -1229,7 +1270,6 @@
         return (along_x, along_y) if product.first == BIT_X else (along_y, along_x)
 
     left_axis = {product.left: product for product in products}
-    far_rights = [at for at in range(count) if 0 <= products[at].left < FAR_LEFTS]
 
     def local(src, dst, sem):
         copy = pltpu.make_async_copy(src, dst, sem)
@@ -1237,22 +1277,12 @@
         return copy
 
     def send_left(at):
-        (_, way), _ = axes(left_axis[at])
         half = left_all[at].shape[1]
-        send_sem, recv_sem = left_send.at[at], left_recv.at[at]
-        mine, others = lanes(lefts[at], core, half), lanes(lefts[at], 1 - core, half)
-        copies = [local(mine, slot(left_all[at], 0), left_own.at[at])]
-        launch(remote(others, slot(left_all[at], 2), send_sem, recv_sem.at[2], me, 1 - core))
-        if at < FAR_LEFTS:
-            far_mine, far_others = lanes(left_far[at], core, half), lanes(left_far[at], 1 - core, half)
-            copies.append(local(far_mine, slot(left_all[at], 1), left_own.at[at]))
-            launch(remote(far_others, slot(left_all[at], 3), send_sem, recv_sem.at[3], me, 1 - core))
-            left_here(left_all[at].at[: 2 * tokens], send_sem)
-        else:
-            launch(remote(mine, slot(left_all[at], 1), send_sem, recv_sem.at[0], targets[way], core))
-            launch(remote(others, left_pass[at], send_sem, recv_sem.at[1], targets[way], core))
-            left_here(left_all[at], send_sem)
-        return left_all[at].at[: len(copies) * tokens], left_own.at[at]
+        for index, ref in enumerate((lefts[at], left_far[at])):
+            local(lanes(ref, core, half), slot(left_all[at], index), left_own.at[at])
+            launch(remote(lanes(ref, 1 - core, half), slot(left_all[at], 2 + index), left_send.at[at], left_recv.at[at], me, 1 - core))
+        left_here(left_all[at].at[: 2 * tokens], left_send.at[at])
+        return left_all[at].at[: 2 * tokens], left_own.at[at]
 
     def send_right(at):
         (mine, way), _ = axes(products[at])
@@ -1265,8 +1295,8 @@
             return None
         copies = [local(own, slot(right_all[at], 0), right_own.at[at])]
         launch(remote(own, slot(right_all[at], 2), send_sem, recv_sem.at[1], me, 1 - core))
-        if at in far_rights:
-            far = right_far[far_rights.index(at)]
+        if at in FAR_RIGHTS:
+            far = right_far[FAR_RIGHTS.index(at)]
             copies.append(local(far, slot(right_all[at], 1), right_own.at[at]))
             launch(remote(far, slot(right_all[at], 3), send_sem, recv_sem.at[2], me, 1 - core))
             left_here(right_all[at].at[: 2 * tokens], send_sem)
@@ -1320,17 +1350,9 @@
         else:
             vec_out[...] = total
 
-    passed = set()
-
     def pass_on(at):
-        left = products[at].left
-        if left == SUMMED or at in far_rights:
+        if products[at].left == SUMMED or at in FAR_RIGHTS:
             return
-        if left not in passed:
-            passed.add(left)
-            arrived(slot(left_all[left], 1), left_recv.at[left, 0])
-            arrived(left_pass[left], left_recv.at[left, 1])
-            launch(remote(left_pass[left], slot(left_all[left], 3), left_send.at[left], left_recv.at[left, 3], me, 1 - core))
         arrived(slot(right_all[at], 1), right_recv.at[at, 0])
         launch(remote(slot(right_all[at], 1), slot(right_all[at], 3), right_send.at[at], right_recv.at[at, 2], me, 1 - core))
 
@@ -1377,8 +1399,7 @@
             return
         if left not in turned:
             turned.add(left)
-            arrived(slot(left_all[left], 2), left_recv.at[left, 2])
-            arrived(slot(left_all[left], 3), left_recv.at[left, 3])
+            arrived(left_all[left].at[2 * tokens :], left_recv.at[left])
             own_slots((LEFT, left))
             height = left_t[left].shape[0]
 
@@ -1699,7 +1720,6 @@
         + [any_spec()] * len(weights),
         out_specs=[any_spec()] * (count - 1) + [vmem_spec()] * 4,
         scratch_shapes=[vmem((4 * tokens, half), BF16) for half in halves]
-        + [vmem((tokens, half), BF16) for half in halves]
         + [vmem((half, 4 * tokens), BF16) for half in halves]
         + [
             vmem((kv_rows if product.left == SUMMED else 4 * tokens, right // 2), BF16)
@@ -1725,7 +1745,7 @@
         + [
             dma((len(lefts),)),
             dma((len(lefts),)),
-            dma((len(lefts), 4)),
+            dma((len(lefts),)),
             dma((count,)),
             dma((count,)),
             dma((count, 3)),
@@ -1780,9 +1800,10 @@
     )
     bucket_ids = jnp.arange(BUCKETS, dtype=jnp.int32)[None, :, None]
     bucket_tiles = (bucket_of.reshape(-1, 1, TILE) == bucket_ids).astype(F32)
-    small = jnp.concatenate(
-        [jnp.stack([self_gain, cross_gain, mlp_gain]).astype(F32), jnp.zeros((5,) + self_gain.shape, F32)]
-    )
+    row = jnp.arange(8, dtype=jnp.int32)[:, None]
+    small = jnp.where(
+        row == 0, self_gain[None], jnp.where(row == 1, cross_gain[None], mlp_gain[None])
+    ).astype(F32)
     table = jnp.pad(bias_table.astype(F32), ((0, 0), (0, 128 - HEADS)))
     sources = Weights(
         query=query_weight,
@@ -1811,23 +1832,23 @@
         made.normed_three, made.hidden, made.cross_mixed, made.normed_two, made.attended, made.normed_one
     )
     products = (
-        Product(0, made.gate_grad, BIT_Y, False, z_then_xy),
-        Product(1, cotangent[0], BIT_X, True, xy_then_z),
-        Product(0, made.up_grad, BIT_Y, False, z_then_yx),
-        Product(SUMMED, made.kv_part, BIT_X, False, z_then_yx),
+        Product(0, made.gate_grad, BIT_Y, False, z_then_yx),
+        Product(1, cotangent[0], BIT_X, True, z_then_yx),
+        Product(0, made.up_grad, BIT_Y, False, z_then_xy),
+        Product(SUMMED, made.kv_part, BIT_Y, False, yx_then_z),
         Product(2, made.branch_two, BIT_X, False, z_then_xy),
-        Product(3, made.cross_q_grad, BIT_Y, False, z_then_xy),
-        Product(4, made.branch_one, BIT_Y, False, z_then_yx),
-        Product(5, None, BIT_X, False, z_then_yx),
-        Product(5, None, BIT_X, False, z_then_xy),
+        Product(3, made.cross_q_grad, BIT_X, False, z_then_xy),
+        Product(4, made.branch_one, BIT_Y, False, z_then_xy),
+        Product(5, None, BIT_X, False, yx_then_z),
+        Product(5, None, BIT_X, False, yx_then_z),
         Product(5, None, BIT_X, False, z_then_yx),
     )
     *wholes, totals, input_grad, encoder_grad, cross_kv_both = weight_grads(
         products,
         lefts,
         [product.right for product in products[:7]],
-        [far.normed_three, far.hidden],
-        [far.gate, far.branch_three, far.up],
+        far[:FAR_LEFTS],
+        far[FAR_LEFTS:],
         [
             block_order,
             held_at,
@@ -1846,9 +1867,9 @@
         [query_weight, key_weight, value_weight, *lent[:3], cross_key, cross_value, *lent[3:]],
     )
     head_width = HEADS * HEAD_DIM
-    cross_kv_w_grad = left_contract(
-        made.encoder_both, cross_kv_both.reshape(-1, 2 * head_width)
-    )
+    cross_kv_rows = cross_kv_both.reshape(-1, 2 * head_width)
+    sum_cross_key = left_contract(made.encoder_both, cross_kv_rows[:, :head_width])
+    sum_cross_value = left_contract(made.encoder_both, cross_kv_rows[:, head_width:])
     (
         sum_gate,
         sum_down,
@@ -1876,8 +1897,8 @@
         sum_table,
         sum_gain_two,
         sum_cross_query,
-        cross_kv_w_grad[:, :head_width],
-        cross_kv_w_grad[:, head_width:],
+        sum_cross_key,
+        sum_cross_value,
         sum_cross_out,
         sum_gain_three,
         sum_gate,

time: 341 us -> 324 us (0.950)
  Pallas kernels: 299 us -> 284 us
  local copies, waits for them, and re-layouts: 9.14 us -> 4.04 us
    pallas_call x1, Pallas kernels: 218 us -> 197 us  [weight_grads(): pl.pallas_call(functools.partial(weight_grad_kernel, products, len(lefts)...]
    pallas_call x1, Pallas kernels: 80.7 us -> 86.7 us  [layer(): pl.pallas_call(layer_kernel, out_shape=[*outputs, *fars, *(shaped(*source...]
where the time goes in v6:
time: 324 us; the launch traced here: 318 us
  Pallas kernels  284 us (88%)
  other arithmetic  23.2 us (7%)
  matrix products  5.46 us (2%)
  local copies, waits for them, and re-layouts  4.04 us (1%)
    pallas_call x1, Pallas kernels, weight_grads(): pl.pallas_call(functools.partial(weight_grad_kernel, products, len(lefts)...  197 us
    pallas_call x1, Pallas kernels, layer(): pl.pallas_call(layer_kernel, out_shape=[*outputs, *fars, *(shaped(*source...  86.7 us
    convert_element_type x9, other arithmetic, on_device_by_heads(): member.astype(F32)  18.5 us

profile of v6, /device:TPU:0, one launch (start us, length us, event | category | flops | bytes accessed | tf_op | source)
XLA Modules:
  0.0 317.7 jit_solution(447715432793239689)
XLA Ops:
  0.7 1.4 select_convert_fusion.small
  2.1 0.7 eq.46
  2.8 0.7 fusion.4.in_bucket.refs_31_
  3.5 1.3 select_reduce_fusion.held_at.refs_24_
  4.8 1.3 pad_convert_fusion.table
  6.1 86.7 %layer.1 = (bf16[128,1024]{1,0:T(8,128)(2,1)}, bf16[16,128,128]{2,1,0:T(8,128)(2,1)}, bf16[16,64,128]{2,1,0:T(8,128)(2,1)}, f32[64,2048]{1,0:T(8,128)}, f32[1,20...) custom-call(bf16[128,1024]{1,0:T(8,128)(2,1)} %bitcast.17, ...), custom_call_target="tpu_custom_call" | custom-call | tf_op jit(solution)/shard_map/layer/pallas_call | solution.py:1095
  92.8 0.0 copy-start.4
  92.8 197.4 %weight_grads.1 = (bf16[512,2816]{1,0:T(8,128)(2,1)}, bf16[1408,1024]{1,0:T(8,128)(2,1)}, bf16[512,2816]{1,0:T(8,128)(2,1)}, bf16[512,1024]{1,0:T(8,128)(2,1)}, ...) custom-call(bf16[128,1024]{1,0:T(8,128)(2,1)} %get-tuple-element.70., ...), custom_call_target="tpu_custom_call" | custom-call | tf_op jit(solution)/shard_map/weight_grads/pallas_call | solution.py:1702
  290.2 0.0 copy-start.3
  290.2 0.0 copy-done.4
  290.2 3.4 %fusion = f32[512,1024]{1,0:T(8,128)} fusion(bf16[512,512]{1,0:T(8,128)(2,1)S(1)} %copy-done.4, bf16[512,2048]{1,0:T(8,128)(2,1)} %bitcast.15), kind=kOutput, calls=%fused_computation | convolution fusion | flops 536870912 | bytes 3670016 | tf_op jit(solution)/shard_map/dot_general | solution.py:29
  293.6 0.0 copy-done.3
  293.6 2.0 fusion.2
  295.7 0.1 copy-done.2
  295.7 0.0 copy-start.1
  295.8 2.9 convert_element_type.44
  298.7 0.0 copy-done.1
  298.7 0.0 copy-start
  298.7 2.9 convert_element_type.45
  301.6 0.0 copy-done
  301.6 0.0 copy-start.10
  301.6 3.2 %convert_element_type.46 = f32[1408,1024]{1,0:T(8,128)} convert(bf16[1408,1024]{1,0:T(8,128)(2,1)S(1)} %copy-done) | non-fusion elementwise | flops 1441792 | bytes 8650752 | tf_op jit(solution)/shard_map/convert_element_type | solution.py:1883
  304.9 0.0 copy-start.9
  304.9 0.0 copy-done.10
  304.9 1.6 convert_element_type.38
  306.5 0.0 copy-start.8
  306.5 0.0 copy-done.9
  306.5 1.6 convert_element_type.39
  308.0 0.0 copy-start.7
  308.0 0.0 copy-done.8
  308.0 1.6 convert_element_type.40
  309.6 0.0 copy-start.6
  309.6 0.0 copy-done.7
  309.6 1.6 convert_element_type.41
  311.2 0.0 copy-done.6
  311.2 1.6 convert_element_type.42
  312.8 0.0 copy-done.5
  312.8 0.0 copy-start.13
  312.8 1.6 convert_element_type.43
  314.3 0.0 copy-done.14
  314.3 0.6 slice.19
  314.9 0.6 slice_bitcast_fusion
  315.5 0.0 copy-done.11
  315.5 0.7 copy.41
  316.2 0.0 copy-done.12
  316.2 0.7 copy.42
  316.9 0.0 copy-done.13
  316.9 0.6 copy.43
  (6 shorter events, 0.0 us)
Async XLA Ops:
  92.8 197.4 %copy-start.4 = (bf16[512,512]{1,0:T(8,128)(2,1)S(1)}, bf16[512,512]{1,0:T(8,128)(2,1)}, u32[]{:S(2)}) copy-start(bf16[512,512]{1,0:T(8,128)(2,1)} %get-tuple-element.114) | copy-start | bytes 1572868
  290.2 3.4 %copy-start.3 = (bf16[2,256,2048]{2,1,0:T(8,128)(2,1)S(1)}, bf16[2,256,2048]{2,1,0:T(8,128)(2,1)}, u32[]{:S(2)}) copy-start(bf16[2,256,2048]{2,1,0:T(8,128)(2,1)} %get-tuple-element.115) | copy-start | bytes 6291460
  293.6 2.1 copy-start.2
  295.7 2.9 copy-start.1
  298.7 2.9 copy-start
  301.6 3.3 %copy-start.10 = (bf16[512,1024]{1,0:T(8,128)(2,1)S(1)}, bf16[512,1024]{1,0:T(8,128)(2,1)}, u32[]{:S(2)}) copy-start(bf16[512,1024]{1,0:T(8,128)(2,1)} %get-tuple-element.109) | copy-start | bytes 3145732
  304.9 1.6 copy-start.9
  306.5 1.6 copy-start.8
  308.0 1.6 copy-start.7
  309.6 1.6 copy-start.6
  311.2 1.6 copy-start.5
  312.7 1.6 copy-start.14
  312.8 2.8 copy-start.11
  312.8 3.5 %copy-start.12 = (bf16[128,1024]{1,0:T(8,128)(2,1)S(1)}, bf16[128,1024]{1,0:T(8,128)(2,1)}, u32[]{:S(2)}) copy-start(bf16[128,1024]{1,0:T(8,128)(2,1)} %get-tuple-element.106) | copy-start | bytes 786436
  312.8 4.2 %copy-start.13 = (bf16[16,1024]{1,0:T(8,128)(2,1)S(1)}, bf16[16,1024]{1,0:T(8,128)(2,1)}, u32[]{:S(2)}) copy-start(bf16[16,1024]{1,0:T(8,128)(2,1)} %get-tuple-element.107) | copy-start | bytes 98308

commit v7 on v6

--- a/solution.py
+++ b/solution.py
@@ -670,6 +670,9 @@
     encoder_both: Any
 
 
+M = Made(*range(23))
+
+
 class Far(NamedTuple):
     normed_three: Any
     hidden: Any
@@ -741,12 +744,13 @@
         return taken
 
     sources = take(len(W))
-    out = Made(*take(len(Made._fields)))
+    saved = Made(*take(len(Made._fields)))
     far = Far(*take(len(Far._fields)))
     lent = take(len(LENT))
     weights = take(len(W))
     own = Scratch(*take(len(Scratch._fields)))
-    (own_sem, weight_own, weight_send, weight_recv, lent_send, lent_recv, far_send, far_recv, all_own, all_send, all_recv) = refs
+    out = Made(*take(len(Made._fields)))
+    (save_sem, own_sem, weight_own, weight_send, weight_recv, lent_send, lent_recv, far_send, far_recv, all_own, all_send, all_recv) = refs
     me, core = lax.axis_index("ctx"), lax.axis_index("wsh")
     peers = lax.axis_size("ctx")
     x, y = lax.rem(me, 2), lax.rem(me // 2, 2)
@@ -787,6 +791,12 @@
             half = source.shape[1] // 2
             source = source.at[:, pl.ds(pl.multiple_of((1 - (x, y)[bit]) * half, 128), half)]
         launch(source, far[at], far_send.at[at], far_recv.at[at], me ^ (1 << bit), core)
+
+    def save(*made):
+        for at in made:
+            copy = pltpu.make_async_copy(out[at], saved[at], save_sem.at[at])
+            copy.start()
+            finish.append(copy.wait)
 
     small_sem, table_sem, encoder_sem = (len(Far._fields) + at for at in range(3))
     local = {}
@@ -881,6 +891,7 @@
     encoder_arrival = to_all(2, encoder, own.encoder_all, spread=False)
     to_pair(FAR.branch_three, cotangent, halves=True)
     to_pair(FAR.normed_one, out.normed_one)
+    save(M.normed_one, M.gain_one, M.bias_lines)
     place_bias = out.bias_lines
     pairs_arrival()
     lone_arrival()
@@ -891,6 +902,7 @@
         *attend_scratch(held_at.shape[0]),
     )
     mixed_arrival = to_all(3, own.mixed_out, own.mixed_in)
+    save(M.pairs, M.lone, M.attn_sum, M.log_norm)
 
     encoder_arrival()
     encoder_rows = jnp.concatenate([own.encoder_all[at] for at in range(peers)], axis=0)
@@ -906,10 +918,12 @@
         out.attended[:BLOCK, head_pair(pair)] = first
         out.attended[BLOCK:, head_pair(pair)] = second
     to_pair(FAR.attended, out.attended)
+    save(M.attended)
     own.after_self[...] = tokens_in[...].astype(F32) + times(out.attended[...], W.out)
     after_self = own.after_self[...]
     out.normed_two[...] = (after_self * norm_parts(after_self) * gain_two).astype(BF16)
     to_pair(FAR.normed_two, out.normed_two)
+    save(M.normed_two)
     own.cross_queries[...] = times(out.normed_two[...], W.cross_query).astype(BF16)
 
     for pair in range(peers // 2):
@@ -922,10 +936,12 @@
             mixed.append(left_contract(exact.astype(BF16), own.cross_values[:, head(at)]))
         out.cross_mixed[:, head_pair(pair)] = jnp.concatenate(mixed, axis=1).astype(BF16)
     to_pair(FAR.cross_mixed, out.cross_mixed)
+    save(M.cross_mixed)
     own.after_cross[...] = own.after_self[...] + times(out.cross_mixed[...], W.cross_out)
     after_cross = own.after_cross[...]
     out.normed_three[...] = (after_cross * norm_parts(after_cross) * gain_three).astype(BF16)
     to_pair(FAR.normed_three, out.normed_three)
+    save(M.normed_three)
 
     normed_three = out.normed_three[...]
     gate, up, down = weight(W.gate), weight(W.up), weight(W.down)
@@ -937,6 +953,7 @@
         curve = jnp.tanh(GELU_RATE * (gate_act + GELU_CUBE * gate_act * gate_act * gate_act))
         out.hidden[:, cols] = (0.5 * gate_act * (1.0 + curve) * up_act).astype(BF16)
     to_pair(FAR.hidden, out.hidden)
+    save(M.hidden)
     out.result[...] = (own.after_cross[...] + times(out.hidden[...], W.down)).astype(BF16)
 
     branch_three = cotangent[...]
@@ -957,12 +974,14 @@
         if side is not y:
             to_pair(FAR.gate, out.gate_grad, halves=True)
             to_pair(FAR.up, out.up_grad, halves=True)
+    save(M.result, M.gate_grad, M.up_grad)
     normed_grad = times_back(out.gate_grad[...], W.gate) + times_back(out.up_grad[...], W.up)
     back, gain_three_grad = norm_backward(own.after_cross[...], gain_three, normed_grad)
     out.resid_grad[...] = cotangent[...].astype(F32) + back
     out.branch_two[...] = out.resid_grad[...].astype(BF16)
 
     to_pair(FAR.branch_two, out.branch_two, halves=True)
+    save(M.branch_two)
     own.mix_grad[...] = times_back(out.branch_two[...], W.cross_out).astype(BF16)
     for pair in range(peers // 2):
         terms = []
@@ -983,11 +1002,14 @@
         values_cols = slice(width + cols.start, width + cols.stop)
         for ref, into, at in ((out.cross_q_grad, cols, 0), (out.kv_part, cols, 1), (out.kv_part, values_cols, 2)):
             ref[:, into] = jnp.concatenate([terms[0][at], terms[1][at]], axis=1).astype(BF16)
+    save(M.cross_q_grad, M.kv_part)
     normed_grad = times_back(out.cross_q_grad[...], W.cross_query)
     back, gain_two_grad = norm_backward(own.after_self[...], gain_two, normed_grad)
     out.resid_grad[...] += back
     out.branch_one[...] = out.resid_grad[...].astype(BF16)
+    save(M.resid_grad, M.branch_one)
     out.dattn[...] = times_back(out.branch_one[...], W.out).astype(BF16)
+    save(M.dattn)
 
     for half in range(2):
         for index in range(4):
@@ -995,6 +1017,7 @@
             out.gain_grads[half, index : index + 1, :] = gain_two_grad[:, cols]
             out.gain_grads[half, 4 + index : 5 + index, :] = gain_three_grad[:, cols]
         out.gain_grads[half, 8:, :] = jnp.zeros((4, 128), F32)
+    save(M.gain_grads)
 
     other_half = pl.ds(pl.multiple_of((1 - core) * (width // 2), 128), width // 2)
     for at in range(peers):
@@ -1005,6 +1028,7 @@
             far_send.at[encoder_sem], far_recv.at[encoder_sem], me, 1 - core,
         ).start()
     arrived(out.encoder_both.at[count:], far_recv.at[encoder_sem])
+    save(M.encoder_both)
     finish.append(
         lambda: remote(
             out.encoder_both.at[count:], out.encoder_both.at[count:], far_send.at[encoder_sem], own_sem, me, 1 - core
@@ -1096,10 +1120,12 @@
         layer_kernel,
         out_shape=[*outputs, *fars, *(shaped(*sources[at].shape) for at in LENT)],
         in_specs=[vmem_spec()] * 6 + [smem_spec] * 2 + [any_spec()] * len(W),
-        out_specs=[vmem_spec()] * len(outputs) + [any_spec()] * (len(fars) + len(LENT)),
+        out_specs=[any_spec()] * (len(outputs) + len(fars) + len(LENT)),
         scratch_shapes=[vmem((2 * each.shape[0], each.shape[1]), BF16) for each in sources]
         + list(buffers)
+        + [vmem(each.shape, each.dtype) for each in outputs]
         + [
+            dma((len(outputs),)),
             dma,
             dma((len(W),)),
             dma((len(W),)),

time: 324 us -> 321 us (level)
  no operation moved by 1% of the time
where the time goes in v7:
time: 321 us; the launch traced here: 315 us
  Pallas kernels  281 us (88%)
  other arithmetic  23.2 us (7%)
  matrix products  5.46 us (2%)
  local copies, waits for them, and re-layouts  4.04 us (1%)
    pallas_call x1, Pallas kernels, weight_grads(): pl.pallas_call(functools.partial(weight_grad_kernel, products, len(lefts)...  197 us
    pallas_call x1, Pallas kernels, layer(): pl.pallas_call(layer_kernel, out_shape=[*outputs, *fars, *(shaped(*source...  83.6 us
    convert_element_type x9, other arithmetic, on_device_by_heads(): member.astype(F32)  18.5 us

profile of v7, /device:TPU:0, one launch (start us, length us, event | category | flops | bytes accessed | tf_op | source)
XLA Modules:
  0.0 314.7 jit_solution(5892643323582111617)
XLA Ops:
  0.7 1.4 select_convert_fusion.small
  2.1 0.7 eq.46
  2.8 0.7 fusion.4.in_bucket.refs_31_
  3.5 1.3 select_reduce_fusion.held_at.refs_24_
  4.8 1.3 pad_convert_fusion.table
  6.1 83.6 %layer.1 = (bf16[128,1024]{1,0:T(8,128)(2,1)}, bf16[16,128,128]{2,1,0:T(8,128)(2,1)}, bf16[16,64,128]{2,1,0:T(8,128)(2,1)}, f32[64,2048]{1,0:T(8,128)}, f32[1,20...) custom-call(bf16[128,1024]{1,0:T(8,128)(2,1)} %bitcast.17, ...), custom_call_target="tpu_custom_call" | custom-call | tf_op jit(solution)/shard_map/layer/pallas_call | solution.py:1119
  89.7 0.0 copy-start.4
  89.7 197.4 %weight_grads.1 = (bf16[512,2816]{1,0:T(8,128)(2,1)}, bf16[1408,1024]{1,0:T(8,128)(2,1)}, bf16[512,2816]{1,0:T(8,128)(2,1)}, bf16[512,1024]{1,0:T(8,128)(2,1)}, ...) custom-call(bf16[128,1024]{1,0:T(8,128)(2,1)} %get-tuple-element.70., ...), custom_call_target="tpu_custom_call" | custom-call | tf_op jit(solution)/shard_map/weight_grads/pallas_call | solution.py:1728
  287.1 0.0 copy-start.3
  287.2 0.0 copy-done.4
  287.2 3.4 %fusion = f32[512,1024]{1,0:T(8,128)} fusion(bf16[512,512]{1,0:T(8,128)(2,1)S(1)} %copy-done.4, bf16[512,2048]{1,0:T(8,128)(2,1)} %bitcast.15), kind=kOutput, calls=%fused_computation | convolution fusion | flops 536870912 | bytes 3670016 | tf_op jit(solution)/shard_map/dot_general | solution.py:29
  290.6 0.0 copy-done.3
  290.6 0.0 copy-start.2
  290.6 2.0 fusion.2
  292.6 0.1 copy-done.2
  292.7 0.0 copy-start.1
  292.7 2.9 convert_element_type.44
  295.7 0.0 copy-done.1
  295.7 0.0 copy-start
  295.7 2.9 convert_element_type.45
  298.6 0.0 copy-done
  298.6 3.2 %convert_element_type.46 = f32[1408,1024]{1,0:T(8,128)} convert(bf16[1408,1024]{1,0:T(8,128)(2,1)S(1)} %copy-done) | non-fusion elementwise | flops 1441792 | bytes 8650752 | tf_op jit(solution)/shard_map/convert_element_type | solution.py:1909
  301.9 0.0 copy-start.9
  301.9 0.0 copy-done.10
  301.9 1.6 convert_element_type.38
  303.4 0.0 copy-start.8
  303.4 0.0 copy-done.9
  303.4 1.6 convert_element_type.39
  305.0 0.0 copy-start.7
  305.0 0.0 copy-done.8
  305.0 1.6 convert_element_type.40
  306.6 0.0 copy-start.6
  306.6 0.0 copy-done.7
  306.6 1.6 convert_element_type.41
  308.1 0.0 copy-done.6
  308.2 1.6 convert_element_type.42
  309.7 0.0 copy-done.5
  309.7 0.0 copy-start.13
  309.7 1.6 convert_element_type.43
  311.3 0.0 copy-done.14
  311.3 0.6 slice.19
  311.9 0.6 slice_bitcast_fusion
  312.5 0.0 copy-done.11
  312.5 0.7 copy.41
  313.2 0.0 copy-done.12
  313.2 0.7 copy.42
  313.9 0.0 copy-done.13
  313.9 0.6 copy.43
  (6 shorter events, 0.0 us)
Async XLA Ops:
  89.7 197.5 %copy-start.4 = (bf16[512,512]{1,0:T(8,128)(2,1)S(1)}, bf16[512,512]{1,0:T(8,128)(2,1)}, u32[]{:S(2)}) copy-start(bf16[512,512]{1,0:T(8,128)(2,1)} %get-tuple-element.114) | copy-start | bytes 1572868
  287.1 3.4 %copy-start.3 = (bf16[2,256,2048]{2,1,0:T(8,128)(2,1)S(1)}, bf16[2,256,2048]{2,1,0:T(8,128)(2,1)}, u32[]{:S(2)}) copy-start(bf16[2,256,2048]{2,1,0:T(8,128)(2,1)} %get-tuple-element.115) | copy-start | bytes 6291460
  290.6 2.1 copy-start.2
  292.7 2.9 copy-start.1
  295.7 2.9 copy-start
  298.6 3.3 %copy-start.10 = (bf16[512,1024]{1,0:T(8,128)(2,1)S(1)}, bf16[512,1024]{1,0:T(8,128)(2,1)}, u32[]{:S(2)}) copy-start(bf16[512,1024]{1,0:T(8,128)(2,1)} %get-tuple-element.109) | copy-start | bytes 3145732
  301.9 1.6 copy-start.9
  303.4 1.6 copy-start.8
  305.0 1.6 copy-start.7
  306.6 1.6 copy-start.6
  308.1 1.6 copy-start.5
  309.7 1.6 copy-start.14
  309.7 2.8 copy-start.11
  309.7 3.5 %copy-start.12 = (bf16[128,1024]{1,0:T(8,128)(2,1)S(1)}, bf16[128,1024]{1,0:T(8,128)(2,1)}, u32[]{:S(2)}) copy-start(bf16[128,1024]{1,0:T(8,128)(2,1)} %get-tuple-element.106) | copy-start | bytes 786436
  309.7 4.2 %copy-start.13 = (bf16[16,1024]{1,0:T(8,128)(2,1)S(1)}, bf16[16,1024]{1,0:T(8,128)(2,1)}, u32[]{:S(2)}) copy-start(bf16[16,1024]{1,0:T(8,128)(2,1)} %get-tuple-element.107) | copy-start | bytes 98308

commit v8 on v7

--- a/solution.py
+++ b/solution.py
@@ -889,12 +889,12 @@
         )
     lone_arrival = to_all(1, own.lone_out, out.lone)
     encoder_arrival = to_all(2, encoder, own.encoder_all, spread=False)
-    to_pair(FAR.branch_three, cotangent, halves=True)
-    to_pair(FAR.normed_one, out.normed_one)
     save(M.normed_one, M.gain_one, M.bias_lines)
     place_bias = out.bias_lines
     pairs_arrival()
     lone_arrival()
+    to_pair(FAR.branch_three, cotangent, halves=True)
+    to_pair(FAR.normed_one, out.normed_one)
     pl.run_scoped(
         functools.partial(
             attend, order, held_at, out.pairs, out.lone, place_bias, own.mixed_out, out.attn_sum, out.log_norm

time: 321 us -> 322 us (level)
  no operation moved by 1% of the time
where the time goes in v8:
time: 322 us; the launch traced here: 316 us
  Pallas kernels  282 us (88%)
  other arithmetic  23.2 us (7%)
  matrix products  5.46 us (2%)
  local copies, waits for them, and re-layouts  4.04 us (1%)
    pallas_call x1, Pallas kernels, weight_grads(): pl.pallas_call(functools.partial(weight_grad_kernel, products, len(lefts)...  196 us
    pallas_call x1, Pallas kernels, layer(): pl.pallas_call(layer_kernel, out_shape=[*outputs, *fars, *(shaped(*source...  86.5 us
    convert_element_type x9, other arithmetic, on_device_by_heads(): member.astype(F32)  18.5 us

profile of v8, /device:TPU:0, one launch (start us, length us, event | category | flops | bytes accessed | tf_op | source)
XLA Modules:
  0.0 316.0 jit_solution(1196553681564375616)
XLA Ops:
  0.7 1.4 select_convert_fusion.small
  2.1 0.7 eq.46
  2.8 0.7 fusion.4.in_bucket.refs_31_
  3.5 1.3 select_reduce_fusion.held_at.refs_24_
  4.8 1.3 pad_convert_fusion.table
  6.1 86.5 %layer.1 = (bf16[128,1024]{1,0:T(8,128)(2,1)}, bf16[16,128,128]{2,1,0:T(8,128)(2,1)}, bf16[16,64,128]{2,1,0:T(8,128)(2,1)}, f32[64,2048]{1,0:T(8,128)}, f32[1,20...) custom-call(bf16[128,1024]{1,0:T(8,128)(2,1)} %bitcast.17, ...), custom_call_target="tpu_custom_call" | custom-call | tf_op jit(solution)/shard_map/layer/pallas_call | solution.py:1119
  92.5 0.0 copy-start.4
  92.5 195.9 %weight_grads.1 = (bf16[512,2816]{1,0:T(8,128)(2,1)}, bf16[1408,1024]{1,0:T(8,128)(2,1)}, bf16[512,2816]{1,0:T(8,128)(2,1)}, bf16[512,1024]{1,0:T(8,128)(2,1)}, ...) custom-call(bf16[128,1024]{1,0:T(8,128)(2,1)} %get-tuple-element.70., ...), custom_call_target="tpu_custom_call" | custom-call | tf_op jit(solution)/shard_map/weight_grads/pallas_call | solution.py:1728
  288.4 0.0 copy-start.3
  288.4 0.0 copy-done.4
  288.4 3.4 %fusion = f32[512,1024]{1,0:T(8,128)} fusion(bf16[512,512]{1,0:T(8,128)(2,1)S(1)} %copy-done.4, bf16[512,2048]{1,0:T(8,128)(2,1)} %bitcast.15), kind=kOutput, calls=%fused_computation | convolution fusion | flops 536870912 | bytes 3670016 | tf_op jit(solution)/shard_map/dot_general | solution.py:29
  291.9 0.0 copy-done.3
  291.9 0.0 copy-start.2
  291.9 2.0 fusion.2
  293.9 0.1 copy-done.2
  294.0 0.0 copy-start.1
  294.0 2.9 convert_element_type.44
  296.9 0.0 copy-done.1
  296.9 0.0 copy-start
  296.9 2.9 convert_element_type.45
  299.9 0.0 copy-done
  299.9 0.0 copy-start.10
  299.9 3.2 %convert_element_type.46 = f32[1408,1024]{1,0:T(8,128)} convert(bf16[1408,1024]{1,0:T(8,128)(2,1)S(1)} %copy-done) | non-fusion elementwise | flops 1441792 | bytes 8650752 | tf_op jit(solution)/shard_map/convert_element_type | solution.py:1909
  303.1 0.0 copy-start.9
  303.1 0.0 copy-done.10
  303.1 1.6 convert_element_type.38
  304.7 0.0 copy-start.8
  304.7 0.0 copy-done.9
  304.7 1.6 convert_element_type.39
  306.3 0.0 copy-done.8
  306.3 1.6 convert_element_type.40
  307.8 0.0 copy-start.6
  307.8 0.0 copy-done.7
  307.8 1.6 convert_element_type.41
  309.4 0.0 copy-done.6
  309.4 1.6 convert_element_type.42
  311.0 0.0 copy-done.5
  311.0 0.0 copy-start.13
  311.0 1.6 convert_element_type.43
  312.6 0.0 copy-done.14
  312.6 0.6 slice.19
  313.2 0.6 slice_bitcast_fusion
  313.8 0.0 copy-done.11
  313.8 0.7 copy.41
  314.5 0.0 copy-done.12
  314.5 0.7 copy.42
  315.2 0.0 copy-done.13
  315.2 0.6 copy.43
  (6 shorter events, 0.0 us)
Async XLA Ops:
  92.5 195.9 %copy-start.4 = (bf16[512,512]{1,0:T(8,128)(2,1)S(1)}, bf16[512,512]{1,0:T(8,128)(2,1)}, u32[]{:S(2)}) copy-start(bf16[512,512]{1,0:T(8,128)(2,1)} %get-tuple-element.114) | copy-start | bytes 1572868
  288.4 3.4 %copy-start.3 = (bf16[2,256,2048]{2,1,0:T(8,128)(2,1)S(1)}, bf16[2,256,2048]{2,1,0:T(8,128)(2,1)}, u32[]{:S(2)}) copy-start(bf16[2,256,2048]{2,1,0:T(8,128)(2,1)} %get-tuple-element.115) | copy-start | bytes 6291460
  291.9 2.1 copy-start.2
  294.0 2.9 copy-start.1
  296.9 2.9 copy-start
  299.9 3.3 %copy-start.10 = (bf16[512,1024]{1,0:T(8,128)(2,1)S(1)}, bf16[512,1024]{1,0:T(8,128)(2,1)}, u32[]{:S(2)}) copy-start(bf16[512,1024]{1,0:T(8,128)(2,1)} %get-tuple-element.109) | copy-start | bytes 3145732
  303.1 1.6 copy-start.9
  304.7 1.6 copy-start.8
  306.3 1.6 copy-start.7
  307.8 1.6 copy-start.6
  309.4 1.6 copy-start.5
  311.0 1.6 copy-start.14
  311.0 2.8 copy-start.11
  311.0 3.5 %copy-start.12 = (bf16[128,1024]{1,0:T(8,128)(2,1)S(1)}, bf16[128,1024]{1,0:T(8,128)(2,1)}, u32[]{:S(2)}) copy-start(bf16[128,1024]{1,0:T(8,128)(2,1)} %get-tuple-element.106) | copy-start | bytes 786436
  311.0 4.2 %copy-start.13 = (bf16[16,1024]{1,0:T(8,128)(2,1)S(1)}, bf16[16,1024]{1,0:T(8,128)(2,1)}, u32[]{:S(2)}) copy-start(bf16[16,1024]{1,0:T(8,128)(2,1)} %get-tuple-element.107) | copy-start | bytes 98308
